TPU v7x, 32 devices: a whole 2x2x4 slice. The times are simulated.
32 devices in a mesh: grp: 2 (over y), ex: 4 (over z), lay: 2 (over x), sub: 2 (over core).
Axes of the slice: x: 2, y: 2, z: 4, core: 2. Of those that a mesh axis runs over, the one named last changes fastest.
Arguments:
- layer_inputs: bfloat16 [2, 2048, 4096], P('lay', ('grp', 'ex'), 'sub'), parts along dimension 1, may hold values from -6 to 6
- output_grads: bfloat16 [2, 2048, 4096], P('lay', ('grp', 'ex'), 'sub'), parts along dimension 1, may hold values from -0.59765625 to 0.59765625
- basis_in: bfloat16 [2, 32, 4096], P('lay', None, 'sub'), may hold values from -0.09375 to 0.09375
- basis_out: bfloat16 [2, 32, 4096], P('lay', None, 'sub'), may hold values from -0.09375 to 0.09375
- queries: bfloat16 [2, 64, 1024], P('lay', 'ex', 'sub'), may hold values from -0.1875 to 0.1875
Outputs:
- gram: float32 [4, 1024, 1024], P(('grp', 'lay'), 'ex', 'sub'), parts along dimension 0
- scores: float32 [32, 64], P(('grp', 'ex'), ('lay', 'sub')), parts along dimension 0
There are 2 independent parts, one for each index of `grp`. A program takes and returns all parts, laid end to end along the dimension named above; an argument that names none is the same for every part. Nothing has to cross between parts.
All inputs are finite; a program needn't handle non-finite values.
Results may differ from a plain program's by a relative error of at most 0.0003.
Values may be sent and summed in bfloat16 or wider, within the bound.
No kernel may reach another device: no remote copies, remote signals or barrier semaphores. Data moves between devices by JAX's collectives and lax.ppermute only.
A program may use at most 64 MiB of HBM per device.

v0:
```python
import jax
import jax.numpy as jnp
from jax import lax
from jax.sharding import PartitionSpec as P

LEN = 64


def body(layer_inputs, output_grads, basis_in, basis_out, queries):
    contract = (((1,), (1,)), ((), ()))
    proj_x = lax.dot_general(
        basis_in[0], layer_inputs[0], contract, preferred_element_type=jnp.float32
    )
    proj_g = lax.dot_general(
        basis_out[0], output_grads[0], contract, preferred_element_type=jnp.float32
    )
    proj_x, proj_g = lax.psum((proj_x, proj_g), "sub")
    basis = basis_in.shape[1]
    example_count = layer_inputs.shape[1] // LEN
    width = basis * basis
    grads = jnp.einsum(
        "ael,bel->eab",
        proj_g.reshape(basis, example_count, LEN),
        proj_x.reshape(basis, example_count, LEN),
        precision=lax.Precision.HIGHEST,
    ).reshape(example_count, width)
    half_width = width // lax.axis_size("sub")
    col_start = lax.axis_index("sub") * half_width
    own_cols = lax.dynamic_slice_in_dim(grads, col_start, half_width, 1)
    all_examples = example_count * lax.axis_size("ex")
    gram_block = lax.psum_scatter(
        jnp.dot(grads.T, own_cols, precision=lax.Precision.HIGHEST),
        "ex",
        scatter_dimension=0,
        tiled=True,
    )
    gram = (gram_block / all_examples)[None]
    partial_scores = jnp.dot(
        own_cols,
        lax.all_gather(queries[0], "ex", axis=0, tiled=True).astype(jnp.float32).T,
        precision=lax.Precision.HIGHEST,
    )
    scores = lax.psum_scatter(partial_scores, ("lay", "sub"), scatter_dimension=1, tiled=True)
    return (gram, scores)


def solution(mesh):
    in_specs = (
        P("lay", ("grp", "ex"), "sub"),
        P("lay", ("grp", "ex"), "sub"),
        P("lay", None, "sub"),
        P("lay", None, "sub"),
        P("lay", "ex", "sub"),
    )
    out_specs = (P(("grp", "lay"), "ex", "sub"), P(("grp", "ex"), ("lay", "sub")))
    return jax.shard_map(body, mesh=mesh, in_specs=in_specs, out_specs=out_specs, check_vma=False)
```

profile of v0, /device:TPU:0, one launch (start us, length us, event | category | flops | bytes accessed | tf_op | source)
XLA Modules:
  0.0 112.0 jit_solution(8337404121544575702)
XLA Ops:
  7.2 0.0 copy-start
  7.2 0.0 copy-start.1
  7.2 0.0 all-reduce.3.cloned.1.call-start
  7.2 1.2 %copy-done = bf16[1,256,2048]{2,1,0:T(8,128)(2,1)S(1)} copy-done((bf16[1,256,2048]{2,1,0:T(8,128)(2,1)S(1)}, bf16[1,256,2048]{2,1,0:T(8,128)(2,1)}, u32[]{:S(2)}) %copy-start) | copy-done | bytes 1048600
  8.4 1.3 %fusion = f32[32,256]{1,0:T(8,128)S(1)} fusion(bf16[1,256,2048]{2,1,0:T(8,128)(2,1)S(1)} %copy-done, bf16[1,32,2048]{2,1,0:T(8,128)(2,1)} %param.7), kind=kOutput, calls=%fused_computation.1 | convolution fusion | flops 33554432 | bytes 1212416 | tf_op jit(solution)/shard_map/dot_general | solution.py:11
  9.7 0.1 reshape.14
  9.8 0.6 copy.10
  10.5 1.7 %fusion.2 = f32[32,256]{1,0:T(8,128)S(1)} fusion(bf16[1,256,2048]{2,1,0:T(8,128)(2,1)} %param.6, bf16[1,32,2048]{2,1,0:T(8,128)(2,1)} %param.8), kind=kOutput, calls=%fused_computation.3 | convolution fusion | flops 33554432 | bytes 1212416 | tf_op jit(solution)/shard_map/dot_general | solution.py:14
  12.2 0.1 reshape.13
  12.3 0.6 copy.9
  12.9 0.0 all-reduce.3.cloned.1.call-update
  12.9 0.0 reduce-scatter.7.cloned.1.call-start
  13.0 0.0 copy-done.1
  13.0 14.9 %all-gather = bf16[1,64,512]{2,1,0:T(8,128)(2,1)S(1)} all-gather(bf16[1,16,512]{2,1,0:T(8,128)(2,1)S(1)} %copy-done.1), channel_id=2, replica_groups=mesh['grp'=2,'ex'=4,'lay'=2,'sub'=2] {'ex'}, dimensions={1}, use_global_device_ids=true | all-gather | bytes 81920 | tf_op jit(solution)/shard_map/all_gather | solution.py:40
  27.9 5.8 %all-reduce.3.cloned.1.call-done = (f32[32,4,64]{2,0,1:T(8,128)}, f32[32,4,64]{2,0,1:T(8,128)}) async-done(((f32[32,4,64]{2,0,1:T(8,128)}, f32[32,4,64]{2,0,1:T(8,128)}), (f32[32,4,64]{2,0,1:T(8,128)}, f32[32,4,64]{2,0,1:T(8,128)})) %all-reduce.3.cloned.1.call-update) | async-done | bytes 65552 | tf_op jit(solution)/shard_map/psum | solution.py:17
  33.8 1.1 fusion.12
  34.9 0.1 reshape.15
  35.0 0.8 convolution_bitcast_fusion
  35.8 0.0 reduce-scatter.7.cloned.1.call-update
  35.8 0.0 reduce-scatter.5.cloned.1.call-start
  35.8 3.2 %fusion.8 = f32[1024,512]{1,0:T(8,128)} fusion(f32[4,1024]{1,0:T(4,128)S(1)} %reshape.15, s32[]{:T(128)S(6)} %select_n.3), kind=kOutput, calls=%fused_computation.10 | convolution fusion | flops 25165824 | bytes 2121732 | tf_op jit(solution)/shard_map/dot_general | solution.py:32
  39.0 0.0 reduce-scatter.5.cloned.1.call-update
  39.1 18.2 %reduce-scatter.7.cloned.1.call-done = f32[16,4]{1,0:T(8,128)} async-done(((f32[64,4]{1,0:T(8,128)}), f32[16,4]{1,0:T(8,128)}) %reduce-scatter.7.cloned.1.call-update) | async-done | bytes 272
  57.3 1.3 %copy.12 = f32[4,16]{1,0:T(4,128)} copy(f32[4,16]{0,1:T(8,128)} %bitcast.23) | data formatting | bytes 512
  58.6 45.0 %reduce-scatter.5.cloned.1.call-done = f32[256,512]{1,0:T(8,128)} async-done(((f32[1024,512]{1,0:T(8,128)}), f32[256,512]{1,0:T(8,128)}) %reduce-scatter.5.cloned.1.call-update) | async-done | bytes 524304 | tf_op jit(solution)/shard_map/reduce_scatter | solution.py:31
  103.6 1.9 %multiply_bitcast_fusion = f32[1,256,512]{2,1,0:T(8,128)} fusion(f32[256,512]{1,0:T(8,128)} %reduce-scatter.5.cloned.1.call-done), kind=kLoop, calls=%fused_computation.5 | loop fusion | flops 131072 | bytes 1048576 | tf_op jit(solution)/shard_map/broadcast_in_dim | solution.py:37
Async XLA Ops:
  7.2 1.2 %copy-start = (bf16[1,256,2048]{2,1,0:T(8,128)(2,1)S(1)}, bf16[1,256,2048]{2,1,0:T(8,128)(2,1)}, u32[]{:S(2)}) copy-start(bf16[1,256,2048]{2,1,0:T(8,128)(2,1)} %param.5) | copy-start | bytes 3145732
  7.2 5.8 %copy-start.1 = (bf16[1,16,512]{2,1,0:T(8,128)(2,1)S(1)}, bf16[1,16,512]{2,1,0:T(8,128)(2,1)}, u32[]{:S(2)}) copy-start(bf16[1,16,512]{2,1,0:T(8,128)(2,1)} %param.9) | copy-start | bytes 49156
  7.2 26.6 %all-reduce.3.cloned.1.call-start = ((), (), s32[]{:S(2)}) async-start(), calls=%async_computation.4 | async-start | bytes 262144 | tf_op jit(solution)/shard_map/psum | solution.py:17
  12.9 44.4 %reduce-scatter.7.cloned.1.call-start = ((), (), s32[]{:S(2)}) async-start(), calls=%async_computation.3 | async-start | bytes 40960
  35.8 67.8 %reduce-scatter.5.cloned.1.call-start = ((), (), s32[]{:S(2)}) async-start(), calls=%async_computation.2 | async-start | bytes 2621440 | tf_op jit(solution)/shard_map/reduce_scatter | solution.py:31
Sparse Core Ops, SparseCore 0:
  13.1 20.6 all-reduce.2
  36.7 20.5 reduce-scatter.6
  59.7 43.8 reduce-scatter.4
where the time goes:
time: 112 us
  waiting for transfers between devices  69.1 us (62%)
  blocking collectives  14.9 us (13%)
  between operations  13.8 us (12%)
  matrix products  8.12 us (7%)
  local copies, waits for them, and re-layouts  4.07 us (4%)
  other arithmetic  1.87 us (2%)
    reduce_scatter x1, waiting for transfers between devices, body(): lax.psum_scatter(jnp.dot(grads.T, own_cols, precision=lax.Precision.HIGHE...  45 us
    unnamed x4, waiting for transfers between devices  18.3 us
    all_gather x1, blocking collectives, body(): lax.all_gather(queries[0], 'ex', axis=0, tiled=True).astype(jnp.float32)  14.9 us
    psum x1, waiting for transfers between devices, body(): proj_x, proj_g = lax.psum((proj_x, proj_g), 'sub')  5.84 us
    dot_general x1, matrix products, body(): jnp.dot(grads.T, own_cols, precision=lax.Precision.HIGHEST)  3.19 us
    unnamed x5, local copies, waits for them, and re-layouts  2.52 us
  transfers between devices with their start and end apart: 3, of which 3 were waited for; matrix products, arithmetic and copies ran while one was open for 4% of the time, Pallas kernels for 0%

commit v1 on v0

v1 whole, which is shorter than its diff:
```python
import jax
import jax.numpy as jnp
from jax import lax
from jax.sharding import PartitionSpec as P

LEN = 64
HIGHEST = lax.Precision.HIGHEST


def solution(mesh):
    n_ex, n_lay, n_sub = mesh.shape["ex"], mesh.shape["lay"], mesh.shape["sub"]
    n_blk = n_lay * n_sub
    per_blk = n_ex // n_blk

    def flat(ex, lay, sub):
        return (ex * n_lay + lay) * n_sub + sub

    def query_round(k):
        pairs = []
        for ex in range(n_ex):
            at = (ex + k) % n_ex
            for blk in range(n_blk):
                source = flat(blk * per_blk + at // n_blk, (at % n_blk) // n_sub, at % n_sub)
                pairs.append((source, flat(ex, blk // n_sub, blk % n_sub)))
        return pairs

    def rotate(value, axis, size, k):
        return lax.ppermute(value, axis, [((i + k) % size, i) for i in range(size)])

    def body(layer_inputs, output_grads, basis_in, basis_out, queries):
        ex, lay, sub = lax.axis_index("ex"), lax.axis_index("lay"), lax.axis_index("sub")
        got = jnp.stack([lax.ppermute(queries[0], ("ex", "lay", "sub"), query_round(k)) for k in range(n_ex)])
        got = jnp.roll(got, ex, axis=0)
        rows, half = queries.shape[1:]
        got = got.reshape(per_blk, n_lay, n_sub, rows, half).transpose(1, 0, 3, 2, 4)
        got = got.reshape(n_lay, per_blk * rows, n_sub * half).astype(jnp.float32)

        contract = (((1,), (1,)), ((), ()))
        proj_x = lax.dot_general(basis_in[0], layer_inputs[0], contract, preferred_element_type=jnp.float32)
        proj_g = lax.dot_general(basis_out[0], output_grads[0], contract, preferred_element_type=jnp.float32)
        proj = jnp.stack([proj_x, proj_g])
        total = proj
        for k in range(1, n_sub):
            total = total + rotate(proj, "sub", n_sub, k)
        basis = basis_in.shape[1]
        own = layer_inputs.shape[1] // LEN
        width = basis * basis
        total = total.reshape(2, basis, own, LEN)
        grads = jnp.einsum("ael,bel->eab", total[1], total[0], precision=HIGHEST).reshape(own, width)

        gathered = jnp.concatenate([grads] + [rotate(grads, "ex", n_ex, k) for k in range(1, n_ex)])
        scores = 0.0
        for k in range(n_lay):
            other = rotate(grads, "lay", n_lay, k) if k else grads
            here = lax.dynamic_index_in_dim(got, (lay + k) % n_lay, 0, keepdims=False)
            scores = scores + jnp.dot(other, here.T, precision=HIGHEST)
        n_rows, n_cols = width // n_ex, width // n_sub
        left = lax.dynamic_slice_in_dim(gathered, ex * n_rows, n_rows, 1)
        right = lax.dynamic_slice_in_dim(gathered, sub * n_cols, n_cols, 1)
        gram = jnp.dot(left.T, right, precision=HIGHEST) / (own * n_ex)
        return gram[None], scores

    in_specs = (
        P("lay", ("grp", "ex"), "sub"),
        P("lay", ("grp", "ex"), "sub"),
        P("lay", None, "sub"),
        P("lay", None, "sub"),
        P("lay", "ex", "sub"),
    )
    out_specs = (P(("grp", "lay"), "ex", "sub"), P(("grp", "ex"), ("lay", "sub")))
    return jax.shard_map(body, mesh=mesh, in_specs=in_specs, out_specs=out_specs, check_vma=False)
```

time: 112 us -> 25.2 us (0.23)
  waiting for transfers between devices: 69.1 us -> 2.97 us
  starting transfers between devices: 0.12 us -> 16.4 us
  blocking collectives: 14.9 us -> 0 us
  between operations: 13.8 us -> 0.83 us
  matrix products: 8.12 us -> 4.21 us
  local copies, waits for them, and re-layouts: 4.07 us -> 0.45 us
  other arithmetic: 1.87 us -> 0.05 us
    reduce_scatter x1 -> x0, waiting for transfers between devices: 45 us -> none  [body(): lax.psum_scatter(jnp.dot(grads.T, own_cols, precision=lax.Precision.HIGHE...]
    unnamed x4 -> x0, waiting for transfers between devices: 18.3 us -> none
    ppermute x0 -> x9, starting transfers between devices: none -> 16.4 us  [the longest x5 8.52 us: rotate(): return lax.ppermute(value, axis, [((i + k) % size, i) for i in range(size)])]
    all_gather x1 -> x0, blocking collectives: 14.9 us -> none  [body(): lax.all_gather(queries[0], 'ex', axis=0, tiled=True).astype(jnp.float32)]
    psum x1 -> x0, waiting for transfers between devices: 5.84 us -> none  [body(): proj_x, proj_g = lax.psum((proj_x, proj_g), 'sub')]
    ppermute x0 -> x9, waiting for transfers between devices: none -> 2.97 us  [the longest x5 2.96 us: rotate(): return lax.ppermute(value, axis, [((i + k) % size, i) for i in range(size)])]
    unnamed x5 -> x13, local copies, waits for them, and re-layouts: 2.52 us -> 0.04 us
    broadcast_in_dim x1 -> x0, other arithmetic: 1.87 us -> none  [body(): gram = (gram_block / all_examples)[None]]
  transfers between devices with their start and end apart: 3 -> 9, of which waited for: 3 -> 3; matrix products, arithmetic and copies ran while one was open for 4% -> 14% of each run, Pallas kernels for 0% -> 0%
where the time goes in v1:
time: 25.2 us; the launch traced here: 24.9 us
  starting transfers between devices  16.4 us (65%)
  matrix products  4.21 us (17%)
  waiting for transfers between devices  2.97 us (12%)
  between operations  0.83 us (3%)
  local copies, waits for them, and re-layouts  0.45 us (2%)
    ppermute x5, starting transfers between devices, rotate(): return lax.ppermute(value, axis, [((i + k) % size, i) for i in range(size)])  8.52 us
    ppermute x4, starting transfers between devices, body(): lax.ppermute(queries[0], ('ex', 'lay', 'sub'), query_round(k))  7.91 us
    ppermute x5, waiting for transfers between devices, rotate(): return lax.ppermute(value, axis, [((i + k) % size, i) for i in range(size)])  2.96 us
    dot_general x1, matrix products, body(): gram = jnp.dot(left.T, right, precision=HIGHEST) / (own * n_ex)  1.42 us
    dot_general x1, matrix products, body(): lax.dot_general(basis_in[0], layer_inputs[0], contract, preferred_element...  1.31 us
    dot_general x2, matrix products, body(): scores = scores + jnp.dot(other, here.T, precision=HIGHEST)  0.85 us
  transfers between devices with their start and end apart: 9, of which 3 were waited for; matrix products, arithmetic and copies ran while one was open for 14% of the time, Pallas kernels for 0%

profile of v1, /device:TPU:0, one launch (start us, length us, event | category | flops | bytes accessed | tf_op | source)
XLA Modules:
  0.0 24.9 jit_solution(7531575144873052153)
XLA Ops:
  0.6 0.0 copy-start
  0.6 0.0 copy-start.1
  0.7 0.0 copy-start.2
  0.7 3.1 %collective-permute-start.7 = (bf16[16,512]{1,0:T(8,128)(2,1)}, bf16[16,512]{1,0:T(8,128)(2,1)S(1)}, u32[]{:S(2)}, u32[]{:S(2)}) collective-permute-start(bf16[16,512]{1,0:T(8,128)(2,1)} %bitcast.45), channel_id=1, source_target_pairs={{3,0},{7,1},{11,2},{15,3},{0,4},{4,5},{8,6},{12,7},{1,8},{5,9},{9,... | collective-permute-start | bytes 49160 | tf_op jit(solution)/shard_map/ppermute | solution.py:32
  3.8 2.4 %collective-permute-start.6 = (bf16[16,512]{1,0:T(8,128)(2,1)}, bf16[16,512]{1,0:T(8,128)(2,1)S(1)}, u32[]{:S(2)}, u32[]{:S(2)}) collective-permute-start(bf16[16,512]{1,0:T(8,128)(2,1)} %bitcast.46), channel_id=1, source_target_pairs={{2,0},{6,1},{10,2},{14,3},{3,4},{7,5},{11,6},{15,7},{0,8},{4,9},{8... | collective-permute-start | bytes 49160 | tf_op jit(solution)/shard_map/ppermute | solution.py:32
  6.1 1.1 %collective-permute-start.5 = (bf16[16,512]{1,0:T(8,128)(2,1)}, bf16[16,512]{1,0:T(8,128)(2,1)S(1)}, u32[]{:S(2)}, u32[]{:S(2)}) collective-permute-start(bf16[16,512]{1,0:T(8,128)(2,1)} %bitcast.47), channel_id=1, source_target_pairs={{1,0},{5,1},{9,2},{13,3},{2,4},{6,5},{10,6},{14,7},{3,8},{7,9},{11... | collective-permute-start | bytes 49160 | tf_op jit(solution)/shard_map/ppermute | solution.py:32
  7.2 1.4 %collective-permute-start.4 = (bf16[16,512]{1,0:T(8,128)(2,1)}, bf16[16,512]{1,0:T(8,128)(2,1)S(1)}, u32[]{:S(2)}, u32[]{:S(2)}) collective-permute-start(bf16[16,512]{1,0:T(8,128)(2,1)} %bitcast.48), channel_id=1, source_target_pairs={{0,0},{4,1},{8,2},{12,3},{1,4},{5,5},{9,6},{13,7},{2,8},{6,9},{10,... | collective-permute-start | bytes 49160 | tf_op jit(solution)/shard_map/ppermute | solution.py:32
  8.6 0.0 copy-done
  8.6 1.3 %convolution_bitcast_fusion.1 = f32[1,32,256]{2,1,0:T(8,128)S(1)} fusion(bf16[1,256,2048]{2,1,0:T(8,128)(2,1)S(1)} %copy-done, bf16[1,32,2048]{2,1,0:T(8,128)(2,1)} %param.7), kind=kOutput, calls=%fused_computation.3 | convolution fusion | flops 33554432 | bytes 1212416 | tf_op jit(solution)/shard_map/dot_general | solution.py:39
  9.9 0.0 copy-done.1
  9.9 0.0 copy-done.2
  9.9 0.4 %convolution_bitcast_fusion = f32[1,32,256]{2,1,0:T(8,128)S(1)} fusion(bf16[1,256,2048]{2,1,0:T(8,128)(2,1)S(1)} %copy-done.1, bf16[1,32,2048]{2,1,0:T(8,128)(2,1)S(1)} %copy-done.2), kind=kOutput, calls=%fused_computation.2 | convolution fusion | flops 33554432 | bytes 1212416 | tf_op jit(solution)/shard_map/dot_general | solution.py:40
  10.4 0.6 %collective-permute-start = (f32[2,32,256]{2,1,0:T(8,128)S(1)}, f32[2,32,256]{2,1,0:T(8,128)S(1)}, u32[]{:S(2)}, u32[]{:S(2)}) collective-permute-start(f32[2,32,256]{2,1,0:T(8,128)S(1)} %pad_maximum_fusion), channel_id=1, source_target_pairs={{1,0},{0,1},{3,2},{2,3},{5,4},{4,5},{7,6},{6,7},{9,8},{8,9},{11,10... | collective-permute-start | bytes 196616 | tf_op jit(solution)/shard_map/ppermute | solution.py:28
  10.9 0.0 collective-permute-done.4
  10.9 0.0 collective-permute-done.5
  11.0 0.0 collective-permute-done.6
  11.0 0.0 collective-permute-done.7
  11.1 0.1 copy.13
  11.2 0.6 %collective-permute-done = f32[2,32,256]{2,1,0:T(8,128)S(1)} collective-permute-done((f32[2,32,256]{2,1,0:T(8,128)S(1)}, f32[2,32,256]{2,1,0:T(8,128)S(1)}, u32[]{:S(2)}, u32[]{:S(2)}) %collective-permute-start) | collective-permute-done | bytes 65568 | tf_op jit(solution)/shard_map/ppermute | solution.py:28
  11.9 0.1 squeeze.35
  12.0 0.1 squeeze.36
  12.1 0.2 fusion.5
  12.3 0.1 reshape.18
  12.4 4.1 %collective-permute-start.8 = (f32[4,1024]{1,0:T(4,128)S(1)}, f32[4,1024]{1,0:T(4,128)S(1)}, u32[]{:S(2)}, u32[]{:S(2)}) collective-permute-start(f32[4,1024]{1,0:T(4,128)S(1)} %reshape.18), channel_id=1, source_target_pairs={{2,0},{0,2},{3,1},{1,3},{6,4},{4,6},{7,5},{5,7},{10,8},{8,10},{11,... | collective-permute-start | bytes 49160 | tf_op jit(solution)/shard_map/ppermute | solution.py:28
  16.5 0.5 %collective-permute-start.3 = (f32[4,1024]{1,0:T(4,128)S(1)}, f32[4,1024]{1,0:T(4,128)S(1)}, u32[]{:S(2)}, u32[]{:S(2)}) collective-permute-start(f32[4,1024]{1,0:T(4,128)S(1)} %reshape.18), channel_id=1, source_target_pairs={{12,0},{0,4},{4,8},{8,12},{13,1},{1,5},{5,9},{9,13},{14,2},{2,6},{... | collective-permute-start | bytes 49160 | tf_op jit(solution)/shard_map/ppermute | solution.py:28
  17.0 1.6 %collective-permute-start.2 = (f32[4,1024]{1,0:T(4,128)S(1)}, f32[4,1024]{1,0:T(4,128)S(1)}, u32[]{:S(2)}, u32[]{:S(2)}) collective-permute-start(f32[4,1024]{1,0:T(4,128)S(1)} %reshape.18), channel_id=1, source_target_pairs={{8,0},{12,4},{0,8},{4,12},{9,1},{13,5},{1,9},{5,13},{10,2},{14,6},... | collective-permute-start | bytes 49160 | tf_op jit(solution)/shard_map/ppermute | solution.py:28
  18.5 1.8 %collective-permute-start.1 = (f32[4,1024]{1,0:T(4,128)S(1)}, f32[4,1024]{1,0:T(4,128)S(1)}, u32[]{:S(2)}, u32[]{:S(2)}) collective-permute-start(f32[4,1024]{1,0:T(4,128)S(1)} %reshape.18), channel_id=1, source_target_pairs={{4,0},{8,4},{12,8},{0,12},{5,1},{9,5},{13,9},{1,13},{6,2},{10,6},{... | collective-permute-start | bytes 49160 | tf_op jit(solution)/shard_map/ppermute | solution.py:28
  20.3 0.1 fusion.9
  20.4 1.6 %collective-permute-done.3 = f32[4,1024]{1,0:T(4,128)S(1)} collective-permute-done((f32[4,1024]{1,0:T(4,128)S(1)}, f32[4,1024]{1,0:T(4,128)S(1)}, u32[]{:S(2)}, u32[]{:S(2)}) %collective-permute-start.3) | collective-permute-done | bytes 16416 | tf_op jit(solution)/shard_map/ppermute | solution.py:28
  22.0 0.0 collective-permute-done.2
  22.0 0.7 %collective-permute-done.1 = f32[4,1024]{1,0:T(4,128)S(1)} collective-permute-done((f32[4,1024]{1,0:T(4,128)S(1)}, f32[4,1024]{1,0:T(4,128)S(1)}, u32[]{:S(2)}, u32[]{:S(2)}) %collective-permute-start.1) | collective-permute-done | bytes 16416 | tf_op jit(solution)/shard_map/ppermute | solution.py:28
  22.8 1.4 %fusion = f32[1,256,512]{2,1,0:T(8,128)} fusion(f32[16,1024]{1,0:T(8,128)S(1)} %pad_maximum_fusion.1, s32[]{:T(128)S(6)} %select_n.37, s32[]{:T(128)S(6)} %select_n.36), kind=kOutput, calls=%fused_computation.1 | convolution fusion | flops 25296896 | bytes 573448 | tf_op jit(solution)/shard_map/dot_general | solution.py:60
  24.2 0.0 collective-permute-done.8
  24.2 0.7 %convolution_add_fusion = f32[4,16]{1,0:T(4,128)} fusion(f32[4,16]{1,0:T(4,128)S(1)} %fusion.9, f32[4,1024]{1,0:T(4,128)S(1)} %collective-permute-done.8, bf16[2,16,1024]{2,1,0:T(8,128)(2,1)S(1)} %reshape.20, s32[]{:T(128)S(6)} %select_n.43), kind=kOutput, calls=%fused_computation.4 | convolution fusion | flops 786496 | bytes 51460 | tf_op jit(solution)/shard_map/dot_general | solution.py:56
  (14 shorter events, 0.1 us)
Async XLA Ops:
  0.6 7.9 %copy-start = (bf16[1,256,2048]{2,1,0:T(8,128)(2,1)S(1)}, bf16[1,256,2048]{2,1,0:T(8,128)(2,1)}, u32[]{:S(2)}) copy-start(bf16[1,256,2048]{2,1,0:T(8,128)(2,1)} %param.5) | copy-start | bytes 3145732
  0.6 9.3 %copy-start.1 = (bf16[1,256,2048]{2,1,0:T(8,128)(2,1)S(1)}, bf16[1,256,2048]{2,1,0:T(8,128)(2,1)}, u32[]{:S(2)}) copy-start(bf16[1,256,2048]{2,1,0:T(8,128)(2,1)} %param.6) | copy-start | bytes 3145732
  0.7 9.3 %copy-start.2 = (bf16[1,32,2048]{2,1,0:T(8,128)(2,1)S(1)}, bf16[1,32,2048]{2,1,0:T(8,128)(2,1)}, u32[]{:S(2)}) copy-start(bf16[1,32,2048]{2,1,0:T(8,128)(2,1)} %param.8) | copy-start | bytes 393220
  0.7 10.3 %collective-permute-start.7 = (bf16[16,512]{1,0:T(8,128)(2,1)}, bf16[16,512]{1,0:T(8,128)(2,1)S(1)}, u32[]{:S(2)}, u32[]{:S(2)}) collective-permute-start(bf16[16,512]{1,0:T(8,128)(2,1)} %bitcast.45), channel_id=1, source_target_pairs={{3,0},{7,1},{11,2},{15,3},{0,4},{4,5},{8,6},{12,7},{1,8},{5,9},{9,... | collective-permute-start | bytes 49160 | tf_op jit(solution)/shard_map/ppermute | solution.py:32
  3.8 7.2 %collective-permute-start.6 = (bf16[16,512]{1,0:T(8,128)(2,1)}, bf16[16,512]{1,0:T(8,128)(2,1)S(1)}, u32[]{:S(2)}, u32[]{:S(2)}) collective-permute-start(bf16[16,512]{1,0:T(8,128)(2,1)} %bitcast.46), channel_id=1, source_target_pairs={{2,0},{6,1},{10,2},{14,3},{3,4},{7,5},{11,6},{15,7},{0,8},{4,9},{8... | collective-permute-start | bytes 49160 | tf_op jit(solution)/shard_map/ppermute | solution.py:32
  6.1 4.8 %collective-permute-start.5 = (bf16[16,512]{1,0:T(8,128)(2,1)}, bf16[16,512]{1,0:T(8,128)(2,1)S(1)}, u32[]{:S(2)}, u32[]{:S(2)}) collective-permute-start(bf16[16,512]{1,0:T(8,128)(2,1)} %bitcast.47), channel_id=1, source_target_pairs={{1,0},{5,1},{9,2},{13,3},{2,4},{6,5},{10,6},{14,7},{3,8},{7,9},{11... | collective-permute-start | bytes 49160 | tf_op jit(solution)/shard_map/ppermute | solution.py:32
  7.2 3.7 %collective-permute-start.4 = (bf16[16,512]{1,0:T(8,128)(2,1)}, bf16[16,512]{1,0:T(8,128)(2,1)S(1)}, u32[]{:S(2)}, u32[]{:S(2)}) collective-permute-start(bf16[16,512]{1,0:T(8,128)(2,1)} %bitcast.48), channel_id=1, source_target_pairs={{0,0},{4,1},{8,2},{12,3},{1,4},{5,5},{9,6},{13,7},{2,8},{6,9},{10,... | collective-permute-start | bytes 49160 | tf_op jit(solution)/shard_map/ppermute | solution.py:32
  10.4 1.5 %collective-permute-start = (f32[2,32,256]{2,1,0:T(8,128)S(1)}, f32[2,32,256]{2,1,0:T(8,128)S(1)}, u32[]{:S(2)}, u32[]{:S(2)}) collective-permute-start(f32[2,32,256]{2,1,0:T(8,128)S(1)} %pad_maximum_fusion), channel_id=1, source_target_pairs={{1,0},{0,1},{3,2},{2,3},{5,4},{4,5},{7,6},{6,7},{9,8},{8,9},{11,10... | collective-permute-start | bytes 196616 | tf_op jit(solution)/shard_map/ppermute | solution.py:28
  12.4 11.8 %collective-permute-start.8 = (f32[4,1024]{1,0:T(4,128)S(1)}, f32[4,1024]{1,0:T(4,128)S(1)}, u32[]{:S(2)}, u32[]{:S(2)}) collective-permute-start(f32[4,1024]{1,0:T(4,128)S(1)} %reshape.18), channel_id=1, source_target_pairs={{2,0},{0,2},{3,1},{1,3},{6,4},{4,6},{7,5},{5,7},{10,8},{8,10},{11,... | collective-permute-start | bytes 49160 | tf_op jit(solution)/shard_map/ppermute | solution.py:28
  16.5 5.5 %collective-permute-start.3 = (f32[4,1024]{1,0:T(4,128)S(1)}, f32[4,1024]{1,0:T(4,128)S(1)}, u32[]{:S(2)}, u32[]{:S(2)}) collective-permute-start(f32[4,1024]{1,0:T(4,128)S(1)} %reshape.18), channel_id=1, source_target_pairs={{12,0},{0,4},{4,8},{8,12},{13,1},{1,5},{5,9},{9,13},{14,2},{2,6},{... | collective-permute-start | bytes 49160 | tf_op jit(solution)/shard_map/ppermute | solution.py:28
  17.0 5.1 %collective-permute-start.2 = (f32[4,1024]{1,0:T(4,128)S(1)}, f32[4,1024]{1,0:T(4,128)S(1)}, u32[]{:S(2)}, u32[]{:S(2)}) collective-permute-start(f32[4,1024]{1,0:T(4,128)S(1)} %reshape.18), channel_id=1, source_target_pairs={{8,0},{12,4},{0,8},{4,12},{9,1},{13,5},{1,9},{5,13},{10,2},{14,6},... | collective-permute-start | bytes 49160 | tf_op jit(solution)/shard_map/ppermute | solution.py:28
  18.5 4.2 %collective-permute-start.1 = (f32[4,1024]{1,0:T(4,128)S(1)}, f32[4,1024]{1,0:T(4,128)S(1)}, u32[]{:S(2)}, u32[]{:S(2)}) collective-permute-start(f32[4,1024]{1,0:T(4,128)S(1)} %reshape.18), channel_id=1, source_target_pairs={{4,0},{8,4},{12,8},{0,12},{5,1},{9,5},{13,9},{1,13},{6,2},{10,6},{... | collective-permute-start | bytes 49160 | tf_op jit(solution)/shard_map/ppermute | solution.py:28

commit v2 on v1

v2 whole, which is shorter than its diff:
```python
import jax
import jax.numpy as jnp
from jax import lax
from jax.sharding import PartitionSpec as P

LEN = 64
HIGHEST = lax.Precision.HIGHEST


def solution(mesh):
    n_ex, n_lay, n_sub = mesh.shape["ex"], mesh.shape["lay"], mesh.shape["sub"]

    def to_all(value, axes):
        return lax.all_to_all(value, axes, 0, 0, tiled=False)

    def body(layer_inputs, output_grads, basis_in, basis_out, queries):
        ex, sub = lax.axis_index("ex"), lax.axis_index("sub")
        contract = (((1,), (1,)), ((), ()))
        proj_x = lax.dot_general(basis_in[0], layer_inputs[0], contract, preferred_element_type=jnp.float32)
        proj_g = lax.dot_general(basis_out[0], output_grads[0], contract, preferred_element_type=jnp.float32)
        proj = jnp.stack([proj_x, proj_g])
        total = proj
        for k in range(1, n_sub):
            total = total + lax.ppermute(proj, "sub", [((i + k) % n_sub, i) for i in range(n_sub)])
        basis = basis_in.shape[1]
        own = layer_inputs.shape[1] // LEN
        width = basis * basis
        n_rows, n_cols = width // n_ex, width // n_sub
        total = total.reshape(2, basis, own, LEN)
        grads = jnp.einsum("ael,bel->eab", total[1], total[0], precision=HIGHEST).reshape(own, width)
        rounded = lax.reduce_precision(grads, 8, 7)
        high = rounded.astype(jnp.bfloat16)
        low = (grads - rounded).astype(jnp.bfloat16)

        rows = queries.shape[1]
        sent = jnp.concatenate([high, low, queries[0].reshape(-1, width)])
        got = to_all(jnp.broadcast_to(sent, (n_ex, *sent.shape)), "ex")
        all_queries = got[:, 2 * own :].reshape(n_ex * rows, n_cols)
        own_cols = lax.dynamic_slice_in_dim(grads, sub * n_cols, n_cols, 1)
        partial = jnp.dot(own_cols, all_queries.astype(jnp.float32).T, precision=HIGHEST)
        partial = partial.reshape(own, n_lay * n_sub, -1).swapaxes(0, 1)
        scores = to_all(partial, ("lay", "sub")).sum(0)

        high = got[:, :own].reshape(-1, width)
        low = got[:, own : 2 * own].reshape(-1, width)
        left = lax.dynamic_slice_in_dim(jnp.concatenate([high, low, high]), ex * n_rows, n_rows, 1)
        right = lax.dynamic_slice_in_dim(jnp.concatenate([high, high, low]), sub * n_cols, n_cols, 1)
        gram = jnp.dot(left.T, right, preferred_element_type=jnp.float32) / (own * n_ex)
        return gram[None], scores

    in_specs = (
        P("lay", ("grp", "ex"), "sub"),
        P("lay", ("grp", "ex"), "sub"),
        P("lay", None, "sub"),
        P("lay", None, "sub"),
        P("lay", "ex", "sub"),
    )
    out_specs = (P(("grp", "lay"), "ex", "sub"), P(("grp", "ex"), ("lay", "sub")))
    return jax.shard_map(body, mesh=mesh, in_specs=in_specs, out_specs=out_specs, check_vma=False)
```

time: 25.2 us -> 27.8 us (1.10)
  waiting for transfers between devices: 2.97 us -> 9.64 us
  starting transfers between devices: 16.4 us -> 9.95 us
  local copies, waits for them, and re-layouts: 0.45 us -> 2.46 us
  other arithmetic: 0.05 us -> 0.64 us
    ppermute x9 -> x1, starting transfers between devices: 16.4 us -> 0.52 us  [body(): lax.ppermute(proj, 'sub', [((i + k) % n_sub, i) for i in range(n_sub)])]
    all_to_all x0 -> x2, starting transfers between devices: none -> 9.44 us  [to_all(): return lax.all_to_all(value, axes, 0, 0, tiled=False)]
    all_to_all x0 -> x2, waiting for transfers between devices: none -> 8.93 us  [to_all(): return lax.all_to_all(value, axes, 0, 0, tiled=False)]
    ppermute x9 -> x1, waiting for transfers between devices: 2.97 us -> 0.71 us  [body(): lax.ppermute(proj, 'sub', [((i + k) % n_sub, i) for i in range(n_sub)])]
    unnamed x13 -> x8, local copies, waits for them, and re-layouts: 0.04 us -> 1.41 us
    broadcast_in_dim x0 -> x1, local copies, waits for them, and re-layouts: none -> 0.66 us  [body(): got = to_all(jnp.broadcast_to(sent, (n_ex, *sent.shape)), 'ex')]
    reduce_sum x0 -> x1, other arithmetic: none -> 0.59 us  [body(): scores = to_all(partial, ('lay', 'sub')).sum(0)]
    dot_general x3 -> x2, matrix products: 2.27 us -> 2.01 us  [the longest x1 1.06 us: body(): jnp.dot(left.T, right, preferred_element_type=jnp.float32) / (own * n_ex)]
  transfers between devices with their start and end apart: 9 -> 3, of which waited for: 3 -> 3; matrix products, arithmetic and copies ran while one was open for 14% -> 4% of each run, Pallas kernels for 0% -> 0%
where the time goes in v2:
time: 27.8 us; the launch traced here: 27.4 us
  starting transfers between devices  9.95 us (36%)
  waiting for transfers between devices  9.64 us (35%)
  matrix products  3.94 us (14%)
  local copies, waits for them, and re-layouts  2.46 us (9%)
  between operations  0.79 us (3%)
  other arithmetic  0.64 us (2%)
    all_to_all x2, starting transfers between devices, to_all(): return lax.all_to_all(value, axes, 0, 0, tiled=False)  9.44 us
    all_to_all x2, waiting for transfers between devices, to_all(): return lax.all_to_all(value, axes, 0, 0, tiled=False)  8.93 us
    unnamed x8, local copies, waits for them, and re-layouts  1.41 us
    dot_general x1, matrix products, body(): lax.dot_general(basis_in[0], layer_inputs[0], contract, preferred_element...  1.31 us
    dot_general x1, matrix products, body(): jnp.dot(left.T, right, preferred_element_type=jnp.float32) / (own * n_ex)  1.06 us
    dot_general x1, matrix products, body(): jnp.dot(own_cols, all_queries.astype(jnp.float32).T, precision=HIGHEST)  0.95 us
    ppermute x1, waiting for transfers between devices, body(): lax.ppermute(proj, 'sub', [((i + k) % n_sub, i) for i in range(n_sub)])  0.71 us
    broadcast_in_dim x1, local copies, waits for them, and re-layouts, body(): got = to_all(jnp.broadcast_to(sent, (n_ex, *sent.shape)), 'ex')  0.66 us
  transfers between devices with their start and end apart: 3, of which 3 were waited for; matrix products, arithmetic and copies ran while one was open for 4% of the time, Pallas kernels for 0%

profile of v2, /device:TPU:0, one launch (start us, length us, event | category | flops | bytes accessed | tf_op | source)
XLA Modules:
  0.0 27.4 jit_solution(11772855983233679851)
XLA Ops:
  0.6 0.0 copy-start
  0.6 0.0 copy-start.2
  0.7 0.0 copy-start.1
  0.7 1.2 %copy-done = bf16[1,256,2048]{2,1,0:T(8,128)(2,1)S(1)} copy-done((bf16[1,256,2048]{2,1,0:T(8,128)(2,1)S(1)}, bf16[1,256,2048]{2,1,0:T(8,128)(2,1)}, u32[]{:S(2)}) %copy-start) | copy-done | bytes 1048600
  1.9 1.3 %convolution_bitcast_fusion.1 = f32[1,32,256]{2,1,0:T(8,128)S(1)} fusion(bf16[1,256,2048]{2,1,0:T(8,128)(2,1)S(1)} %copy-done, bf16[1,32,2048]{2,1,0:T(8,128)(2,1)} %param.7), kind=kOutput, calls=%fused_computation.3 | convolution fusion | flops 33554432 | bytes 1212416 | tf_op jit(solution)/shard_map/dot_general | solution.py:19
  3.2 0.0 copy-done.2
  3.2 0.0 copy-done.1
  3.2 0.4 %convolution_bitcast_fusion = f32[1,32,256]{2,1,0:T(8,128)S(1)} fusion(bf16[1,256,2048]{2,1,0:T(8,128)(2,1)S(1)} %copy-done.1, bf16[1,32,2048]{2,1,0:T(8,128)(2,1)S(1)} %copy-done.2), kind=kOutput, calls=%fused_computation.2 | convolution fusion | flops 33554432 | bytes 1212416 | tf_op jit(solution)/shard_map/dot_general | solution.py:20
  3.6 0.0 copy-start.3
  3.7 0.5 %collective-permute-start = (f32[2,32,256]{2,1,0:T(8,128)S(1)}, f32[2,32,256]{2,1,0:T(8,128)S(1)}, u32[]{:S(2)}, u32[]{:S(2)}) collective-permute-start(f32[2,32,256]{2,1,0:T(8,128)S(1)} %pad_maximum_fusion), channel_id=1, source_target_pairs={{1,0},{0,1},{3,2},{2,3},{5,4},{4,5},{7,6},{6,7},{9,8},{8,9},{11,10... | collective-permute-start | bytes 196616 | tf_op jit(solution)/shard_map/ppermute | solution.py:24
  4.2 0.2 copy-done.3
  4.4 0.7 %collective-permute-done = f32[2,32,256]{2,1,0:T(8,128)S(1)} collective-permute-done((f32[2,32,256]{2,1,0:T(8,128)S(1)}, f32[2,32,256]{2,1,0:T(8,128)S(1)}, u32[]{:S(2)}, u32[]{:S(2)}) %collective-permute-start) | collective-permute-done | bytes 65568 | tf_op jit(solution)/shard_map/ppermute | solution.py:24
  5.1 0.1 squeeze.22
  5.2 0.1 squeeze.23
  5.3 0.2 fusion.5
  5.5 0.1 reshape.22
  5.7 0.7 %broadcast_in_dim.6 = bf16[4,16,1024]{2,1,0:T(8,128)(2,1)} broadcast(bf16[16,1024]{1,0:T(8,128)(2,1)S(1)} %pad_maximum_fusion.1), dimensions={1,2} | broadcast | bytes 163840 | tf_op jit(solution)/shard_map/broadcast_in_dim | solution.py:37
  6.3 6.2 %all-to-all-start = ((bf16[4,16,1024]{2,1,0:T(8,128)(2,1)}), bf16[4,16,1024]{2,1,0:T(8,128)(2,1)S(1)}, u32[]{:S(2)}, u32[]{:S(2)}) async-start(bf16[4,16,1024]{2,1,0:T(8,128)(2,1)} %broadcast_in_dim.6), calls=%async_computation | async-start | bytes 262144 | tf_op jit(solution)/shard_map/all_to_all | solution.py:14
  12.5 6.2 %all-to-all-done = bf16[4,16,1024]{2,1,0:T(8,128)(2,1)S(1)} async-done(((bf16[4,16,1024]{2,1,0:T(8,128)(2,1)}), bf16[4,16,1024]{2,1,0:T(8,128)(2,1)S(1)}, u32[]{:S(2)}, u32[]{:S(2)}) %all-to-all-start) | async-done | bytes 131104 | tf_op jit(solution)/shard_map/all_to_all | solution.py:14
  18.9 0.9 %convolution_bitcast_fusion.2 = f32[4,4,16]{2,1,0:T(4,128)} fusion(bf16[4,16,512]{2,1,0:T(8,128)(2,1)S(1)} %dot_general.21, f32[4,1024]{1,0:T(4,128)S(1)} %reshape.22, s32[]{:T(128)S(6)} %select_n.8), kind=kOutput, calls=%fused_computation.4 | convolution fusion | flops 1572864 | bytes 74756 | tf_op jit(solution)/shard_map/dot_general | solution.py:40
  19.8 3.2 %all-to-all-start.1 = ((f32[4,4,16]{2,1,0:T(4,128)}), f32[4,4,16]{2,1,0:T(4,128)S(1)}, u32[]{:S(2)}, u32[]{:S(2)}) async-start(f32[4,4,16]{2,1,0:T(4,128)} %convolution_bitcast_fusion.2), calls=%async_computation.1 | async-start | bytes 16384 | tf_op jit(solution)/shard_map/all_to_all | solution.py:14
  23.1 1.1 %fusion = f32[1,256,512]{2,1,0:T(8,128)} fusion(s32[]{:T(128)S(6)} %select_n.8, bf16[16,1024]{1,0:T(8,128)(2,1)S(1)} %reshape.23, bf16[16,1024]{1,0:T(8,128)(2,1)S(1)} %reshape.24, s32[]{:T(128)S(6)} %select_n.7), kind=kOutput, calls=%fused_computation.1 | convolution fusion | flops 12935168 | bytes 655368 | tf_op jit(solution)/shard_map/dot_general | solution.py:48
  24.1 2.7 %all-to-all-done.1 = f32[4,4,16]{2,1,0:T(4,128)S(1)} async-done(((f32[4,4,16]{2,1,0:T(4,128)}), f32[4,4,16]{2,1,0:T(4,128)S(1)}, u32[]{:S(2)}, u32[]{:S(2)}) %all-to-all-start.1) | async-done | bytes 1056 | tf_op jit(solution)/shard_map/all_to_all | solution.py:14
  26.8 0.6 %reduce_sum.9 = f32[4,16]{1,0:T(4,128)} reduce(f32[4,4,16]{2,1,0:T(4,128)S(1)} %all-to-all-done.1, f32[]{:T(128)} %constant.21.clone.1), dimensions={0}, to_apply=%region_0.0 | reduce | flops 192 | bytes 1284 | tf_op jit(solution)/shard_map/reduce_sum | solution.py:42
  (11 shorter events, 0.2 us)
Async XLA Ops:
  0.6 1.2 %copy-start = (bf16[1,256,2048]{2,1,0:T(8,128)(2,1)S(1)}, bf16[1,256,2048]{2,1,0:T(8,128)(2,1)}, u32[]{:S(2)}) copy-start(bf16[1,256,2048]{2,1,0:T(8,128)(2,1)} %param.5) | copy-start | bytes 3145732
  0.6 2.5 %copy-start.2 = (bf16[1,32,2048]{2,1,0:T(8,128)(2,1)S(1)}, bf16[1,32,2048]{2,1,0:T(8,128)(2,1)}, u32[]{:S(2)}) copy-start(bf16[1,32,2048]{2,1,0:T(8,128)(2,1)} %param.8) | copy-start | bytes 393220
  0.7 2.5 %copy-start.1 = (bf16[1,256,2048]{2,1,0:T(8,128)(2,1)S(1)}, bf16[1,256,2048]{2,1,0:T(8,128)(2,1)}, u32[]{:S(2)}) copy-start(bf16[1,256,2048]{2,1,0:T(8,128)(2,1)} %param.6) | copy-start | bytes 3145732
  3.6 0.7 %copy-start.3 = (bf16[1,16,512]{2,1,0:T(8,128)(2,1)S(1)}, bf16[1,16,512]{2,1,0:T(8,128)(2,1)}, u32[]{:S(2)}) copy-start(bf16[1,16,512]{2,1,0:T(8,128)(2,1)} %param.9) | copy-start | bytes 49156
  3.7 1.4 %collective-permute-start = (f32[2,32,256]{2,1,0:T(8,128)S(1)}, f32[2,32,256]{2,1,0:T(8,128)S(1)}, u32[]{:S(2)}, u32[]{:S(2)}) collective-permute-start(f32[2,32,256]{2,1,0:T(8,128)S(1)} %pad_maximum_fusion), channel_id=1, source_target_pairs={{1,0},{0,1},{3,2},{2,3},{5,4},{4,5},{7,6},{6,7},{9,8},{8,9},{11,10... | collective-permute-start | bytes 196616 | tf_op jit(solution)/shard_map/ppermute | solution.py:24
  6.3 12.5 %all-to-all-start = ((bf16[4,16,1024]{2,1,0:T(8,128)(2,1)}), bf16[4,16,1024]{2,1,0:T(8,128)(2,1)S(1)}, u32[]{:S(2)}, u32[]{:S(2)}) async-start(bf16[4,16,1024]{2,1,0:T(8,128)(2,1)} %broadcast_in_dim.6), calls=%async_computation | async-start | bytes 262144 | tf_op jit(solution)/shard_map/all_to_all | solution.py:14
  19.8 7.0 %all-to-all-start.1 = ((f32[4,4,16]{2,1,0:T(4,128)}), f32[4,4,16]{2,1,0:T(4,128)S(1)}, u32[]{:S(2)}, u32[]{:S(2)}) async-start(f32[4,4,16]{2,1,0:T(4,128)} %convolution_bitcast_fusion.2), calls=%async_computation.1 | async-start | bytes 16384 | tf_op jit(solution)/shard_map/all_to_all | solution.py:14

commit v3 on v2

v3 whole, which is shorter than its diff:
```python
import functools

import jax
import jax.numpy as jnp
from jax import lax
from jax.experimental import pallas as pl
from jax.experimental.pallas import tpu as pltpu
from jax.sharding import PartitionSpec as P

LEN = 64
CHUNKS = 4
F32, BF16 = jnp.float32, jnp.bfloat16
VMEM = pl.BlockSpec(memory_space=pltpu.VMEM)
ANY = pl.BlockSpec(memory_space=pl.ANY)
LAST = (((1,), (1,)), ((), ()))
FIRST = (((0,), (0,)), ((), ()))


def project_kernel(x_ref, g_ref, bi_ref, bo_ref, out_ref, x_buf, g_buf, bi_buf, bo_buf, sems):
    step = x_buf.shape[2]
    copies = [
        pltpu.make_async_copy(bi_ref.at[0], bi_buf, sems.at[0]),
        pltpu.make_async_copy(bo_ref.at[0], bo_buf, sems.at[1]),
    ]
    for k in range(CHUNKS):
        cols = pl.ds(k * step, step)
        copies.append(pltpu.make_async_copy(x_ref.at[0, :, cols], x_buf.at[k], sems.at[2 + 2 * k]))
        copies.append(pltpu.make_async_copy(g_ref.at[0, :, cols], g_buf.at[k], sems.at[3 + 2 * k]))
    for copy in copies:
        copy.start()
    copies[0].wait()
    copies[1].wait()
    total = None
    for k in range(CHUNKS):
        cols = pl.ds(k * step, step)
        bi, bo = bi_buf[:, cols], bo_buf[:, cols]
        none = jnp.zeros_like(bi)
        copies[2 + 2 * k].wait()
        part = lax.dot_general(x_buf[k], jnp.concatenate([bi, none, bi, none]), LAST, preferred_element_type=F32)
        total = part if total is None else total + part
        copies[3 + 2 * k].wait()
        total += lax.dot_general(g_buf[k], jnp.concatenate([none, bo, none, bo]), LAST, preferred_element_type=F32)
    out_ref[...] = total


def grads_kernel(basis, n_sub, *refs):
    parts, q_ref, out_ref, own_ref = refs[:n_sub], refs[n_sub], refs[n_sub + 1], refs[n_sub + 2]
    total = parts[0][...]
    for part in parts[1:]:
        total += part[...]
    tokens, lanes = total.shape
    pair = 2 * basis
    high = total.astype(BF16).astype(F32)
    rest = total - high
    mid = rest.astype(BF16).astype(F32)
    low = rest - mid
    first = lax.broadcasted_iota(jnp.int32, (tokens, lanes), 1) < pair
    pieces = jnp.concatenate([jnp.where(first, high, mid), jnp.where(first, low, 0.0)], axis=1).astype(BF16)

    row = lax.broadcasted_iota(jnp.int32, (2 * lanes, lanes), 0) % pair
    col = lax.broadcasted_iota(jnp.int32, (2 * lanes, lanes), 1)
    pick_x = jnp.where(row == col % basis, 1.0, 0.0).astype(BF16)
    tiled_x = jnp.dot(pieces, pick_x, preferred_element_type=F32)
    gap = row - basis - col // basis
    own = tokens // LEN
    tiles = []
    for j in range(basis * basis // lanes):
        pick_g = jnp.where(gap == j * (lanes // basis), 1.0, 0.0).astype(BF16)
        product = jnp.dot(pieces, pick_g, preferred_element_type=F32) * tiled_x
        tiles.append(product.reshape(own, LEN, lanes).sum(axis=1))
    grads = jnp.concatenate(tiles, axis=1)
    high = grads.astype(BF16).astype(F32)
    low = grads - high
    half = grads.shape[1] // n_sub
    rows = []
    for h in range(n_sub):
        cols = slice(h * half, (h + 1) * half)
        rows += [high[:, cols], low[:, cols]]
    packed = jnp.concatenate(rows, axis=0).astype(BF16)
    own_ref[...] = packed
    out_ref[0, : packed.shape[0], :] = packed
    out_ref[0, packed.shape[0] :, :] = q_ref[...]


def final_kernel(n_ex, n_lay, n_sub, own, order, *refs):
    others, gots = refs[: n_lay - 1], refs[n_lay - 1 : -2]
    gram_ref, scores_ref = refs[-2:]
    ex, lay, sub = lax.axis_index("ex"), lax.axis_index("lay"), lax.axis_index("sub")
    n_blk = n_lay * n_sub
    per_blk = n_ex // n_blk
    used = 2 * own * n_sub
    half = gots[0].shape[2]
    n_rows, per_half = half * n_sub // n_ex, n_ex // n_sub
    places = [(got, at) for got in gots for at in range(got.shape[0])]

    def halves_of(pieces):
        pieces = pieces.astype(F32)
        return [pieces[h * 2 * own : (h + 1) * 2 * own] for h in range(n_sub)]

    layers = [halves_of(gots[0][0, :used, :])] + [halves_of(other[...]) for other in others]
    blocks = [0.0] * per_blk
    for (got, at), slot in zip(places, order):
        source = slot ^ ex
        l, h = source % n_blk // n_sub, source % n_sub
        grads = layers[0][0]
        for k in range(n_lay):
            for i in range(n_sub):
                grads = jnp.where(((lay + k) % n_lay == l) & (h == i), layers[k][i], grads)
        part = lax.dot_general(grads.astype(BF16), got[at, used:, :], LAST, preferred_element_type=F32)
        part = part[:own] + part[own:]
        for j in range(per_blk):
            blocks[j] += part if per_blk == 1 else jnp.where(source // n_blk == j, part, 0.0)
    scores_ref[...] = blocks[0] if per_blk == 1 else jnp.concatenate(blocks, axis=1)

    lefts, rights = [], []
    for got, at in places:
        halves = halves_of(got[at, :used, :])
        right = halves[0]
        for h in range(1, n_sub):
            right = jnp.where(sub == h, halves[h], right)
        left = None
        for e in range(n_ex):
            piece = halves[e // per_half][:, (e % per_half) * n_rows : (e % per_half + 1) * n_rows]
            left = piece if left is None else jnp.where(ex == e, piece, left)
        lefts += [left, pltpu.roll(left, own, 0)]
        rights += [right, right]
    left = jnp.concatenate(lefts, axis=0).astype(BF16)
    right = jnp.concatenate(rights, axis=0).astype(BF16)
    gram = lax.dot_general(left, right, FIRST, preferred_element_type=F32)
    gram_ref[0] = gram * (1.0 / (own * n_ex))


def solution(mesh):
    n_ex, n_lay, n_sub = mesh.shape["ex"], mesh.shape["lay"], mesh.shape["sub"]
    n_blk = n_lay * n_sub
    per_blk = n_ex // n_blk

    def flat(ex, lay, sub):
        return (ex * n_lay + lay) * n_sub + sub

    query_pairs = [
        (flat(blk * per_blk + ex // n_blk, ex % n_blk // n_sub, ex % n_sub), flat(ex, blk // n_sub, blk % n_sub))
        for ex in range(n_ex)
        for blk in range(n_blk)
    ]

    def rotate(value, axis, size, k):
        return lax.ppermute(value, axis, [((i + k) % size, i) for i in range(size)])

    def body(layer_inputs, output_grads, basis_in, basis_out, queries):
        _, tokens, depth = layer_inputs.shape
        basis = basis_in.shape[1]
        own = tokens // LEN
        width = basis * basis
        rows, half = queries.shape[1:]
        used = 2 * own * n_sub
        chunk = lax.ppermute(queries[0], ("ex", "lay", "sub"), query_pairs)

        proj = pl.pallas_call(
            project_kernel,
            out_shape=jax.ShapeDtypeStruct((tokens, 4 * basis), F32),
            in_specs=[ANY] * 4,
            out_specs=VMEM,
            scratch_shapes=[
                pltpu.VMEM((CHUNKS, tokens, depth // CHUNKS), BF16),
                pltpu.VMEM((CHUNKS, tokens, depth // CHUNKS), BF16),
                pltpu.VMEM((basis, depth), BF16),
                pltpu.VMEM((basis, depth), BF16),
                pltpu.SemaphoreType.DMA((2 + 2 * CHUNKS,)),
            ],
            compiler_params=pltpu.CompilerParams(vmem_limit_bytes=60 * 1024 * 1024),
            name="project",
        )(layer_inputs, output_grads, basis_in, basis_out)
        parts = [proj] + [rotate(proj, "sub", n_sub, k) for k in range(1, n_sub)]

        got, grads = pl.pallas_call(
            functools.partial(grads_kernel, basis, n_sub),
            out_shape=(
                jax.ShapeDtypeStruct((1, used + rows, half), BF16),
                jax.ShapeDtypeStruct((used, half), BF16),
            ),
            in_specs=[VMEM] * (n_sub + 1),
            out_specs=(VMEM, VMEM),
            compiler_params=pltpu.CompilerParams(vmem_limit_bytes=16 * 1024 * 1024),
            name="grads",
        )(*parts, chunk)

        others = [rotate(grads, "lay", n_lay, k) for k in range(1, n_lay)]
        gots, order, far = [got], [0], n_ex // 2
        while far:
            sent = gots[0] if len(gots) == 1 else jnp.concatenate(gots)
            gots.append(lax.ppermute(sent, "ex", [(i, i ^ far) for i in range(n_ex)]))
            order += [k ^ far for k in order]
            far //= 2

        gram, scores = pl.pallas_call(
            functools.partial(final_kernel, n_ex, n_lay, n_sub, own, order),
            out_shape=(
                jax.ShapeDtypeStruct((1, width // n_ex, half), F32),
                jax.ShapeDtypeStruct((own, rows * per_blk), F32),
            ),
            in_specs=[VMEM] * (len(others) + len(gots)),
            out_specs=(VMEM, VMEM),
            compiler_params=pltpu.CompilerParams(vmem_limit_bytes=16 * 1024 * 1024),
            name="gram_and_scores",
        )(*others, *gots)
        return gram, scores

    in_specs = (
        P("lay", ("grp", "ex"), "sub"),
        P("lay", ("grp", "ex"), "sub"),
        P("lay", None, "sub"),
        P("lay", None, "sub"),
        P("lay", "ex", "sub"),
    )
    out_specs = (P(("grp", "lay"), "ex", "sub"), P(("grp", "ex"), ("lay", "sub")))
    return jax.shard_map(body, mesh=mesh, in_specs=in_specs, out_specs=out_specs, check_vma=False)
```

time: 27.8 us -> 25.9 us (0.932)
  Pallas kernels: 0 us -> 4.97 us
  matrix products: 3.94 us -> 0 us
  waiting for transfers between devices: 9.64 us -> 5.74 us
  starting transfers between devices: 9.95 us -> 13.5 us
  local copies, waits for them, and re-layouts: 2.46 us -> 0.91 us
  other arithmetic: 0.64 us -> 0.01 us
    ppermute x1 -> x5, starting transfers between devices: 0.52 us -> 13.5 us  [the longest x2 11.9 us: body(): gots.append(lax.ppermute(sent, 'ex', [(i, i ^ far) for i in range(n_ex)]))]
    all_to_all x2 -> x0, starting transfers between devices: 9.44 us -> none  [to_all(): return lax.all_to_all(value, axes, 0, 0, tiled=False)]
    all_to_all x2 -> x0, waiting for transfers between devices: 8.93 us -> none  [to_all(): return lax.all_to_all(value, axes, 0, 0, tiled=False)]
    ppermute x1 -> x5, waiting for transfers between devices: 0.71 us -> 5.74 us  [the longest x2 3.84 us: rotate(): return lax.ppermute(value, axis, [((i + k) % size, i) for i in range(size)])]
    pallas_call x0 -> x3, Pallas kernels: none -> 4.97 us  [the longest x1 3.43 us: body(): pl.pallas_call(project_kernel, out_shape=jax.ShapeDtypeStruct((tokens, 4...]
    dot_general x5 -> x0, matrix products: 3.94 us -> none  [the longest x1 1.31 us: body(): lax.dot_general(basis_in[0], layer_inputs[0], contract, preferred_element...]
    broadcast_in_dim x1 -> x0, local copies, waits for them, and re-layouts: 0.66 us -> none  [body(): got = to_all(jnp.broadcast_to(sent, (n_ex, *sent.shape)), 'ex')]
    reduce_sum x1 -> x0, other arithmetic: 0.59 us -> none  [body(): scores = to_all(partial, ('lay', 'sub')).sum(0)]
  transfers between devices with their start and end apart: 3 -> 5, of which waited for: 3 -> 3; matrix products, arithmetic and copies ran while one was open for 4% -> 0% of each run, Pallas kernels for 0% -> 0%
where the time goes in v3:
time: 25.9 us; the launch traced here: 25.8 us
  starting transfers between devices  13.5 us (52%)
  waiting for transfers between devices  5.74 us (22%)
  Pallas kernels  4.97 us (19%)
  local copies, waits for them, and re-layouts  0.91 us (4%)
  between operations  0.67 us (3%)
    ppermute x2, starting transfers between devices, body(): gots.append(lax.ppermute(sent, 'ex', [(i, i ^ far) for i in range(n_ex)]))  11.9 us
    ppermute x2, waiting for transfers between devices, rotate(): return lax.ppermute(value, axis, [((i + k) % size, i) for i in range(size)])  3.84 us
    pallas_call x1, Pallas kernels, body(): pl.pallas_call(project_kernel, out_shape=jax.ShapeDtypeStruct((tokens, 4...  3.43 us
    ppermute x2, waiting for transfers between devices, body(): gots.append(lax.ppermute(sent, 'ex', [(i, i ^ far) for i in range(n_ex)]))  1.9 us
    pallas_call x1, Pallas kernels, body(): pl.pallas_call(functools.partial(final_kernel, n_ex, n_lay, n_sub, own, o...  1.06 us
    ppermute x2, starting transfers between devices, rotate(): return lax.ppermute(value, axis, [((i + k) % size, i) for i in range(size)])  0.95 us
    unnamed x4, local copies, waits for them, and re-layouts  0.91 us
    ppermute x1, starting transfers between devices, body(): chunk = lax.ppermute(queries[0], ('ex', 'lay', 'sub'), query_pairs)  0.65 us
  transfers between devices with their start and end apart: 5, of which 3 were waited for; matrix products, arithmetic and copies ran while one was open for 0% of the time, Pallas kernels for 0%

profile of v3, /device:TPU:0, one launch (start us, length us, event | category | flops | bytes accessed | tf_op | source)
XLA Modules:
  0.0 25.8 jit_solution(6417897116688717125)
XLA Ops:
  0.6 0.0 copy-start.1
  0.6 3.4 %project.1.refs_0_ = f32[256,128]{1,0:T(8,128)} custom-call(bf16[1,256,2048]{2,1,0:T(8,128)(2,1)} %x_ref.1, bf16[1,256,2048]{2,1,0:T(8,128)(2,1)} %g_ref.1, bf16[1,32,2048]{2,1,0:T(8,128)(2,1)} %bi_ref.1, bf16[1,32,2048]{2,1,0:T(8,128)(2,1)} %bo_ref.1), custom_call_target="tpu_custom_call" | custom-call | tf_op jit(solution)/shard_map/project/pallas_call | solution.py:159
  4.1 0.5 %collective-permute-start = (f32[256,128]{1,0:T(8,128)}, f32[256,128]{1,0:T(8,128)S(1)}, u32[]{:S(2)}, u32[]{:S(2)}) collective-permute-start(f32[256,128]{1,0:T(8,128)} %project.1.refs_0_), channel_id=1, source_target_pairs={{1,0},{0,1},{3,2},{2,3},{5,4},{4,5},{7,6},{6,7},{9,8},{8,9},{11,10... | collective-permute-start | bytes 393224 | tf_op jit(solution)/shard_map/ppermute | solution.py:148
  4.6 0.0 copy-done.1
  4.6 0.7 %collective-permute-start.1 = (bf16[16,512]{1,0:T(8,128)(2,1)S(1)}, bf16[16,512]{1,0:T(8,128)(2,1)S(1)}, u32[]{:S(2)}, u32[]{:S(2)}) collective-permute-start(bf16[16,512]{1,0:T(8,128)(2,1)S(1)} %bitcast.1), channel_id=1, source_target_pairs={{0,0},{4,1},{8,2},{12,3},{1,4},{5,5},{9,6},{13,7},{2,8},{6,9},{10,... | collective-permute-start | bytes 49160 | tf_op jit(solution)/shard_map/ppermute | solution.py:157
  5.3 0.0 collective-permute-done.1.refs_2_
  5.3 0.5 %collective-permute-done.refs_1_ = f32[256,128]{1,0:T(8,128)S(1)} collective-permute-done((f32[256,128]{1,0:T(8,128)}, f32[256,128]{1,0:T(8,128)S(1)}, u32[]{:S(2)}, u32[]{:S(2)}) %collective-permute-start) | collective-permute-done | bytes 131104 | tf_op jit(solution)/shard_map/ppermute | solution.py:148
  5.8 0.0 copy-start
  5.8 0.9 %copy-done = f32[256,128]{1,0:T(8,128)S(1)} copy-done((f32[256,128]{1,0:T(8,128)S(1)}, f32[256,128]{1,0:T(8,128)}, u32[]{:S(2)}) %copy-start) | copy-done | bytes 131096
  6.7 0.5 %grads.1 = (bf16[1,32,512]{2,1,0:T(8,128)(2,1)S(1)}, bf16[16,512]{1,0:T(8,128)(2,1)S(1)}) custom-call(f32[256,128]{1,0:T(8,128)S(1)} %copy-done, f32[256,128]{1,0:T(8,128)S(1)} %collective-permute-done.refs_1_, bf16[16,512]{1,0:T(8,128)(2,1)S(1)} %collective-permute-done.1.refs_2_), custom_call_target="tpu_custom_call" | custom-call | tf_op jit(solution)/shard_map/grads/pallas_call | solution.py:176
  7.2 9.9 %collective-permute-start.3 = (bf16[1,32,512]{2,1,0:T(8,128)(2,1)S(1)}, bf16[1,32,512]{2,1,0:T(8,128)(2,1)S(1)}, u32[]{:S(2)}, u32[]{:S(2)}) collective-permute-start(bf16[1,32,512]{2,1,0:T(8,128)(2,1)S(1)} %get-tuple-element.5.refs_1_), channel_id=1, source_target_pairs={{0,8},{4,12},{8,0},{12,4},{1,9},{5,13},{9,1},{13,5},{2,10},{6,14},... | collective-permute-start | bytes 98312 | tf_op jit(solution)/shard_map/ppermute | solution.py:192
  17.1 1.9 %collective-permute-done.3.refs_2_ = bf16[1,32,512]{2,1,0:T(8,128)(2,1)S(1)} collective-permute-done((bf16[1,32,512]{2,1,0:T(8,128)(2,1)S(1)}, bf16[1,32,512]{2,1,0:T(8,128)(2,1)S(1)}, u32[]{:S(2)}, u32[]{:S(2)}) %collective-permute-start.3) | collective-permute-done | bytes 32800 | tf_op jit(solution)/shard_map/ppermute | solution.py:192
  19.0 2.0 %collective-permute-start.4 = (bf16[2,32,512]{2,1,0:T(8,128)(2,1)S(1)}, bf16[2,32,512]{2,1,0:T(8,128)(2,1)S(1)}, u32[]{:S(2)}, u32[]{:S(2)}) collective-permute-start(bf16[2,32,512]{2,1,0:T(8,128)(2,1)S(1)} %pad_maximum_fusion), channel_id=1, source_target_pairs={{0,4},{4,0},{8,12},{12,8},{1,5},{5,1},{9,13},{13,9},{2,6},{6,2},{1... | collective-permute-start | bytes 196616 | tf_op jit(solution)/shard_map/ppermute | solution.py:192
  21.0 0.4 %collective-permute-start.2 = (bf16[16,512]{1,0:T(8,128)(2,1)S(1)}, bf16[16,512]{1,0:T(8,128)(2,1)S(1)}, u32[]{:S(2)}, u32[]{:S(2)}) collective-permute-start(bf16[16,512]{1,0:T(8,128)(2,1)S(1)} %get-tuple-element.4), channel_id=1, source_target_pairs={{2,0},{0,2},{3,1},{1,3},{6,4},{4,6},{7,5},{5,7},{10,8},{8,10},{11,... | collective-permute-start | bytes 49160 | tf_op jit(solution)/shard_map/ppermute | solution.py:148
  21.4 3.3 %collective-permute-done.2.refs_0_ = bf16[16,512]{1,0:T(8,128)(2,1)S(1)} collective-permute-done((bf16[16,512]{1,0:T(8,128)(2,1)S(1)}, bf16[16,512]{1,0:T(8,128)(2,1)S(1)}, u32[]{:S(2)}, u32[]{:S(2)}) %collective-permute-start.2) | collective-permute-done | bytes 16416 | tf_op jit(solution)/shard_map/ppermute | solution.py:148
  24.7 0.0 collective-permute-done.4.refs_3_
  24.7 1.1 %gram_and_scores.1 = (f32[1,256,512]{2,1,0:T(8,128)}, f32[4,16]{1,0:T(4,128)}) custom-call(bf16[16,512]{1,0:T(8,128)(2,1)S(1)} %collective-permute-done.2.refs_0_, bf16[1,32,512]{2,1,0:T(8,128)(2,1)S(1)} %get-tuple-element.5.refs_1_, bf16[1,32,512]{2,1,0:T(8,128)(2,1)S(1)} %collective-permute-done.3.refs_2_, ...), custom_call_target="tpu_custom_call" | custom-call | tf_op jit(solution)/shard_map/gram_and_scores/pallas_call | solution.py:196
  (1 shorter events, 0.0 us)
Async XLA Ops:
  0.6 4.0 %copy-start.1 = (bf16[1,16,512]{2,1,0:T(8,128)(2,1)S(1)}, bf16[1,16,512]{2,1,0:T(8,128)(2,1)}, u32[]{:S(2)}) copy-start(bf16[1,16,512]{2,1,0:T(8,128)(2,1)} %param.9) | copy-start | bytes 49156
  4.1 1.7 %collective-permute-start = (f32[256,128]{1,0:T(8,128)}, f32[256,128]{1,0:T(8,128)S(1)}, u32[]{:S(2)}, u32[]{:S(2)}) collective-permute-start(f32[256,128]{1,0:T(8,128)} %project.1.refs_0_), channel_id=1, source_target_pairs={{1,0},{0,1},{3,2},{2,3},{5,4},{4,5},{7,6},{6,7},{9,8},{8,9},{11,10... | collective-permute-start | bytes 393224 | tf_op jit(solution)/shard_map/ppermute | solution.py:148
  4.6 0.7 %collective-permute-start.1 = (bf16[16,512]{1,0:T(8,128)(2,1)S(1)}, bf16[16,512]{1,0:T(8,128)(2,1)S(1)}, u32[]{:S(2)}, u32[]{:S(2)}) collective-permute-start(bf16[16,512]{1,0:T(8,128)(2,1)S(1)} %bitcast.1), channel_id=1, source_target_pairs={{0,0},{4,1},{8,2},{12,3},{1,4},{5,5},{9,6},{13,7},{2,8},{6,9},{10,... | collective-permute-start | bytes 49160 | tf_op jit(solution)/shard_map/ppermute | solution.py:157
  5.8 0.9 %copy-start = (f32[256,128]{1,0:T(8,128)S(1)}, f32[256,128]{1,0:T(8,128)}, u32[]{:S(2)}) copy-start(f32[256,128]{1,0:T(8,128)} %project.1.refs_0_) | copy-start | bytes 393220
  7.2 11.8 %collective-permute-start.3 = (bf16[1,32,512]{2,1,0:T(8,128)(2,1)S(1)}, bf16[1,32,512]{2,1,0:T(8,128)(2,1)S(1)}, u32[]{:S(2)}, u32[]{:S(2)}) collective-permute-start(bf16[1,32,512]{2,1,0:T(8,128)(2,1)S(1)} %get-tuple-element.5.refs_1_), channel_id=1, source_target_pairs={{0,8},{4,12},{8,0},{12,4},{1,9},{5,13},{9,1},{13,5},{2,10},{6,14},... | collective-permute-start | bytes 98312 | tf_op jit(solution)/shard_map/ppermute | solution.py:192
  19.0 5.7 %collective-permute-start.4 = (bf16[2,32,512]{2,1,0:T(8,128)(2,1)S(1)}, bf16[2,32,512]{2,1,0:T(8,128)(2,1)S(1)}, u32[]{:S(2)}, u32[]{:S(2)}) collective-permute-start(bf16[2,32,512]{2,1,0:T(8,128)(2,1)S(1)} %pad_maximum_fusion), channel_id=1, source_target_pairs={{0,4},{4,0},{8,12},{12,8},{1,5},{5,1},{9,13},{13,9},{2,6},{6,2},{1... | collective-permute-start | bytes 196616 | tf_op jit(solution)/shard_map/ppermute | solution.py:192
  21.0 3.7 %collective-permute-start.2 = (bf16[16,512]{1,0:T(8,128)(2,1)S(1)}, bf16[16,512]{1,0:T(8,128)(2,1)S(1)}, u32[]{:S(2)}, u32[]{:S(2)}) collective-permute-start(bf16[16,512]{1,0:T(8,128)(2,1)S(1)} %get-tuple-element.4), channel_id=1, source_target_pairs={{2,0},{0,2},{3,1},{1,3},{6,4},{4,6},{7,5},{5,7},{10,8},{8,10},{11,... | collective-permute-start | bytes 49160 | tf_op jit(solution)/shard_map/ppermute | solution.py:148

commit v4 on v3

--- a/solution.py
+++ b/solution.py
@@ -8,64 +8,59 @@
 from jax.sharding import PartitionSpec as P
 
 LEN = 64
-CHUNKS = 4
 F32, BF16 = jnp.float32, jnp.bfloat16
 VMEM = pl.BlockSpec(memory_space=pltpu.VMEM)
-ANY = pl.BlockSpec(memory_space=pl.ANY)
 LAST = (((1,), (1,)), ((), ()))
 FIRST = (((0,), (0,)), ((), ()))
 
 
-def project_kernel(x_ref, g_ref, bi_ref, bo_ref, out_ref, x_buf, g_buf, bi_buf, bo_buf, sems):
-    step = x_buf.shape[2]
-    copies = [
-        pltpu.make_async_copy(bi_ref.at[0], bi_buf, sems.at[0]),
-        pltpu.make_async_copy(bo_ref.at[0], bo_buf, sems.at[1]),
-    ]
-    for k in range(CHUNKS):
-        cols = pl.ds(k * step, step)
-        copies.append(pltpu.make_async_copy(x_ref.at[0, :, cols], x_buf.at[k], sems.at[2 + 2 * k]))
-        copies.append(pltpu.make_async_copy(g_ref.at[0, :, cols], g_buf.at[k], sems.at[3 + 2 * k]))
-    for copy in copies:
-        copy.start()
-    copies[0].wait()
-    copies[1].wait()
+def project_kernel(x_ref, g_ref, bi_ref, bo_ref, out_ref):
+    bi, bo = bi_ref[0], bo_ref[0]
+    none = jnp.zeros_like(bi)
+    half = out_ref.shape[0]
     total = None
-    for k in range(CHUNKS):
-        cols = pl.ds(k * step, step)
-        bi, bo = bi_buf[:, cols], bo_buf[:, cols]
-        none = jnp.zeros_like(bi)
-        copies[2 + 2 * k].wait()
-        part = lax.dot_general(x_buf[k], jnp.concatenate([bi, none, bi, none]), LAST, preferred_element_type=F32)
+    for at, (values, basis) in enumerate([(x_ref, bi), (g_ref, bo)] * 2):
+        rows = pl.ds(at // 2 * half, half)
+        weights = jnp.concatenate([basis if i == at else none for i in range(4)])
+        part = lax.dot_general(values[0, rows, :], weights, LAST, preferred_element_type=F32)
         total = part if total is None else total + part
-        copies[3 + 2 * k].wait()
-        total += lax.dot_general(g_buf[k], jnp.concatenate([none, bo, none, bo]), LAST, preferred_element_type=F32)
     out_ref[...] = total
 
 
+def prepare_kernel(basis, q_ref, chunk_ref, pick_x_ref, pick_g_ref):
+    chunk_ref[...] = q_ref[...]
+    rows, width = pick_g_ref.shape
+    lanes, pair = pick_x_ref.shape[1], 2 * basis
+    row = lax.broadcasted_iota(jnp.int32, (rows, lanes), 0) % pair
+    col = lax.broadcasted_iota(jnp.int32, (rows, lanes), 1)
+    pick_x_ref[...] = jnp.where(row == col % basis, 1.0, 0.0).astype(BF16)
+    gap = row - basis - col // basis
+    for j in range(width // lanes):
+        pick_g_ref[:, j * lanes : (j + 1) * lanes] = jnp.where(gap == j * (lanes // basis), 1.0, 0.0).astype(BF16)
+
+
 def grads_kernel(basis, n_sub, *refs):
-    parts, q_ref, out_ref, own_ref = refs[:n_sub], refs[n_sub], refs[n_sub + 1], refs[n_sub + 2]
+    parts, (q_ref, pick_x_ref, pick_g_ref, out_ref, own_ref) = refs[:n_sub], refs[n_sub:]
     total = parts[0][...]
     for part in parts[1:]:
         total += part[...]
-    tokens, lanes = total.shape
+    lanes = total.shape[1]
     pair = 2 * basis
     high = total.astype(BF16).astype(F32)
     rest = total - high
     mid = rest.astype(BF16).astype(F32)
     low = rest - mid
-    first = lax.broadcasted_iota(jnp.int32, (tokens, lanes), 1) < pair
-    pieces = jnp.concatenate([jnp.where(first, high, mid), jnp.where(first, low, 0.0)], axis=1).astype(BF16)
-
-    row = lax.broadcasted_iota(jnp.int32, (2 * lanes, lanes), 0) % pair
-    col = lax.broadcasted_iota(jnp.int32, (2 * lanes, lanes), 1)
-    pick_x = jnp.where(row == col % basis, 1.0, 0.0).astype(BF16)
-    tiled_x = jnp.dot(pieces, pick_x, preferred_element_type=F32)
-    gap = row - basis - col // basis
+    first = lax.broadcasted_iota(jnp.int32, total.shape, 1) < pair
+    top = [jnp.where(first, high, pltpu.roll(mid, pair, 1)), jnp.where(first, low, 0.0)]
+    bottom = [jnp.where(first, pltpu.roll(high, pair, 1), mid), jnp.where(first, pltpu.roll(low, pair, 1), 0.0)]
+    pieces = jnp.concatenate([jnp.concatenate(top, axis=1), jnp.concatenate(bottom, axis=1)]).astype(BF16)
+    tokens = pieces.shape[0]
+
+    tiled_x = jnp.dot(pieces, pick_x_ref[...], preferred_element_type=F32)
     own = tokens // LEN
     tiles = []
     for j in range(basis * basis // lanes):
-        pick_g = jnp.where(gap == j * (lanes // basis), 1.0, 0.0).astype(BF16)
+        pick_g = pick_g_ref[:, j * lanes : (j + 1) * lanes]
         product = jnp.dot(pieces, pick_g, preferred_element_type=F32) * tiled_x
         tiles.append(product.reshape(own, LEN, lanes).sum(axis=1))
     grads = jnp.concatenate(tiles, axis=1)
@@ -82,7 +77,7 @@
     out_ref[0, packed.shape[0] :, :] = q_ref[...]
 
 
-def final_kernel(n_ex, n_lay, n_sub, own, order, *refs):
+def final_kernel(n_ex, n_lay, n_sub, own, turn, order, *refs):
     others, gots = refs[: n_lay - 1], refs[n_lay - 1 : -2]
     gram_ref, scores_ref = refs[-2:]
     ex, lay, sub = lax.axis_index("ex"), lax.axis_index("lay"), lax.axis_index("sub")
@@ -100,7 +95,7 @@
     layers = [halves_of(gots[0][0, :used, :])] + [halves_of(other[...]) for other in others]
     blocks = [0.0] * per_blk
     for (got, at), slot in zip(places, order):
-        source = slot ^ ex
+        source = slot ^ turn ^ ex
         l, h = source % n_blk // n_sub, source % n_sub
         grads = layers[0][0]
         for k in range(n_lay):
@@ -138,10 +133,14 @@
     def flat(ex, lay, sub):
         return (ex * n_lay + lay) * n_sub + sub
 
+    turn = 2
+
+    def query_source(ex, blk):
+        at = ex ^ turn
+        return flat(blk * per_blk + at // n_blk, at % n_blk // n_sub, at % n_sub)
+
     query_pairs = [
-        (flat(blk * per_blk + ex // n_blk, ex % n_blk // n_sub, ex % n_sub), flat(ex, blk // n_sub, blk % n_sub))
-        for ex in range(n_ex)
-        for blk in range(n_blk)
+        (query_source(ex, blk), flat(ex, blk // n_sub, blk % n_sub)) for ex in range(n_ex) for blk in range(n_blk)
     ]
 
     def rotate(value, axis, size, k):
@@ -158,20 +157,28 @@
 
         proj = pl.pallas_call(
             project_kernel,
-            out_shape=jax.ShapeDtypeStruct((tokens, 4 * basis), F32),
-            in_specs=[ANY] * 4,
+            out_shape=jax.ShapeDtypeStruct((tokens // 2, 4 * basis), F32),
+            in_specs=[VMEM] * 4,
             out_specs=VMEM,
-            scratch_shapes=[
-                pltpu.VMEM((CHUNKS, tokens, depth // CHUNKS), BF16),
-                pltpu.VMEM((CHUNKS, tokens, depth // CHUNKS), BF16),
-                pltpu.VMEM((basis, depth), BF16),
-                pltpu.VMEM((basis, depth), BF16),
-                pltpu.SemaphoreType.DMA((2 + 2 * CHUNKS,)),
-            ],
-            compiler_params=pltpu.CompilerParams(vmem_limit_bytes=60 * 1024 * 1024),
+            compiler_params=pltpu.CompilerParams(vmem_limit_bytes=16 * 1024 * 1024),
+            cost_estimate=pl.CostEstimate(flops=10**11, bytes_accessed=10**9, transcendentals=0),
             name="project",
         )(layer_inputs, output_grads, basis_in, basis_out)
         parts = [proj] + [rotate(proj, "sub", n_sub, k) for k in range(1, n_sub)]
+
+        prepared = pl.pallas_call(
+            functools.partial(prepare_kernel, basis),
+            out_shape=(
+                jax.ShapeDtypeStruct((rows, half), BF16),
+                jax.ShapeDtypeStruct((8 * basis, 4 * basis), BF16),
+                jax.ShapeDtypeStruct((8 * basis, width), BF16),
+            ),
+            in_specs=[VMEM],
+            out_specs=(VMEM,) * 3,
+            compiler_params=pltpu.CompilerParams(vmem_limit_bytes=16 * 1024 * 1024),
+            cost_estimate=pl.CostEstimate(flops=10**11, bytes_accessed=10**9, transcendentals=0),
+            name="prepare",
+        )(chunk)
 
         got, grads = pl.pallas_call(
             functools.partial(grads_kernel, basis, n_sub),
@@ -179,22 +186,25 @@
                 jax.ShapeDtypeStruct((1, used + rows, half), BF16),
                 jax.ShapeDtypeStruct((used, half), BF16),
             ),
-            in_specs=[VMEM] * (n_sub + 1),
+            in_specs=[VMEM] * (n_sub + 3),
             out_specs=(VMEM, VMEM),
             compiler_params=pltpu.CompilerParams(vmem_limit_bytes=16 * 1024 * 1024),
             name="grads",
-        )(*parts, chunk)
+        )(*parts, *prepared)
 
         others = [rotate(grads, "lay", n_lay, k) for k in range(1, n_lay)]
         gots, order, far = [got], [0], n_ex // 2
         while far:
             sent = gots[0] if len(gots) == 1 else jnp.concatenate(gots)
-            gots.append(lax.ppermute(sent, "ex", [(i, i ^ far) for i in range(n_ex)]))
+            back = lax.ppermute(sent, "ex", [(i, i ^ far) for i in range(n_ex)])
+            if len(gots) == 1:
+                back, others = lax.optimization_barrier((back, others))
+            gots.append(back)
             order += [k ^ far for k in order]
             far //= 2
 
         gram, scores = pl.pallas_call(
-            functools.partial(final_kernel, n_ex, n_lay, n_sub, own, order),
+            functools.partial(final_kernel, n_ex, n_lay, n_sub, own, turn, order),
             out_shape=(
                 jax.ShapeDtypeStruct((1, width // n_ex, half), F32),
                 jax.ShapeDtypeStruct((own, rows * per_blk), F32),

time: 25.9 us -> 23.2 us (0.90)
  starting transfers between devices: 13.5 us -> 7.03 us
  local copies, waits for them, and re-layouts: 0.91 us -> 4.26 us
  waiting for transfers between devices: 5.74 us -> 8.62 us
  Pallas kernels: 4.97 us -> 2.43 us
    ppermute x2, starting transfers between devices: 11.9 us -> 1.75 us  [body(): back = lax.ppermute(sent, 'ex', [(i, i ^ far) for i in range(n_ex)])]
    ppermute x1, starting transfers between devices: 0.65 us -> 4.09 us  [body(): chunk = lax.ppermute(queries[0], ('ex', 'lay', 'sub'), query_pairs)]
    unnamed x4 -> x8, local copies, waits for them, and re-layouts: 0.91 us -> 4.26 us
    pallas_call x2 -> x3, Pallas kernels: 4.48 us -> 1.89 us  [the longest x1 1.06 us: body(): pl.pallas_call(functools.partial(final_kernel, n_ex, n_lay, n_sub, own, t...]
    ppermute x2, waiting for transfers between devices: 1.9 us -> 4.14 us  [body(): back = lax.ppermute(sent, 'ex', [(i, i ^ far) for i in range(n_ex)])]
    ppermute x2, waiting for transfers between devices: 3.84 us -> 4.48 us  [rotate(): return lax.ppermute(value, axis, [((i + k) % size, i) for i in range(size)])]
  transfers between devices with their start and end apart: 5 -> 5, of which waited for: 3 -> 3; matrix products, arithmetic and copies ran while one was open for 0% -> 0% of each run, Pallas kernels for 0% -> 4%
where the time goes in v4:
time: 23.2 us; the launch traced here: 23 us
  waiting for transfers between devices  8.62 us (37%)
  starting transfers between devices  7.03 us (30%)
  local copies, waits for them, and re-layouts  4.26 us (18%)
  Pallas kernels  2.43 us (10%)
  between operations  0.66 us (3%)
    ppermute x2, waiting for transfers between devices, rotate(): return lax.ppermute(value, axis, [((i + k) % size, i) for i in range(size)])  4.48 us
    unnamed x8, local copies, waits for them, and re-layouts  4.26 us
    ppermute x2, waiting for transfers between devices, body(): back = lax.ppermute(sent, 'ex', [(i, i ^ far) for i in range(n_ex)])  4.14 us
    ppermute x1, starting transfers between devices, body(): chunk = lax.ppermute(queries[0], ('ex', 'lay', 'sub'), query_pairs)  4.09 us
    ppermute x2, starting transfers between devices, body(): back = lax.ppermute(sent, 'ex', [(i, i ^ far) for i in range(n_ex)])  1.75 us
    ppermute x2, starting transfers between devices, rotate(): return lax.ppermute(value, axis, [((i + k) % size, i) for i in range(size)])  1.2 us
    pallas_call x1, Pallas kernels, body(): pl.pallas_call(functools.partial(final_kernel, n_ex, n_lay, n_sub, own, t...  1.06 us
    pallas_call x1, Pallas kernels, body(): pl.pallas_call(project_kernel, out_shape=jax.ShapeDtypeStruct((tokens //...  0.68 us
  transfers between devices with their start and end apart: 5, of which 3 were waited for; matrix products, arithmetic and copies ran while one was open for 0% of the time, Pallas kernels for 4%

profile of v4, /device:TPU:0, one launch (start us, length us, event | category | flops | bytes accessed | tf_op | source)
XLA Modules:
  0.0 23.0 jit_solution(13173988981055668269)
XLA Ops:
  0.6 4.1 %collective-permute-start.1 = (bf16[16,512]{1,0:T(8,128)(2,1)}, bf16[16,512]{1,0:T(8,128)(2,1)S(1)}, u32[]{:S(2)}, u32[]{:S(2)}) collective-permute-start(bf16[16,512]{1,0:T(8,128)(2,1)} %bitcast.1), channel_id=1, source_target_pairs={{2,0},{6,1},{10,2},{14,3},{3,4},{7,5},{11,6},{15,7},{0,8},{4,9},{8... | collective-permute-start | bytes 49160 | tf_op jit(solution)/shard_map/ppermute | solution.py:156
  4.7 0.0 copy-start
  4.7 1.2 %copy-done = bf16[1,256,2048]{2,1,0:T(8,128)(2,1)S(1)} copy-done((bf16[1,256,2048]{2,1,0:T(8,128)(2,1)S(1)}, bf16[1,256,2048]{2,1,0:T(8,128)(2,1)}, u32[]{:S(2)}) %copy-start) | copy-done | bytes 1048600
  5.9 0.0 copy-start.1
  5.9 1.2 %copy-done.1 = bf16[1,256,2048]{2,1,0:T(8,128)(2,1)S(1)} copy-done((bf16[1,256,2048]{2,1,0:T(8,128)(2,1)S(1)}, bf16[1,256,2048]{2,1,0:T(8,128)(2,1)}, u32[]{:S(2)}) %copy-start.1) | copy-done | bytes 1048600
  7.2 0.0 copy-start.2
  7.2 0.9 %copy-done.2 = bf16[1,32,2048]{2,1,0:T(8,128)(2,1)S(1)} copy-done((bf16[1,32,2048]{2,1,0:T(8,128)(2,1)S(1)}, bf16[1,32,2048]{2,1,0:T(8,128)(2,1)}, u32[]{:S(2)}) %copy-start.2) | copy-done | bytes 131096
  8.1 0.0 copy-start.3
  8.1 0.9 %copy-done.3 = bf16[1,32,2048]{2,1,0:T(8,128)(2,1)S(1)} copy-done((bf16[1,32,2048]{2,1,0:T(8,128)(2,1)S(1)}, bf16[1,32,2048]{2,1,0:T(8,128)(2,1)}, u32[]{:S(2)}) %copy-start.3) | copy-done | bytes 131096
  9.0 0.7 %project.1.refs_0_ = f32[128,128]{1,0:T(8,128)S(1)} custom-call(bf16[1,256,2048]{2,1,0:T(8,128)(2,1)S(1)} %copy-done, bf16[1,256,2048]{2,1,0:T(8,128)(2,1)S(1)} %copy-done.1, bf16[1,32,2048]{2,1,0:T(8,128)(2,1)S(1)} %copy-done.2, bf16[1,32,2048]{2,1,0:T(8,128)(2,1)S(1)} %copy-done.3), custom_call_target="tpu_custom_call" | custom-call | flops 99999997952 | bytes 1000000000 | tf_op jit(solution)/shard_map/project/pallas_call | solution.py:158
  9.7 1.2 %collective-permute-start = (f32[128,128]{1,0:T(8,128)S(1)}, f32[128,128]{1,0:T(8,128)S(1)}, u32[]{:S(2)}, u32[]{:S(2)}) collective-permute-start(f32[128,128]{1,0:T(8,128)S(1)} %project.1.refs_0_), channel_id=1, source_target_pairs={{1,0},{0,1},{3,2},{2,3},{5,4},{4,5},{7,6},{6,7},{9,8},{8,9},{11,10... | collective-permute-start | bytes 196616 | tf_op jit(solution)/shard_map/ppermute | solution.py:147
  10.9 0.0 collective-permute-done.1.q_ref
  10.9 0.2 prepare.1
  11.0 0.7 %collective-permute-done.refs_1_ = f32[128,128]{1,0:T(8,128)S(1)} collective-permute-done((f32[128,128]{1,0:T(8,128)S(1)}, f32[128,128]{1,0:T(8,128)S(1)}, u32[]{:S(2)}, u32[]{:S(2)}) %collective-permute-start) | collective-permute-done | bytes 65568 | tf_op jit(solution)/shard_map/ppermute | solution.py:147
  11.8 0.5 %grads.1 = (bf16[1,32,512]{2,1,0:T(8,128)(2,1)S(1)}, bf16[16,512]{1,0:T(8,128)(2,1)S(1)}) custom-call(f32[128,128]{1,0:T(8,128)S(1)} %project.1.refs_0_, f32[128,128]{1,0:T(8,128)S(1)} %collective-permute-done.refs_1_, bf16[16,512]{1,0:T(8,128)(2,1)S(1)} %get-tuple-element.9.refs_2_, bf16[256,128]{1,0:T(8,128)(2,1)S(1)} %get-tuple-element.10.refs_3_, ...), custom_call_target="tpu_custom_call" | custom-call | tf_op jit(solution)/shard_map/grads/pallas_call | solution.py:183
  12.3 1.6 %collective-permute-start.2 = (bf16[1,32,512]{2,1,0:T(8,128)(2,1)S(1)}, bf16[1,32,512]{2,1,0:T(8,128)(2,1)S(1)}, u32[]{:S(2)}, u32[]{:S(2)}) collective-permute-start(bf16[1,32,512]{2,1,0:T(8,128)(2,1)S(1)} %get-tuple-element.12.refs_1_), channel_id=1, source_target_pairs={{0,8},{4,12},{8,0},{12,4},{1,9},{5,13},{9,1},{13,5},{2,10},{6,14},... | collective-permute-start | bytes 98312 | tf_op jit(solution)/shard_map/ppermute | solution.py:199
  13.9 0.0 collective-permute-start.3
  13.9 3.7 %collective-permute-done.3.refs_0_ = bf16[16,512]{1,0:T(8,128)(2,1)S(1)} collective-permute-done((bf16[16,512]{1,0:T(8,128)(2,1)S(1)}, bf16[16,512]{1,0:T(8,128)(2,1)S(1)}, u32[]{:S(2)}, u32[]{:S(2)}) %collective-permute-start.3) | collective-permute-done | bytes 16416 | tf_op jit(solution)/shard_map/ppermute | solution.py:147
  17.6 0.0 collective-permute-done.2.refs_2_
  17.6 0.2 collective-permute-start.4
  17.8 4.1 %collective-permute-done.4.refs_3_ = bf16[2,32,512]{2,1,0:T(8,128)(2,1)S(1)} collective-permute-done((bf16[2,32,512]{2,1,0:T(8,128)(2,1)S(1)}, bf16[2,32,512]{2,1,0:T(8,128)(2,1)S(1)}, u32[]{:S(2)}, u32[]{:S(2)}) %collective-permute-start.4) | collective-permute-done | bytes 65568 | tf_op jit(solution)/shard_map/ppermute | solution.py:199
  21.9 1.1 %gram_and_scores.1 = (f32[1,256,512]{2,1,0:T(8,128)}, f32[4,16]{1,0:T(4,128)}) custom-call(bf16[16,512]{1,0:T(8,128)(2,1)S(1)} %collective-permute-done.3.refs_0_, bf16[1,32,512]{2,1,0:T(8,128)(2,1)S(1)} %get-tuple-element.12.refs_1_, bf16[1,32,512]{2,1,0:T(8,128)(2,1)S(1)} %collective-permute-done.2.refs_2_, ...), custom_call_target="tpu_custom_call" | custom-call | tf_op jit(solution)/shard_map/gram_and_scores/pallas_call | solution.py:206
  (1 shorter events, 0.0 us)
Async XLA Ops:
  0.6 10.2 %collective-permute-start.1 = (bf16[16,512]{1,0:T(8,128)(2,1)}, bf16[16,512]{1,0:T(8,128)(2,1)S(1)}, u32[]{:S(2)}, u32[]{:S(2)}) collective-permute-start(bf16[16,512]{1,0:T(8,128)(2,1)} %bitcast.1), channel_id=1, source_target_pairs={{2,0},{6,1},{10,2},{14,3},{3,4},{7,5},{11,6},{15,7},{0,8},{4,9},{8... | collective-permute-start | bytes 49160 | tf_op jit(solution)/shard_map/ppermute | solution.py:156
  4.7 1.2 %copy-start = (bf16[1,256,2048]{2,1,0:T(8,128)(2,1)S(1)}, bf16[1,256,2048]{2,1,0:T(8,128)(2,1)}, u32[]{:S(2)}) copy-start(bf16[1,256,2048]{2,1,0:T(8,128)(2,1)} %x_ref.1) | copy-start | bytes 3145732
  5.9 1.2 %copy-start.1 = (bf16[1,256,2048]{2,1,0:T(8,128)(2,1)S(1)}, bf16[1,256,2048]{2,1,0:T(8,128)(2,1)}, u32[]{:S(2)}) copy-start(bf16[1,256,2048]{2,1,0:T(8,128)(2,1)} %g_ref.1) | copy-start | bytes 3145732
  7.2 0.9 %copy-start.2 = (bf16[1,32,2048]{2,1,0:T(8,128)(2,1)S(1)}, bf16[1,32,2048]{2,1,0:T(8,128)(2,1)}, u32[]{:S(2)}) copy-start(bf16[1,32,2048]{2,1,0:T(8,128)(2,1)} %bi_ref.1) | copy-start | bytes 393220
  8.1 0.9 %copy-start.3 = (bf16[1,32,2048]{2,1,0:T(8,128)(2,1)S(1)}, bf16[1,32,2048]{2,1,0:T(8,128)(2,1)}, u32[]{:S(2)}) copy-start(bf16[1,32,2048]{2,1,0:T(8,128)(2,1)} %bo_ref.1) | copy-start | bytes 393220
  9.7 2.1 %collective-permute-start = (f32[128,128]{1,0:T(8,128)S(1)}, f32[128,128]{1,0:T(8,128)S(1)}, u32[]{:S(2)}, u32[]{:S(2)}) collective-permute-start(f32[128,128]{1,0:T(8,128)S(1)} %project.1.refs_0_), channel_id=1, source_target_pairs={{1,0},{0,1},{3,2},{2,3},{5,4},{4,5},{7,6},{6,7},{9,8},{8,9},{11,10... | collective-permute-start | bytes 196616 | tf_op jit(solution)/shard_map/ppermute | solution.py:147
  12.3 5.3 %collective-permute-start.2 = (bf16[1,32,512]{2,1,0:T(8,128)(2,1)S(1)}, bf16[1,32,512]{2,1,0:T(8,128)(2,1)S(1)}, u32[]{:S(2)}, u32[]{:S(2)}) collective-permute-start(bf16[1,32,512]{2,1,0:T(8,128)(2,1)S(1)} %get-tuple-element.12.refs_1_), channel_id=1, source_target_pairs={{0,8},{4,12},{8,0},{12,4},{1,9},{5,13},{9,1},{13,5},{2,10},{6,14},... | collective-permute-start | bytes 98312 | tf_op jit(solution)/shard_map/ppermute | solution.py:199
  13.9 3.7 %collective-permute-start.3 = (bf16[16,512]{1,0:T(8,128)(2,1)S(1)}, bf16[16,512]{1,0:T(8,128)(2,1)S(1)}, u32[]{:S(2)}, u32[]{:S(2)}) collective-permute-start(bf16[16,512]{1,0:T(8,128)(2,1)S(1)} %get-tuple-element.13), channel_id=1, source_target_pairs={{2,0},{0,2},{3,1},{1,3},{6,4},{4,6},{7,5},{5,7},{10,8},{8,10},{11,... | collective-permute-start | bytes 49160 | tf_op jit(solution)/shard_map/ppermute | solution.py:147
  17.6 4.3 %collective-permute-start.4 = (bf16[2,32,512]{2,1,0:T(8,128)(2,1)S(1)}, bf16[2,32,512]{2,1,0:T(8,128)(2,1)S(1)}, u32[]{:S(2)}, u32[]{:S(2)}) collective-permute-start(bf16[2,32,512]{2,1,0:T(8,128)(2,1)S(1)} %pad_maximum_fusion), channel_id=1, source_target_pairs={{0,4},{4,0},{8,12},{12,8},{1,5},{5,1},{9,13},{13,9},{2,6},{6,2},{1... | collective-permute-start | bytes 196616 | tf_op jit(solution)/shard_map/ppermute | solution.py:199

commit v5 on v2

v5 whole, which is shorter than its diff:
```python
import functools

import jax
import jax.numpy as jnp
from jax import lax
from jax.experimental import pallas as pl
from jax.experimental.pallas import tpu as pltpu
from jax.sharding import PartitionSpec as P

LEN = 64
AXES = ("ex", "lay", "sub")
F32, BF16 = jnp.float32, jnp.bfloat16
VMEM = pl.BlockSpec(memory_space=pltpu.VMEM)
LAST = (((1,), (1,)), ((), ()))
FIRST = (((0,), (0,)), ((), ()))
PARAMS = pltpu.CompilerParams(vmem_limit_bytes=16 * 1024 * 1024)


def prepare_kernel(basis, q_ref, chunk_ref, pick_x_ref, pick_g_ref):
    chunk_ref[...] = q_ref[...]
    rows, width = pick_g_ref.shape
    lanes, pair = pick_x_ref.shape[1], 2 * basis
    row = lax.broadcasted_iota(jnp.int32, (rows, lanes), 0) % pair
    col = lax.broadcasted_iota(jnp.int32, (rows, lanes), 1)
    pick_x_ref[...] = jnp.where(row == col % basis, 1.0, 0.0).astype(BF16)
    gap = row - basis - col // basis
    for j in range(width // lanes):
        pick_g_ref[:, j * lanes : (j + 1) * lanes] = jnp.where(gap == j * (lanes // basis), 1.0, 0.0).astype(BF16)


def grads_kernel(n_sub, *refs):
    parts, (pick_x_ref, pick_g_ref, out_ref) = refs[:n_sub], refs[n_sub:]
    total = parts[0][...]
    for part in parts[1:]:
        total += part[...]
    high = total.astype(BF16).astype(F32)
    rest = total - high
    mid = rest.astype(BF16).astype(F32)
    pieces = jnp.concatenate([high, mid, rest - mid]).astype(BF16)
    own = pieces.shape[1] // LEN
    lanes, width = pick_x_ref.shape[1], pick_g_ref.shape[1]
    tiled_x = lax.dot_general(pieces, pick_x_ref[...], FIRST, preferred_element_type=F32)
    tiles = []
    for j in range(width // lanes):
        pick_g = pick_g_ref[:, j * lanes : (j + 1) * lanes]
        product = lax.dot_general(pieces, pick_g, FIRST, preferred_element_type=F32) * tiled_x
        tiles.append(product.reshape(own, LEN, lanes).sum(axis=1))
    grads = jnp.concatenate(tiles, axis=1)
    high = grads.astype(BF16).astype(F32)
    low = grads - high
    half = width // n_sub
    rows = []
    for h in range(n_sub):
        cols = slice(h * half, (h + 1) * half)
        rows += [high[:, cols], low[:, cols]]
    out_ref[...] = jnp.concatenate(rows, axis=0).astype(BF16)


def final_kernel(n_ex, n_lay, n_sub, own, moves, mine_ref, got_ref, gram_ref, scores_ref):
    ex, lay, sub = lax.axis_index("ex"), lax.axis_index("lay"), lax.axis_index("sub")
    rounds = got_ref.shape[0] // n_sub
    group, per_blk = n_ex // n_lay, n_ex // (n_lay * n_sub)
    used, half = 2 * own * n_sub, got_ref.shape[2]
    rows = (got_ref.shape[1] - used) // n_sub
    n_rows, per_half = half * n_sub // n_ex, n_ex // n_sub

    def halves_of(pieces):
        pieces = pieces[:used].astype(F32)
        return [pieces[h * 2 * own : (h + 1) * 2 * own] for h in range(n_sub)]

    def choose(values, index):
        if isinstance(index, int):
            return values[index]
        result = values[0]
        for i in range(1, len(values)):
            result = jnp.where(index == i, values[i], result)
        return result

    mine = mine_ref[0]
    layers, slots = [halves_of(mine)], [(mine, sub, ex)]
    for at, (axis, k) in enumerate(moves):
        core = at % n_sub
        piece = got_ref[lax.rem(core - sub + n_sub, n_sub) * rounds + at // n_sub]
        if axis == "ex":
            slots.append((piece, core, ex ^ k))
        else:
            layers.append(halves_of(piece))

    blocks = [0.0] * per_blk
    for piece, core, source in slots:
        layer = lax.rem(source // group + n_lay - 1, n_lay)
        behind = lax.rem(layer - lay + n_lay, n_lay)
        grads = [choose([halves[h] for halves in layers], behind) for h in range(n_sub)]
        part = 0.0
        for k in range(n_sub):
            part += lax.dot_general(
                choose(grads, (core + k) % n_sub).astype(BF16),
                piece[used + k * rows : used + (k + 1) * rows],
                LAST,
                preferred_element_type=F32,
            )
        part = part[:own] + part[own:]
        for j in range(per_blk):
            blocks[j] += jnp.where(lax.rem(source, group) == sub * per_blk + j, part, 0.0)
    scores_ref[...] = blocks[0] if per_blk == 1 else jnp.concatenate(blocks, axis=1)

    lefts, rights = [], []
    for piece, _, _ in slots:
        halves = halves_of(piece)
        cuts = [halves[e // per_half][:, e % per_half * n_rows : (e % per_half + 1) * n_rows] for e in range(n_ex)]
        left, right = choose(cuts, ex), choose(halves, sub)
        lefts += [left, pltpu.roll(left, own, 0)]
        rights += [right, right]
    left = jnp.concatenate(lefts, axis=0).astype(BF16)
    right = jnp.concatenate(rights, axis=0).astype(BF16)
    gram = lax.dot_general(left, right, FIRST, preferred_element_type=F32)
    gram_ref[0] = gram * (1.0 / (own * n_ex))


def solution(mesh):
    n_ex, n_lay, n_sub = mesh.shape["ex"], mesh.shape["lay"], mesh.shape["sub"]
    group, per_blk = n_ex // n_lay, n_ex // (n_lay * n_sub)

    def flat(ex, lay, sub):
        return (ex * n_lay + lay) * n_sub + sub

    devices = [(ex, lay, sub) for ex in range(n_ex) for lay in range(n_lay) for sub in range(n_sub)]

    query_pairs = [
        (flat(ex, lay, sub), flat((lay + 1) % n_lay * group + ex % group, ex // group, sub)) for ex, lay, sub in devices
    ]

    far = [("ex", k) for k in range(3, n_ex)]
    across = [("lay", k) for k in range(1, n_lay)]
    moves = [("ex", 1), ("ex", 2)]
    while far or across:
        moves += across[:1] + far[:1]
        across, far = across[1:], far[1:]
    rounds = -(-len(moves) // n_sub)

    def source_of(at, ex, lay, sub):
        axis, k = moves[min(at * n_sub + sub, len(moves) - 1)]
        return flat(ex ^ k, lay, sub) if axis == "ex" else flat(ex, (lay + k) % n_lay, sub)

    def rotate(value, k):
        return lax.ppermute(value, "sub", [((i + k) % n_sub, i) for i in range(n_sub)])

    def body(layer_inputs, output_grads, basis_in, basis_out, queries):
        _, tokens, depth = layer_inputs.shape
        basis = basis_in.shape[1]
        own = tokens // LEN
        width = basis * basis
        rows, half = queries.shape[1:]

        chunk = lax.ppermute(queries[0], AXES, query_pairs)
        proj_x = lax.dot_general(basis_in[0], layer_inputs[0], LAST, preferred_element_type=F32)
        proj_g = lax.dot_general(basis_out[0], output_grads[0], LAST, preferred_element_type=F32)
        proj = jnp.concatenate([proj_x, proj_g])
        parts = [proj] + [rotate(proj, k) for k in range(1, n_sub)]

        chunk, pick_x, pick_g = pl.pallas_call(
            functools.partial(prepare_kernel, basis),
            out_shape=(
                jax.ShapeDtypeStruct((rows, half), BF16),
                jax.ShapeDtypeStruct((6 * basis, 4 * basis), BF16),
                jax.ShapeDtypeStruct((6 * basis, width), BF16),
            ),
            in_specs=[VMEM],
            out_specs=(VMEM,) * 3,
            compiler_params=PARAMS,
            cost_estimate=pl.CostEstimate(flops=10**11, bytes_accessed=10**9, transcendentals=0),
            name="prepare",
        )(chunk)
        chunks = [chunk] + [rotate(chunk, k) for k in range(1, n_sub)]

        grads = pl.pallas_call(
            functools.partial(grads_kernel, n_sub),
            out_shape=jax.ShapeDtypeStruct((2 * own * n_sub, half), BF16),
            in_specs=[VMEM] * (n_sub + 2),
            out_specs=VMEM,
            compiler_params=PARAMS,
            name="grads",
        )(*parts, pick_x, pick_g)

        mine = jnp.concatenate([grads] + chunks)[None]
        received = []
        for at in range(rounds):
            pairs = [(source_of(at, *device), flat(*device)) for device in devices]
            received.append(lax.ppermute(mine, AXES, pairs))
        received = jnp.concatenate(received)
        got = jnp.concatenate([received] + [rotate(received, k) for k in range(1, n_sub)])

        return pl.pallas_call(
            functools.partial(final_kernel, n_ex, n_lay, n_sub, own, moves),
            out_shape=(
                jax.ShapeDtypeStruct((1, width // n_ex, half), F32),
                jax.ShapeDtypeStruct((own, rows * per_blk), F32),
            ),
            in_specs=[VMEM] * 2,
            out_specs=(VMEM, VMEM),
            compiler_params=PARAMS,
            name="gram_and_scores",
        )(mine, got)

    in_specs = (
        P("lay", ("grp", "ex"), "sub"),
        P("lay", ("grp", "ex"), "sub"),
        P("lay", None, "sub"),
        P("lay", None, "sub"),
        P("lay", "ex", "sub"),
    )
    out_specs = (P(("grp", "lay"), "ex", "sub"), P(("grp", "ex"), ("lay", "sub")))
    return jax.shard_map(body, mesh=mesh, in_specs=in_specs, out_specs=out_specs, check_vma=False)
```

time: 27.8 us -> 18.1 us (0.65)
  waiting for transfers between devices: 9.64 us -> 4.17 us
  local copies, waits for them, and re-layouts: 2.46 us -> 0.02 us
  matrix products: 3.94 us -> 1.72 us
  Pallas kernels: 0 us -> 1.73 us
  other arithmetic: 0.64 us -> 0.06 us
  starting transfers between devices: 9.95 us -> 9.47 us
    all_to_all x2 -> x0, starting transfers between devices: 9.44 us -> none  [to_all(): return lax.all_to_all(value, axes, 0, 0, tiled=False)]
    ppermute x1 -> x6, starting transfers between devices: 0.52 us -> 9.47 us  [the longest x1 4.09 us: body(): chunk = lax.ppermute(queries[0], AXES, query_pairs)]
    all_to_all x2 -> x0, waiting for transfers between devices: 8.93 us -> none  [to_all(): return lax.all_to_all(value, axes, 0, 0, tiled=False)]
    ppermute x1 -> x6, waiting for transfers between devices: 0.71 us -> 4.17 us  [the longest x2 2.66 us: body(): received.append(lax.ppermute(mine, AXES, pairs))]
    dot_general x5 -> x2, matrix products: 3.94 us -> 1.72 us  [the longest x1 1.31 us: body(): lax.dot_general(basis_in[0], layer_inputs[0], LAST, preferred_element_typ...]
    pallas_call x0 -> x3, Pallas kernels: none -> 1.73 us  [the longest x1 1.08 us: body(): pl.pallas_call(functools.partial(final_kernel, n_ex, n_lay, n_sub, own, m...]
    unnamed x8 -> x6, local copies, waits for them, and re-layouts: 1.41 us -> 0.02 us
    broadcast_in_dim x1 -> x0, local copies, waits for them, and re-layouts: 0.66 us -> none  [body(): got = to_all(jnp.broadcast_to(sent, (n_ex, *sent.shape)), 'ex')]
  transfers between devices with their start and end apart: 3 -> 6, of which waited for: 3 -> 4; matrix products, arithmetic and copies ran while one was open for 4% -> 10% of each run, Pallas kernels for 0% -> 4%
where the time goes in v5:
time: 18.1 us; the launch traced here: 17.9 us
  starting transfers between devices  9.47 us (52%)
  waiting for transfers between devices  4.17 us (23%)
  Pallas kernels  1.73 us (10%)
  matrix products  1.72 us (10%)
  between operations  0.75 us (4%)
    ppermute x1, starting transfers between devices, body(): chunk = lax.ppermute(queries[0], AXES, query_pairs)  4.09 us
    ppermute x2, starting transfers between devices, body(): received.append(lax.ppermute(mine, AXES, pairs))  3.04 us
    ppermute x2, waiting for transfers between devices, body(): received.append(lax.ppermute(mine, AXES, pairs))  2.66 us
    ppermute x3, starting transfers between devices, rotate(): lax.ppermute(value, 'sub', [((i + k) % n_sub, i) for i in range(n_sub)])  2.35 us
    ppermute x3, waiting for transfers between devices, rotate(): lax.ppermute(value, 'sub', [((i + k) % n_sub, i) for i in range(n_sub)])  1.5 us
    dot_general x1, matrix products, body(): lax.dot_general(basis_in[0], layer_inputs[0], LAST, preferred_element_typ...  1.31 us
    pallas_call x1, Pallas kernels, body(): pl.pallas_call(functools.partial(final_kernel, n_ex, n_lay, n_sub, own, m...  1.08 us
    pallas_call x1, Pallas kernels, body(): pl.pallas_call(functools.partial(grads_kernel, n_sub), out_shape=jax.Shap...  0.53 us
  transfers between devices with their start and end apart: 6, of which 4 were waited for; matrix products, arithmetic and copies ran while one was open for 10% of the time, Pallas kernels for 4%

profile of v5, /device:TPU:0, one launch (start us, length us, event | category | flops | bytes accessed | tf_op | source)
XLA Modules:
  0.0 17.9 jit_solution(5342737144242033367)
XLA Ops:
  0.6 0.0 copy-start
  0.6 0.0 copy-start.1
  0.7 0.0 copy-start.2
  0.7 4.1 %collective-permute-start.1 = (bf16[16,512]{1,0:T(8,128)(2,1)}, bf16[16,512]{1,0:T(8,128)(2,1)S(1)}, u32[]{:S(2)}, u32[]{:S(2)}) collective-permute-start(bf16[16,512]{1,0:T(8,128)(2,1)} %bitcast.15), channel_id=1, source_target_pairs={{0,8},{1,9},{2,0},{3,1},{4,12},{5,13},{6,4},{7,5},{8,10},{9,11},{1... | collective-permute-start | bytes 49160 | tf_op jit(solution)/shard_map/ppermute | solution.py:155
  4.8 0.0 copy-done
  4.8 1.3 %fusion.2 = f32[32,256]{1,0:T(8,128)S(1)} fusion(bf16[1,256,2048]{2,1,0:T(8,128)(2,1)S(1)} %copy-done, bf16[1,32,2048]{2,1,0:T(8,128)(2,1)} %param.7), kind=kOutput, calls=%fused_computation.2 | convolution fusion | flops 33554432 | bytes 1212416 | tf_op jit(solution)/shard_map/dot_general | solution.py:156
  6.1 0.0 copy-done.1
  6.1 0.0 copy-done.2
  6.1 0.4 %fusion = f32[32,256]{1,0:T(8,128)S(1)} fusion(bf16[1,256,2048]{2,1,0:T(8,128)(2,1)S(1)} %copy-done.1, bf16[1,32,2048]{2,1,0:T(8,128)(2,1)S(1)} %copy-done.2), kind=kOutput, calls=%fused_computation | convolution fusion | flops 33554432 | bytes 1212416 | tf_op jit(solution)/shard_map/dot_general | solution.py:157
  6.5 0.1 collective-permute-start
  6.6 0.0 collective-permute-done.1.q_ref
  6.6 0.1 prepare.1
  6.8 0.6 %collective-permute-start.2 = (bf16[16,512]{1,0:T(8,128)(2,1)S(1)}, bf16[16,512]{1,0:T(8,128)(2,1)S(1)}, u32[]{:S(2)}, u32[]{:S(2)}) collective-permute-start(bf16[16,512]{1,0:T(8,128)(2,1)S(1)} %get-tuple-element.7), channel_id=1, source_target_pairs={{1,0},{0,1},{3,2},{2,3},{5,4},{4,5},{7,6},{6,7},{9,8},{8,9},{11,10... | collective-permute-start | bytes 49160 | tf_op jit(solution)/shard_map/ppermute | solution.py:146
  7.3 0.6 %collective-permute-done.refs_1_ = f32[64,256]{1,0:T(8,128)S(1)} collective-permute-done((f32[64,256]{1,0:T(8,128)S(1)}, f32[64,256]{1,0:T(8,128)S(1)}, u32[]{:S(2)}, u32[]{:S(2)}) %collective-permute-start) | collective-permute-done | bytes 65568 | tf_op jit(solution)/shard_map/ppermute | solution.py:146
  7.9 0.5 %grads.1 = bf16[16,512]{1,0:T(8,128)(2,1)S(1)} custom-call(f32[64,256]{1,0:T(8,128)S(1)} %pad_maximum_fusion.2.refs_0_, f32[64,256]{1,0:T(8,128)S(1)} %collective-permute-done.refs_1_, bf16[192,128]{1,0:T(8,128)(2,1)S(1)} %get-tuple-element.5.refs_2_, bf16[192,1024]{1,0:T(8,128)(2,1)S(1)} %get-tuple-element.6.refs_3_), custom_call_target="tpu_custom_call" | custom-call | tf_op jit(solution)/shard_map/grads/pallas_call | solution.py:176
  8.4 0.0 collective-permute-done.2
  8.4 1.5 %collective-permute-start.4 = (bf16[1,48,512]{2,1,0:T(8,128)(2,1)S(1)}, bf16[1,48,512]{2,1,0:T(8,128)(2,1)S(1)}, u32[]{:S(2)}, u32[]{:S(2)}) collective-permute-start(bf16[1,48,512]{2,1,0:T(8,128)(2,1)S(1)} %maximum_bitcast_fusion.mine_ref), channel_id=1, source_target_pairs={{2,0},{13,1},{0,2},{15,3},{6,4},{9,5},{4,6},{11,7},{10,8},{5,9},{8... | collective-permute-start | bytes 147464 | tf_op jit(solution)/shard_map/ppermute | solution.py:189
  9.9 1.5 %collective-permute-start.3 = (bf16[1,48,512]{2,1,0:T(8,128)(2,1)S(1)}, bf16[1,48,512]{2,1,0:T(8,128)(2,1)S(1)}, u32[]{:S(2)}, u32[]{:S(2)}) collective-permute-start(bf16[1,48,512]{2,1,0:T(8,128)(2,1)S(1)} %maximum_bitcast_fusion.mine_ref), channel_id=1, source_target_pairs={{4,0},{9,1},{6,2},{11,3},{0,4},{13,5},{2,6},{15,7},{12,8},{1,9},{1... | collective-permute-start | bytes 147464 | tf_op jit(solution)/shard_map/ppermute | solution.py:189
  11.5 1.1 %collective-permute-done.4 = bf16[1,48,512]{2,1,0:T(8,128)(2,1)S(1)} collective-permute-done((bf16[1,48,512]{2,1,0:T(8,128)(2,1)S(1)}, bf16[1,48,512]{2,1,0:T(8,128)(2,1)S(1)}, u32[]{:S(2)}, u32[]{:S(2)}) %collective-permute-start.4) | collective-permute-done | bytes 49184 | tf_op jit(solution)/shard_map/ppermute | solution.py:189
  12.6 1.5 %collective-permute-done.3 = bf16[1,48,512]{2,1,0:T(8,128)(2,1)S(1)} collective-permute-done((bf16[1,48,512]{2,1,0:T(8,128)(2,1)S(1)}, bf16[1,48,512]{2,1,0:T(8,128)(2,1)S(1)}, u32[]{:S(2)}, u32[]{:S(2)}) %collective-permute-start.3) | collective-permute-done | bytes 49184 | tf_op jit(solution)/shard_map/ppermute | solution.py:189
  14.1 1.7 %collective-permute-start.5 = (bf16[2,48,512]{2,1,0:T(8,128)(2,1)S(1)}, bf16[2,48,512]{2,1,0:T(8,128)(2,1)S(1)}, u32[]{:S(2)}, u32[]{:S(2)}) collective-permute-start(bf16[2,48,512]{2,1,0:T(8,128)(2,1)S(1)} %pad_maximum_fusion.1), channel_id=1, source_target_pairs={{1,0},{0,1},{3,2},{2,3},{5,4},{4,5},{7,6},{6,7},{9,8},{8,9},{11,10... | collective-permute-start | bytes 294920 | tf_op jit(solution)/shard_map/ppermute | solution.py:146
  15.9 0.9 %collective-permute-done.5 = bf16[2,48,512]{2,1,0:T(8,128)(2,1)S(1)} collective-permute-done((bf16[2,48,512]{2,1,0:T(8,128)(2,1)S(1)}, bf16[2,48,512]{2,1,0:T(8,128)(2,1)S(1)}, u32[]{:S(2)}, u32[]{:S(2)}) %collective-permute-start.5) | collective-permute-done | bytes 98336 | tf_op jit(solution)/shard_map/ppermute | solution.py:146
  16.8 1.1 %gram_and_scores.1 = (f32[1,256,512]{2,1,0:T(8,128)}, f32[4,16]{1,0:T(4,128)}) custom-call(bf16[1,48,512]{2,1,0:T(8,128)(2,1)S(1)} %maximum_bitcast_fusion.mine_ref, bf16[4,48,512]{2,1,0:T(8,128)(2,1)S(1)} %pad_maximum_fusion.got_ref), custom_call_target="tpu_custom_call" | custom-call | tf_op jit(solution)/shard_map/gram_and_scores/pallas_call | solution.py:193
  (4 shorter events, 0.1 us)
Async XLA Ops:
  0.6 4.1 %copy-start = (bf16[1,256,2048]{2,1,0:T(8,128)(2,1)S(1)}, bf16[1,256,2048]{2,1,0:T(8,128)(2,1)}, u32[]{:S(2)}) copy-start(bf16[1,256,2048]{2,1,0:T(8,128)(2,1)} %param.5) | copy-start | bytes 3145732
  0.6 5.4 %copy-start.1 = (bf16[1,256,2048]{2,1,0:T(8,128)(2,1)S(1)}, bf16[1,256,2048]{2,1,0:T(8,128)(2,1)}, u32[]{:S(2)}) copy-start(bf16[1,256,2048]{2,1,0:T(8,128)(2,1)} %param.6) | copy-start | bytes 3145732
  0.7 5.4 %copy-start.2 = (bf16[1,32,2048]{2,1,0:T(8,128)(2,1)S(1)}, bf16[1,32,2048]{2,1,0:T(8,128)(2,1)}, u32[]{:S(2)}) copy-start(bf16[1,32,2048]{2,1,0:T(8,128)(2,1)} %param.8) | copy-start | bytes 393220
  0.7 6.0 %collective-permute-start.1 = (bf16[16,512]{1,0:T(8,128)(2,1)}, bf16[16,512]{1,0:T(8,128)(2,1)S(1)}, u32[]{:S(2)}, u32[]{:S(2)}) collective-permute-start(bf16[16,512]{1,0:T(8,128)(2,1)} %bitcast.15), channel_id=1, source_target_pairs={{0,8},{1,9},{2,0},{3,1},{4,12},{5,13},{6,4},{7,5},{8,10},{9,11},{1... | collective-permute-start | bytes 49160 | tf_op jit(solution)/shard_map/ppermute | solution.py:155
  6.5 1.3 %collective-permute-start = (f32[64,256]{1,0:T(8,128)S(1)}, f32[64,256]{1,0:T(8,128)S(1)}, u32[]{:S(2)}, u32[]{:S(2)}) collective-permute-start(f32[64,256]{1,0:T(8,128)S(1)} %pad_maximum_fusion.2.refs_0_), channel_id=1, source_target_pairs={{1,0},{0,1},{3,2},{2,3},{5,4},{4,5},{7,6},{6,7},{9,8},{8,9},{11,10... | collective-permute-start | bytes 196616 | tf_op jit(solution)/shard_map/ppermute | solution.py:146
  6.8 1.6 %collective-permute-start.2 = (bf16[16,512]{1,0:T(8,128)(2,1)S(1)}, bf16[16,512]{1,0:T(8,128)(2,1)S(1)}, u32[]{:S(2)}, u32[]{:S(2)}) collective-permute-start(bf16[16,512]{1,0:T(8,128)(2,1)S(1)} %get-tuple-element.7), channel_id=1, source_target_pairs={{1,0},{0,1},{3,2},{2,3},{5,4},{4,5},{7,6},{6,7},{9,8},{8,9},{11,10... | collective-permute-start | bytes 49160 | tf_op jit(solution)/shard_map/ppermute | solution.py:146
  8.4 4.2 %collective-permute-start.4 = (bf16[1,48,512]{2,1,0:T(8,128)(2,1)S(1)}, bf16[1,48,512]{2,1,0:T(8,128)(2,1)S(1)}, u32[]{:S(2)}, u32[]{:S(2)}) collective-permute-start(bf16[1,48,512]{2,1,0:T(8,128)(2,1)S(1)} %maximum_bitcast_fusion.mine_ref), channel_id=1, source_target_pairs={{2,0},{13,1},{0,2},{15,3},{6,4},{9,5},{4,6},{11,7},{10,8},{5,9},{8... | collective-permute-start | bytes 147464 | tf_op jit(solution)/shard_map/ppermute | solution.py:189
  9.9 4.2 %collective-permute-start.3 = (bf16[1,48,512]{2,1,0:T(8,128)(2,1)S(1)}, bf16[1,48,512]{2,1,0:T(8,128)(2,1)S(1)}, u32[]{:S(2)}, u32[]{:S(2)}) collective-permute-start(bf16[1,48,512]{2,1,0:T(8,128)(2,1)S(1)} %maximum_bitcast_fusion.mine_ref), channel_id=1, source_target_pairs={{4,0},{9,1},{6,2},{11,3},{0,4},{13,5},{2,6},{15,7},{12,8},{1,9},{1... | collective-permute-start | bytes 147464 | tf_op jit(solution)/shard_map/ppermute | solution.py:189
  14.1 2.7 %collective-permute-start.5 = (bf16[2,48,512]{2,1,0:T(8,128)(2,1)S(1)}, bf16[2,48,512]{2,1,0:T(8,128)(2,1)S(1)}, u32[]{:S(2)}, u32[]{:S(2)}) collective-permute-start(bf16[2,48,512]{2,1,0:T(8,128)(2,1)S(1)} %pad_maximum_fusion.1), channel_id=1, source_target_pairs={{1,0},{0,1},{3,2},{2,3},{5,4},{4,5},{7,6},{6,7},{9,8},{8,9},{11,10... | collective-permute-start | bytes 294920 | tf_op jit(solution)/shard_map/ppermute | solution.py:146

commit v6 on v5

v6 whole, which is shorter than its diff:
```python
import functools

import jax
import jax.numpy as jnp
from jax import lax
from jax.experimental import pallas as pl
from jax.experimental.pallas import tpu as pltpu
from jax.sharding import PartitionSpec as P

LEN = 64
AXES = ("ex", "lay", "sub")
F32, BF16 = jnp.float32, jnp.bfloat16
VMEM = pl.BlockSpec(memory_space=pltpu.VMEM)
LAST = (((1,), (1,)), ((), ()))
FIRST = (((0,), (0,)), ((), ()))
PARAMS = pltpu.CompilerParams(vmem_limit_bytes=16 * 1024 * 1024)


def picks_kernel(basis, pick_x_ref, pick_g_ref):
    rows, width = pick_g_ref.shape
    lanes, pair = pick_x_ref.shape[1], 2 * basis
    row = lax.broadcasted_iota(jnp.int32, (rows, lanes), 0) % pair
    col = lax.broadcasted_iota(jnp.int32, (rows, lanes), 1)
    pick_x_ref[...] = jnp.where(row == col % basis, 1.0, 0.0).astype(BF16)
    gap = row - basis - col // basis
    for j in range(width // lanes):
        pick_g_ref[:, j * lanes : (j + 1) * lanes] = jnp.where(gap == j * (lanes // basis), 1.0, 0.0).astype(BF16)


def grads_kernel(n_sub, *refs):
    parts, (pick_x_ref, pick_g_ref, out_ref) = refs[:n_sub], refs[n_sub:]
    total = parts[0][...]
    for part in parts[1:]:
        total += part[...]
    high = total.astype(BF16).astype(F32)
    rest = total - high
    mid = rest.astype(BF16).astype(F32)
    pieces = jnp.concatenate([high, mid, rest - mid]).astype(BF16)
    own = pieces.shape[1] // LEN
    lanes, width = pick_x_ref.shape[1], pick_g_ref.shape[1]
    tiled_x = lax.dot_general(pieces, pick_x_ref[...], FIRST, preferred_element_type=F32)
    tiles = []
    for j in range(width // lanes):
        pick_g = pick_g_ref[:, j * lanes : (j + 1) * lanes]
        product = lax.dot_general(pieces, pick_g, FIRST, preferred_element_type=F32) * tiled_x
        tiles.append(product.reshape(own, LEN, lanes).sum(axis=1))
    grads = jnp.concatenate(tiles, axis=1)
    high = grads.astype(BF16).astype(F32)
    low = grads - high
    half = width // n_sub
    rows = []
    for h in range(n_sub):
        cols = slice(h * half, (h + 1) * half)
        rows += [high[:, cols], low[:, cols]]
    out_ref[0] = jnp.concatenate(rows, axis=0).astype(BF16)


def halves_of(pieces, n_sub):
    pieces = pieces.astype(F32)
    size = pieces.shape[0] // n_sub
    return [pieces[h * size : (h + 1) * size] for h in range(n_sub)]


def layer_scores(halves, k, units, turns, n_ex, n_lay, n_sub):
    ex, lay = lax.axis_index("ex"), lax.axis_index("lay")
    n_blk = n_lay * n_sub
    own = halves[0].shape[0] // 2
    grads = [half.astype(BF16) for half in halves]
    blocks = [0.0] * (n_ex // n_blk)
    for unit_ref, turn in zip(units, turns):
        source = ex ^ turn
        part = 0.0
        for h in range(n_sub):
            part += lax.dot_general(grads[h], unit_ref[h], LAST, preferred_element_type=F32)
        part = part[:own] + part[own:]
        fits = source % n_blk // n_sub == lax.rem(lay + k, n_lay)
        for j in range(len(blocks)):
            blocks[j] += jnp.where(fits & (source // n_blk == j), part, 0.0)
    return blocks[0] if len(blocks) == 1 else jnp.concatenate(blocks, axis=1)


def own_scores_kernel(n_ex, n_lay, n_sub, turns, mine_ref, *refs):
    units, out_ref = refs[:-1], refs[-1]
    out_ref[...] = layer_scores(halves_of(mine_ref[0], n_sub), 0, units, turns, n_ex, n_lay, n_sub)


def final_kernel(n_ex, n_lay, n_sub, own, moves, turns, mine_ref, got_ref, *refs):
    partials, units, (gram_ref, scores_ref) = refs[: len(turns)], refs[len(turns) : -2], refs[-2:]
    ex, sub = lax.axis_index("ex"), lax.axis_index("sub")
    rounds = got_ref.shape[0] // n_sub
    half = got_ref.shape[2]
    n_rows, per_half = half * n_sub // n_ex, n_ex // n_sub

    def choose(values, index):
        result = values[0]
        for i in range(1, len(values)):
            result = jnp.where(index == i, values[i], result)
        return result

    slots = [halves_of(mine_ref[0], n_sub)]
    layers = slots[:]
    for at, (axis, k) in enumerate(moves):
        piece = halves_of(got_ref[lax.rem(at % n_sub - sub + n_sub, n_sub) * rounds + at // n_sub], n_sub)
        (slots if axis == "ex" else layers).append(piece)

    lefts, rights = [], []
    for halves in slots:
        cuts = [halves[e // per_half][:, e % per_half * n_rows : (e % per_half + 1) * n_rows] for e in range(n_ex)]
        left, right = choose(cuts, ex), choose(halves, sub)
        lefts += [left, pltpu.roll(left, own, 0)]
        rights += [right, right]
    left = jnp.concatenate(lefts, axis=0).astype(BF16)
    right = jnp.concatenate(rights, axis=0).astype(BF16)
    gram = lax.dot_general(left, right, FIRST, preferred_element_type=F32)
    gram_ref[0] = gram * (1.0 / (own * n_ex))

    scores = sum(partial[...] for partial in partials)
    for k in range(1, n_lay):
        scores += layer_scores(layers[k], k, units, turns, n_ex, n_lay, n_sub)
    scores_ref[...] = scores


def solution(mesh):
    n_ex, n_lay, n_sub = mesh.shape["ex"], mesh.shape["lay"], mesh.shape["sub"]
    n_blk = n_lay * n_sub
    per_blk = n_ex // n_blk

    def flat(ex, lay, sub):
        return (ex * n_lay + lay) * n_sub + sub

    devices = [(ex, lay, sub) for ex in range(n_ex) for lay in range(n_lay) for sub in range(n_sub)]

    turns = [max(k * n_sub, 1) for k in range(n_ex // n_sub)]

    def unit_pairs(turn):
        pairs = []
        for ex, lay, sub in devices:
            at, blk = ex ^ turn, lay * n_sub + sub
            pairs.append((flat(blk * per_blk + at // n_blk, at % n_blk // n_sub, at % n_sub), flat(ex, lay, sub)))
        return pairs

    far = [("ex", k) for k in range(3, n_ex)]
    across = [("lay", k) for k in range(1, n_lay)]
    moves = [("ex", 1), ("ex", 2)]
    while far or across:
        moves += across[:1] + far[:1]
        across, far = across[1:], far[1:]
    rounds = -(-len(moves) // n_sub)

    def source_of(at, ex, lay, sub):
        axis, k = moves[min(at * n_sub + sub, len(moves) - 1)]
        return flat(ex ^ k, lay, sub) if axis == "ex" else flat(ex, (lay + k) % n_lay, sub)

    def rotate(value, k):
        return lax.ppermute(value, "sub", [((i + k) % n_sub, i) for i in range(n_sub)])

    def body(layer_inputs, output_grads, basis_in, basis_out, queries):
        _, tokens, depth = layer_inputs.shape
        basis = basis_in.shape[1]
        own = tokens // LEN
        width = basis * basis
        rows, half = queries.shape[1:]

        unit = jnp.stack([queries[0]] + [rotate(queries[0], k) for k in range(1, n_sub)])
        unit = jnp.roll(unit, lax.axis_index("sub"), axis=0)
        pick_x, pick_g = pl.pallas_call(
            functools.partial(picks_kernel, basis),
            out_shape=(
                jax.ShapeDtypeStruct((6 * basis, 4 * basis), BF16),
                jax.ShapeDtypeStruct((6 * basis, width), BF16),
            ),
            out_specs=(VMEM,) * 2,
            compiler_params=PARAMS,
            cost_estimate=pl.CostEstimate(flops=10**11, bytes_accessed=10**9, transcendentals=0),
            name="picks",
        )()

        proj_x = lax.dot_general(basis_in[0], layer_inputs[0], LAST, preferred_element_type=F32)
        proj_g = lax.dot_general(basis_out[0], output_grads[0], LAST, preferred_element_type=F32)
        proj = jnp.concatenate([proj_x, proj_g])
        proj, unit = lax.optimization_barrier((proj, unit))
        units = [lax.ppermute(unit, AXES, unit_pairs(turn)) for turn in turns]
        parts = [proj] + [rotate(proj, k) for k in range(1, n_sub)]

        mine = pl.pallas_call(
            functools.partial(grads_kernel, n_sub),
            out_shape=jax.ShapeDtypeStruct((1, 2 * own * n_sub, half), BF16),
            in_specs=[VMEM] * (n_sub + 2),
            out_specs=VMEM,
            compiler_params=PARAMS,
            cost_estimate=pl.CostEstimate(flops=10**11, bytes_accessed=10**9, transcendentals=0),
            name="grads",
        )(*parts, pick_x, pick_g)

        received = []
        for at in range(rounds):
            pairs = [(source_of(at, *device), flat(*device)) for device in devices]
            received.append(lax.ppermute(mine, AXES, pairs))
        partials = [
            pl.pallas_call(
                functools.partial(own_scores_kernel, n_ex, n_lay, n_sub, [turn]),
                out_shape=jax.ShapeDtypeStruct((own, rows * per_blk), F32),
                in_specs=[VMEM] * 2,
                out_specs=VMEM,
                compiler_params=PARAMS,
                cost_estimate=pl.CostEstimate(flops=10**11, bytes_accessed=10**9, transcendentals=0),
                name="own_scores",
            )(mine, unit)
            for unit, turn in zip(units, turns)
        ]
        early = len(units) // 2
        received, *partials[:early] = lax.optimization_barrier((jnp.concatenate(received), *partials[:early]))
        got = jnp.concatenate([received] + [rotate(received, k) for k in range(1, n_sub)])

        return pl.pallas_call(
            functools.partial(final_kernel, n_ex, n_lay, n_sub, own, moves, turns),
            out_shape=(
                jax.ShapeDtypeStruct((1, width // n_ex, half), F32),
                jax.ShapeDtypeStruct((own, rows * per_blk), F32),
            ),
            in_specs=[VMEM] * (2 + 2 * len(units)),
            out_specs=(VMEM, VMEM),
            compiler_params=PARAMS,
            name="gram_and_scores",
        )(mine, got, *partials, *units)

    in_specs = (
        P("lay", ("grp", "ex"), "sub"),
        P("lay", ("grp", "ex"), "sub"),
        P("lay", None, "sub"),
        P("lay", None, "sub"),
        P("lay", "ex", "sub"),
    )
    out_specs = (P(("grp", "lay"), "ex", "sub"), P(("grp", "ex"), ("lay", "sub")))
    return jax.shard_map(body, mesh=mesh, in_specs=in_specs, out_specs=out_specs, check_vma=False)
```

time: 18.1 us -> 20.9 us (1.15)
  Pallas kernels: 1.73 us -> 3.46 us
  local copies, waits for them, and re-layouts: 0.02 us -> 1.39 us
  waiting for transfers between devices: 4.17 us -> 3.54 us
  other arithmetic: 0.06 us -> 0.68 us
  starting transfers between devices: 9.47 us -> 9.04 us
    ppermute x3, starting transfers between devices: 2.35 us -> 0.97 us  [rotate(): lax.ppermute(value, 'sub', [((i + k) % n_sub, i) for i in range(n_sub)])]
    unnamed x6 -> x8, local copies, waits for them, and re-layouts: 0.02 us -> 1.39 us
    ppermute x3, waiting for transfers between devices: 1.5 us -> 0.32 us  [rotate(): lax.ppermute(value, 'sub', [((i + k) % n_sub, i) for i in range(n_sub)])]
    pallas_call x1 -> x3, Pallas kernels: 0.11 us -> 1.11 us  [the longest x2 1 us: body(): pl.pallas_call(functools.partial(own_scores_kernel, n_ex, n_lay, n_sub, [...]
    pallas_call x1, Pallas kernels: 1.08 us -> 1.82 us  [body(): pl.pallas_call(functools.partial(final_kernel, n_ex, n_lay, n_sub, own, m...]
    ppermute x2, starting transfers between devices: 3.04 us -> 3.75 us  [body(): received.append(lax.ppermute(mine, AXES, pairs))]
    concatenate x1 -> x2, other arithmetic: 0.01 us -> 0.65 us  [the longest x1 0.64 us: body(): unit = jnp.roll(unit, lax.axis_index('sub'), axis=0)]
    ppermute x2, waiting for transfers between devices: 2.66 us -> 3.22 us  [body(): received.append(lax.ppermute(mine, AXES, pairs))]
  transfers between devices with their start and end apart: 6 -> 7, of which waited for: 4 -> 3; matrix products, arithmetic and copies ran while one was open for 10% -> 8% of each run, Pallas kernels for 4% -> 8%
where the time goes in v6:
time: 20.9 us; the launch traced here: 20.6 us
  starting transfers between devices  9.04 us (43%)
  waiting for transfers between devices  3.54 us (17%)
  Pallas kernels  3.46 us (17%)
  matrix products  1.72 us (8%)
  local copies, waits for them, and re-layouts  1.39 us (7%)
  between operations  0.75 us (4%)
  other arithmetic  0.68 us (3%)
    ppermute x2, starting transfers between devices, body(): units = [lax.ppermute(unit, AXES, unit_pairs(turn)) for turn in turns]  4.31 us
    ppermute x2, starting transfers between devices, body(): received.append(lax.ppermute(mine, AXES, pairs))  3.75 us
    ppermute x2, waiting for transfers between devices, body(): received.append(lax.ppermute(mine, AXES, pairs))  3.22 us
    pallas_call x1, Pallas kernels, body(): pl.pallas_call(functools.partial(final_kernel, n_ex, n_lay, n_sub, own, m...  1.82 us
    unnamed x8, local copies, waits for them, and re-layouts  1.39 us
    dot_general x1, matrix products, body(): lax.dot_general(basis_in[0], layer_inputs[0], LAST, preferred_element_typ...  1.31 us
    pallas_call x2, Pallas kernels, body(): pl.pallas_call(functools.partial(own_scores_kernel, n_ex, n_lay, n_sub, [...  1 us
    ppermute x3, starting transfers between devices, rotate(): lax.ppermute(value, 'sub', [((i + k) % n_sub, i) for i in range(n_sub)])  0.97 us
  transfers between devices with their start and end apart: 7, of which 3 were waited for; matrix products, arithmetic and copies ran while one was open for 8% of the time, Pallas kernels for 8%

profile of v6, /device:TPU:0, one launch (start us, length us, event | category | flops | bytes accessed | tf_op | source)
XLA Modules:
  0.0 20.6 jit_solution(13763346153057917846)
XLA Ops:
  0.6 0.0 copy-start
  0.6 0.0 copy-start.1
  0.7 0.0 copy-start.2
  0.7 0.5 %collective-permute-start = (bf16[16,512]{1,0:T(8,128)(2,1)}, bf16[16,512]{1,0:T(8,128)(2,1)S(1)}, u32[]{:S(2)}, u32[]{:S(2)}) collective-permute-start(bf16[16,512]{1,0:T(8,128)(2,1)} %bitcast.14), channel_id=1, source_target_pairs={{1,0},{0,1},{3,2},{2,3},{5,4},{4,5},{7,6},{6,7},{9,8},{8,9},{11,10... | collective-permute-start | bytes 49160 | tf_op jit(solution)/shard_map/ppermute | solution.py:155
  1.2 0.7 %copy-done = bf16[1,256,2048]{2,1,0:T(8,128)(2,1)S(1)} copy-done((bf16[1,256,2048]{2,1,0:T(8,128)(2,1)S(1)}, bf16[1,256,2048]{2,1,0:T(8,128)(2,1)}, u32[]{:S(2)}) %copy-start) | copy-done | bytes 1048600
  1.9 1.3 %fusion.2 = f32[32,256]{1,0:T(8,128)S(1)} fusion(bf16[1,256,2048]{2,1,0:T(8,128)(2,1)S(1)} %copy-done, bf16[1,32,2048]{2,1,0:T(8,128)(2,1)} %param.7), kind=kOutput, calls=%fused_computation.2 | convolution fusion | flops 33554432 | bytes 1212416 | tf_op jit(solution)/shard_map/dot_general | solution.py:178
  3.2 0.0 copy-done.1
  3.2 0.0 copy-done.2
  3.2 0.4 %fusion = f32[32,256]{1,0:T(8,128)S(1)} fusion(bf16[1,256,2048]{2,1,0:T(8,128)(2,1)S(1)} %copy-done.1, bf16[1,32,2048]{2,1,0:T(8,128)(2,1)S(1)} %copy-done.2), kind=kOutput, calls=%fused_computation | convolution fusion | flops 33554432 | bytes 1212416 | tf_op jit(solution)/shard_map/dot_general | solution.py:179
  3.6 0.0 copy-start.3
  3.7 0.0 collective-permute-done
  3.7 0.7 %copy-done.3 = bf16[1,16,512]{2,1,0:T(8,128)(2,1)S(1)} copy-done((bf16[1,16,512]{2,1,0:T(8,128)(2,1)S(1)}, bf16[1,16,512]{2,1,0:T(8,128)(2,1)}, u32[]{:S(2)}) %copy-start.3) | copy-done | bytes 16408
  4.4 0.6 %fusion.8 = bf16[2,16,512]{2,1,0:T(8,128)(2,1)} fusion(s32[]{:T(128)S(6)} %select_n.14, bf16[1,16,512]{2,1,0:T(8,128)(2,1)S(1)} %copy-done.3, bf16[1,16,512]{2,1,0:T(8,128)(2,1)S(1)} %bitcast.15), kind=kLoop, calls=%fused_computation.14 | loop fusion | flops 49152 | bytes 65540 | tf_op jit(solution)/shard_map/jit(_roll_dynamic)/concatenate | solution.py:165
  5.0 0.5 %collective-permute-start.1 = (f32[64,256]{1,0:T(8,128)S(1)}, f32[64,256]{1,0:T(8,128)S(1)}, u32[]{:S(2)}, u32[]{:S(2)}) collective-permute-start(f32[64,256]{1,0:T(8,128)S(1)} %pad_maximum_fusion.refs_0_), channel_id=1, source_target_pairs={{1,0},{0,1},{3,2},{2,3},{5,4},{4,5},{7,6},{6,7},{9,8},{8,9},{11,10... | collective-permute-start | bytes 196616 | tf_op jit(solution)/shard_map/ppermute | solution.py:155
  5.5 0.1 picks.1
  5.6 3.6 %collective-permute-start.6 = (bf16[2,16,512]{2,1,0:T(8,128)(2,1)}, bf16[2,16,512]{2,1,0:T(8,128)(2,1)}, u32[]{:S(2)}, u32[]{:S(2)}) collective-permute-start(bf16[2,16,512]{2,1,0:T(8,128)(2,1)} %fusion.8), channel_id=1, source_target_pairs={{2,0},{6,1},{10,2},{14,3},{3,4},{7,5},{11,6},{15,7},{0,8},{4,9},{8... | collective-permute-start | bytes 98312 | tf_op jit(solution)/shard_map/ppermute | solution.py:182
  9.2 0.7 %collective-permute-start.4 = (bf16[2,16,512]{2,1,0:T(8,128)(2,1)}, bf16[2,16,512]{2,1,0:T(8,128)(2,1)S(1)}, u32[]{:S(2)}, u32[]{:S(2)}) collective-permute-start(bf16[2,16,512]{2,1,0:T(8,128)(2,1)} %fusion.8), channel_id=1, source_target_pairs={{1,0},{5,1},{9,2},{13,3},{0,4},{4,5},{8,6},{12,7},{3,8},{7,9},{11,... | collective-permute-start | bytes 98312 | tf_op jit(solution)/shard_map/ppermute | solution.py:182
  9.9 0.0 collective-permute-done.1.refs_1_
  9.9 0.5 %grads.1.mine_ref = bf16[1,16,512]{2,1,0:T(8,128)(2,1)S(1)} custom-call(f32[64,256]{1,0:T(8,128)S(1)} %pad_maximum_fusion.refs_0_, f32[64,256]{1,0:T(8,128)S(1)} %collective-permute-done.1.refs_1_, bf16[192,128]{1,0:T(8,128)(2,1)S(1)} %get-tuple-element.9.refs_2_, bf16[192,1024]{1,0:T(8,128)(2,1)S(1)} %get-tuple-element.10.refs_3_), custom_call_target="tpu_custom_call" | custom-call | flops 99999997952 | bytes 1000000000 | tf_op jit(solution)/shard_map/grads/pallas_call | solution.py:185
  10.4 3.4 %collective-permute-start.3 = (bf16[1,16,512]{2,1,0:T(8,128)(2,1)S(1)}, bf16[1,16,512]{2,1,0:T(8,128)(2,1)S(1)}, u32[]{:S(2)}, u32[]{:S(2)}) collective-permute-start(bf16[1,16,512]{2,1,0:T(8,128)(2,1)S(1)} %grads.1.mine_ref), channel_id=1, source_target_pairs={{2,0},{13,1},{0,2},{15,3},{6,4},{9,5},{4,6},{11,7},{10,8},{5,9},{8... | collective-permute-start | bytes 49160 | tf_op jit(solution)/shard_map/ppermute | solution.py:198
  13.8 0.4 %collective-permute-start.2 = (bf16[1,16,512]{2,1,0:T(8,128)(2,1)S(1)}, bf16[1,16,512]{2,1,0:T(8,128)(2,1)S(1)}, u32[]{:S(2)}, u32[]{:S(2)}) collective-permute-start(bf16[1,16,512]{2,1,0:T(8,128)(2,1)S(1)} %grads.1.mine_ref), channel_id=1, source_target_pairs={{4,0},{9,1},{6,2},{11,3},{0,4},{13,5},{2,6},{15,7},{12,8},{1,9},{1... | collective-permute-start | bytes 49160 | tf_op jit(solution)/shard_map/ppermute | solution.py:198
  14.2 0.0 collective-permute-done.4.refs_0_.refs_2_
  14.2 0.1 own_scores.2.refs_0_
  14.3 1.2 %collective-permute-done.3 = bf16[1,16,512]{2,1,0:T(8,128)(2,1)S(1)} collective-permute-done((bf16[1,16,512]{2,1,0:T(8,128)(2,1)S(1)}, bf16[1,16,512]{2,1,0:T(8,128)(2,1)S(1)}, u32[]{:S(2)}, u32[]{:S(2)}) %collective-permute-start.3) | collective-permute-done | bytes 16416 | tf_op jit(solution)/shard_map/ppermute | solution.py:198
  15.5 2.0 %collective-permute-done.2 = bf16[1,16,512]{2,1,0:T(8,128)(2,1)S(1)} collective-permute-done((bf16[1,16,512]{2,1,0:T(8,128)(2,1)S(1)}, bf16[1,16,512]{2,1,0:T(8,128)(2,1)S(1)}, u32[]{:S(2)}, u32[]{:S(2)}) %collective-permute-start.2) | collective-permute-done | bytes 16416 | tf_op jit(solution)/shard_map/ppermute | solution.py:198
  17.5 0.0 collective-permute-start.5
  17.5 0.0 collective-permute-done.6.refs_0_.refs_3_
  17.6 0.9 %own_scores.3.refs_1_ = f32[4,16]{1,0:T(4,128)S(1)} custom-call(bf16[1,16,512]{2,1,0:T(8,128)(2,1)S(1)} %grads.1.mine_ref, bf16[2,16,512]{2,1,0:T(8,128)(2,1)} %collective-permute-done.6.refs_0_.refs_3_), custom_call_target="tpu_custom_call" | custom-call | flops 99999997952 | bytes 1000000000 | tf_op jit(solution)/shard_map/own_scores/pallas_call | solution.py:200
  18.4 0.3 %collective-permute-done.5 = bf16[2,16,512]{2,1,0:T(8,128)(2,1)S(1)} collective-permute-done((bf16[2,16,512]{2,1,0:T(8,128)(2,1)S(1)}, bf16[2,16,512]{2,1,0:T(8,128)(2,1)S(1)}, u32[]{:S(2)}, u32[]{:S(2)}) %collective-permute-start.5) | collective-permute-done | bytes 32800 | tf_op jit(solution)/shard_map/ppermute | solution.py:155
  18.8 1.8 %gram_and_scores.1 = (f32[1,256,512]{2,1,0:T(8,128)}, f32[4,16]{1,0:T(4,128)}) custom-call(bf16[1,16,512]{2,1,0:T(8,128)(2,1)S(1)} %grads.1.mine_ref, bf16[4,16,512]{2,1,0:T(8,128)(2,1)S(1)} %pad_maximum_fusion.1.got_ref, f32[4,16]{1,0:T(4,128)S(1)} %own_scores.2.refs_0_, f32[4,16]{1,0:T(4,128)S(1)} %own_scores.3.refs_1_, ...), custom_call_target="tpu_custom_call" | custom-call | tf_op jit(solution)/shard_map/gram_and_scores/pallas_call | solution.py:215
  (3 shorter events, 0.0 us)
Async XLA Ops:
  0.6 1.2 %copy-start = (bf16[1,256,2048]{2,1,0:T(8,128)(2,1)S(1)}, bf16[1,256,2048]{2,1,0:T(8,128)(2,1)}, u32[]{:S(2)}) copy-start(bf16[1,256,2048]{2,1,0:T(8,128)(2,1)} %param.5) | copy-start | bytes 3145732
  0.6 2.5 %copy-start.1 = (bf16[1,256,2048]{2,1,0:T(8,128)(2,1)S(1)}, bf16[1,256,2048]{2,1,0:T(8,128)(2,1)}, u32[]{:S(2)}) copy-start(bf16[1,256,2048]{2,1,0:T(8,128)(2,1)} %param.6) | copy-start | bytes 3145732
  0.7 2.5 %copy-start.2 = (bf16[1,32,2048]{2,1,0:T(8,128)(2,1)S(1)}, bf16[1,32,2048]{2,1,0:T(8,128)(2,1)}, u32[]{:S(2)}) copy-start(bf16[1,32,2048]{2,1,0:T(8,128)(2,1)} %param.8) | copy-start | bytes 393220
  0.7 3.0 %collective-permute-start = (bf16[16,512]{1,0:T(8,128)(2,1)}, bf16[16,512]{1,0:T(8,128)(2,1)S(1)}, u32[]{:S(2)}, u32[]{:S(2)}) collective-permute-start(bf16[16,512]{1,0:T(8,128)(2,1)} %bitcast.14), channel_id=1, source_target_pairs={{1,0},{0,1},{3,2},{2,3},{5,4},{4,5},{7,6},{6,7},{9,8},{8,9},{11,10... | collective-permute-start | bytes 49160 | tf_op jit(solution)/shard_map/ppermute | solution.py:155
  3.6 0.7 %copy-start.3 = (bf16[1,16,512]{2,1,0:T(8,128)(2,1)S(1)}, bf16[1,16,512]{2,1,0:T(8,128)(2,1)}, u32[]{:S(2)}) copy-start(bf16[1,16,512]{2,1,0:T(8,128)(2,1)} %param.9) | copy-start | bytes 49156
  5.0 4.9 %collective-permute-start.1 = (f32[64,256]{1,0:T(8,128)S(1)}, f32[64,256]{1,0:T(8,128)S(1)}, u32[]{:S(2)}, u32[]{:S(2)}) collective-permute-start(f32[64,256]{1,0:T(8,128)S(1)} %pad_maximum_fusion.refs_0_), channel_id=1, source_target_pairs={{1,0},{0,1},{3,2},{2,3},{5,4},{4,5},{7,6},{6,7},{9,8},{8,9},{11,10... | collective-permute-start | bytes 196616 | tf_op jit(solution)/shard_map/ppermute | solution.py:155
  5.6 12.0 %collective-permute-start.6 = (bf16[2,16,512]{2,1,0:T(8,128)(2,1)}, bf16[2,16,512]{2,1,0:T(8,128)(2,1)}, u32[]{:S(2)}, u32[]{:S(2)}) collective-permute-start(bf16[2,16,512]{2,1,0:T(8,128)(2,1)} %fusion.8), channel_id=1, source_target_pairs={{2,0},{6,1},{10,2},{14,3},{3,4},{7,5},{11,6},{15,7},{0,8},{4,9},{8... | collective-permute-start | bytes 98312 | tf_op jit(solution)/shard_map/ppermute | solution.py:182
  9.2 5.0 %collective-permute-start.4 = (bf16[2,16,512]{2,1,0:T(8,128)(2,1)}, bf16[2,16,512]{2,1,0:T(8,128)(2,1)S(1)}, u32[]{:S(2)}, u32[]{:S(2)}) collective-permute-start(bf16[2,16,512]{2,1,0:T(8,128)(2,1)} %fusion.8), channel_id=1, source_target_pairs={{1,0},{5,1},{9,2},{13,3},{0,4},{4,5},{8,6},{12,7},{3,8},{7,9},{11,... | collective-permute-start | bytes 98312 | tf_op jit(solution)/shard_map/ppermute | solution.py:182
  10.4 5.1 %collective-permute-start.3 = (bf16[1,16,512]{2,1,0:T(8,128)(2,1)S(1)}, bf16[1,16,512]{2,1,0:T(8,128)(2,1)S(1)}, u32[]{:S(2)}, u32[]{:S(2)}) collective-permute-start(bf16[1,16,512]{2,1,0:T(8,128)(2,1)S(1)} %grads.1.mine_ref), channel_id=1, source_target_pairs={{2,0},{13,1},{0,2},{15,3},{6,4},{9,5},{4,6},{11,7},{10,8},{5,9},{8... | collective-permute-start | bytes 49160 | tf_op jit(solution)/shard_map/ppermute | solution.py:198
  13.8 3.7 %collective-permute-start.2 = (bf16[1,16,512]{2,1,0:T(8,128)(2,1)S(1)}, bf16[1,16,512]{2,1,0:T(8,128)(2,1)S(1)}, u32[]{:S(2)}, u32[]{:S(2)}) collective-permute-start(bf16[1,16,512]{2,1,0:T(8,128)(2,1)S(1)} %grads.1.mine_ref), channel_id=1, source_target_pairs={{4,0},{9,1},{6,2},{11,3},{0,4},{13,5},{2,6},{15,7},{12,8},{1,9},{1... | collective-permute-start | bytes 49160 | tf_op jit(solution)/shard_map/ppermute | solution.py:198
  17.5 1.2 %collective-permute-start.5 = (bf16[2,16,512]{2,1,0:T(8,128)(2,1)S(1)}, bf16[2,16,512]{2,1,0:T(8,128)(2,1)S(1)}, u32[]{:S(2)}, u32[]{:S(2)}) collective-permute-start(bf16[2,16,512]{2,1,0:T(8,128)(2,1)S(1)} %pad_maximum_fusion.2), channel_id=1, source_target_pairs={{1,0},{0,1},{3,2},{2,3},{5,4},{4,5},{7,6},{6,7},{9,8},{8,9},{11,10... | collective-permute-start | bytes 98312 | tf_op jit(solution)/shard_map/ppermute | solution.py:155

commit v7 on v5

--- a/solution.py
+++ b/solution.py
@@ -16,8 +16,7 @@
 PARAMS = pltpu.CompilerParams(vmem_limit_bytes=16 * 1024 * 1024)
 
 
-def prepare_kernel(basis, q_ref, chunk_ref, pick_x_ref, pick_g_ref):
-    chunk_ref[...] = q_ref[...]
+def picks_kernel(basis, pick_x_ref, pick_g_ref):
     rows, width = pick_g_ref.shape
     lanes, pair = pick_x_ref.shape[1], 2 * basis
     row = lax.broadcasted_iota(jnp.int32, (rows, lanes), 0) % pair
@@ -28,6 +27,10 @@
         pick_g_ref[:, j * lanes : (j + 1) * lanes] = jnp.where(gap == j * (lanes // basis), 1.0, 0.0).astype(BF16)
 
 
+def chunk_kernel(in_ref, out_ref):
+    out_ref[...] = in_ref[...]
+
+
 def grads_kernel(n_sub, *refs):
     parts, (pick_x_ref, pick_g_ref, out_ref) = refs[:n_sub], refs[n_sub:]
     total = parts[0][...]
@@ -36,14 +39,16 @@
     high = total.astype(BF16).astype(F32)
     rest = total - high
     mid = rest.astype(BF16).astype(F32)
-    pieces = jnp.concatenate([high, mid, rest - mid]).astype(BF16)
-    own = pieces.shape[1] // LEN
+    low = rest - mid
+    pieces = [jnp.concatenate([high, mid]).T, jnp.concatenate([low, jnp.zeros_like(low)]).T]
+    pieces = jnp.concatenate(pieces, axis=1).astype(BF16)
+    own = pieces.shape[0] // LEN
     lanes, width = pick_x_ref.shape[1], pick_g_ref.shape[1]
-    tiled_x = lax.dot_general(pieces, pick_x_ref[...], FIRST, preferred_element_type=F32)
+    tiled_x = jnp.dot(pieces, pick_x_ref[...], preferred_element_type=F32)
     tiles = []
     for j in range(width // lanes):
         pick_g = pick_g_ref[:, j * lanes : (j + 1) * lanes]
-        product = lax.dot_general(pieces, pick_g, FIRST, preferred_element_type=F32) * tiled_x
+        product = jnp.dot(pieces, pick_g, preferred_element_type=F32) * tiled_x
         tiles.append(product.reshape(own, LEN, lanes).sum(axis=1))
     grads = jnp.concatenate(tiles, axis=1)
     high = grads.astype(BF16).astype(F32)
@@ -130,12 +135,8 @@
         (flat(ex, lay, sub), flat((lay + 1) % n_lay * group + ex % group, ex // group, sub)) for ex, lay, sub in devices
     ]
 
-    far = [("ex", k) for k in range(3, n_ex)]
-    across = [("lay", k) for k in range(1, n_lay)]
-    moves = [("ex", 1), ("ex", 2)]
-    while far or across:
-        moves += across[:1] + far[:1]
-        across, far = across[1:], far[1:]
+    moves = [("ex", 1), ("ex", 3), ("lay", 1), ("ex", 2)]
+    moves += [("ex", k) for k in range(4, n_ex)] + [("lay", k) for k in range(2, n_lay)]
     rounds = -(-len(moves) // n_sub)
 
     def source_of(at, ex, lay, sub):
@@ -153,23 +154,30 @@
         rows, half = queries.shape[1:]
 
         chunk = lax.ppermute(queries[0], AXES, query_pairs)
+        pick_x, pick_g = pl.pallas_call(
+            functools.partial(picks_kernel, basis),
+            out_shape=(
+                jax.ShapeDtypeStruct((8 * basis, 4 * basis), BF16),
+                jax.ShapeDtypeStruct((8 * basis, width), BF16),
+            ),
+            out_specs=(VMEM,) * 2,
+            compiler_params=PARAMS,
+            cost_estimate=pl.CostEstimate(flops=3 * 10**8, bytes_accessed=0, transcendentals=0),
+            name="picks",
+        )()
+        basis_in, basis_out, pick_x = lax.optimization_barrier((basis_in, basis_out, pick_x))
         proj_x = lax.dot_general(basis_in[0], layer_inputs[0], LAST, preferred_element_type=F32)
         proj_g = lax.dot_general(basis_out[0], output_grads[0], LAST, preferred_element_type=F32)
         proj = jnp.concatenate([proj_x, proj_g])
         parts = [proj] + [rotate(proj, k) for k in range(1, n_sub)]
-
-        chunk, pick_x, pick_g = pl.pallas_call(
-            functools.partial(prepare_kernel, basis),
-            out_shape=(
-                jax.ShapeDtypeStruct((rows, half), BF16),
-                jax.ShapeDtypeStruct((6 * basis, 4 * basis), BF16),
-                jax.ShapeDtypeStruct((6 * basis, width), BF16),
-            ),
+        chunk = pl.pallas_call(
+            chunk_kernel,
+            out_shape=jax.ShapeDtypeStruct((rows, half), BF16),
             in_specs=[VMEM],
-            out_specs=(VMEM,) * 3,
+            out_specs=VMEM,
             compiler_params=PARAMS,
             cost_estimate=pl.CostEstimate(flops=10**11, bytes_accessed=10**9, transcendentals=0),
-            name="prepare",
+            name="chunk",
         )(chunk)
         chunks = [chunk] + [rotate(chunk, k) for k in range(1, n_sub)]
 

time: 18.1 us -> 17.7 us (0.978)
  matrix products: 1.72 us -> 0.82 us
  local copies, waits for them, and re-layouts: 0.02 us -> 0.5 us
    dot_general x1, matrix products: 1.31 us -> 0.41 us  [body(): lax.dot_general(basis_in[0], layer_inputs[0], LAST, preferred_element_typ...]
    unnamed x6 -> x8, local copies, waits for them, and re-layouts: 0.02 us -> 0.5 us
    ppermute x3, waiting for transfers between devices: 1.5 us -> 1.68 us  [rotate(): lax.ppermute(value, 'sub', [((i + k) % n_sub, i) for i in range(n_sub)])]
    ppermute x3, starting transfers between devices: 2.35 us -> 2.17 us  [rotate(): lax.ppermute(value, 'sub', [((i + k) % n_sub, i) for i in range(n_sub)])]
  transfers between devices with their start and end apart: 6 -> 6, of which waited for: 4 -> 5; matrix products, arithmetic and copies ran while one was open for 10% -> 5% of each run, Pallas kernels for 4% -> 4%
where the time goes in v7:
time: 17.7 us; the launch traced here: 17.6 us
  starting transfers between devices  9.37 us (53%)
  waiting for transfers between devices  4.3 us (24%)
  Pallas kernels  1.76 us (10%)
  matrix products  0.82 us (5%)
  between operations  0.74 us (4%)
  local copies, waits for them, and re-layouts  0.5 us (3%)
    ppermute x1, starting transfers between devices, body(): chunk = lax.ppermute(queries[0], AXES, query_pairs)  4.09 us
    ppermute x2, starting transfers between devices, body(): received.append(lax.ppermute(mine, AXES, pairs))  3.12 us
    ppermute x2, waiting for transfers between devices, body(): received.append(lax.ppermute(mine, AXES, pairs))  2.57 us
    ppermute x3, starting transfers between devices, rotate(): lax.ppermute(value, 'sub', [((i + k) % n_sub, i) for i in range(n_sub)])  2.17 us
    ppermute x3, waiting for transfers between devices, rotate(): lax.ppermute(value, 'sub', [((i + k) % n_sub, i) for i in range(n_sub)])  1.68 us
    pallas_call x1, Pallas kernels, body(): pl.pallas_call(functools.partial(final_kernel, n_ex, n_lay, n_sub, own, m...  1.08 us
    pallas_call x1, Pallas kernels, body(): pl.pallas_call(functools.partial(grads_kernel, n_sub), out_shape=jax.Shap...  0.53 us
    unnamed x8, local copies, waits for them, and re-layouts  0.5 us
  transfers between devices with their start and end apart: 6, of which 5 were waited for; matrix products, arithmetic and copies ran while one was open for 5% of the time, Pallas kernels for 4%

profile of v7, /device:TPU:0, one launch (start us, length us, event | category | flops | bytes accessed | tf_op | source)
XLA Modules:
  0.0 17.6 jit_solution(6385749556689631679)
XLA Ops:
  0.6 0.0 copy-start
  0.6 0.0 copy-start.2
  0.7 0.0 copy-start.1
  0.7 4.1 %collective-permute-start.1 = (bf16[16,512]{1,0:T(8,128)(2,1)}, bf16[16,512]{1,0:T(8,128)(2,1)S(1)}, u32[]{:S(2)}, u32[]{:S(2)}) collective-permute-start(bf16[16,512]{1,0:T(8,128)(2,1)} %bitcast.15), channel_id=1, source_target_pairs={{0,8},{1,9},{2,0},{3,1},{4,12},{5,13},{6,4},{7,5},{8,10},{9,11},{1... | collective-permute-start | bytes 49160 | tf_op jit(solution)/shard_map/ppermute | solution.py:156
  4.8 0.1 picks.1
  4.9 0.0 copy-done
  4.9 0.0 copy-done.2
  4.9 0.0 copy-start.3
  4.9 0.4 %fusion.2 = f32[32,256]{1,0:T(8,128)S(1)} fusion(bf16[1,256,2048]{2,1,0:T(8,128)(2,1)S(1)} %copy-done, bf16[1,32,2048]{2,1,0:T(8,128)(2,1)S(1)} %copy-done.2), kind=kOutput, calls=%fused_computation.2 | convolution fusion | flops 33554432 | bytes 1212416 | tf_op jit(solution)/shard_map/dot_general | solution.py:169
  5.4 0.0 copy-done.1
  5.4 0.5 %copy-done.3 = bf16[1,32,2048]{2,1,0:T(8,128)(2,1)S(1)} copy-done((bf16[1,32,2048]{2,1,0:T(8,128)(2,1)S(1)}, bf16[1,32,2048]{2,1,0:T(8,128)(2,1)}, u32[]{:S(2)}) %copy-start.3) | copy-done | bytes 131096
  5.8 0.4 %fusion = f32[32,256]{1,0:T(8,128)S(1)} fusion(bf16[1,256,2048]{2,1,0:T(8,128)(2,1)S(1)} %copy-done.1, bf16[1,32,2048]{2,1,0:T(8,128)(2,1)S(1)} %copy-done.3), kind=kOutput, calls=%fused_computation | convolution fusion | flops 33554432 | bytes 1212416 | tf_op jit(solution)/shard_map/dot_general | solution.py:170
  6.3 0.1 collective-permute-start
  6.4 0.1 collective-permute-done.1.in_ref
  6.4 0.4 %collective-permute-start.2 = (bf16[16,512]{1,0:T(8,128)(2,1)S(1)}, bf16[16,512]{1,0:T(8,128)(2,1)S(1)}, u32[]{:S(2)}, u32[]{:S(2)}) collective-permute-start(bf16[16,512]{1,0:T(8,128)(2,1)S(1)} %chunk.1), channel_id=1, source_target_pairs={{1,0},{0,1},{3,2},{2,3},{5,4},{4,5},{7,6},{6,7},{9,8},{8,9},{11,10... | collective-permute-start | bytes 49160 | tf_op jit(solution)/shard_map/ppermute | solution.py:147
  6.9 0.7 %collective-permute-done.refs_1_ = f32[64,256]{1,0:T(8,128)S(1)} collective-permute-done((f32[64,256]{1,0:T(8,128)S(1)}, f32[64,256]{1,0:T(8,128)S(1)}, u32[]{:S(2)}, u32[]{:S(2)}) %collective-permute-start) | collective-permute-done | bytes 65568 | tf_op jit(solution)/shard_map/ppermute | solution.py:147
  7.6 0.5 %grads.1 = bf16[16,512]{1,0:T(8,128)(2,1)S(1)} custom-call(f32[64,256]{1,0:T(8,128)S(1)} %pad_maximum_fusion.2.refs_0_, f32[64,256]{1,0:T(8,128)S(1)} %collective-permute-done.refs_1_, bf16[256,128]{1,0:T(8,128)(2,1)S(1)} %get-tuple-element.10.refs_2_, bf16[256,1024]{1,0:T(8,128)(2,1)S(1)} %get-tuple-element.11.refs_3_), custom_call_target="tpu_custom_call" | custom-call | tf_op jit(solution)/shard_map/grads/pallas_call | solution.py:184
  8.1 0.0 collective-permute-done.2
  8.2 1.6 %collective-permute-start.4 = (bf16[1,48,512]{2,1,0:T(8,128)(2,1)S(1)}, bf16[1,48,512]{2,1,0:T(8,128)(2,1)S(1)}, u32[]{:S(2)}, u32[]{:S(2)}) collective-permute-start(bf16[1,48,512]{2,1,0:T(8,128)(2,1)S(1)} %maximum_bitcast_fusion.mine_ref), channel_id=1, source_target_pairs={{2,0},{9,1},{0,2},{11,3},{6,4},{13,5},{4,6},{15,7},{10,8},{1,9},{8... | collective-permute-start | bytes 147464 | tf_op jit(solution)/shard_map/ppermute | solution.py:197
  9.8 1.5 %collective-permute-start.3 = (bf16[1,48,512]{2,1,0:T(8,128)(2,1)S(1)}, bf16[1,48,512]{2,1,0:T(8,128)(2,1)S(1)}, u32[]{:S(2)}, u32[]{:S(2)}) collective-permute-start(bf16[1,48,512]{2,1,0:T(8,128)(2,1)S(1)} %maximum_bitcast_fusion.mine_ref), channel_id=1, source_target_pairs={{4,0},{13,1},{6,2},{15,3},{0,4},{9,5},{2,6},{11,7},{12,8},{5,9},{1... | collective-permute-start | bytes 147464 | tf_op jit(solution)/shard_map/ppermute | solution.py:197
  11.3 1.0 %collective-permute-done.4 = bf16[1,48,512]{2,1,0:T(8,128)(2,1)S(1)} collective-permute-done((bf16[1,48,512]{2,1,0:T(8,128)(2,1)S(1)}, bf16[1,48,512]{2,1,0:T(8,128)(2,1)S(1)}, u32[]{:S(2)}, u32[]{:S(2)}) %collective-permute-start.4) | collective-permute-done | bytes 49184 | tf_op jit(solution)/shard_map/ppermute | solution.py:197
  12.3 1.5 %collective-permute-done.3 = bf16[1,48,512]{2,1,0:T(8,128)(2,1)S(1)} collective-permute-done((bf16[1,48,512]{2,1,0:T(8,128)(2,1)S(1)}, bf16[1,48,512]{2,1,0:T(8,128)(2,1)S(1)}, u32[]{:S(2)}, u32[]{:S(2)}) %collective-permute-start.3) | collective-permute-done | bytes 49184 | tf_op jit(solution)/shard_map/ppermute | solution.py:197
  13.9 1.6 %collective-permute-start.5 = (bf16[2,48,512]{2,1,0:T(8,128)(2,1)S(1)}, bf16[2,48,512]{2,1,0:T(8,128)(2,1)S(1)}, u32[]{:S(2)}, u32[]{:S(2)}) collective-permute-start(bf16[2,48,512]{2,1,0:T(8,128)(2,1)S(1)} %pad_maximum_fusion.1), channel_id=1, source_target_pairs={{1,0},{0,1},{3,2},{2,3},{5,4},{4,5},{7,6},{6,7},{9,8},{8,9},{11,10... | collective-permute-start | bytes 294920 | tf_op jit(solution)/shard_map/ppermute | solution.py:147
  15.5 0.9 %collective-permute-done.5 = bf16[2,48,512]{2,1,0:T(8,128)(2,1)S(1)} collective-permute-done((bf16[2,48,512]{2,1,0:T(8,128)(2,1)S(1)}, bf16[2,48,512]{2,1,0:T(8,128)(2,1)S(1)}, u32[]{:S(2)}, u32[]{:S(2)}) %collective-permute-start.5) | collective-permute-done | bytes 98336 | tf_op jit(solution)/shard_map/ppermute | solution.py:147
  16.5 1.1 %gram_and_scores.1 = (f32[1,256,512]{2,1,0:T(8,128)}, f32[4,16]{1,0:T(4,128)}) custom-call(bf16[1,48,512]{2,1,0:T(8,128)(2,1)S(1)} %maximum_bitcast_fusion.mine_ref, bf16[4,48,512]{2,1,0:T(8,128)(2,1)S(1)} %pad_maximum_fusion.got_ref), custom_call_target="tpu_custom_call" | custom-call | tf_op jit(solution)/shard_map/gram_and_scores/pallas_call | solution.py:201
  (5 shorter events, 0.1 us)
Async XLA Ops:
  0.6 4.3 %copy-start = (bf16[1,256,2048]{2,1,0:T(8,128)(2,1)S(1)}, bf16[1,256,2048]{2,1,0:T(8,128)(2,1)}, u32[]{:S(2)}) copy-start(bf16[1,256,2048]{2,1,0:T(8,128)(2,1)} %param.5) | copy-start | bytes 3145732
  0.6 4.3 %copy-start.2 = (bf16[1,32,2048]{2,1,0:T(8,128)(2,1)S(1)}, bf16[1,32,2048]{2,1,0:T(8,128)(2,1)}, u32[]{:S(2)}) copy-start(bf16[1,32,2048]{2,1,0:T(8,128)(2,1)} %param.7) | copy-start | bytes 393220
  0.7 4.7 %copy-start.1 = (bf16[1,256,2048]{2,1,0:T(8,128)(2,1)S(1)}, bf16[1,256,2048]{2,1,0:T(8,128)(2,1)}, u32[]{:S(2)}) copy-start(bf16[1,256,2048]{2,1,0:T(8,128)(2,1)} %param.6) | copy-start | bytes 3145732
  0.7 5.7 %collective-permute-start.1 = (bf16[16,512]{1,0:T(8,128)(2,1)}, bf16[16,512]{1,0:T(8,128)(2,1)S(1)}, u32[]{:S(2)}, u32[]{:S(2)}) collective-permute-start(bf16[16,512]{1,0:T(8,128)(2,1)} %bitcast.15), channel_id=1, source_target_pairs={{0,8},{1,9},{2,0},{3,1},{4,12},{5,13},{6,4},{7,5},{8,10},{9,11},{1... | collective-permute-start | bytes 49160 | tf_op jit(solution)/shard_map/ppermute | solution.py:156
  4.9 0.9 %copy-start.3 = (bf16[1,32,2048]{2,1,0:T(8,128)(2,1)S(1)}, bf16[1,32,2048]{2,1,0:T(8,128)(2,1)}, u32[]{:S(2)}) copy-start(bf16[1,32,2048]{2,1,0:T(8,128)(2,1)} %param.8) | copy-start | bytes 393220
  6.3 1.3 %collective-permute-start = (f32[64,256]{1,0:T(8,128)S(1)}, f32[64,256]{1,0:T(8,128)S(1)}, u32[]{:S(2)}, u32[]{:S(2)}) collective-permute-start(f32[64,256]{1,0:T(8,128)S(1)} %pad_maximum_fusion.2.refs_0_), channel_id=1, source_target_pairs={{1,0},{0,1},{3,2},{2,3},{5,4},{4,5},{7,6},{6,7},{9,8},{8,9},{11,10... | collective-permute-start | bytes 196616 | tf_op jit(solution)/shard_map/ppermute | solution.py:147
  6.4 1.7 %collective-permute-start.2 = (bf16[16,512]{1,0:T(8,128)(2,1)S(1)}, bf16[16,512]{1,0:T(8,128)(2,1)S(1)}, u32[]{:S(2)}, u32[]{:S(2)}) collective-permute-start(bf16[16,512]{1,0:T(8,128)(2,1)S(1)} %chunk.1), channel_id=1, source_target_pairs={{1,0},{0,1},{3,2},{2,3},{5,4},{4,5},{7,6},{6,7},{9,8},{8,9},{11,10... | collective-permute-start | bytes 49160 | tf_op jit(solution)/shard_map/ppermute | solution.py:147
  8.2 4.2 %collective-permute-start.4 = (bf16[1,48,512]{2,1,0:T(8,128)(2,1)S(1)}, bf16[1,48,512]{2,1,0:T(8,128)(2,1)S(1)}, u32[]{:S(2)}, u32[]{:S(2)}) collective-permute-start(bf16[1,48,512]{2,1,0:T(8,128)(2,1)S(1)} %maximum_bitcast_fusion.mine_ref), channel_id=1, source_target_pairs={{2,0},{9,1},{0,2},{11,3},{6,4},{13,5},{4,6},{15,7},{10,8},{1,9},{8... | collective-permute-start | bytes 147464 | tf_op jit(solution)/shard_map/ppermute | solution.py:197
  9.8 4.1 %collective-permute-start.3 = (bf16[1,48,512]{2,1,0:T(8,128)(2,1)S(1)}, bf16[1,48,512]{2,1,0:T(8,128)(2,1)S(1)}, u32[]{:S(2)}, u32[]{:S(2)}) collective-permute-start(bf16[1,48,512]{2,1,0:T(8,128)(2,1)S(1)} %maximum_bitcast_fusion.mine_ref), channel_id=1, source_target_pairs={{4,0},{13,1},{6,2},{15,3},{0,4},{9,5},{2,6},{11,7},{12,8},{5,9},{1... | collective-permute-start | bytes 147464 | tf_op jit(solution)/shard_map/ppermute | solution.py:197
  13.9 2.6 %collective-permute-start.5 = (bf16[2,48,512]{2,1,0:T(8,128)(2,1)S(1)}, bf16[2,48,512]{2,1,0:T(8,128)(2,1)S(1)}, u32[]{:S(2)}, u32[]{:S(2)}) collective-permute-start(bf16[2,48,512]{2,1,0:T(8,128)(2,1)S(1)} %pad_maximum_fusion.1), channel_id=1, source_target_pairs={{1,0},{0,1},{3,2},{2,3},{5,4},{4,5},{7,6},{6,7},{9,8},{8,9},{11,10... | collective-permute-start | bytes 294920 | tf_op jit(solution)/shard_map/ppermute | solution.py:147

commit v8 on v7

--- a/solution.py
+++ b/solution.py
@@ -87,7 +87,7 @@
         core = at % n_sub
         piece = got_ref[lax.rem(core - sub + n_sub, n_sub) * rounds + at // n_sub]
         if axis == "ex":
-            slots.append((piece, core, ex ^ k))
+            slots.append((piece, core, lax.rem(ex + k, n_ex)))
         else:
             layers.append(halves_of(piece))
 
@@ -135,13 +135,13 @@
         (flat(ex, lay, sub), flat((lay + 1) % n_lay * group + ex % group, ex // group, sub)) for ex, lay, sub in devices
     ]
 
-    moves = [("ex", 1), ("ex", 3), ("lay", 1), ("ex", 2)]
-    moves += [("ex", k) for k in range(4, n_ex)] + [("lay", k) for k in range(2, n_lay)]
+    moves = [("ex", 1), ("ex", 2), ("lay", 1), ("ex", n_ex - 1)]
+    moves += [("ex", k) for k in range(3, n_ex - 1)] + [("lay", k) for k in range(2, n_lay)]
     rounds = -(-len(moves) // n_sub)
 
     def source_of(at, ex, lay, sub):
         axis, k = moves[min(at * n_sub + sub, len(moves) - 1)]
-        return flat(ex ^ k, lay, sub) if axis == "ex" else flat(ex, (lay + k) % n_lay, sub)
+        return flat((ex + k) % n_ex, lay, sub) if axis == "ex" else flat(ex, (lay + k) % n_lay, sub)
 
     def rotate(value, k):
         return lax.ppermute(value, "sub", [((i + k) % n_sub, i) for i in range(n_sub)])

time: 17.7 us -> 17.1 us (0.966)
  starting transfers between devices: 9.37 us -> 8.92 us
    ppermute x3, starting transfers between devices: 2.17 us -> 0.59 us  [rotate(): lax.ppermute(value, 'sub', [((i + k) % n_sub, i) for i in range(n_sub)])]
    ppermute x2, starting transfers between devices: 3.12 us -> 4.25 us  [body(): received.append(lax.ppermute(mine, AXES, pairs))]
    ppermute x2, waiting for transfers between devices: 2.57 us -> 2.06 us  [body(): received.append(lax.ppermute(mine, AXES, pairs))]
    ppermute x3, waiting for transfers between devices: 1.68 us -> 2.03 us  [rotate(): lax.ppermute(value, 'sub', [((i + k) % n_sub, i) for i in range(n_sub)])]
  transfers between devices with their start and end apart: 6 -> 6, of which waited for: 5 -> 4; matrix products, arithmetic and copies ran while one was open for 5% -> 5% of each run, Pallas kernels for 4% -> 4%
where the time goes in v8:
time: 17.1 us; the launch traced here: 17 us
  starting transfers between devices  8.92 us (52%)
  waiting for transfers between devices  4.15 us (24%)
  Pallas kernels  1.76 us (10%)
  matrix products  0.82 us (5%)
  between operations  0.75 us (4%)
  local copies, waits for them, and re-layouts  0.5 us (3%)
    ppermute x2, starting transfers between devices, body(): received.append(lax.ppermute(mine, AXES, pairs))  4.25 us
    ppermute x1, starting transfers between devices, body(): chunk = lax.ppermute(queries[0], AXES, query_pairs)  4.09 us
    ppermute x2, waiting for transfers between devices, body(): received.append(lax.ppermute(mine, AXES, pairs))  2.06 us
    ppermute x3, waiting for transfers between devices, rotate(): lax.ppermute(value, 'sub', [((i + k) % n_sub, i) for i in range(n_sub)])  2.03 us
    pallas_call x1, Pallas kernels, body(): pl.pallas_call(functools.partial(final_kernel, n_ex, n_lay, n_sub, own, m...  1.08 us
    ppermute x3, starting transfers between devices, rotate(): lax.ppermute(value, 'sub', [((i + k) % n_sub, i) for i in range(n_sub)])  0.59 us
    pallas_call x1, Pallas kernels, body(): pl.pallas_call(functools.partial(grads_kernel, n_sub), out_shape=jax.Shap...  0.53 us
    unnamed x8, local copies, waits for them, and re-layouts  0.5 us
  transfers between devices with their start and end apart: 6, of which 4 were waited for; matrix products, arithmetic and copies ran while one was open for 5% of the time, Pallas kernels for 4%

profile of v8, /device:TPU:0, one launch (start us, length us, event | category | flops | bytes accessed | tf_op | source)
XLA Modules:
  0.0 17.0 jit_solution(17746886085694698267)
XLA Ops:
  0.6 0.0 copy-start
  0.6 0.0 copy-start.2
  0.7 0.0 copy-start.1
  0.7 4.1 %collective-permute-start.1 = (bf16[16,512]{1,0:T(8,128)(2,1)}, bf16[16,512]{1,0:T(8,128)(2,1)S(1)}, u32[]{:S(2)}, u32[]{:S(2)}) collective-permute-start(bf16[16,512]{1,0:T(8,128)(2,1)} %bitcast.15), channel_id=1, source_target_pairs={{0,8},{1,9},{2,0},{3,1},{4,12},{5,13},{6,4},{7,5},{8,10},{9,11},{1... | collective-permute-start | bytes 49160 | tf_op jit(solution)/shard_map/ppermute | solution.py:156
  4.8 0.1 picks.1
  4.9 0.0 copy-done
  4.9 0.0 copy-done.2
  4.9 0.0 copy-start.3
  4.9 0.4 %fusion.2 = f32[32,256]{1,0:T(8,128)S(1)} fusion(bf16[1,256,2048]{2,1,0:T(8,128)(2,1)S(1)} %copy-done, bf16[1,32,2048]{2,1,0:T(8,128)(2,1)S(1)} %copy-done.2), kind=kOutput, calls=%fused_computation.2 | convolution fusion | flops 33554432 | bytes 1212416 | tf_op jit(solution)/shard_map/dot_general | solution.py:169
  5.4 0.0 copy-done.1
  5.4 0.5 %copy-done.3 = bf16[1,32,2048]{2,1,0:T(8,128)(2,1)S(1)} copy-done((bf16[1,32,2048]{2,1,0:T(8,128)(2,1)S(1)}, bf16[1,32,2048]{2,1,0:T(8,128)(2,1)}, u32[]{:S(2)}) %copy-start.3) | copy-done | bytes 131096
  5.8 0.4 %fusion = f32[32,256]{1,0:T(8,128)S(1)} fusion(bf16[1,256,2048]{2,1,0:T(8,128)(2,1)S(1)} %copy-done.1, bf16[1,32,2048]{2,1,0:T(8,128)(2,1)S(1)} %copy-done.3), kind=kOutput, calls=%fused_computation | convolution fusion | flops 33554432 | bytes 1212416 | tf_op jit(solution)/shard_map/dot_general | solution.py:170
  6.3 0.1 collective-permute-start
  6.4 0.1 collective-permute-done.1.in_ref
  6.4 0.4 %collective-permute-start.2 = (bf16[16,512]{1,0:T(8,128)(2,1)S(1)}, bf16[16,512]{1,0:T(8,128)(2,1)S(1)}, u32[]{:S(2)}, u32[]{:S(2)}) collective-permute-start(bf16[16,512]{1,0:T(8,128)(2,1)S(1)} %chunk.1), channel_id=1, source_target_pairs={{1,0},{0,1},{3,2},{2,3},{5,4},{4,5},{7,6},{6,7},{9,8},{8,9},{11,10... | collective-permute-start | bytes 49160 | tf_op jit(solution)/shard_map/ppermute | solution.py:147
  6.9 0.7 %collective-permute-done.refs_1_ = f32[64,256]{1,0:T(8,128)S(1)} collective-permute-done((f32[64,256]{1,0:T(8,128)S(1)}, f32[64,256]{1,0:T(8,128)S(1)}, u32[]{:S(2)}, u32[]{:S(2)}) %collective-permute-start) | collective-permute-done | bytes 65568 | tf_op jit(solution)/shard_map/ppermute | solution.py:147
  7.6 0.5 %grads.1 = bf16[16,512]{1,0:T(8,128)(2,1)S(1)} custom-call(f32[64,256]{1,0:T(8,128)S(1)} %pad_maximum_fusion.2.refs_0_, f32[64,256]{1,0:T(8,128)S(1)} %collective-permute-done.refs_1_, bf16[256,128]{1,0:T(8,128)(2,1)S(1)} %get-tuple-element.10.refs_2_, bf16[256,1024]{1,0:T(8,128)(2,1)S(1)} %get-tuple-element.11.refs_3_), custom_call_target="tpu_custom_call" | custom-call | tf_op jit(solution)/shard_map/grads/pallas_call | solution.py:184
  8.1 0.0 collective-permute-done.2
  8.2 1.6 %collective-permute-start.4 = (bf16[1,48,512]{2,1,0:T(8,128)(2,1)S(1)}, bf16[1,48,512]{2,1,0:T(8,128)(2,1)S(1)}, u32[]{:S(2)}, u32[]{:S(2)}) collective-permute-start(bf16[1,48,512]{2,1,0:T(8,128)(2,1)S(1)} %maximum_bitcast_fusion.mine_ref), channel_id=1, source_target_pairs={{2,0},{13,1},{0,2},{15,3},{6,4},{1,5},{4,6},{3,7},{10,8},{5,9},{8,... | collective-permute-start | bytes 147464 | tf_op jit(solution)/shard_map/ppermute | solution.py:197
  9.8 2.6 %collective-permute-start.3 = (bf16[1,48,512]{2,1,0:T(8,128)(2,1)S(1)}, bf16[1,48,512]{2,1,0:T(8,128)(2,1)S(1)}, u32[]{:S(2)}, u32[]{:S(2)}) collective-permute-start(bf16[1,48,512]{2,1,0:T(8,128)(2,1)S(1)} %maximum_bitcast_fusion.mine_ref), channel_id=1, source_target_pairs={{4,0},{9,1},{6,2},{11,3},{8,4},{13,5},{10,6},{15,7},{12,8},{1,9},{... | collective-permute-start | bytes 147464 | tf_op jit(solution)/shard_map/ppermute | solution.py:197
  12.4 0.0 collective-permute-done.4
  12.4 2.1 %collective-permute-done.3 = bf16[1,48,512]{2,1,0:T(8,128)(2,1)S(1)} collective-permute-done((bf16[1,48,512]{2,1,0:T(8,128)(2,1)S(1)}, bf16[1,48,512]{2,1,0:T(8,128)(2,1)S(1)}, u32[]{:S(2)}, u32[]{:S(2)}) %collective-permute-start.3) | collective-permute-done | bytes 49184 | tf_op jit(solution)/shard_map/ppermute | solution.py:197
  14.5 0.1 collective-permute-start.5
  14.6 1.3 %collective-permute-done.5 = bf16[2,48,512]{2,1,0:T(8,128)(2,1)S(1)} collective-permute-done((bf16[2,48,512]{2,1,0:T(8,128)(2,1)S(1)}, bf16[2,48,512]{2,1,0:T(8,128)(2,1)S(1)}, u32[]{:S(2)}, u32[]{:S(2)}) %collective-permute-start.5) | collective-permute-done | bytes 98336 | tf_op jit(solution)/shard_map/ppermute | solution.py:147
  15.9 1.1 %gram_and_scores.1 = (f32[1,256,512]{2,1,0:T(8,128)}, f32[4,16]{1,0:T(4,128)}) custom-call(bf16[1,48,512]{2,1,0:T(8,128)(2,1)S(1)} %maximum_bitcast_fusion.mine_ref, bf16[4,48,512]{2,1,0:T(8,128)(2,1)S(1)} %pad_maximum_fusion.got_ref), custom_call_target="tpu_custom_call" | custom-call | tf_op jit(solution)/shard_map/gram_and_scores/pallas_call | solution.py:201
  (5 shorter events, 0.1 us)
Async XLA Ops:
  0.6 4.3 %copy-start = (bf16[1,256,2048]{2,1,0:T(8,128)(2,1)S(1)}, bf16[1,256,2048]{2,1,0:T(8,128)(2,1)}, u32[]{:S(2)}) copy-start(bf16[1,256,2048]{2,1,0:T(8,128)(2,1)} %param.5) | copy-start | bytes 3145732
  0.6 4.3 %copy-start.2 = (bf16[1,32,2048]{2,1,0:T(8,128)(2,1)S(1)}, bf16[1,32,2048]{2,1,0:T(8,128)(2,1)}, u32[]{:S(2)}) copy-start(bf16[1,32,2048]{2,1,0:T(8,128)(2,1)} %param.7) | copy-start | bytes 393220
  0.7 4.7 %copy-start.1 = (bf16[1,256,2048]{2,1,0:T(8,128)(2,1)S(1)}, bf16[1,256,2048]{2,1,0:T(8,128)(2,1)}, u32[]{:S(2)}) copy-start(bf16[1,256,2048]{2,1,0:T(8,128)(2,1)} %param.6) | copy-start | bytes 3145732
  0.7 5.7 %collective-permute-start.1 = (bf16[16,512]{1,0:T(8,128)(2,1)}, bf16[16,512]{1,0:T(8,128)(2,1)S(1)}, u32[]{:S(2)}, u32[]{:S(2)}) collective-permute-start(bf16[16,512]{1,0:T(8,128)(2,1)} %bitcast.15), channel_id=1, source_target_pairs={{0,8},{1,9},{2,0},{3,1},{4,12},{5,13},{6,4},{7,5},{8,10},{9,11},{1... | collective-permute-start | bytes 49160 | tf_op jit(solution)/shard_map/ppermute | solution.py:156
  4.9 0.9 %copy-start.3 = (bf16[1,32,2048]{2,1,0:T(8,128)(2,1)S(1)}, bf16[1,32,2048]{2,1,0:T(8,128)(2,1)}, u32[]{:S(2)}) copy-start(bf16[1,32,2048]{2,1,0:T(8,128)(2,1)} %param.8) | copy-start | bytes 393220
  6.3 1.3 %collective-permute-start = (f32[64,256]{1,0:T(8,128)S(1)}, f32[64,256]{1,0:T(8,128)S(1)}, u32[]{:S(2)}, u32[]{:S(2)}) collective-permute-start(f32[64,256]{1,0:T(8,128)S(1)} %pad_maximum_fusion.2.refs_0_), channel_id=1, source_target_pairs={{1,0},{0,1},{3,2},{2,3},{5,4},{4,5},{7,6},{6,7},{9,8},{8,9},{11,10... | collective-permute-start | bytes 196616 | tf_op jit(solution)/shard_map/ppermute | solution.py:147
  6.4 1.7 %collective-permute-start.2 = (bf16[16,512]{1,0:T(8,128)(2,1)S(1)}, bf16[16,512]{1,0:T(8,128)(2,1)S(1)}, u32[]{:S(2)}, u32[]{:S(2)}) collective-permute-start(bf16[16,512]{1,0:T(8,128)(2,1)S(1)} %chunk.1), channel_id=1, source_target_pairs={{1,0},{0,1},{3,2},{2,3},{5,4},{4,5},{7,6},{6,7},{9,8},{8,9},{11,10... | collective-permute-start | bytes 49160 | tf_op jit(solution)/shard_map/ppermute | solution.py:147
  8.2 4.2 %collective-permute-start.4 = (bf16[1,48,512]{2,1,0:T(8,128)(2,1)S(1)}, bf16[1,48,512]{2,1,0:T(8,128)(2,1)S(1)}, u32[]{:S(2)}, u32[]{:S(2)}) collective-permute-start(bf16[1,48,512]{2,1,0:T(8,128)(2,1)S(1)} %maximum_bitcast_fusion.mine_ref), channel_id=1, source_target_pairs={{2,0},{13,1},{0,2},{15,3},{6,4},{1,5},{4,6},{3,7},{10,8},{5,9},{8,... | collective-permute-start | bytes 147464 | tf_op jit(solution)/shard_map/ppermute | solution.py:197
  9.8 4.7 %collective-permute-start.3 = (bf16[1,48,512]{2,1,0:T(8,128)(2,1)S(1)}, bf16[1,48,512]{2,1,0:T(8,128)(2,1)S(1)}, u32[]{:S(2)}, u32[]{:S(2)}) collective-permute-start(bf16[1,48,512]{2,1,0:T(8,128)(2,1)S(1)} %maximum_bitcast_fusion.mine_ref), channel_id=1, source_target_pairs={{4,0},{9,1},{6,2},{11,3},{8,4},{13,5},{10,6},{15,7},{12,8},{1,9},{... | collective-permute-start | bytes 147464 | tf_op jit(solution)/shard_map/ppermute | solution.py:197
  14.5 1.4 %collective-permute-start.5 = (bf16[2,48,512]{2,1,0:T(8,128)(2,1)S(1)}, bf16[2,48,512]{2,1,0:T(8,128)(2,1)S(1)}, u32[]{:S(2)}, u32[]{:S(2)}) collective-permute-start(bf16[2,48,512]{2,1,0:T(8,128)(2,1)S(1)} %pad_maximum_fusion.1), channel_id=1, source_target_pairs={{1,0},{0,1},{3,2},{2,3},{5,4},{4,5},{7,6},{6,7},{9,8},{8,9},{11,10... | collective-permute-start | bytes 294920 | tf_op jit(solution)/shard_map/ppermute | solution.py:147

commit v9 on v8

--- a/solution.py
+++ b/solution.py
@@ -99,7 +99,7 @@
         part = 0.0
         for k in range(n_sub):
             part += lax.dot_general(
-                choose(grads, (core + k) % n_sub).astype(BF16),
+                choose(grads, (core + k + n_sub - 1) % n_sub).astype(BF16),
                 piece[used + k * rows : used + (k + 1) * rows],
                 LAST,
                 preferred_element_type=F32,
@@ -132,7 +132,8 @@
     devices = [(ex, lay, sub) for ex in range(n_ex) for lay in range(n_lay) for sub in range(n_sub)]
 
     query_pairs = [
-        (flat(ex, lay, sub), flat((lay + 1) % n_lay * group + ex % group, ex // group, sub)) for ex, lay, sub in devices
+        (flat(ex, lay, sub), flat((lay + 1) % n_lay * group + ex % group, ex // group, (sub + 1) % n_sub))
+        for ex, lay, sub in devices
     ]
 
     moves = [("ex", 1), ("ex", 2), ("lay", 1), ("ex", n_ex - 1)]

time: 17.1 us -> 16.9 us (0.988)
  starting transfers between devices: 8.92 us -> 8.5 us
  waiting for transfers between devices: 4.15 us -> 4.36 us
    ppermute x1, starting transfers between devices: 4.09 us -> 3.53 us  [body(): chunk = lax.ppermute(queries[0], AXES, query_pairs)]
    ppermute x3, starting transfers between devices: 0.59 us -> 0.91 us  [rotate(): lax.ppermute(value, 'sub', [((i + k) % n_sub, i) for i in range(n_sub)])]
    ppermute x2, waiting for transfers between devices: 2.06 us -> 2.27 us  [body(): received.append(lax.ppermute(mine, AXES, pairs))]
    ppermute x2, starting transfers between devices: 4.25 us -> 4.06 us  [body(): received.append(lax.ppermute(mine, AXES, pairs))]
where the time goes in v9:
time: 16.9 us; the launch traced here: 16.7 us
  starting transfers between devices  8.5 us (50%)
  waiting for transfers between devices  4.36 us (26%)
  Pallas kernels  1.77 us (10%)
  matrix products  0.82 us (5%)
  between operations  0.74 us (4%)
  local copies, waits for them, and re-layouts  0.5 us (3%)
    ppermute x2, starting transfers between devices, body(): received.append(lax.ppermute(mine, AXES, pairs))  4.06 us
    ppermute x1, starting transfers between devices, body(): chunk = lax.ppermute(queries[0], AXES, query_pairs)  3.53 us
    ppermute x2, waiting for transfers between devices, body(): received.append(lax.ppermute(mine, AXES, pairs))  2.27 us
    ppermute x3, waiting for transfers between devices, rotate(): lax.ppermute(value, 'sub', [((i + k) % n_sub, i) for i in range(n_sub)])  2.09 us
    pallas_call x1, Pallas kernels, body(): pl.pallas_call(functools.partial(final_kernel, n_ex, n_lay, n_sub, own, m...  1.08 us
    ppermute x3, starting transfers between devices, rotate(): lax.ppermute(value, 'sub', [((i + k) % n_sub, i) for i in range(n_sub)])  0.91 us
    pallas_call x1, Pallas kernels, body(): pl.pallas_call(functools.partial(grads_kernel, n_sub), out_shape=jax.Shap...  0.54 us
    unnamed x8, local copies, waits for them, and re-layouts  0.5 us
  transfers between devices with their start and end apart: 6, of which 4 were waited for; matrix products, arithmetic and copies ran while one was open for 5% of the time, Pallas kernels for 4%

profile of v9, /device:TPU:0, one launch (start us, length us, event | category | flops | bytes accessed | tf_op | source)
XLA Modules:
  0.0 16.7 jit_solution(15042674732104906069)
XLA Ops:
  0.6 0.0 copy-start
  0.6 0.0 copy-start.2
  0.7 0.0 copy-start.1
  0.7 3.5 %collective-permute-start.1 = (bf16[16,512]{1,0:T(8,128)(2,1)}, bf16[16,512]{1,0:T(8,128)(2,1)S(1)}, u32[]{:S(2)}, u32[]{:S(2)}) collective-permute-start(bf16[16,512]{1,0:T(8,128)(2,1)} %bitcast.15), channel_id=1, source_target_pairs={{0,9},{1,8},{2,1},{3,0},{4,13},{5,12},{6,5},{7,4},{8,11},{9,10},{1... | collective-permute-start | bytes 49160 | tf_op jit(solution)/shard_map/ppermute | solution.py:157
  4.2 0.1 picks.1
  4.4 0.0 copy-done
  4.4 0.0 copy-done.2
  4.4 0.0 copy-start.3
  4.4 0.4 %fusion.2 = f32[32,256]{1,0:T(8,128)S(1)} fusion(bf16[1,256,2048]{2,1,0:T(8,128)(2,1)S(1)} %copy-done, bf16[1,32,2048]{2,1,0:T(8,128)(2,1)S(1)} %copy-done.2), kind=kOutput, calls=%fused_computation.2 | convolution fusion | flops 33554432 | bytes 1212416 | tf_op jit(solution)/shard_map/dot_general | solution.py:170
  4.8 0.0 copy-done.1
  4.8 0.5 %copy-done.3 = bf16[1,32,2048]{2,1,0:T(8,128)(2,1)S(1)} copy-done((bf16[1,32,2048]{2,1,0:T(8,128)(2,1)S(1)}, bf16[1,32,2048]{2,1,0:T(8,128)(2,1)}, u32[]{:S(2)}) %copy-start.3) | copy-done | bytes 131096
  5.3 0.4 %fusion = f32[32,256]{1,0:T(8,128)S(1)} fusion(bf16[1,256,2048]{2,1,0:T(8,128)(2,1)S(1)} %copy-done.1, bf16[1,32,2048]{2,1,0:T(8,128)(2,1)S(1)} %copy-done.3), kind=kOutput, calls=%fused_computation | convolution fusion | flops 33554432 | bytes 1212416 | tf_op jit(solution)/shard_map/dot_general | solution.py:171
  5.7 0.7 %collective-permute-start = (f32[64,256]{1,0:T(8,128)S(1)}, f32[64,256]{1,0:T(8,128)S(1)}, u32[]{:S(2)}, u32[]{:S(2)}) collective-permute-start(f32[64,256]{1,0:T(8,128)S(1)} %pad_maximum_fusion.2.refs_0_), channel_id=1, source_target_pairs={{1,0},{0,1},{3,2},{2,3},{5,4},{4,5},{7,6},{6,7},{9,8},{8,9},{11,10... | collective-permute-start | bytes 196616 | tf_op jit(solution)/shard_map/ppermute | solution.py:148
  6.5 0.0 collective-permute-done.1.in_ref
  6.5 0.1 collective-permute-start.2
  6.6 0.8 %collective-permute-done.refs_1_ = f32[64,256]{1,0:T(8,128)S(1)} collective-permute-done((f32[64,256]{1,0:T(8,128)S(1)}, f32[64,256]{1,0:T(8,128)S(1)}, u32[]{:S(2)}, u32[]{:S(2)}) %collective-permute-start) | collective-permute-done | bytes 65568 | tf_op jit(solution)/shard_map/ppermute | solution.py:148
  7.4 0.5 %grads.1 = bf16[16,512]{1,0:T(8,128)(2,1)S(1)} custom-call(f32[64,256]{1,0:T(8,128)S(1)} %pad_maximum_fusion.2.refs_0_, f32[64,256]{1,0:T(8,128)S(1)} %collective-permute-done.refs_1_, bf16[256,128]{1,0:T(8,128)(2,1)S(1)} %get-tuple-element.10.refs_2_, bf16[256,1024]{1,0:T(8,128)(2,1)S(1)} %get-tuple-element.11.refs_3_), custom_call_target="tpu_custom_call" | custom-call | tf_op jit(solution)/shard_map/grads/pallas_call | solution.py:185
  7.9 0.0 collective-permute-done.2
  7.9 1.2 %collective-permute-start.4 = (bf16[1,48,512]{2,1,0:T(8,128)(2,1)S(1)}, bf16[1,48,512]{2,1,0:T(8,128)(2,1)S(1)}, u32[]{:S(2)}, u32[]{:S(2)}) collective-permute-start(bf16[1,48,512]{2,1,0:T(8,128)(2,1)S(1)} %maximum_bitcast_fusion.mine_ref), channel_id=1, source_target_pairs={{2,0},{13,1},{0,2},{15,3},{6,4},{1,5},{4,6},{3,7},{10,8},{5,9},{8,... | collective-permute-start | bytes 147464 | tf_op jit(solution)/shard_map/ppermute | solution.py:198
  9.1 2.9 %collective-permute-start.3 = (bf16[1,48,512]{2,1,0:T(8,128)(2,1)S(1)}, bf16[1,48,512]{2,1,0:T(8,128)(2,1)S(1)}, u32[]{:S(2)}, u32[]{:S(2)}) collective-permute-start(bf16[1,48,512]{2,1,0:T(8,128)(2,1)S(1)} %maximum_bitcast_fusion.mine_ref), channel_id=1, source_target_pairs={{4,0},{9,1},{6,2},{11,3},{8,4},{13,5},{10,6},{15,7},{12,8},{1,9},{... | collective-permute-start | bytes 147464 | tf_op jit(solution)/shard_map/ppermute | solution.py:198
  12.0 0.1 collective-permute-done.4
  12.1 2.2 %collective-permute-done.3 = bf16[1,48,512]{2,1,0:T(8,128)(2,1)S(1)} collective-permute-done((bf16[1,48,512]{2,1,0:T(8,128)(2,1)S(1)}, bf16[1,48,512]{2,1,0:T(8,128)(2,1)S(1)}, u32[]{:S(2)}, u32[]{:S(2)}) %collective-permute-start.3) | collective-permute-done | bytes 49184 | tf_op jit(solution)/shard_map/ppermute | solution.py:198
  14.3 0.1 collective-permute-start.5
  14.3 1.3 %collective-permute-done.5 = bf16[2,48,512]{2,1,0:T(8,128)(2,1)S(1)} collective-permute-done((bf16[2,48,512]{2,1,0:T(8,128)(2,1)S(1)}, bf16[2,48,512]{2,1,0:T(8,128)(2,1)S(1)}, u32[]{:S(2)}, u32[]{:S(2)}) %collective-permute-start.5) | collective-permute-done | bytes 98336 | tf_op jit(solution)/shard_map/ppermute | solution.py:148
  15.7 1.1 %gram_and_scores.1 = (f32[1,256,512]{2,1,0:T(8,128)}, f32[4,16]{1,0:T(4,128)}) custom-call(bf16[1,48,512]{2,1,0:T(8,128)(2,1)S(1)} %maximum_bitcast_fusion.mine_ref, bf16[4,48,512]{2,1,0:T(8,128)(2,1)S(1)} %pad_maximum_fusion.got_ref), custom_call_target="tpu_custom_call" | custom-call | tf_op jit(solution)/shard_map/gram_and_scores/pallas_call | solution.py:202
  (5 shorter events, 0.1 us)
Async XLA Ops:
  0.6 3.7 %copy-start = (bf16[1,256,2048]{2,1,0:T(8,128)(2,1)S(1)}, bf16[1,256,2048]{2,1,0:T(8,128)(2,1)}, u32[]{:S(2)}) copy-start(bf16[1,256,2048]{2,1,0:T(8,128)(2,1)} %param.5) | copy-start | bytes 3145732
  0.6 3.7 %copy-start.2 = (bf16[1,32,2048]{2,1,0:T(8,128)(2,1)S(1)}, bf16[1,32,2048]{2,1,0:T(8,128)(2,1)}, u32[]{:S(2)}) copy-start(bf16[1,32,2048]{2,1,0:T(8,128)(2,1)} %param.7) | copy-start | bytes 393220
  0.7 4.2 %copy-start.1 = (bf16[1,256,2048]{2,1,0:T(8,128)(2,1)S(1)}, bf16[1,256,2048]{2,1,0:T(8,128)(2,1)}, u32[]{:S(2)}) copy-start(bf16[1,256,2048]{2,1,0:T(8,128)(2,1)} %param.6) | copy-start | bytes 3145732
  0.7 5.8 %collective-permute-start.1 = (bf16[16,512]{1,0:T(8,128)(2,1)}, bf16[16,512]{1,0:T(8,128)(2,1)S(1)}, u32[]{:S(2)}, u32[]{:S(2)}) collective-permute-start(bf16[16,512]{1,0:T(8,128)(2,1)} %bitcast.15), channel_id=1, source_target_pairs={{0,9},{1,8},{2,1},{3,0},{4,13},{5,12},{6,5},{7,4},{8,11},{9,10},{1... | collective-permute-start | bytes 49160 | tf_op jit(solution)/shard_map/ppermute | solution.py:157
  4.4 0.9 %copy-start.3 = (bf16[1,32,2048]{2,1,0:T(8,128)(2,1)S(1)}, bf16[1,32,2048]{2,1,0:T(8,128)(2,1)}, u32[]{:S(2)}) copy-start(bf16[1,32,2048]{2,1,0:T(8,128)(2,1)} %param.8) | copy-start | bytes 393220
  5.7 1.6 %collective-permute-start = (f32[64,256]{1,0:T(8,128)S(1)}, f32[64,256]{1,0:T(8,128)S(1)}, u32[]{:S(2)}, u32[]{:S(2)}) collective-permute-start(f32[64,256]{1,0:T(8,128)S(1)} %pad_maximum_fusion.2.refs_0_), channel_id=1, source_target_pairs={{1,0},{0,1},{3,2},{2,3},{5,4},{4,5},{7,6},{6,7},{9,8},{8,9},{11,10... | collective-permute-start | bytes 196616 | tf_op jit(solution)/shard_map/ppermute | solution.py:148
  6.5 1.4 %collective-permute-start.2 = (bf16[16,512]{1,0:T(8,128)(2,1)S(1)}, bf16[16,512]{1,0:T(8,128)(2,1)S(1)}, u32[]{:S(2)}, u32[]{:S(2)}) collective-permute-start(bf16[16,512]{1,0:T(8,128)(2,1)S(1)} %chunk.1), channel_id=1, source_target_pairs={{1,0},{0,1},{3,2},{2,3},{5,4},{4,5},{7,6},{6,7},{9,8},{8,9},{11,10... | collective-permute-start | bytes 49160 | tf_op jit(solution)/shard_map/ppermute | solution.py:148
  7.9 4.1 %collective-permute-start.4 = (bf16[1,48,512]{2,1,0:T(8,128)(2,1)S(1)}, bf16[1,48,512]{2,1,0:T(8,128)(2,1)S(1)}, u32[]{:S(2)}, u32[]{:S(2)}) collective-permute-start(bf16[1,48,512]{2,1,0:T(8,128)(2,1)S(1)} %maximum_bitcast_fusion.mine_ref), channel_id=1, source_target_pairs={{2,0},{13,1},{0,2},{15,3},{6,4},{1,5},{4,6},{3,7},{10,8},{5,9},{8,... | collective-permute-start | bytes 147464 | tf_op jit(solution)/shard_map/ppermute | solution.py:198
  9.1 5.1 %collective-permute-start.3 = (bf16[1,48,512]{2,1,0:T(8,128)(2,1)S(1)}, bf16[1,48,512]{2,1,0:T(8,128)(2,1)S(1)}, u32[]{:S(2)}, u32[]{:S(2)}) collective-permute-start(bf16[1,48,512]{2,1,0:T(8,128)(2,1)S(1)} %maximum_bitcast_fusion.mine_ref), channel_id=1, source_target_pairs={{4,0},{9,1},{6,2},{11,3},{8,4},{13,5},{10,6},{15,7},{12,8},{1,9},{... | collective-permute-start | bytes 147464 | tf_op jit(solution)/shard_map/ppermute | solution.py:198
  14.3 1.4 %collective-permute-start.5 = (bf16[2,48,512]{2,1,0:T(8,128)(2,1)S(1)}, bf16[2,48,512]{2,1,0:T(8,128)(2,1)S(1)}, u32[]{:S(2)}, u32[]{:S(2)}) collective-permute-start(bf16[2,48,512]{2,1,0:T(8,128)(2,1)S(1)} %pad_maximum_fusion.1), channel_id=1, source_target_pairs={{1,0},{0,1},{3,2},{2,3},{5,4},{4,5},{7,6},{6,7},{9,8},{8,9},{11,10... | collective-permute-start | bytes 294920 | tf_op jit(solution)/shard_map/ppermute | solution.py:148

commit v10 on v9

--- a/solution.py
+++ b/solution.py
@@ -84,8 +84,10 @@
     mine = mine_ref[0]
     layers, slots = [halves_of(mine)], [(mine, sub, ex)]
     for at, (axis, k) in enumerate(moves):
-        core = at % n_sub
-        piece = got_ref[lax.rem(core - sub + n_sub, n_sub) * rounds + at // n_sub]
+        core, turn = at % n_sub, at // n_sub
+        if core == 0 and turn < 2:
+            turn = jnp.where((ex + lay) % 2 == 0, 1 - turn, turn)
+        piece = got_ref[lax.rem(core - sub + n_sub, n_sub) * rounds + turn]
         if axis == "ex":
             slots.append((piece, core, lax.rem(ex + k, n_ex)))
         else:
@@ -141,6 +143,8 @@
     rounds = -(-len(moves) // n_sub)
 
     def source_of(at, ex, lay, sub):
+        if sub == 0 and at < 2 and (ex + lay) % 2 == 0:
+            at = 1 - at
         axis, k = moves[min(at * n_sub + sub, len(moves) - 1)]
         return flat((ex + k) % n_ex, lay, sub) if axis == "ex" else flat(ex, (lay + k) % n_lay, sub)
 

time: 16.9 us -> 16.9 us (level)
  starting transfers between devices: 8.5 us -> 8.96 us
  waiting for transfers between devices: 4.36 us -> 3.94 us
    ppermute x3, starting transfers between devices: 0.91 us -> 1.49 us  [rotate(): lax.ppermute(value, 'sub', [((i + k) % n_sub, i) for i in range(n_sub)])]
    ppermute x3, waiting for transfers between devices: 2.09 us -> 1.75 us  [rotate(): lax.ppermute(value, 'sub', [((i + k) % n_sub, i) for i in range(n_sub)])]
where the time goes in v10:
time: 16.9 us; the launch traced here: 16.8 us
  starting transfers between devices  8.96 us (53%)
  waiting for transfers between devices  3.94 us (23%)
  Pallas kernels  1.77 us (10%)
  matrix products  0.82 us (5%)
  between operations  0.73 us (4%)
  local copies, waits for them, and re-layouts  0.5 us (3%)
    ppermute x2, starting transfers between devices, body(): received.append(lax.ppermute(mine, AXES, pairs))  3.94 us
    ppermute x1, starting transfers between devices, body(): chunk = lax.ppermute(queries[0], AXES, query_pairs)  3.53 us
    ppermute x2, waiting for transfers between devices, body(): received.append(lax.ppermute(mine, AXES, pairs))  2.19 us
    ppermute x3, waiting for transfers between devices, rotate(): lax.ppermute(value, 'sub', [((i + k) % n_sub, i) for i in range(n_sub)])  1.75 us
    ppermute x3, starting transfers between devices, rotate(): lax.ppermute(value, 'sub', [((i + k) % n_sub, i) for i in range(n_sub)])  1.49 us
    pallas_call x1, Pallas kernels, body(): pl.pallas_call(functools.partial(final_kernel, n_ex, n_lay, n_sub, own, m...  1.08 us
    pallas_call x1, Pallas kernels, body(): pl.pallas_call(functools.partial(grads_kernel, n_sub), out_shape=jax.Shap...  0.54 us
    unnamed x8, local copies, waits for them, and re-layouts  0.5 us
  transfers between devices with their start and end apart: 6, of which 4 were waited for; matrix products, arithmetic and copies ran while one was open for 5% of the time, Pallas kernels for 4%

profile of v10, /device:TPU:0, one launch (start us, length us, event | category | flops | bytes accessed | tf_op | source)
XLA Modules:
  0.0 16.8 jit_solution(13451118517304519427)
XLA Ops:
  0.6 0.0 copy-start
  0.6 0.0 copy-start.2
  0.7 0.0 copy-start.1
  0.7 3.5 %collective-permute-start.1 = (bf16[16,512]{1,0:T(8,128)(2,1)}, bf16[16,512]{1,0:T(8,128)(2,1)S(1)}, u32[]{:S(2)}, u32[]{:S(2)}) collective-permute-start(bf16[16,512]{1,0:T(8,128)(2,1)} %bitcast.15), channel_id=1, source_target_pairs={{0,9},{1,8},{2,1},{3,0},{4,13},{5,12},{6,5},{7,4},{8,11},{9,10},{1... | collective-permute-start | bytes 49160 | tf_op jit(solution)/shard_map/ppermute | solution.py:161
  4.2 0.1 picks.1
  4.4 0.0 copy-done
  4.4 0.0 copy-done.2
  4.4 0.0 copy-start.3
  4.4 0.4 %fusion.2 = f32[32,256]{1,0:T(8,128)S(1)} fusion(bf16[1,256,2048]{2,1,0:T(8,128)(2,1)S(1)} %copy-done, bf16[1,32,2048]{2,1,0:T(8,128)(2,1)S(1)} %copy-done.2), kind=kOutput, calls=%fused_computation.2 | convolution fusion | flops 33554432 | bytes 1212416 | tf_op jit(solution)/shard_map/dot_general | solution.py:174
  4.8 0.0 copy-done.1
  4.8 0.5 %copy-done.3 = bf16[1,32,2048]{2,1,0:T(8,128)(2,1)S(1)} copy-done((bf16[1,32,2048]{2,1,0:T(8,128)(2,1)S(1)}, bf16[1,32,2048]{2,1,0:T(8,128)(2,1)}, u32[]{:S(2)}) %copy-start.3) | copy-done | bytes 131096
  5.3 0.4 %fusion = f32[32,256]{1,0:T(8,128)S(1)} fusion(bf16[1,256,2048]{2,1,0:T(8,128)(2,1)S(1)} %copy-done.1, bf16[1,32,2048]{2,1,0:T(8,128)(2,1)S(1)} %copy-done.3), kind=kOutput, calls=%fused_computation | convolution fusion | flops 33554432 | bytes 1212416 | tf_op jit(solution)/shard_map/dot_general | solution.py:175
  5.7 0.7 %collective-permute-start = (f32[64,256]{1,0:T(8,128)S(1)}, f32[64,256]{1,0:T(8,128)S(1)}, u32[]{:S(2)}, u32[]{:S(2)}) collective-permute-start(f32[64,256]{1,0:T(8,128)S(1)} %pad_maximum_fusion.2.refs_0_), channel_id=1, source_target_pairs={{1,0},{0,1},{3,2},{2,3},{5,4},{4,5},{7,6},{6,7},{9,8},{8,9},{11,10... | collective-permute-start | bytes 196616 | tf_op jit(solution)/shard_map/ppermute | solution.py:152
  6.5 0.0 collective-permute-done.1.in_ref
  6.5 0.1 collective-permute-start.2
  6.6 0.8 %collective-permute-done.refs_1_ = f32[64,256]{1,0:T(8,128)S(1)} collective-permute-done((f32[64,256]{1,0:T(8,128)S(1)}, f32[64,256]{1,0:T(8,128)S(1)}, u32[]{:S(2)}, u32[]{:S(2)}) %collective-permute-start) | collective-permute-done | bytes 65568 | tf_op jit(solution)/shard_map/ppermute | solution.py:152
  7.4 0.5 %grads.1 = bf16[16,512]{1,0:T(8,128)(2,1)S(1)} custom-call(f32[64,256]{1,0:T(8,128)S(1)} %pad_maximum_fusion.2.refs_0_, f32[64,256]{1,0:T(8,128)S(1)} %collective-permute-done.refs_1_, bf16[256,128]{1,0:T(8,128)(2,1)S(1)} %get-tuple-element.10.refs_2_, bf16[256,1024]{1,0:T(8,128)(2,1)S(1)} %get-tuple-element.11.refs_3_), custom_call_target="tpu_custom_call" | custom-call | tf_op jit(solution)/shard_map/grads/pallas_call | solution.py:189
  7.9 0.0 collective-permute-done.2
  7.9 1.2 %collective-permute-start.4 = (bf16[1,48,512]{2,1,0:T(8,128)(2,1)S(1)}, bf16[1,48,512]{2,1,0:T(8,128)(2,1)S(1)}, u32[]{:S(2)}, u32[]{:S(2)}) collective-permute-start(bf16[1,48,512]{2,1,0:T(8,128)(2,1)S(1)} %maximum_bitcast_fusion.mine_ref), channel_id=1, source_target_pairs={{4,0},{13,1},{0,2},{15,3},{6,4},{1,5},{10,6},{3,7},{12,8},{5,9},{8... | collective-permute-start | bytes 147464 | tf_op jit(solution)/shard_map/ppermute | solution.py:202
  9.1 2.7 %collective-permute-start.3 = (bf16[1,48,512]{2,1,0:T(8,128)(2,1)S(1)}, bf16[1,48,512]{2,1,0:T(8,128)(2,1)S(1)}, u32[]{:S(2)}, u32[]{:S(2)}) collective-permute-start(bf16[1,48,512]{2,1,0:T(8,128)(2,1)S(1)} %maximum_bitcast_fusion.mine_ref), channel_id=1, source_target_pairs={{2,0},{9,1},{6,2},{11,3},{8,4},{13,5},{4,6},{15,7},{10,8},{1,9},{1... | collective-permute-start | bytes 147464 | tf_op jit(solution)/shard_map/ppermute | solution.py:202
  11.9 0.2 %collective-permute-done.4 = bf16[1,48,512]{2,1,0:T(8,128)(2,1)S(1)} collective-permute-done((bf16[1,48,512]{2,1,0:T(8,128)(2,1)S(1)}, bf16[1,48,512]{2,1,0:T(8,128)(2,1)S(1)}, u32[]{:S(2)}, u32[]{:S(2)}) %collective-permute-start.4) | collective-permute-done | bytes 49184 | tf_op jit(solution)/shard_map/ppermute | solution.py:202
  12.1 2.0 %collective-permute-done.3 = bf16[1,48,512]{2,1,0:T(8,128)(2,1)S(1)} collective-permute-done((bf16[1,48,512]{2,1,0:T(8,128)(2,1)S(1)}, bf16[1,48,512]{2,1,0:T(8,128)(2,1)S(1)}, u32[]{:S(2)}, u32[]{:S(2)}) %collective-permute-start.3) | collective-permute-done | bytes 49184 | tf_op jit(solution)/shard_map/ppermute | solution.py:202
  14.1 0.7 %collective-permute-start.5 = (bf16[2,48,512]{2,1,0:T(8,128)(2,1)S(1)}, bf16[2,48,512]{2,1,0:T(8,128)(2,1)S(1)}, u32[]{:S(2)}, u32[]{:S(2)}) collective-permute-start(bf16[2,48,512]{2,1,0:T(8,128)(2,1)S(1)} %pad_maximum_fusion.1), channel_id=1, source_target_pairs={{1,0},{0,1},{3,2},{2,3},{5,4},{4,5},{7,6},{6,7},{9,8},{8,9},{11,10... | collective-permute-start | bytes 294920 | tf_op jit(solution)/shard_map/ppermute | solution.py:152
  14.7 0.9 %collective-permute-done.5 = bf16[2,48,512]{2,1,0:T(8,128)(2,1)S(1)} collective-permute-done((bf16[2,48,512]{2,1,0:T(8,128)(2,1)S(1)}, bf16[2,48,512]{2,1,0:T(8,128)(2,1)S(1)}, u32[]{:S(2)}, u32[]{:S(2)}) %collective-permute-start.5) | collective-permute-done | bytes 98336 | tf_op jit(solution)/shard_map/ppermute | solution.py:152
  15.7 1.1 %gram_and_scores.1 = (f32[1,256,512]{2,1,0:T(8,128)}, f32[4,16]{1,0:T(4,128)}) custom-call(bf16[1,48,512]{2,1,0:T(8,128)(2,1)S(1)} %maximum_bitcast_fusion.mine_ref, bf16[4,48,512]{2,1,0:T(8,128)(2,1)S(1)} %pad_maximum_fusion.got_ref), custom_call_target="tpu_custom_call" | custom-call | tf_op jit(solution)/shard_map/gram_and_scores/pallas_call | solution.py:206
  (5 shorter events, 0.1 us)
Async XLA Ops:
  0.6 3.7 %copy-start = (bf16[1,256,2048]{2,1,0:T(8,128)(2,1)S(1)}, bf16[1,256,2048]{2,1,0:T(8,128)(2,1)}, u32[]{:S(2)}) copy-start(bf16[1,256,2048]{2,1,0:T(8,128)(2,1)} %param.5) | copy-start | bytes 3145732
  0.6 3.7 %copy-start.2 = (bf16[1,32,2048]{2,1,0:T(8,128)(2,1)S(1)}, bf16[1,32,2048]{2,1,0:T(8,128)(2,1)}, u32[]{:S(2)}) copy-start(bf16[1,32,2048]{2,1,0:T(8,128)(2,1)} %param.7) | copy-start | bytes 393220
  0.7 4.2 %copy-start.1 = (bf16[1,256,2048]{2,1,0:T(8,128)(2,1)S(1)}, bf16[1,256,2048]{2,1,0:T(8,128)(2,1)}, u32[]{:S(2)}) copy-start(bf16[1,256,2048]{2,1,0:T(8,128)(2,1)} %param.6) | copy-start | bytes 3145732
  0.7 5.8 %collective-permute-start.1 = (bf16[16,512]{1,0:T(8,128)(2,1)}, bf16[16,512]{1,0:T(8,128)(2,1)S(1)}, u32[]{:S(2)}, u32[]{:S(2)}) collective-permute-start(bf16[16,512]{1,0:T(8,128)(2,1)} %bitcast.15), channel_id=1, source_target_pairs={{0,9},{1,8},{2,1},{3,0},{4,13},{5,12},{6,5},{7,4},{8,11},{9,10},{1... | collective-permute-start | bytes 49160 | tf_op jit(solution)/shard_map/ppermute | solution.py:161
  4.4 0.9 %copy-start.3 = (bf16[1,32,2048]{2,1,0:T(8,128)(2,1)S(1)}, bf16[1,32,2048]{2,1,0:T(8,128)(2,1)}, u32[]{:S(2)}) copy-start(bf16[1,32,2048]{2,1,0:T(8,128)(2,1)} %param.8) | copy-start | bytes 393220
  5.7 1.6 %collective-permute-start = (f32[64,256]{1,0:T(8,128)S(1)}, f32[64,256]{1,0:T(8,128)S(1)}, u32[]{:S(2)}, u32[]{:S(2)}) collective-permute-start(f32[64,256]{1,0:T(8,128)S(1)} %pad_maximum_fusion.2.refs_0_), channel_id=1, source_target_pairs={{1,0},{0,1},{3,2},{2,3},{5,4},{4,5},{7,6},{6,7},{9,8},{8,9},{11,10... | collective-permute-start | bytes 196616 | tf_op jit(solution)/shard_map/ppermute | solution.py:152
  6.5 1.4 %collective-permute-start.2 = (bf16[16,512]{1,0:T(8,128)(2,1)S(1)}, bf16[16,512]{1,0:T(8,128)(2,1)S(1)}, u32[]{:S(2)}, u32[]{:S(2)}) collective-permute-start(bf16[16,512]{1,0:T(8,128)(2,1)S(1)} %chunk.1), channel_id=1, source_target_pairs={{1,0},{0,1},{3,2},{2,3},{5,4},{4,5},{7,6},{6,7},{9,8},{8,9},{11,10... | collective-permute-start | bytes 49160 | tf_op jit(solution)/shard_map/ppermute | solution.py:152
  7.9 4.1 %collective-permute-start.4 = (bf16[1,48,512]{2,1,0:T(8,128)(2,1)S(1)}, bf16[1,48,512]{2,1,0:T(8,128)(2,1)S(1)}, u32[]{:S(2)}, u32[]{:S(2)}) collective-permute-start(bf16[1,48,512]{2,1,0:T(8,128)(2,1)S(1)} %maximum_bitcast_fusion.mine_ref), channel_id=1, source_target_pairs={{4,0},{13,1},{0,2},{15,3},{6,4},{1,5},{10,6},{3,7},{12,8},{5,9},{8... | collective-permute-start | bytes 147464 | tf_op jit(solution)/shard_map/ppermute | solution.py:202
  9.1 4.9 %collective-permute-start.3 = (bf16[1,48,512]{2,1,0:T(8,128)(2,1)S(1)}, bf16[1,48,512]{2,1,0:T(8,128)(2,1)S(1)}, u32[]{:S(2)}, u32[]{:S(2)}) collective-permute-start(bf16[1,48,512]{2,1,0:T(8,128)(2,1)S(1)} %maximum_bitcast_fusion.mine_ref), channel_id=1, source_target_pairs={{2,0},{9,1},{6,2},{11,3},{8,4},{13,5},{4,6},{15,7},{10,8},{1,9},{1... | collective-permute-start | bytes 147464 | tf_op jit(solution)/shard_map/ppermute | solution.py:202
  14.1 1.6 %collective-permute-start.5 = (bf16[2,48,512]{2,1,0:T(8,128)(2,1)S(1)}, bf16[2,48,512]{2,1,0:T(8,128)(2,1)S(1)}, u32[]{:S(2)}, u32[]{:S(2)}) collective-permute-start(bf16[2,48,512]{2,1,0:T(8,128)(2,1)S(1)} %pad_maximum_fusion.1), channel_id=1, source_target_pairs={{1,0},{0,1},{3,2},{2,3},{5,4},{4,5},{7,6},{6,7},{9,8},{8,9},{11,10... | collective-permute-start | bytes 294920 | tf_op jit(solution)/shard_map/ppermute | solution.py:152

commit v11 on v9

--- a/solution.py
+++ b/solution.py
@@ -61,57 +61,44 @@
     out_ref[...] = jnp.concatenate(rows, axis=0).astype(BF16)
 
 
-def final_kernel(n_ex, n_lay, n_sub, own, moves, mine_ref, got_ref, gram_ref, scores_ref):
+def swap_kernel(lacked, first_ref, second_ref, out_ref):
+    second = lacked(lax.axis_index("ex"), lax.axis_index("lay"), lax.axis_index("sub")) == 1
+    out_ref[0] = first_ref[0]
+    out_ref[1] = second_ref[0]
+
+    @pl.when(second)
+    def _():
+        out_ref[2:] = second_ref[1:]
+
+    @pl.when(jnp.logical_not(second))
+    def _():
+        out_ref[2:] = first_ref[1:]
+
+
+def final_kernel(plan, n_ex, n_sub, own, *refs):
+    parts, (gram_ref, scores_ref, all_ref) = refs[:-3], refs[-3:]
+    start = 0
+    for part in parts:
+        all_ref[start : start + part.shape[0]] = part[...]
+        start += part.shape[0]
     ex, lay, sub = lax.axis_index("ex"), lax.axis_index("lay"), lax.axis_index("sub")
-    rounds = got_ref.shape[0] // n_sub
-    group, per_blk = n_ex // n_lay, n_ex // (n_lay * n_sub)
-    used, half = 2 * own * n_sub, got_ref.shape[2]
-    rows = (got_ref.shape[1] - used) // n_sub
+    slots, layers, units = plan(ex, lay, sub)
+    half = all_ref.shape[2]
     n_rows, per_half = half * n_sub // n_ex, n_ex // n_sub
 
-    def halves_of(pieces):
-        pieces = pieces[:used].astype(F32)
+    def halves_of(block):
+        pieces = all_ref[block].astype(F32)
         return [pieces[h * 2 * own : (h + 1) * 2 * own] for h in range(n_sub)]
 
     def choose(values, index):
-        if isinstance(index, int):
-            return values[index]
         result = values[0]
         for i in range(1, len(values)):
             result = jnp.where(index == i, values[i], result)
         return result
 
-    mine = mine_ref[0]
-    layers, slots = [halves_of(mine)], [(mine, sub, ex)]
-    for at, (axis, k) in enumerate(moves):
-        core = at % n_sub
-        piece = got_ref[lax.rem(core - sub + n_sub, n_sub) * rounds + at // n_sub]
-        if axis == "ex":
-            slots.append((piece, core, lax.rem(ex + k, n_ex)))
-        else:
-            layers.append(halves_of(piece))
-
-    blocks = [0.0] * per_blk
-    for piece, core, source in slots:
-        layer = lax.rem(source // group + n_lay - 1, n_lay)
-        behind = lax.rem(layer - lay + n_lay, n_lay)
-        grads = [choose([halves[h] for halves in layers], behind) for h in range(n_sub)]
-        part = 0.0
-        for k in range(n_sub):
-            part += lax.dot_general(
-                choose(grads, (core + k + n_sub - 1) % n_sub).astype(BF16),
-                piece[used + k * rows : used + (k + 1) * rows],
-                LAST,
-                preferred_element_type=F32,
-            )
-        part = part[:own] + part[own:]
-        for j in range(per_blk):
-            blocks[j] += jnp.where(lax.rem(source, group) == sub * per_blk + j, part, 0.0)
-    scores_ref[...] = blocks[0] if per_blk == 1 else jnp.concatenate(blocks, axis=1)
-
     lefts, rights = [], []
-    for piece, _, _ in slots:
-        halves = halves_of(piece)
+    for block in slots:
+        halves = halves_of(block)
         cuts = [halves[e // per_half][:, e % per_half * n_rows : (e % per_half + 1) * n_rows] for e in range(n_ex)]
         left, right = choose(cuts, ex), choose(halves, sub)
         lefts += [left, pltpu.roll(left, own, 0)]
@@ -121,6 +108,20 @@
     gram = lax.dot_general(left, right, FIRST, preferred_element_type=F32)
     gram_ref[0] = gram * (1.0 / (own * n_ex))
 
+    layers = [halves_of(block) for block in layers]
+    blocks = {}
+    for block, behind, core, column, fits in units:
+        grads = [choose([halves[h] for halves in layers], behind) for h in range(n_sub)]
+        part = 0.0
+        for h in range(n_sub):
+            turned = choose(grads, lax.rem(core + h + n_sub - 1, n_sub)).astype(BF16)
+            part += lax.dot_general(turned, all_ref[block + h], LAST, preferred_element_type=F32)
+        part = part[:own] + part[own:]
+        part = part if fits is None else jnp.where(fits, part, 0.0)
+        blocks[column] = blocks.get(column, 0.0) + part
+    blocks = [blocks[column] for column in sorted(blocks)]
+    scores_ref[...] = blocks[0] if len(blocks) == 1 else jnp.concatenate(blocks, axis=1)
+
 
 def solution(mesh):
     n_ex, n_lay, n_sub = mesh.shape["ex"], mesh.shape["lay"], mesh.shape["sub"]
@@ -132,17 +133,65 @@
     devices = [(ex, lay, sub) for ex in range(n_ex) for lay in range(n_lay) for sub in range(n_sub)]
 
     query_pairs = [
-        (flat(ex, lay, sub), flat((lay + 1) % n_lay * group + ex % group, ex // group, (sub + 1) % n_sub))
+        (
+            flat(ex, lay, sub),
+            flat(ex % group * n_lay + (lay + n_lay - 1) % n_lay, ex // group, (sub + 1) % n_sub),
+        )
         for ex, lay, sub in devices
     ]
 
-    moves = [("ex", 1), ("ex", 2), ("lay", 1), ("ex", n_ex - 1)]
-    moves += [("ex", k) for k in range(3, n_ex - 1)] + [("lay", k) for k in range(2, n_lay)]
+    moves = [("lay", 1), ("ex", n_ex - 1), ("ex", n_ex // 2), ("ex", 1)]
+    moves += [("ex", k) for k in range(2, n_ex - 1) if k != n_ex // 2] + [("lay", k) for k in range(2, n_lay)]
     rounds = -(-len(moves) // n_sub)
 
+    def turned(ex, lay):
+        return (ex // (n_ex // 2) + lay) % 2 == 0
+
     def source_of(at, ex, lay, sub):
+        if sub == 0 and at < 2 and turned(ex, lay):
+            at = 1 - at
         axis, k = moves[min(at * n_sub + sub, len(moves) - 1)]
         return flat((ex + k) % n_ex, lay, sub) if axis == "ex" else flat(ex, (lay + k) % n_lay, sub)
+
+    compact = (n_ex, n_lay, n_sub) == (4, 2, 2)
+
+    def lacked(ex, lay, sub):
+        return jnp.where(sub == 0, jnp.where(turned(ex, lay), 0, 1), 1 - (ex + ex // 2) % 2)
+
+    def compact_plan(ex, lay, sub):
+        across = lacked(ex, lay, 0)
+        beside = lacked(ex, lay, 1)
+
+        def grads_at(core, turn):
+            return jnp.where(sub == core, 3 + 3 * turn, 9 + turn)
+
+        slots = [0, grads_at(0, across), grads_at(1, 0), grads_at(1, 1)]
+        layers = [0, grads_at(0, 1 - across)]
+        same = jnp.where(ex // 2 == sub, 1, jnp.where(sub == 0, 4 + 3 * across, 11))
+        other = jnp.where(sub == 0, 11, 4 + 3 * (1 - beside))
+        near = jnp.where((sub == 1) & (ex // 2 == 0), 0, sub)
+        units = [(same, (ex + 1 + lay) % 2, near, 0, None), (other, (ex + lay) % 2, 1, 0, None)]
+        return slots, layers, units
+
+    def general_plan(ex, lay, sub):
+        size = 1 + n_sub
+        slots, layers, sources = [0], [0], [(ex, sub)]
+        for at, (axis, k) in enumerate(moves):
+            core, turn = at % n_sub, at // n_sub
+            if core == 0 and turn < 2:
+                turn = jnp.where(turned(ex, lay), 1 - turn, turn)
+            block = (1 + (core - sub + n_sub) % n_sub * rounds + turn) * size
+            if axis == "ex":
+                slots.append(block)
+                sources.append(((ex + k) % n_ex, core))
+            else:
+                layers.append(block)
+        units = []
+        for block, (source, core) in zip(slots, sources):
+            behind, row = (source % n_lay + 1 - lay + n_lay) % n_lay, source // n_lay
+            for column in range(per_blk):
+                units.append((block + 1, behind, core, column, row == sub * per_blk + column))
+        return slots, layers, units
 
     def rotate(value, k):
         return lax.ppermute(value, "sub", [((i + k) % n_sub, i) for i in range(n_sub)])
@@ -191,25 +240,37 @@
             name="grads",
         )(*parts, pick_x, pick_g)
 
-        mine = jnp.concatenate([grads] + chunks)[None]
+        mine = jnp.stack([grads] + chunks)
         received = []
         for at in range(rounds):
             pairs = [(source_of(at, *device), flat(*device)) for device in devices]
             received.append(lax.ppermute(mine, AXES, pairs))
-        received = jnp.concatenate(received)
-        got = jnp.concatenate([received] + [rotate(received, k) for k in range(1, n_sub)])
+        if compact:
+            swapped = pl.pallas_call(
+                functools.partial(swap_kernel, lacked),
+                out_shape=jax.ShapeDtypeStruct((4, rows, half), BF16),
+                in_specs=[VMEM] * 2,
+                out_specs=VMEM,
+                compiler_params=PARAMS,
+                name="swap",
+            )(*received)
+            blocks = [mine] + received + [rotate(swapped, 1)]
+        else:
+            both = jnp.concatenate(received)
+            blocks = [mine, both] + [rotate(both, k) for k in range(1, n_sub)]
 
         return pl.pallas_call(
-            functools.partial(final_kernel, n_ex, n_lay, n_sub, own, moves),
+            functools.partial(final_kernel, compact_plan if compact else general_plan, n_ex, n_sub, own),
             out_shape=(
                 jax.ShapeDtypeStruct((1, width // n_ex, half), F32),
                 jax.ShapeDtypeStruct((own, rows * per_blk), F32),
             ),
-            in_specs=[VMEM] * 2,
+            in_specs=[VMEM] * len(blocks),
             out_specs=(VMEM, VMEM),
+            scratch_shapes=[pltpu.VMEM((sum(block.shape[0] for block in blocks), rows, half), BF16)],
             compiler_params=PARAMS,
             name="gram_and_scores",
-        )(mine, got)
+        )(*blocks)
 
     in_specs = (
         P("lay", ("grp", "ex"), "sub"),

time: 16.9 us -> 15.9 us (0.941)
  starting transfers between devices: 8.5 us -> 7.06 us
  waiting for transfers between devices: 4.36 us -> 4.71 us
    ppermute x1, starting transfers between devices: 3.53 us -> 2.52 us  [body(): chunk = lax.ppermute(queries[0], AXES, query_pairs)]
    ppermute x2, waiting for transfers between devices: 2.27 us -> 2.77 us  [body(): received.append(lax.ppermute(mine, AXES, pairs))]
    ppermute x2, starting transfers between devices: 4.06 us -> 3.6 us  [body(): received.append(lax.ppermute(mine, AXES, pairs))]
    pallas_call x1 -> x2, Pallas kernels: 1.08 us -> 1.08 us  [the longest x1 1.08 us: body(): pl.pallas_call(functools.partial(final_kernel, compact_plan if compact el...]
where the time goes in v11:
time: 15.9 us; the launch traced here: 15.6 us
  starting transfers between devices  7.06 us (44%)
  waiting for transfers between devices  4.71 us (30%)
  Pallas kernels  1.77 us (11%)
  matrix products  0.82 us (5%)
  between operations  0.73 us (5%)
  local copies, waits for them, and re-layouts  0.5 us (3%)
    ppermute x2, starting transfers between devices, body(): received.append(lax.ppermute(mine, AXES, pairs))  3.6 us
    ppermute x2, waiting for transfers between devices, body(): received.append(lax.ppermute(mine, AXES, pairs))  2.77 us
    ppermute x1, starting transfers between devices, body(): chunk = lax.ppermute(queries[0], AXES, query_pairs)  2.52 us
    ppermute x3, waiting for transfers between devices, rotate(): lax.ppermute(value, 'sub', [((i + k) % n_sub, i) for i in range(n_sub)])  1.94 us
    pallas_call x1, Pallas kernels, body(): pl.pallas_call(functools.partial(final_kernel, compact_plan if compact el...  1.08 us
    ppermute x3, starting transfers between devices, rotate(): lax.ppermute(value, 'sub', [((i + k) % n_sub, i) for i in range(n_sub)])  0.95 us
    pallas_call x1, Pallas kernels, body(): pl.pallas_call(functools.partial(grads_kernel, n_sub), out_shape=jax.Shap...  0.53 us
    unnamed x8, local copies, waits for them, and re-layouts  0.5 us
  transfers between devices with their start and end apart: 6, of which 4 were waited for; matrix products, arithmetic and copies ran while one was open for 5% of the time, Pallas kernels for 4%

profile of v11, /device:TPU:0, one launch (start us, length us, event | category | flops | bytes accessed | tf_op | source)
XLA Modules:
  0.0 15.6 jit_solution(883010642283485023)
XLA Ops:
  0.6 0.0 copy-start
  0.6 0.0 copy-start.2
  0.7 0.0 copy-start.1
  0.7 2.5 %collective-permute-start.1 = (bf16[16,512]{1,0:T(8,128)(2,1)}, bf16[16,512]{1,0:T(8,128)(2,1)S(1)}, u32[]{:S(2)}, u32[]{:S(2)}) collective-permute-start(bf16[16,512]{1,0:T(8,128)(2,1)} %bitcast.19), channel_id=1, source_target_pairs={{0,5},{1,4},{2,1},{3,0},{4,13},{5,12},{6,9},{7,8},{8,7},{9,6},{10,... | collective-permute-start | bytes 49160 | tf_op jit(solution)/shard_map/ppermute | solution.py:206
  3.2 0.1 picks.1
  3.3 0.0 copy-done
  3.3 0.0 copy-done.2
  3.4 0.0 copy-start.3
  3.4 0.4 %fusion = f32[32,256]{1,0:T(8,128)S(1)} fusion(bf16[1,256,2048]{2,1,0:T(8,128)(2,1)S(1)} %copy-done, bf16[1,32,2048]{2,1,0:T(8,128)(2,1)S(1)} %copy-done.2), kind=kOutput, calls=%fused_computation | convolution fusion | flops 33554432 | bytes 1212416 | tf_op jit(solution)/shard_map/dot_general | solution.py:220
  3.8 0.0 copy-done.1
  3.8 0.5 %copy-done.3 = bf16[1,32,2048]{2,1,0:T(8,128)(2,1)S(1)} copy-done((bf16[1,32,2048]{2,1,0:T(8,128)(2,1)S(1)}, bf16[1,32,2048]{2,1,0:T(8,128)(2,1)}, u32[]{:S(2)}) %copy-start.3) | copy-done | bytes 131096
  4.3 0.4 %fusion.2 = f32[32,256]{1,0:T(8,128)S(1)} fusion(bf16[1,256,2048]{2,1,0:T(8,128)(2,1)S(1)} %copy-done.1, bf16[1,32,2048]{2,1,0:T(8,128)(2,1)S(1)} %copy-done.3), kind=kOutput, calls=%fused_computation.2 | convolution fusion | flops 33554432 | bytes 1212416 | tf_op jit(solution)/shard_map/dot_general | solution.py:219
  4.7 0.7 %collective-permute-start = (f32[64,256]{1,0:T(8,128)S(1)}, f32[64,256]{1,0:T(8,128)S(1)}, u32[]{:S(2)}, u32[]{:S(2)}) collective-permute-start(f32[64,256]{1,0:T(8,128)S(1)} %pad_maximum_fusion.refs_0_), channel_id=1, source_target_pairs={{1,0},{0,1},{3,2},{2,3},{5,4},{4,5},{7,6},{6,7},{9,8},{8,9},{11,10... | collective-permute-start | bytes 196616 | tf_op jit(solution)/shard_map/ppermute | solution.py:197
  5.4 0.0 collective-permute-done.1.in_ref
  5.4 0.1 collective-permute-start.2
  5.5 0.8 %collective-permute-done.refs_1_ = f32[64,256]{1,0:T(8,128)S(1)} collective-permute-done((f32[64,256]{1,0:T(8,128)S(1)}, f32[64,256]{1,0:T(8,128)S(1)}, u32[]{:S(2)}, u32[]{:S(2)}) %collective-permute-start) | collective-permute-done | bytes 65568 | tf_op jit(solution)/shard_map/ppermute | solution.py:197
  6.3 0.5 %grads.1 = bf16[16,512]{1,0:T(8,128)(2,1)S(1)} custom-call(f32[64,256]{1,0:T(8,128)S(1)} %pad_maximum_fusion.refs_0_, f32[64,256]{1,0:T(8,128)S(1)} %collective-permute-done.refs_1_, bf16[256,128]{1,0:T(8,128)(2,1)S(1)} %get-tuple-element.10.refs_2_, bf16[256,1024]{1,0:T(8,128)(2,1)S(1)} %get-tuple-element.11.refs_3_), custom_call_target="tpu_custom_call" | custom-call | tf_op jit(solution)/shard_map/grads/pallas_call | solution.py:234
  6.9 0.0 collective-permute-done.2
  6.9 2.3 %collective-permute-start.3 = (bf16[3,16,512]{2,1,0:T(8,128)(2,1)S(1)}, bf16[3,16,512]{2,1,0:T(8,128)(2,1)S(1)}, u32[]{:S(2)}, u32[]{:S(2)}) collective-permute-start(bf16[3,16,512]{2,1,0:T(8,128)(2,1)S(1)} %pad_maximum_fusion.1.refs_0_), channel_id=1, source_target_pairs={{8,0},{13,1},{0,2},{15,3},{12,4},{1,5},{4,6},{3,7},{10,8},{5,9},{2... | collective-permute-start | bytes 147464 | tf_op jit(solution)/shard_map/ppermute | solution.py:247
  9.2 1.3 %collective-permute-start.4 = (bf16[3,16,512]{2,1,0:T(8,128)(2,1)S(1)}, bf16[3,16,512]{2,1,0:T(8,128)(2,1)S(1)}, u32[]{:S(2)}, u32[]{:S(2)}) collective-permute-start(bf16[3,16,512]{2,1,0:T(8,128)(2,1)S(1)} %pad_maximum_fusion.1.refs_0_), channel_id=1, source_target_pairs={{2,0},{5,1},{10,2},{7,3},{6,4},{9,5},{14,6},{11,7},{0,8},{13,9},{8... | collective-permute-start | bytes 147464 | tf_op jit(solution)/shard_map/ppermute | solution.py:247
  10.5 2.0 %collective-permute-done.3.first_ref.refs_1_ = bf16[3,16,512]{2,1,0:T(8,128)(2,1)S(1)} collective-permute-done((bf16[3,16,512]{2,1,0:T(8,128)(2,1)S(1)}, bf16[3,16,512]{2,1,0:T(8,128)(2,1)S(1)}, u32[]{:S(2)}, u32[]{:S(2)}) %collective-permute-start.3) | collective-permute-done | bytes 49184 | tf_op jit(solution)/shard_map/ppermute | solution.py:247
  12.5 0.7 %collective-permute-done.4.second_ref.refs_2_ = bf16[3,16,512]{2,1,0:T(8,128)(2,1)S(1)} collective-permute-done((bf16[3,16,512]{2,1,0:T(8,128)(2,1)S(1)}, bf16[3,16,512]{2,1,0:T(8,128)(2,1)S(1)}, u32[]{:S(2)}, u32[]{:S(2)}) %collective-permute-start.4) | collective-permute-done | bytes 49184 | tf_op jit(solution)/shard_map/ppermute | solution.py:247
  13.3 0.1 collective-permute-start.5
  13.4 1.1 %collective-permute-done.5.refs_3_ = bf16[4,16,512]{2,1,0:T(8,128)(2,1)S(1)} collective-permute-done((bf16[4,16,512]{2,1,0:T(8,128)(2,1)S(1)}, bf16[4,16,512]{2,1,0:T(8,128)(2,1)S(1)}, u32[]{:S(2)}, u32[]{:S(2)}) %collective-permute-start.5) | collective-permute-done | bytes 65568 | tf_op jit(solution)/shard_map/ppermute | solution.py:197
  14.5 1.1 %gram_and_scores.1 = (f32[1,256,512]{2,1,0:T(8,128)}, f32[4,16]{1,0:T(4,128)}) custom-call(bf16[3,16,512]{2,1,0:T(8,128)(2,1)S(1)} %pad_maximum_fusion.1.refs_0_, bf16[3,16,512]{2,1,0:T(8,128)(2,1)S(1)} %collective-permute-done.3.first_ref.refs_1_, bf16[3,16,512]{2,1,0:T(8,128)(2,1)S(1)} %collective-permute-done.4.second_ref.refs_2_, ...), custom_call_target="tpu_custom_call" | custom-call | tf_op jit(solution)/shard_map/gram_and_scores/pallas_call | solution.py:262
  (4 shorter events, 0.0 us)
Async XLA Ops:
  0.6 2.7 %copy-start = (bf16[1,256,2048]{2,1,0:T(8,128)(2,1)S(1)}, bf16[1,256,2048]{2,1,0:T(8,128)(2,1)}, u32[]{:S(2)}) copy-start(bf16[1,256,2048]{2,1,0:T(8,128)(2,1)} %param.6) | copy-start | bytes 3145732
  0.6 2.7 %copy-start.2 = (bf16[1,32,2048]{2,1,0:T(8,128)(2,1)S(1)}, bf16[1,32,2048]{2,1,0:T(8,128)(2,1)}, u32[]{:S(2)}) copy-start(bf16[1,32,2048]{2,1,0:T(8,128)(2,1)} %param.8) | copy-start | bytes 393220
  0.7 3.1 %copy-start.1 = (bf16[1,256,2048]{2,1,0:T(8,128)(2,1)S(1)}, bf16[1,256,2048]{2,1,0:T(8,128)(2,1)}, u32[]{:S(2)}) copy-start(bf16[1,256,2048]{2,1,0:T(8,128)(2,1)} %param.5) | copy-start | bytes 3145732
  0.7 4.8 %collective-permute-start.1 = (bf16[16,512]{1,0:T(8,128)(2,1)}, bf16[16,512]{1,0:T(8,128)(2,1)S(1)}, u32[]{:S(2)}, u32[]{:S(2)}) collective-permute-start(bf16[16,512]{1,0:T(8,128)(2,1)} %bitcast.19), channel_id=1, source_target_pairs={{0,5},{1,4},{2,1},{3,0},{4,13},{5,12},{6,9},{7,8},{8,7},{9,6},{10,... | collective-permute-start | bytes 49160 | tf_op jit(solution)/shard_map/ppermute | solution.py:206
  3.4 0.9 %copy-start.3 = (bf16[1,32,2048]{2,1,0:T(8,128)(2,1)S(1)}, bf16[1,32,2048]{2,1,0:T(8,128)(2,1)}, u32[]{:S(2)}) copy-start(bf16[1,32,2048]{2,1,0:T(8,128)(2,1)} %param.7) | copy-start | bytes 393220
  4.7 1.6 %collective-permute-start = (f32[64,256]{1,0:T(8,128)S(1)}, f32[64,256]{1,0:T(8,128)S(1)}, u32[]{:S(2)}, u32[]{:S(2)}) collective-permute-start(f32[64,256]{1,0:T(8,128)S(1)} %pad_maximum_fusion.refs_0_), channel_id=1, source_target_pairs={{1,0},{0,1},{3,2},{2,3},{5,4},{4,5},{7,6},{6,7},{9,8},{8,9},{11,10... | collective-permute-start | bytes 196616 | tf_op jit(solution)/shard_map/ppermute | solution.py:197
  5.4 1.4 %collective-permute-start.2 = (bf16[16,512]{1,0:T(8,128)(2,1)S(1)}, bf16[16,512]{1,0:T(8,128)(2,1)S(1)}, u32[]{:S(2)}, u32[]{:S(2)}) collective-permute-start(bf16[16,512]{1,0:T(8,128)(2,1)S(1)} %chunk.1), channel_id=1, source_target_pairs={{1,0},{0,1},{3,2},{2,3},{5,4},{4,5},{7,6},{6,7},{9,8},{8,9},{11,10... | collective-permute-start | bytes 49160 | tf_op jit(solution)/shard_map/ppermute | solution.py:197
  6.9 5.6 %collective-permute-start.3 = (bf16[3,16,512]{2,1,0:T(8,128)(2,1)S(1)}, bf16[3,16,512]{2,1,0:T(8,128)(2,1)S(1)}, u32[]{:S(2)}, u32[]{:S(2)}) collective-permute-start(bf16[3,16,512]{2,1,0:T(8,128)(2,1)S(1)} %pad_maximum_fusion.1.refs_0_), channel_id=1, source_target_pairs={{8,0},{13,1},{0,2},{15,3},{12,4},{1,5},{4,6},{3,7},{10,8},{5,9},{2... | collective-permute-start | bytes 147464 | tf_op jit(solution)/shard_map/ppermute | solution.py:247
  9.2 4.1 %collective-permute-start.4 = (bf16[3,16,512]{2,1,0:T(8,128)(2,1)S(1)}, bf16[3,16,512]{2,1,0:T(8,128)(2,1)S(1)}, u32[]{:S(2)}, u32[]{:S(2)}) collective-permute-start(bf16[3,16,512]{2,1,0:T(8,128)(2,1)S(1)} %pad_maximum_fusion.1.refs_0_), channel_id=1, source_target_pairs={{2,0},{5,1},{10,2},{7,3},{6,4},{9,5},{14,6},{11,7},{0,8},{13,9},{8... | collective-permute-start | bytes 147464 | tf_op jit(solution)/shard_map/ppermute | solution.py:247
  13.3 1.3 %collective-permute-start.5 = (bf16[4,16,512]{2,1,0:T(8,128)(2,1)S(1)}, bf16[4,16,512]{2,1,0:T(8,128)(2,1)S(1)}, u32[]{:S(2)}, u32[]{:S(2)}) collective-permute-start(bf16[4,16,512]{2,1,0:T(8,128)(2,1)S(1)} %swap.1), channel_id=1, source_target_pairs={{1,0},{0,1},{3,2},{2,3},{5,4},{4,5},{7,6},{6,7},{9,8},{8,9},{11,10... | collective-permute-start | bytes 196616 | tf_op jit(solution)/shard_map/ppermute | solution.py:197

commit v12 on v11

--- a/solution.py
+++ b/solution.py
@@ -27,7 +27,7 @@
         pick_g_ref[:, j * lanes : (j + 1) * lanes] = jnp.where(gap == j * (lanes // basis), 1.0, 0.0).astype(BF16)
 
 
-def chunk_kernel(in_ref, out_ref):
+def take_kernel(in_ref, out_ref):
     out_ref[...] = in_ref[...]
 
 
@@ -61,10 +61,18 @@
     out_ref[...] = jnp.concatenate(rows, axis=0).astype(BF16)
 
 
-def swap_kernel(lacked, first_ref, second_ref, out_ref):
-    second = lacked(lax.axis_index("ex"), lax.axis_index("lay"), lax.axis_index("sub")) == 1
+def swap_kernel(lacked, across_ref, first_ref, second_ref, out_ref):
+    sub = lax.axis_index("sub")
+    second = (sub != 0) & lacked(lax.axis_index("ex"))
     out_ref[0] = first_ref[0]
-    out_ref[1] = second_ref[0]
+
+    @pl.when(sub == 0)
+    def _():
+        out_ref[1] = across_ref[0]
+
+    @pl.when(sub != 0)
+    def _():
+        out_ref[1] = second_ref[0]
 
     @pl.when(second)
     def _():
@@ -140,58 +148,68 @@
         for ex, lay, sub in devices
     ]
 
-    moves = [("lay", 1), ("ex", n_ex - 1), ("ex", n_ex // 2), ("ex", 1)]
-    moves += [("ex", k) for k in range(2, n_ex - 1) if k != n_ex // 2] + [("lay", k) for k in range(2, n_lay)]
-    rounds = -(-len(moves) // n_sub)
-
-    def turned(ex, lay):
-        return (ex // (n_ex // 2) + lay) % 2 == 0
-
-    def source_of(at, ex, lay, sub):
-        if sub == 0 and at < 2 and turned(ex, lay):
-            at = 1 - at
-        axis, k = moves[min(at * n_sub + sub, len(moves) - 1)]
-        return flat((ex + k) % n_ex, lay, sub) if axis == "ex" else flat(ex, (lay + k) % n_lay, sub)
+    rest = [k for k in range(2, n_ex - 1) if k != n_ex // 2]
+    moves = [(n_ex // 2, n_ex - 1), ((rest + [None])[0], 1)]
+    rest = rest[1:]
+    while rest:
+        moves.append((rest[0], (rest + [None])[1]))
+        rest = rest[2:]
+
+    def ex_pairs(move):
+        return [
+            (flat((ex + move[sub]) % n_ex, lay, sub), flat(ex, lay, sub))
+            for ex, lay, sub in devices
+            if move[sub] is not None
+        ]
+
+    def lay_pairs(k):
+        core = (k - 1) % n_sub
+        return [(flat(ex, (lay + k) % n_lay, core), flat(ex, lay, core)) for ex, lay, sub in devices if sub == core]
 
     compact = (n_ex, n_lay, n_sub) == (4, 2, 2)
 
-    def lacked(ex, lay, sub):
-        return jnp.where(sub == 0, jnp.where(turned(ex, lay), 0, 1), 1 - (ex + ex // 2) % 2)
+    def lacked(ex):
+        return (ex + ex // 2) % 2 == 0
 
     def compact_plan(ex, lay, sub):
-        across = lacked(ex, lay, 0)
-        beside = lacked(ex, lay, 1)
-
-        def grads_at(core, turn):
-            return jnp.where(sub == core, 3 + 3 * turn, 9 + turn)
-
-        slots = [0, grads_at(0, across), grads_at(1, 0), grads_at(1, 1)]
-        layers = [0, grads_at(0, 1 - across)]
-        same = jnp.where(ex // 2 == sub, 1, jnp.where(sub == 0, 4 + 3 * across, 11))
-        other = jnp.where(sub == 0, 11, 4 + 3 * (1 - beside))
-        near = jnp.where((sub == 1) & (ex // 2 == 0), 0, sub)
-        units = [(same, (ex + 1 + lay) % 2, near, 0, None), (other, (ex + lay) % 2, 1, 0, None)]
+        slots = [0, jnp.where(sub == 0, 3, 10), jnp.where(sub == 1, 3, 10), jnp.where(sub == 1, 6, 11)]
+        layers = [0, jnp.where(sub == 0, 9, 11)]
+        same = jnp.where(ex // 2 == sub, 1, jnp.where(sub == 0, 4, 12))
+        other = jnp.where(sub == 0, 12, jnp.where(lacked(ex), 4, 7))
+        core = jnp.where((sub == 1) & (ex // 2 == 0), 0, sub)
+        units = [(same, (ex + 1 + lay) % 2, core, 0, None), (other, (ex + lay) % 2, 1, 0, None)]
         return slots, layers, units
 
     def general_plan(ex, lay, sub):
         size = 1 + n_sub
+        per_core = len(moves) * size + n_lay - 1
         slots, layers, sources = [0], [0], [(ex, sub)]
-        for at, (axis, k) in enumerate(moves):
-            core, turn = at % n_sub, at // n_sub
-            if core == 0 and turn < 2:
-                turn = jnp.where(turned(ex, lay), 1 - turn, turn)
-            block = (1 + (core - sub + n_sub) % n_sub * rounds + turn) * size
-            if axis == "ex":
-                slots.append(block)
-                sources.append(((ex + k) % n_ex, core))
-            else:
-                layers.append(block)
+        for core in range(n_sub):
+            start = size + (core - sub + n_sub) % n_sub * per_core
+            for at, move in enumerate(moves):
+                if move[core] is not None:
+                    slots.append(start + at * size)
+                    sources.append(((ex + move[core]) % n_ex, core))
+        for k in range(1, n_lay):
+            start = size + ((k - 1) % n_sub - sub + n_sub) % n_sub * per_core
+            layers.append(start + len(moves) * size + k - 1)
         units = []
         for block, (source, core) in zip(slots, sources):
             behind, row = (source % n_lay + 1 - lay + n_lay) % n_lay, source // n_lay
             for column in range(per_blk):
                 units.append((block + 1, behind, core, column, row == sub * per_blk + column))
         return slots, layers, units
+
+    def take(value, name):
+        return pl.pallas_call(
+            take_kernel,
+            out_shape=jax.ShapeDtypeStruct(value.shape, value.dtype),
+            in_specs=[VMEM],
+            out_specs=VMEM,
+            compiler_params=PARAMS,
+            cost_estimate=pl.CostEstimate(flops=10**11, bytes_accessed=10**9, transcendentals=0),
+            name=name,
+        )(value)
 
     def rotate(value, k):
         return lax.ppermute(value, "sub", [((i + k) % n_sub, i) for i in range(n_sub)])
@@ -220,15 +238,7 @@
         proj_g = lax.dot_general(basis_out[0], output_grads[0], LAST, preferred_element_type=F32)
         proj = jnp.concatenate([proj_x, proj_g])
         parts = [proj] + [rotate(proj, k) for k in range(1, n_sub)]
-        chunk = pl.pallas_call(
-            chunk_kernel,
-            out_shape=jax.ShapeDtypeStruct((rows, half), BF16),
-            in_specs=[VMEM],
-            out_specs=VMEM,
-            compiler_params=PARAMS,
-            cost_estimate=pl.CostEstimate(flops=10**11, bytes_accessed=10**9, transcendentals=0),
-            name="chunk",
-        )(chunk)
+        chunk = take(chunk, "take_chunk")
         chunks = [chunk] + [rotate(chunk, k) for k in range(1, n_sub)]
 
         grads = pl.pallas_call(
@@ -240,23 +250,22 @@
             name="grads",
         )(*parts, pick_x, pick_g)
 
-        mine = jnp.stack([grads] + chunks)
-        received = []
-        for at in range(rounds):
-            pairs = [(source_of(at, *device), flat(*device)) for device in devices]
-            received.append(lax.ppermute(mine, AXES, pairs))
+        grads = grads[None]
+        across = [take(lax.ppermute(grads, AXES, lay_pairs(k)), "take_across") for k in range(1, n_lay)]
+        mine = jnp.concatenate([grads] + [chunk[None] for chunk in chunks])
+        received = [lax.ppermute(mine, AXES, ex_pairs(move)) for move in moves]
         if compact:
             swapped = pl.pallas_call(
                 functools.partial(swap_kernel, lacked),
                 out_shape=jax.ShapeDtypeStruct((4, rows, half), BF16),
-                in_specs=[VMEM] * 2,
+                in_specs=[VMEM] * 3,
                 out_specs=VMEM,
                 compiler_params=PARAMS,
                 name="swap",
-            )(*received)
-            blocks = [mine] + received + [rotate(swapped, 1)]
+            )(*across, *received)
+            blocks = [mine] + received + across + [rotate(swapped, 1)]
         else:
-            both = jnp.concatenate(received)
+            both = jnp.concatenate(received + across)
             blocks = [mine, both] + [rotate(both, k) for k in range(1, n_sub)]
 
         return pl.pallas_call(

time: 15.9 us -> 18.5 us (1.16)
  starting transfers between devices: 7.06 us -> 9.82 us
    ppermute x2 -> x3, starting transfers between devices: 3.6 us -> 6.4 us  [the longest x1 3.61 us: body(): lax.ppermute(grads, AXES, lay_pairs(k))]
    ppermute x2 -> x3, waiting for transfers between devices: 2.77 us -> 2.61 us  [the longest x2 2.61 us: body(): received = [lax.ppermute(mine, AXES, ex_pairs(move)) for move in moves]]
  transfers between devices with their start and end apart: 6 -> 7, of which waited for: 4 -> 3; matrix products, arithmetic and copies ran while one was open for 5% -> 5% of each run, Pallas kernels for 4% -> 4%
where the time goes in v12:
time: 18.5 us; the launch traced here: 18.3 us
  starting transfers between devices  9.82 us (53%)
  waiting for transfers between devices  4.66 us (25%)
  Pallas kernels  1.75 us (9%)
  matrix products  0.82 us (4%)
  between operations  0.77 us (4%)
  local copies, waits for them, and re-layouts  0.5 us (3%)
    ppermute x1, starting transfers between devices, body(): lax.ppermute(grads, AXES, lay_pairs(k))  3.61 us
    ppermute x2, starting transfers between devices, body(): received = [lax.ppermute(mine, AXES, ex_pairs(move)) for move in moves]  2.78 us
    ppermute x2, waiting for transfers between devices, body(): received = [lax.ppermute(mine, AXES, ex_pairs(move)) for move in moves]  2.61 us
    ppermute x1, starting transfers between devices, body(): chunk = lax.ppermute(queries[0], AXES, query_pairs)  2.52 us
    ppermute x3, waiting for transfers between devices, rotate(): lax.ppermute(value, 'sub', [((i + k) % n_sub, i) for i in range(n_sub)])  2.05 us
    pallas_call x1, Pallas kernels, body(): pl.pallas_call(functools.partial(final_kernel, compact_plan if compact el...  1.06 us
    ppermute x3, starting transfers between devices, rotate(): lax.ppermute(value, 'sub', [((i + k) % n_sub, i) for i in range(n_sub)])  0.91 us
    pallas_call x1, Pallas kernels, body(): pl.pallas_call(functools.partial(grads_kernel, n_sub), out_shape=jax.Shap...  0.53 us
  transfers between devices with their start and end apart: 7, of which 3 were waited for; matrix products, arithmetic and copies ran while one was open for 5% of the time, Pallas kernels for 4%

profile of v12, /device:TPU:0, one launch (start us, length us, event | category | flops | bytes accessed | tf_op | source)
XLA Modules:
  0.0 18.3 jit_solution(13162507520415833511)
XLA Ops:
  0.6 0.0 copy-start
  0.6 0.0 copy-start.2
  0.7 0.0 copy-start.1
  0.7 2.5 %collective-permute-start.1 = (bf16[16,512]{1,0:T(8,128)(2,1)}, bf16[16,512]{1,0:T(8,128)(2,1)S(1)}, u32[]{:S(2)}, u32[]{:S(2)}) collective-permute-start(bf16[16,512]{1,0:T(8,128)(2,1)} %bitcast.20), channel_id=1, source_target_pairs={{0,5},{1,4},{2,1},{3,0},{4,13},{5,12},{6,9},{7,8},{8,7},{9,6},{10,... | collective-permute-start | bytes 49160 | tf_op jit(solution)/shard_map/ppermute | solution.py:224
  3.2 0.1 picks.1
  3.3 0.0 copy-done
  3.3 0.0 copy-done.2
  3.4 0.0 copy-start.3
  3.4 0.4 %fusion = f32[32,256]{1,0:T(8,128)S(1)} fusion(bf16[1,256,2048]{2,1,0:T(8,128)(2,1)S(1)} %copy-done, bf16[1,32,2048]{2,1,0:T(8,128)(2,1)S(1)} %copy-done.2), kind=kOutput, calls=%fused_computation | convolution fusion | flops 33554432 | bytes 1212416 | tf_op jit(solution)/shard_map/dot_general | solution.py:238
  3.8 0.0 copy-done.1
  3.8 0.5 %copy-done.3 = bf16[1,32,2048]{2,1,0:T(8,128)(2,1)S(1)} copy-done((bf16[1,32,2048]{2,1,0:T(8,128)(2,1)S(1)}, bf16[1,32,2048]{2,1,0:T(8,128)(2,1)}, u32[]{:S(2)}) %copy-start.3) | copy-done | bytes 131096
  4.3 0.4 %fusion.2 = f32[32,256]{1,0:T(8,128)S(1)} fusion(bf16[1,256,2048]{2,1,0:T(8,128)(2,1)S(1)} %copy-done.1, bf16[1,32,2048]{2,1,0:T(8,128)(2,1)S(1)} %copy-done.3), kind=kOutput, calls=%fused_computation.2 | convolution fusion | flops 33554432 | bytes 1212416 | tf_op jit(solution)/shard_map/dot_general | solution.py:237
  4.7 0.7 %collective-permute-start = (f32[64,256]{1,0:T(8,128)S(1)}, f32[64,256]{1,0:T(8,128)S(1)}, u32[]{:S(2)}, u32[]{:S(2)}) collective-permute-start(f32[64,256]{1,0:T(8,128)S(1)} %pad_maximum_fusion.refs_0_), channel_id=1, source_target_pairs={{1,0},{0,1},{3,2},{2,3},{5,4},{4,5},{7,6},{6,7},{9,8},{8,9},{11,10... | collective-permute-start | bytes 196616 | tf_op jit(solution)/shard_map/ppermute | solution.py:215
  5.4 0.0 collective-permute-done.1.in_ref
  5.4 0.1 collective-permute-start.2
  5.5 0.8 %collective-permute-done.refs_1_ = f32[64,256]{1,0:T(8,128)S(1)} collective-permute-done((f32[64,256]{1,0:T(8,128)S(1)}, f32[64,256]{1,0:T(8,128)S(1)}, u32[]{:S(2)}, u32[]{:S(2)}) %collective-permute-start) | collective-permute-done | bytes 65568 | tf_op jit(solution)/shard_map/ppermute | solution.py:215
  6.3 0.5 %grads.1 = bf16[16,512]{1,0:T(8,128)(2,1)S(1)} custom-call(f32[64,256]{1,0:T(8,128)S(1)} %pad_maximum_fusion.refs_0_, f32[64,256]{1,0:T(8,128)S(1)} %collective-permute-done.refs_1_, bf16[256,128]{1,0:T(8,128)(2,1)S(1)} %get-tuple-element.10.refs_2_, bf16[256,1024]{1,0:T(8,128)(2,1)S(1)} %get-tuple-element.11.refs_3_), custom_call_target="tpu_custom_call" | custom-call | tf_op jit(solution)/shard_map/grads/pallas_call | solution.py:244
  6.9 3.6 %collective-permute-start.5 = (bf16[1,16,512]{2,1,0:T(8,128)(2,1)S(1)}, bf16[1,16,512]{2,1,0:T(8,128)(2,1)S(1)}, u32[]{:S(2)}, u32[]{:S(2)}) collective-permute-start(bf16[1,16,512]{2,1,0:T(8,128)(2,1)S(1)} %bitcast.16), channel_id=1, source_target_pairs={{2,0},{0,2},{6,4},{4,6},{10,8},{8,10},{14,12},{12,14},{18,16},{16,... | collective-permute-start | bytes 49160 | tf_op jit(solution)/shard_map/ppermute | solution.py:254
  10.5 0.0 collective-permute-done.2
  10.5 2.1 %collective-permute-start.3 = (bf16[3,16,512]{2,1,0:T(8,128)(2,1)S(1)}, bf16[3,16,512]{2,1,0:T(8,128)(2,1)S(1)}, u32[]{:S(2)}, u32[]{:S(2)}) collective-permute-start(bf16[3,16,512]{2,1,0:T(8,128)(2,1)S(1)} %pad_maximum_fusion.1.refs_0_), channel_id=1, source_target_pairs={{8,0},{13,1},{10,2},{15,3},{12,4},{1,5},{14,6},{3,7},{0,8},{5,9},{... | collective-permute-start | bytes 147464 | tf_op jit(solution)/shard_map/ppermute | solution.py:256
  12.7 0.7 %collective-permute-start.4 = (bf16[3,16,512]{2,1,0:T(8,128)(2,1)S(1)}, bf16[3,16,512]{2,1,0:T(8,128)(2,1)S(1)}, u32[]{:S(2)}, u32[]{:S(2)}) collective-permute-start(bf16[3,16,512]{2,1,0:T(8,128)(2,1)S(1)} %pad_maximum_fusion.1.refs_0_), channel_id=1, source_target_pairs={{5,1},{7,3},{9,5},{11,7},{13,9},{15,11},{1,13},{3,15},{21,17},{23,... | collective-permute-start | bytes 147464 | tf_op jit(solution)/shard_map/ppermute | solution.py:256
  13.3 0.0 collective-permute-done.5.in_ref
  13.3 2.6 %collective-permute-done.3.first_ref.refs_1_ = bf16[3,16,512]{2,1,0:T(8,128)(2,1)S(1)} collective-permute-done((bf16[3,16,512]{2,1,0:T(8,128)(2,1)S(1)}, bf16[3,16,512]{2,1,0:T(8,128)(2,1)S(1)}, u32[]{:S(2)}, u32[]{:S(2)}) %collective-permute-start.3) | collective-permute-done | bytes 49184 | tf_op jit(solution)/shard_map/ppermute | solution.py:256
  15.9 0.0 collective-permute-done.4.second_ref.refs_2_
  16.0 0.1 collective-permute-start.6
  16.0 1.2 %collective-permute-done.6.refs_4_ = bf16[4,16,512]{2,1,0:T(8,128)(2,1)S(1)} collective-permute-done((bf16[4,16,512]{2,1,0:T(8,128)(2,1)S(1)}, bf16[4,16,512]{2,1,0:T(8,128)(2,1)S(1)}, u32[]{:S(2)}, u32[]{:S(2)}) %collective-permute-start.6) | collective-permute-done | bytes 65568 | tf_op jit(solution)/shard_map/ppermute | solution.py:215
  17.3 1.1 %gram_and_scores.1 = (f32[1,256,512]{2,1,0:T(8,128)}, f32[4,16]{1,0:T(4,128)}) custom-call(bf16[3,16,512]{2,1,0:T(8,128)(2,1)S(1)} %pad_maximum_fusion.1.refs_0_, bf16[3,16,512]{2,1,0:T(8,128)(2,1)S(1)} %collective-permute-done.3.first_ref.refs_1_, bf16[3,16,512]{2,1,0:T(8,128)(2,1)S(1)} %collective-permute-done.4.second_ref.refs_2_, ...), custom_call_target="tpu_custom_call" | custom-call | tf_op jit(solution)/shard_map/gram_and_scores/pallas_call | solution.py:271
  (5 shorter events, 0.0 us)
Async XLA Ops:
  0.6 2.7 %copy-start = (bf16[1,256,2048]{2,1,0:T(8,128)(2,1)S(1)}, bf16[1,256,2048]{2,1,0:T(8,128)(2,1)}, u32[]{:S(2)}) copy-start(bf16[1,256,2048]{2,1,0:T(8,128)(2,1)} %param.6) | copy-start | bytes 3145732
  0.6 2.7 %copy-start.2 = (bf16[1,32,2048]{2,1,0:T(8,128)(2,1)S(1)}, bf16[1,32,2048]{2,1,0:T(8,128)(2,1)}, u32[]{:S(2)}) copy-start(bf16[1,32,2048]{2,1,0:T(8,128)(2,1)} %param.8) | copy-start | bytes 393220
  0.7 3.1 %copy-start.1 = (bf16[1,256,2048]{2,1,0:T(8,128)(2,1)S(1)}, bf16[1,256,2048]{2,1,0:T(8,128)(2,1)}, u32[]{:S(2)}) copy-start(bf16[1,256,2048]{2,1,0:T(8,128)(2,1)} %param.5) | copy-start | bytes 3145732
  0.7 4.8 %collective-permute-start.1 = (bf16[16,512]{1,0:T(8,128)(2,1)}, bf16[16,512]{1,0:T(8,128)(2,1)S(1)}, u32[]{:S(2)}, u32[]{:S(2)}) collective-permute-start(bf16[16,512]{1,0:T(8,128)(2,1)} %bitcast.20), channel_id=1, source_target_pairs={{0,5},{1,4},{2,1},{3,0},{4,13},{5,12},{6,9},{7,8},{8,7},{9,6},{10,... | collective-permute-start | bytes 49160 | tf_op jit(solution)/shard_map/ppermute | solution.py:224
  3.4 0.9 %copy-start.3 = (bf16[1,32,2048]{2,1,0:T(8,128)(2,1)S(1)}, bf16[1,32,2048]{2,1,0:T(8,128)(2,1)}, u32[]{:S(2)}) copy-start(bf16[1,32,2048]{2,1,0:T(8,128)(2,1)} %param.7) | copy-start | bytes 393220
  4.7 1.6 %collective-permute-start = (f32[64,256]{1,0:T(8,128)S(1)}, f32[64,256]{1,0:T(8,128)S(1)}, u32[]{:S(2)}, u32[]{:S(2)}) collective-permute-start(f32[64,256]{1,0:T(8,128)S(1)} %pad_maximum_fusion.refs_0_), channel_id=1, source_target_pairs={{1,0},{0,1},{3,2},{2,3},{5,4},{4,5},{7,6},{6,7},{9,8},{8,9},{11,10... | collective-permute-start | bytes 196616 | tf_op jit(solution)/shard_map/ppermute | solution.py:215
  5.4 5.1 %collective-permute-start.2 = (bf16[16,512]{1,0:T(8,128)(2,1)S(1)}, bf16[16,512]{1,0:T(8,128)(2,1)S(1)}, u32[]{:S(2)}, u32[]{:S(2)}) collective-permute-start(bf16[16,512]{1,0:T(8,128)(2,1)S(1)} %take_chunk.1), channel_id=1, source_target_pairs={{1,0},{0,1},{3,2},{2,3},{5,4},{4,5},{7,6},{6,7},{9,8},{8,9},{11,10... | collective-permute-start | bytes 49160 | tf_op jit(solution)/shard_map/ppermute | solution.py:215
  6.9 6.4 %collective-permute-start.5 = (bf16[1,16,512]{2,1,0:T(8,128)(2,1)S(1)}, bf16[1,16,512]{2,1,0:T(8,128)(2,1)S(1)}, u32[]{:S(2)}, u32[]{:S(2)}) collective-permute-start(bf16[1,16,512]{2,1,0:T(8,128)(2,1)S(1)} %bitcast.16), channel_id=1, source_target_pairs={{2,0},{0,2},{6,4},{4,6},{10,8},{8,10},{14,12},{12,14},{18,16},{16,... | collective-permute-start | bytes 49160 | tf_op jit(solution)/shard_map/ppermute | solution.py:254
  10.5 5.4 %collective-permute-start.3 = (bf16[3,16,512]{2,1,0:T(8,128)(2,1)S(1)}, bf16[3,16,512]{2,1,0:T(8,128)(2,1)S(1)}, u32[]{:S(2)}, u32[]{:S(2)}) collective-permute-start(bf16[3,16,512]{2,1,0:T(8,128)(2,1)S(1)} %pad_maximum_fusion.1.refs_0_), channel_id=1, source_target_pairs={{8,0},{13,1},{10,2},{15,3},{12,4},{1,5},{14,6},{3,7},{0,8},{5,9},{... | collective-permute-start | bytes 147464 | tf_op jit(solution)/shard_map/ppermute | solution.py:256
  12.7 3.3 %collective-permute-start.4 = (bf16[3,16,512]{2,1,0:T(8,128)(2,1)S(1)}, bf16[3,16,512]{2,1,0:T(8,128)(2,1)S(1)}, u32[]{:S(2)}, u32[]{:S(2)}) collective-permute-start(bf16[3,16,512]{2,1,0:T(8,128)(2,1)S(1)} %pad_maximum_fusion.1.refs_0_), channel_id=1, source_target_pairs={{5,1},{7,3},{9,5},{11,7},{13,9},{15,11},{1,13},{3,15},{21,17},{23,... | collective-permute-start | bytes 147464 | tf_op jit(solution)/shard_map/ppermute | solution.py:256
  16.0 1.3 %collective-permute-start.6 = (bf16[4,16,512]{2,1,0:T(8,128)(2,1)S(1)}, bf16[4,16,512]{2,1,0:T(8,128)(2,1)S(1)}, u32[]{:S(2)}, u32[]{:S(2)}) collective-permute-start(bf16[4,16,512]{2,1,0:T(8,128)(2,1)S(1)} %swap.1), channel_id=1, source_target_pairs={{1,0},{0,1},{3,2},{2,3},{5,4},{4,5},{7,6},{6,7},{9,8},{8,9},{11,10... | collective-permute-start | bytes 196616 | tf_op jit(solution)/shard_map/ppermute | solution.py:215

commit v13 on v11

--- a/solution.py
+++ b/solution.py
@@ -151,7 +151,8 @@
         if sub == 0 and at < 2 and turned(ex, lay):
             at = 1 - at
         axis, k = moves[min(at * n_sub + sub, len(moves) - 1)]
-        return flat((ex + k) % n_ex, lay, sub) if axis == "ex" else flat(ex, (lay + k) % n_lay, sub)
+        sender = (sub + 1) % n_sub
+        return flat((ex + k) % n_ex, lay, sender) if axis == "ex" else flat(ex, (lay + k) % n_lay, sender)
 
     compact = (n_ex, n_lay, n_sub) == (4, 2, 2)
 
@@ -169,8 +170,8 @@
         layers = [0, grads_at(0, 1 - across)]
         same = jnp.where(ex // 2 == sub, 1, jnp.where(sub == 0, 4 + 3 * across, 11))
         other = jnp.where(sub == 0, 11, 4 + 3 * (1 - beside))
-        near = jnp.where((sub == 1) & (ex // 2 == 0), 0, sub)
-        units = [(same, (ex + 1 + lay) % 2, near, 0, None), (other, (ex + lay) % 2, 1, 0, None)]
+        near = jnp.where(ex // 2 == sub, sub, 1)
+        units = [(same, (ex + 1 + lay) % 2, near, 0, None), (other, (ex + lay) % 2, 0, 0, None)]
         return slots, layers, units
 
     def general_plan(ex, lay, sub):
@@ -183,7 +184,7 @@
             block = (1 + (core - sub + n_sub) % n_sub * rounds + turn) * size
             if axis == "ex":
                 slots.append(block)
-                sources.append(((ex + k) % n_ex, core))
+                sources.append(((ex + k) % n_ex, (core + 1) % n_sub))
             else:
                 layers.append(block)
         units = []

time: 15.9 us -> 16.2 us (1.019)
  the two profiles are of different devices: /device:TPU:0 before, /device:TPU:3 now
where the time goes in v13:
time: 16.2 us; the launch traced here: 16 us
  waiting for transfers between devices  6.27 us (39%)
  starting transfers between devices  4.9 us (30%)
  Pallas kernels  1.77 us (11%)
  local copies, waits for them, and re-layouts  1.55 us (10%)
  matrix products  0.82 us (5%)
  between operations  0.7 us (4%)
    ppermute x2, waiting for transfers between devices, body(): received.append(lax.ppermute(mine, AXES, pairs))  3.82 us
    ppermute x3, starting transfers between devices, rotate(): lax.ppermute(value, 'sub', [((i + k) % n_sub, i) for i in range(n_sub)])  2.49 us
    ppermute x2, starting transfers between devices, body(): received.append(lax.ppermute(mine, AXES, pairs))  2.36 us
    unnamed x8, local copies, waits for them, and re-layouts  1.55 us
    ppermute x1, waiting for transfers between devices, body(): chunk = lax.ppermute(queries[0], AXES, query_pairs)  1.25 us
    ppermute x3, waiting for transfers between devices, rotate(): lax.ppermute(value, 'sub', [((i + k) % n_sub, i) for i in range(n_sub)])  1.2 us
    pallas_call x1, Pallas kernels, body(): pl.pallas_call(functools.partial(final_kernel, compact_plan if compact el...  1.07 us
    pallas_call x1, Pallas kernels, body(): pl.pallas_call(functools.partial(grads_kernel, n_sub), out_shape=jax.Shap...  0.53 us
  transfers between devices with their start and end apart: 6, of which 5 were waited for; matrix products, arithmetic and copies ran while one was open for 5% of the time, Pallas kernels for 4%

profile of v13, /device:TPU:3, one launch (start us, length us, event | category | flops | bytes accessed | tf_op | source)
XLA Modules:
  0.0 16.0 jit_solution(14783275826716095459)
XLA Ops:
  0.6 0.0 copy-start
  0.6 0.0 copy-start.2
  0.7 0.0 copy-start.1
  0.7 0.1 collective-permute-start.1
  0.7 0.2 picks.1
  0.9 1.0 %copy-done = bf16[1,256,2048]{2,1,0:T(8,128)(2,1)S(1)} copy-done((bf16[1,256,2048]{2,1,0:T(8,128)(2,1)S(1)}, bf16[1,256,2048]{2,1,0:T(8,128)(2,1)}, u32[]{:S(2)}) %copy-start) | copy-done | bytes 1048600
  1.9 0.0 copy-done.2
  1.9 0.0 copy-start.3
  1.9 0.4 %fusion = f32[32,256]{1,0:T(8,128)S(1)} fusion(bf16[1,256,2048]{2,1,0:T(8,128)(2,1)S(1)} %copy-done, bf16[1,32,2048]{2,1,0:T(8,128)(2,1)S(1)} %copy-done.2), kind=kOutput, calls=%fused_computation | convolution fusion | flops 33554432 | bytes 1212416 | tf_op jit(solution)/shard_map/dot_general | solution.py:221
  2.3 0.0 copy-done.1
  2.3 0.5 %copy-done.3 = bf16[1,32,2048]{2,1,0:T(8,128)(2,1)S(1)} copy-done((bf16[1,32,2048]{2,1,0:T(8,128)(2,1)S(1)}, bf16[1,32,2048]{2,1,0:T(8,128)(2,1)}, u32[]{:S(2)}) %copy-start.3) | copy-done | bytes 131096
  2.8 0.4 %fusion.2 = f32[32,256]{1,0:T(8,128)S(1)} fusion(bf16[1,256,2048]{2,1,0:T(8,128)(2,1)S(1)} %copy-done.1, bf16[1,32,2048]{2,1,0:T(8,128)(2,1)S(1)} %copy-done.3), kind=kOutput, calls=%fused_computation.2 | convolution fusion | flops 33554432 | bytes 1212416 | tf_op jit(solution)/shard_map/dot_general | solution.py:220
  3.3 0.7 %collective-permute-start = (f32[64,256]{1,0:T(8,128)S(1)}, f32[64,256]{1,0:T(8,128)S(1)}, u32[]{:S(2)}, u32[]{:S(2)}) collective-permute-start(f32[64,256]{1,0:T(8,128)S(1)} %pad_maximum_fusion.refs_0_), channel_id=1, source_target_pairs={{1,0},{0,1},{3,2},{2,3},{5,4},{4,5},{7,6},{6,7},{9,8},{8,9},{11,10... | collective-permute-start | bytes 196616 | tf_op jit(solution)/shard_map/ppermute | solution.py:198
  4.0 1.2 %collective-permute-done.1.in_ref = bf16[16,512]{1,0:T(8,128)(2,1)S(1)} collective-permute-done((bf16[16,512]{1,0:T(8,128)(2,1)}, bf16[16,512]{1,0:T(8,128)(2,1)S(1)}, u32[]{:S(2)}, u32[]{:S(2)}) %collective-permute-start.1) | collective-permute-done | bytes 16416 | tf_op jit(solution)/shard_map/ppermute | solution.py:207
  5.3 0.4 %collective-permute-start.2 = (bf16[16,512]{1,0:T(8,128)(2,1)S(1)}, bf16[16,512]{1,0:T(8,128)(2,1)S(1)}, u32[]{:S(2)}, u32[]{:S(2)}) collective-permute-start(bf16[16,512]{1,0:T(8,128)(2,1)S(1)} %chunk.1), channel_id=1, source_target_pairs={{1,0},{0,1},{3,2},{2,3},{5,4},{4,5},{7,6},{6,7},{9,8},{8,9},{11,10... | collective-permute-start | bytes 49160 | tf_op jit(solution)/shard_map/ppermute | solution.py:198
  5.7 0.0 collective-permute-done.refs_1_
  5.7 0.5 %grads.1 = bf16[16,512]{1,0:T(8,128)(2,1)S(1)} custom-call(f32[64,256]{1,0:T(8,128)S(1)} %pad_maximum_fusion.refs_0_, f32[64,256]{1,0:T(8,128)S(1)} %collective-permute-done.refs_1_, bf16[256,128]{1,0:T(8,128)(2,1)S(1)} %get-tuple-element.10.refs_2_, bf16[256,1024]{1,0:T(8,128)(2,1)S(1)} %get-tuple-element.11.refs_3_), custom_call_target="tpu_custom_call" | custom-call | tf_op jit(solution)/shard_map/grads/pallas_call | solution.py:235
  6.2 0.3 %collective-permute-done.2 = bf16[16,512]{1,0:T(8,128)(2,1)S(1)} collective-permute-done((bf16[16,512]{1,0:T(8,128)(2,1)S(1)}, bf16[16,512]{1,0:T(8,128)(2,1)S(1)}, u32[]{:S(2)}, u32[]{:S(2)}) %collective-permute-start.2) | collective-permute-done | bytes 16416 | tf_op jit(solution)/shard_map/ppermute | solution.py:198
  6.5 1.7 %collective-permute-start.3 = (bf16[3,16,512]{2,1,0:T(8,128)(2,1)S(1)}, bf16[3,16,512]{2,1,0:T(8,128)(2,1)S(1)}, u32[]{:S(2)}, u32[]{:S(2)}) collective-permute-start(bf16[3,16,512]{2,1,0:T(8,128)(2,1)S(1)} %pad_maximum_fusion.1.refs_0_), channel_id=1, source_target_pairs={{9,0},{12,1},{1,2},{14,3},{13,4},{0,5},{5,6},{2,7},{11,8},{4,9},{3... | collective-permute-start | bytes 147464 | tf_op jit(solution)/shard_map/ppermute | solution.py:248
  8.3 0.6 %collective-permute-start.4 = (bf16[3,16,512]{2,1,0:T(8,128)(2,1)S(1)}, bf16[3,16,512]{2,1,0:T(8,128)(2,1)S(1)}, u32[]{:S(2)}, u32[]{:S(2)}) collective-permute-start(bf16[3,16,512]{2,1,0:T(8,128)(2,1)S(1)} %pad_maximum_fusion.1.refs_0_), channel_id=1, source_target_pairs={{3,0},{4,1},{11,2},{6,3},{7,4},{8,5},{15,6},{10,7},{1,8},{12,9},{9... | collective-permute-start | bytes 147464 | tf_op jit(solution)/shard_map/ppermute | solution.py:248
  8.9 3.3 %collective-permute-done.3.first_ref.refs_1_ = bf16[3,16,512]{2,1,0:T(8,128)(2,1)S(1)} collective-permute-done((bf16[3,16,512]{2,1,0:T(8,128)(2,1)S(1)}, bf16[3,16,512]{2,1,0:T(8,128)(2,1)S(1)}, u32[]{:S(2)}, u32[]{:S(2)}) %collective-permute-start.3) | collective-permute-done | bytes 49184 | tf_op jit(solution)/shard_map/ppermute | solution.py:248
  12.2 0.5 %collective-permute-done.4.second_ref.refs_2_ = bf16[3,16,512]{2,1,0:T(8,128)(2,1)S(1)} collective-permute-done((bf16[3,16,512]{2,1,0:T(8,128)(2,1)S(1)}, bf16[3,16,512]{2,1,0:T(8,128)(2,1)S(1)}, u32[]{:S(2)}, u32[]{:S(2)}) %collective-permute-start.4) | collective-permute-done | bytes 49184 | tf_op jit(solution)/shard_map/ppermute | solution.py:248
  12.7 1.4 %collective-permute-start.5 = (bf16[4,16,512]{2,1,0:T(8,128)(2,1)S(1)}, bf16[4,16,512]{2,1,0:T(8,128)(2,1)S(1)}, u32[]{:S(2)}, u32[]{:S(2)}) collective-permute-start(bf16[4,16,512]{2,1,0:T(8,128)(2,1)S(1)} %swap.1), channel_id=1, source_target_pairs={{1,0},{0,1},{3,2},{2,3},{5,4},{4,5},{7,6},{6,7},{9,8},{8,9},{11,10... | collective-permute-start | bytes 196616 | tf_op jit(solution)/shard_map/ppermute | solution.py:198
  14.1 0.9 %collective-permute-done.5.refs_3_ = bf16[4,16,512]{2,1,0:T(8,128)(2,1)S(1)} collective-permute-done((bf16[4,16,512]{2,1,0:T(8,128)(2,1)S(1)}, bf16[4,16,512]{2,1,0:T(8,128)(2,1)S(1)}, u32[]{:S(2)}, u32[]{:S(2)}) %collective-permute-start.5) | collective-permute-done | bytes 65568 | tf_op jit(solution)/shard_map/ppermute | solution.py:198
  15.0 1.1 %gram_and_scores.1 = (f32[1,256,512]{2,1,0:T(8,128)}, f32[4,16]{1,0:T(4,128)}) custom-call(bf16[3,16,512]{2,1,0:T(8,128)(2,1)S(1)} %pad_maximum_fusion.1.refs_0_, bf16[3,16,512]{2,1,0:T(8,128)(2,1)S(1)} %collective-permute-done.3.first_ref.refs_1_, bf16[3,16,512]{2,1,0:T(8,128)(2,1)S(1)} %collective-permute-done.4.second_ref.refs_2_, ...), custom_call_target="tpu_custom_call" | custom-call | tf_op jit(solution)/shard_map/gram_and_scores/pallas_call | solution.py:263
  (4 shorter events, 0.0 us)
Async XLA Ops:
  0.6 1.2 %copy-start = (bf16[1,256,2048]{2,1,0:T(8,128)(2,1)S(1)}, bf16[1,256,2048]{2,1,0:T(8,128)(2,1)}, u32[]{:S(2)}) copy-start(bf16[1,256,2048]{2,1,0:T(8,128)(2,1)} %param.6) | copy-start | bytes 3145732
  0.6 1.2 %copy-start.2 = (bf16[1,32,2048]{2,1,0:T(8,128)(2,1)S(1)}, bf16[1,32,2048]{2,1,0:T(8,128)(2,1)}, u32[]{:S(2)}) copy-start(bf16[1,32,2048]{2,1,0:T(8,128)(2,1)} %param.8) | copy-start | bytes 393220
  0.7 1.6 %copy-start.1 = (bf16[1,256,2048]{2,1,0:T(8,128)(2,1)S(1)}, bf16[1,256,2048]{2,1,0:T(8,128)(2,1)}, u32[]{:S(2)}) copy-start(bf16[1,256,2048]{2,1,0:T(8,128)(2,1)} %param.5) | copy-start | bytes 3145732
  0.7 4.6 %collective-permute-start.1 = (bf16[16,512]{1,0:T(8,128)(2,1)}, bf16[16,512]{1,0:T(8,128)(2,1)S(1)}, u32[]{:S(2)}, u32[]{:S(2)}) collective-permute-start(bf16[16,512]{1,0:T(8,128)(2,1)} %bitcast.19), channel_id=1, source_target_pairs={{0,5},{1,4},{2,1},{3,0},{4,13},{5,12},{6,9},{7,8},{8,7},{9,6},{10,... | collective-permute-start | bytes 49160 | tf_op jit(solution)/shard_map/ppermute | solution.py:207
  1.9 1.0 %copy-start.3 = (bf16[1,32,2048]{2,1,0:T(8,128)(2,1)S(1)}, bf16[1,32,2048]{2,1,0:T(8,128)(2,1)}, u32[]{:S(2)}) copy-start(bf16[1,32,2048]{2,1,0:T(8,128)(2,1)} %param.7) | copy-start | bytes 393220
  3.3 2.4 %collective-permute-start = (f32[64,256]{1,0:T(8,128)S(1)}, f32[64,256]{1,0:T(8,128)S(1)}, u32[]{:S(2)}, u32[]{:S(2)}) collective-permute-start(f32[64,256]{1,0:T(8,128)S(1)} %pad_maximum_fusion.refs_0_), channel_id=1, source_target_pairs={{1,0},{0,1},{3,2},{2,3},{5,4},{4,5},{7,6},{6,7},{9,8},{8,9},{11,10... | collective-permute-start | bytes 196616 | tf_op jit(solution)/shard_map/ppermute | solution.py:198
  5.3 1.2 %collective-permute-start.2 = (bf16[16,512]{1,0:T(8,128)(2,1)S(1)}, bf16[16,512]{1,0:T(8,128)(2,1)S(1)}, u32[]{:S(2)}, u32[]{:S(2)}) collective-permute-start(bf16[16,512]{1,0:T(8,128)(2,1)S(1)} %chunk.1), channel_id=1, source_target_pairs={{1,0},{0,1},{3,2},{2,3},{5,4},{4,5},{7,6},{6,7},{9,8},{8,9},{11,10... | collective-permute-start | bytes 49160 | tf_op jit(solution)/shard_map/ppermute | solution.py:198
  6.5 5.7 %collective-permute-start.3 = (bf16[3,16,512]{2,1,0:T(8,128)(2,1)S(1)}, bf16[3,16,512]{2,1,0:T(8,128)(2,1)S(1)}, u32[]{:S(2)}, u32[]{:S(2)}) collective-permute-start(bf16[3,16,512]{2,1,0:T(8,128)(2,1)S(1)} %pad_maximum_fusion.1.refs_0_), channel_id=1, source_target_pairs={{9,0},{12,1},{1,2},{14,3},{13,4},{0,5},{5,6},{2,7},{11,8},{4,9},{3... | collective-permute-start | bytes 147464 | tf_op jit(solution)/shard_map/ppermute | solution.py:248
  8.3 4.4 %collective-permute-start.4 = (bf16[3,16,512]{2,1,0:T(8,128)(2,1)S(1)}, bf16[3,16,512]{2,1,0:T(8,128)(2,1)S(1)}, u32[]{:S(2)}, u32[]{:S(2)}) collective-permute-start(bf16[3,16,512]{2,1,0:T(8,128)(2,1)S(1)} %pad_maximum_fusion.1.refs_0_), channel_id=1, source_target_pairs={{3,0},{4,1},{11,2},{6,3},{7,4},{8,5},{15,6},{10,7},{1,8},{12,9},{9... | collective-permute-start | bytes 147464 | tf_op jit(solution)/shard_map/ppermute | solution.py:248
  12.7 2.3 %collective-permute-start.5 = (bf16[4,16,512]{2,1,0:T(8,128)(2,1)S(1)}, bf16[4,16,512]{2,1,0:T(8,128)(2,1)S(1)}, u32[]{:S(2)}, u32[]{:S(2)}) collective-permute-start(bf16[4,16,512]{2,1,0:T(8,128)(2,1)S(1)} %swap.1), channel_id=1, source_target_pairs={{1,0},{0,1},{3,2},{2,3},{5,4},{4,5},{7,6},{6,7},{9,8},{8,9},{11,10... | collective-permute-start | bytes 196616 | tf_op jit(solution)/shard_map/ppermute | solution.py:198

commit v14 on v13

--- a/solution.py
+++ b/solution.py
@@ -144,14 +144,17 @@
     moves += [("ex", k) for k in range(2, n_ex - 1) if k != n_ex // 2] + [("lay", k) for k in range(2, n_lay)]
     rounds = -(-len(moves) // n_sub)
 
+    def sender_of(at, sub):
+        return (sub + (at == 1)) % n_sub
+
     def turned(ex, lay):
         return (ex // (n_ex // 2) + lay) % 2 == 0
 
     def source_of(at, ex, lay, sub):
+        sender = sender_of(at, sub)
         if sub == 0 and at < 2 and turned(ex, lay):
             at = 1 - at
         axis, k = moves[min(at * n_sub + sub, len(moves) - 1)]
-        sender = (sub + 1) % n_sub
         return flat((ex + k) % n_ex, lay, sender) if axis == "ex" else flat(ex, (lay + k) % n_lay, sender)
 
     compact = (n_ex, n_lay, n_sub) == (4, 2, 2)
@@ -170,8 +173,9 @@
         layers = [0, grads_at(0, 1 - across)]
         same = jnp.where(ex // 2 == sub, 1, jnp.where(sub == 0, 4 + 3 * across, 11))
         other = jnp.where(sub == 0, 11, 4 + 3 * (1 - beside))
-        near = jnp.where(ex // 2 == sub, sub, 1)
-        units = [(same, (ex + 1 + lay) % 2, near, 0, None), (other, (ex + lay) % 2, 0, 0, None)]
+        near = jnp.where(ex // 2 == sub, sub, across)
+        far = jnp.where(sub == 0, 1 - beside, beside)
+        units = [(same, (ex + 1 + lay) % 2, near, 0, None), (other, (ex + lay) % 2, far, 0, None)]
         return slots, layers, units
 
     def general_plan(ex, lay, sub):
@@ -184,7 +188,7 @@
             block = (1 + (core - sub + n_sub) % n_sub * rounds + turn) * size
             if axis == "ex":
                 slots.append(block)
-                sources.append(((ex + k) % n_ex, (core + 1) % n_sub))
+                sources.append(((ex + k) % n_ex, sender_of(turn, core)))
             else:
                 layers.append(block)
         units = []

time: 16.2 us -> 15.5 us (0.957)
  the two profiles are of different devices: /device:TPU:3 before, /device:TPU:0 now
where the time goes in v14:
time: 15.5 us; the launch traced here: 15.4 us
  starting transfers between devices  8.07 us (52%)
  waiting for transfers between devices  3.46 us (22%)
  Pallas kernels  1.77 us (11%)
  matrix products  0.82 us (5%)
  between operations  0.73 us (5%)
  local copies, waits for them, and re-layouts  0.5 us (3%)
    ppermute x2, starting transfers between devices, body(): received.append(lax.ppermute(mine, AXES, pairs))  4.37 us
    ppermute x1, starting transfers between devices, body(): chunk = lax.ppermute(queries[0], AXES, query_pairs)  2.52 us
    ppermute x2, waiting for transfers between devices, body(): received.append(lax.ppermute(mine, AXES, pairs))  1.75 us
    ppermute x3, waiting for transfers between devices, rotate(): lax.ppermute(value, 'sub', [((i + k) % n_sub, i) for i in range(n_sub)])  1.71 us
    ppermute x3, starting transfers between devices, rotate(): lax.ppermute(value, 'sub', [((i + k) % n_sub, i) for i in range(n_sub)])  1.18 us
    pallas_call x1, Pallas kernels, body(): pl.pallas_call(functools.partial(final_kernel, compact_plan if compact el...  1.07 us
    pallas_call x1, Pallas kernels, body(): pl.pallas_call(functools.partial(grads_kernel, n_sub), out_shape=jax.Shap...  0.53 us
    unnamed x8, local copies, waits for them, and re-layouts  0.5 us
  transfers between devices with their start and end apart: 6, of which 4 were waited for; matrix products, arithmetic and copies ran while one was open for 5% of the time, Pallas kernels for 4%

profile of v14, /device:TPU:0, one launch (start us, length us, event | category | flops | bytes accessed | tf_op | source)
XLA Modules:
  0.0 15.4 jit_solution(6364820331916377756)
XLA Ops:
  0.6 0.0 copy-start
  0.6 0.0 copy-start.2
  0.7 0.0 copy-start.1
  0.7 2.5 %collective-permute-start.1 = (bf16[16,512]{1,0:T(8,128)(2,1)}, bf16[16,512]{1,0:T(8,128)(2,1)S(1)}, u32[]{:S(2)}, u32[]{:S(2)}) collective-permute-start(bf16[16,512]{1,0:T(8,128)(2,1)} %bitcast.19), channel_id=1, source_target_pairs={{0,5},{1,4},{2,1},{3,0},{4,13},{5,12},{6,9},{7,8},{8,7},{9,6},{10,... | collective-permute-start | bytes 49160 | tf_op jit(solution)/shard_map/ppermute | solution.py:211
  3.2 0.1 picks.1
  3.3 0.0 copy-done
  3.3 0.0 copy-done.2
  3.4 0.0 copy-start.3
  3.4 0.4 %fusion = f32[32,256]{1,0:T(8,128)S(1)} fusion(bf16[1,256,2048]{2,1,0:T(8,128)(2,1)S(1)} %copy-done, bf16[1,32,2048]{2,1,0:T(8,128)(2,1)S(1)} %copy-done.2), kind=kOutput, calls=%fused_computation | convolution fusion | flops 33554432 | bytes 1212416 | tf_op jit(solution)/shard_map/dot_general | solution.py:225
  3.8 0.0 copy-done.1
  3.8 0.5 %copy-done.3 = bf16[1,32,2048]{2,1,0:T(8,128)(2,1)S(1)} copy-done((bf16[1,32,2048]{2,1,0:T(8,128)(2,1)S(1)}, bf16[1,32,2048]{2,1,0:T(8,128)(2,1)}, u32[]{:S(2)}) %copy-start.3) | copy-done | bytes 131096
  4.3 0.4 %fusion.2 = f32[32,256]{1,0:T(8,128)S(1)} fusion(bf16[1,256,2048]{2,1,0:T(8,128)(2,1)S(1)} %copy-done.1, bf16[1,32,2048]{2,1,0:T(8,128)(2,1)S(1)} %copy-done.3), kind=kOutput, calls=%fused_computation.2 | convolution fusion | flops 33554432 | bytes 1212416 | tf_op jit(solution)/shard_map/dot_general | solution.py:224
  4.7 0.7 %collective-permute-start = (f32[64,256]{1,0:T(8,128)S(1)}, f32[64,256]{1,0:T(8,128)S(1)}, u32[]{:S(2)}, u32[]{:S(2)}) collective-permute-start(f32[64,256]{1,0:T(8,128)S(1)} %pad_maximum_fusion.refs_0_), channel_id=1, source_target_pairs={{1,0},{0,1},{3,2},{2,3},{5,4},{4,5},{7,6},{6,7},{9,8},{8,9},{11,10... | collective-permute-start | bytes 196616 | tf_op jit(solution)/shard_map/ppermute | solution.py:202
  5.4 0.0 collective-permute-done.1.in_ref
  5.4 0.1 collective-permute-start.2
  5.5 0.8 %collective-permute-done.refs_1_ = f32[64,256]{1,0:T(8,128)S(1)} collective-permute-done((f32[64,256]{1,0:T(8,128)S(1)}, f32[64,256]{1,0:T(8,128)S(1)}, u32[]{:S(2)}, u32[]{:S(2)}) %collective-permute-start) | collective-permute-done | bytes 65568 | tf_op jit(solution)/shard_map/ppermute | solution.py:202
  6.3 0.5 %grads.1 = bf16[16,512]{1,0:T(8,128)(2,1)S(1)} custom-call(f32[64,256]{1,0:T(8,128)S(1)} %pad_maximum_fusion.refs_0_, f32[64,256]{1,0:T(8,128)S(1)} %collective-permute-done.refs_1_, bf16[256,128]{1,0:T(8,128)(2,1)S(1)} %get-tuple-element.10.refs_2_, bf16[256,1024]{1,0:T(8,128)(2,1)S(1)} %get-tuple-element.11.refs_3_), custom_call_target="tpu_custom_call" | custom-call | tf_op jit(solution)/shard_map/grads/pallas_call | solution.py:239
  6.9 0.0 collective-permute-done.2
  6.9 2.3 %collective-permute-start.3 = (bf16[3,16,512]{2,1,0:T(8,128)(2,1)S(1)}, bf16[3,16,512]{2,1,0:T(8,128)(2,1)S(1)}, u32[]{:S(2)}, u32[]{:S(2)}) collective-permute-start(bf16[3,16,512]{2,1,0:T(8,128)(2,1)S(1)} %pad_maximum_fusion.1.refs_0_), channel_id=1, source_target_pairs={{8,0},{13,1},{0,2},{15,3},{12,4},{1,5},{4,6},{3,7},{10,8},{5,9},{2... | collective-permute-start | bytes 147464 | tf_op jit(solution)/shard_map/ppermute | solution.py:252
  9.2 2.1 %collective-permute-start.4 = (bf16[3,16,512]{2,1,0:T(8,128)(2,1)S(1)}, bf16[3,16,512]{2,1,0:T(8,128)(2,1)S(1)}, u32[]{:S(2)}, u32[]{:S(2)}) collective-permute-start(bf16[3,16,512]{2,1,0:T(8,128)(2,1)S(1)} %pad_maximum_fusion.1.refs_0_), channel_id=1, source_target_pairs={{3,0},{4,1},{11,2},{6,3},{7,4},{8,5},{15,6},{10,7},{1,8},{12,9},{9... | collective-permute-start | bytes 147464 | tf_op jit(solution)/shard_map/ppermute | solution.py:252
  11.3 1.2 %collective-permute-done.3.first_ref.refs_1_ = bf16[3,16,512]{2,1,0:T(8,128)(2,1)S(1)} collective-permute-done((bf16[3,16,512]{2,1,0:T(8,128)(2,1)S(1)}, bf16[3,16,512]{2,1,0:T(8,128)(2,1)S(1)}, u32[]{:S(2)}, u32[]{:S(2)}) %collective-permute-start.3) | collective-permute-done | bytes 49184 | tf_op jit(solution)/shard_map/ppermute | solution.py:252
  12.5 0.5 %collective-permute-done.4.second_ref.refs_2_ = bf16[3,16,512]{2,1,0:T(8,128)(2,1)S(1)} collective-permute-done((bf16[3,16,512]{2,1,0:T(8,128)(2,1)S(1)}, bf16[3,16,512]{2,1,0:T(8,128)(2,1)S(1)}, u32[]{:S(2)}, u32[]{:S(2)}) %collective-permute-start.4) | collective-permute-done | bytes 49184 | tf_op jit(solution)/shard_map/ppermute | solution.py:252
  13.0 0.3 %collective-permute-start.5 = (bf16[4,16,512]{2,1,0:T(8,128)(2,1)S(1)}, bf16[4,16,512]{2,1,0:T(8,128)(2,1)S(1)}, u32[]{:S(2)}, u32[]{:S(2)}) collective-permute-start(bf16[4,16,512]{2,1,0:T(8,128)(2,1)S(1)} %swap.1), channel_id=1, source_target_pairs={{1,0},{0,1},{3,2},{2,3},{5,4},{4,5},{7,6},{6,7},{9,8},{8,9},{11,10... | collective-permute-start | bytes 196616 | tf_op jit(solution)/shard_map/ppermute | solution.py:202
  13.4 0.9 %collective-permute-done.5.refs_3_ = bf16[4,16,512]{2,1,0:T(8,128)(2,1)S(1)} collective-permute-done((bf16[4,16,512]{2,1,0:T(8,128)(2,1)S(1)}, bf16[4,16,512]{2,1,0:T(8,128)(2,1)S(1)}, u32[]{:S(2)}, u32[]{:S(2)}) %collective-permute-start.5) | collective-permute-done | bytes 65568 | tf_op jit(solution)/shard_map/ppermute | solution.py:202
  14.3 1.1 %gram_and_scores.1 = (f32[1,256,512]{2,1,0:T(8,128)}, f32[4,16]{1,0:T(4,128)}) custom-call(bf16[3,16,512]{2,1,0:T(8,128)(2,1)S(1)} %pad_maximum_fusion.1.refs_0_, bf16[3,16,512]{2,1,0:T(8,128)(2,1)S(1)} %collective-permute-done.3.first_ref.refs_1_, bf16[3,16,512]{2,1,0:T(8,128)(2,1)S(1)} %collective-permute-done.4.second_ref.refs_2_, ...), custom_call_target="tpu_custom_call" | custom-call | tf_op jit(solution)/shard_map/gram_and_scores/pallas_call | solution.py:267
  (4 shorter events, 0.0 us)
Async XLA Ops:
  0.6 2.7 %copy-start = (bf16[1,256,2048]{2,1,0:T(8,128)(2,1)S(1)}, bf16[1,256,2048]{2,1,0:T(8,128)(2,1)}, u32[]{:S(2)}) copy-start(bf16[1,256,2048]{2,1,0:T(8,128)(2,1)} %param.6) | copy-start | bytes 3145732
  0.6 2.7 %copy-start.2 = (bf16[1,32,2048]{2,1,0:T(8,128)(2,1)S(1)}, bf16[1,32,2048]{2,1,0:T(8,128)(2,1)}, u32[]{:S(2)}) copy-start(bf16[1,32,2048]{2,1,0:T(8,128)(2,1)} %param.8) | copy-start | bytes 393220
  0.7 3.1 %copy-start.1 = (bf16[1,256,2048]{2,1,0:T(8,128)(2,1)S(1)}, bf16[1,256,2048]{2,1,0:T(8,128)(2,1)}, u32[]{:S(2)}) copy-start(bf16[1,256,2048]{2,1,0:T(8,128)(2,1)} %param.5) | copy-start | bytes 3145732
  0.7 4.8 %collective-permute-start.1 = (bf16[16,512]{1,0:T(8,128)(2,1)}, bf16[16,512]{1,0:T(8,128)(2,1)S(1)}, u32[]{:S(2)}, u32[]{:S(2)}) collective-permute-start(bf16[16,512]{1,0:T(8,128)(2,1)} %bitcast.19), channel_id=1, source_target_pairs={{0,5},{1,4},{2,1},{3,0},{4,13},{5,12},{6,9},{7,8},{8,7},{9,6},{10,... | collective-permute-start | bytes 49160 | tf_op jit(solution)/shard_map/ppermute | solution.py:211
  3.4 0.9 %copy-start.3 = (bf16[1,32,2048]{2,1,0:T(8,128)(2,1)S(1)}, bf16[1,32,2048]{2,1,0:T(8,128)(2,1)}, u32[]{:S(2)}) copy-start(bf16[1,32,2048]{2,1,0:T(8,128)(2,1)} %param.7) | copy-start | bytes 393220
  4.7 1.6 %collective-permute-start = (f32[64,256]{1,0:T(8,128)S(1)}, f32[64,256]{1,0:T(8,128)S(1)}, u32[]{:S(2)}, u32[]{:S(2)}) collective-permute-start(f32[64,256]{1,0:T(8,128)S(1)} %pad_maximum_fusion.refs_0_), channel_id=1, source_target_pairs={{1,0},{0,1},{3,2},{2,3},{5,4},{4,5},{7,6},{6,7},{9,8},{8,9},{11,10... | collective-permute-start | bytes 196616 | tf_op jit(solution)/shard_map/ppermute | solution.py:202
  5.4 1.4 %collective-permute-start.2 = (bf16[16,512]{1,0:T(8,128)(2,1)S(1)}, bf16[16,512]{1,0:T(8,128)(2,1)S(1)}, u32[]{:S(2)}, u32[]{:S(2)}) collective-permute-start(bf16[16,512]{1,0:T(8,128)(2,1)S(1)} %chunk.1), channel_id=1, source_target_pairs={{1,0},{0,1},{3,2},{2,3},{5,4},{4,5},{7,6},{6,7},{9,8},{8,9},{11,10... | collective-permute-start | bytes 49160 | tf_op jit(solution)/shard_map/ppermute | solution.py:202
  6.9 5.6 %collective-permute-start.3 = (bf16[3,16,512]{2,1,0:T(8,128)(2,1)S(1)}, bf16[3,16,512]{2,1,0:T(8,128)(2,1)S(1)}, u32[]{:S(2)}, u32[]{:S(2)}) collective-permute-start(bf16[3,16,512]{2,1,0:T(8,128)(2,1)S(1)} %pad_maximum_fusion.1.refs_0_), channel_id=1, source_target_pairs={{8,0},{13,1},{0,2},{15,3},{12,4},{1,5},{4,6},{3,7},{10,8},{5,9},{2... | collective-permute-start | bytes 147464 | tf_op jit(solution)/shard_map/ppermute | solution.py:252
  9.2 3.8 %collective-permute-start.4 = (bf16[3,16,512]{2,1,0:T(8,128)(2,1)S(1)}, bf16[3,16,512]{2,1,0:T(8,128)(2,1)S(1)}, u32[]{:S(2)}, u32[]{:S(2)}) collective-permute-start(bf16[3,16,512]{2,1,0:T(8,128)(2,1)S(1)} %pad_maximum_fusion.1.refs_0_), channel_id=1, source_target_pairs={{3,0},{4,1},{11,2},{6,3},{7,4},{8,5},{15,6},{10,7},{1,8},{12,9},{9... | collective-permute-start | bytes 147464 | tf_op jit(solution)/shard_map/ppermute | solution.py:252
  13.0 1.3 %collective-permute-start.5 = (bf16[4,16,512]{2,1,0:T(8,128)(2,1)S(1)}, bf16[4,16,512]{2,1,0:T(8,128)(2,1)S(1)}, u32[]{:S(2)}, u32[]{:S(2)}) collective-permute-start(bf16[4,16,512]{2,1,0:T(8,128)(2,1)S(1)} %swap.1), channel_id=1, source_target_pairs={{1,0},{0,1},{3,2},{2,3},{5,4},{4,5},{7,6},{6,7},{9,8},{8,9},{11,10... | collective-permute-start | bytes 196616 | tf_op jit(solution)/shard_map/ppermute | solution.py:202

commit v15 on v14

--- a/solution.py
+++ b/solution.py
@@ -11,6 +11,7 @@
 AXES = ("ex", "lay", "sub")
 F32, BF16 = jnp.float32, jnp.bfloat16
 VMEM = pl.BlockSpec(memory_space=pltpu.VMEM)
+ANY = pl.BlockSpec(memory_space=pl.ANY)
 LAST = (((1,), (1,)), ((), ()))
 FIRST = (((0,), (0,)), ((), ()))
 PARAMS = pltpu.CompilerParams(vmem_limit_bytes=16 * 1024 * 1024)
@@ -76,7 +77,7 @@
 
 
 def final_kernel(plan, n_ex, n_sub, own, *refs):
-    parts, (gram_ref, scores_ref, all_ref) = refs[:-3], refs[-3:]
+    parts, (gram_ref, scores_ref, all_ref, gram_buf, scores_buf, sems) = refs[:-6], refs[-6:]
     start = 0
     for part in parts:
         all_ref[start : start + part.shape[0]] = part[...]
@@ -105,8 +106,14 @@
         rights += [right, right]
     left = jnp.concatenate(lefts, axis=0).astype(BF16)
     right = jnp.concatenate(rights, axis=0).astype(BF16)
-    gram = lax.dot_general(left, right, FIRST, preferred_element_type=F32)
-    gram_ref[0] = gram * (1.0 / (own * n_ex))
+    copies = []
+    step = n_rows // gram_buf.shape[0]
+    for at in range(gram_buf.shape[0]):
+        rows = slice(at * step, (at + 1) * step)
+        gram = lax.dot_general(left[:, rows], right, FIRST, preferred_element_type=F32)
+        gram_buf[at] = gram * (1.0 / (own * n_ex))
+        copies.append(pltpu.make_async_copy(gram_buf.at[at], gram_ref.at[0, rows, :], sems.at[at]))
+        copies[-1].start()
 
     layers = [halves_of(block) for block in layers]
     blocks = {}
@@ -120,7 +127,11 @@
         part = part if fits is None else jnp.where(fits, part, 0.0)
         blocks[column] = blocks.get(column, 0.0) + part
     blocks = [blocks[column] for column in sorted(blocks)]
-    scores_ref[...] = blocks[0] if len(blocks) == 1 else jnp.concatenate(blocks, axis=1)
+    scores_buf[...] = blocks[0] if len(blocks) == 1 else jnp.concatenate(blocks, axis=1)
+    copies.append(pltpu.make_async_copy(scores_buf, scores_ref, sems.at[len(copies)]))
+    copies[-1].start()
+    for copy in copies:
+        copy.wait()
 
 
 def solution(mesh):
@@ -264,6 +275,7 @@
             both = jnp.concatenate(received)
             blocks = [mine, both] + [rotate(both, k) for k in range(1, n_sub)]
 
+        pieces = 2 if width // n_ex % 256 == 0 else 1
         return pl.pallas_call(
             functools.partial(final_kernel, compact_plan if compact else general_plan, n_ex, n_sub, own),
             out_shape=(
@@ -271,8 +283,13 @@
                 jax.ShapeDtypeStruct((own, rows * per_blk), F32),
             ),
             in_specs=[VMEM] * len(blocks),
-            out_specs=(VMEM, VMEM),
-            scratch_shapes=[pltpu.VMEM((sum(block.shape[0] for block in blocks), rows, half), BF16)],
+            out_specs=(ANY, ANY),
+            scratch_shapes=[
+                pltpu.VMEM((sum(block.shape[0] for block in blocks), rows, half), BF16),
+                pltpu.VMEM((pieces, width // n_ex // pieces, half), F32),
+                pltpu.VMEM((own, rows * per_blk), F32),
+                pltpu.SemaphoreType.DMA((pieces + 1,)),
+            ],
             compiler_params=PARAMS,
             name="gram_and_scores",
         )(*blocks)

time: 15.5 us -> 15.5 us (level)
  no operation moved by 1% of the time
where the time goes in v15:
time: 15.5 us; the launch traced here: 15.3 us
  starting transfers between devices  8.07 us (52%)
  waiting for transfers between devices  3.46 us (22%)
  Pallas kernels  1.74 us (11%)
  matrix products  0.82 us (5%)
  between operations  0.73 us (5%)
  local copies, waits for them, and re-layouts  0.5 us (3%)
    ppermute x2, starting transfers between devices, body(): received.append(lax.ppermute(mine, AXES, pairs))  4.37 us
    ppermute x1, starting transfers between devices, body(): chunk = lax.ppermute(queries[0], AXES, query_pairs)  2.52 us
    ppermute x2, waiting for transfers between devices, body(): received.append(lax.ppermute(mine, AXES, pairs))  1.75 us
    ppermute x3, waiting for transfers between devices, rotate(): lax.ppermute(value, 'sub', [((i + k) % n_sub, i) for i in range(n_sub)])  1.71 us
    ppermute x3, starting transfers between devices, rotate(): lax.ppermute(value, 'sub', [((i + k) % n_sub, i) for i in range(n_sub)])  1.18 us
    pallas_call x1, Pallas kernels, body(): pl.pallas_call(functools.partial(final_kernel, compact_plan if compact el...  1.05 us
    pallas_call x1, Pallas kernels, body(): pl.pallas_call(functools.partial(grads_kernel, n_sub), out_shape=jax.Shap...  0.53 us
    unnamed x8, local copies, waits for them, and re-layouts  0.5 us
  transfers between devices with their start and end apart: 6, of which 4 were waited for; matrix products, arithmetic and copies ran while one was open for 5% of the time, Pallas kernels for 4%

profile of v15, /device:TPU:0, one launch (start us, length us, event | category | flops | bytes accessed | tf_op | source)
XLA Modules:
  0.0 15.3 jit_solution(6301899208472947406)
XLA Ops:
  0.6 0.0 copy-start
  0.6 0.0 copy-start.2
  0.7 0.0 copy-start.1
  0.7 2.5 %collective-permute-start.1 = (bf16[16,512]{1,0:T(8,128)(2,1)}, bf16[16,512]{1,0:T(8,128)(2,1)S(1)}, u32[]{:S(2)}, u32[]{:S(2)}) collective-permute-start(bf16[16,512]{1,0:T(8,128)(2,1)} %bitcast.19), channel_id=1, source_target_pairs={{0,5},{1,4},{2,1},{3,0},{4,13},{5,12},{6,9},{7,8},{8,7},{9,6},{10,... | collective-permute-start | bytes 49160 | tf_op jit(solution)/shard_map/ppermute | solution.py:222
  3.2 0.1 picks.1
  3.3 0.0 copy-done
  3.3 0.0 copy-done.2
  3.4 0.0 copy-start.3
  3.4 0.4 %fusion = f32[32,256]{1,0:T(8,128)S(1)} fusion(bf16[1,256,2048]{2,1,0:T(8,128)(2,1)S(1)} %copy-done, bf16[1,32,2048]{2,1,0:T(8,128)(2,1)S(1)} %copy-done.2), kind=kOutput, calls=%fused_computation | convolution fusion | flops 33554432 | bytes 1212416 | tf_op jit(solution)/shard_map/dot_general | solution.py:236
  3.8 0.0 copy-done.1
  3.8 0.5 %copy-done.3 = bf16[1,32,2048]{2,1,0:T(8,128)(2,1)S(1)} copy-done((bf16[1,32,2048]{2,1,0:T(8,128)(2,1)S(1)}, bf16[1,32,2048]{2,1,0:T(8,128)(2,1)}, u32[]{:S(2)}) %copy-start.3) | copy-done | bytes 131096
  4.3 0.4 %fusion.2 = f32[32,256]{1,0:T(8,128)S(1)} fusion(bf16[1,256,2048]{2,1,0:T(8,128)(2,1)S(1)} %copy-done.1, bf16[1,32,2048]{2,1,0:T(8,128)(2,1)S(1)} %copy-done.3), kind=kOutput, calls=%fused_computation.2 | convolution fusion | flops 33554432 | bytes 1212416 | tf_op jit(solution)/shard_map/dot_general | solution.py:235
  4.7 0.7 %collective-permute-start = (f32[64,256]{1,0:T(8,128)S(1)}, f32[64,256]{1,0:T(8,128)S(1)}, u32[]{:S(2)}, u32[]{:S(2)}) collective-permute-start(f32[64,256]{1,0:T(8,128)S(1)} %pad_maximum_fusion.refs_0_), channel_id=1, source_target_pairs={{1,0},{0,1},{3,2},{2,3},{5,4},{4,5},{7,6},{6,7},{9,8},{8,9},{11,10... | collective-permute-start | bytes 196616 | tf_op jit(solution)/shard_map/ppermute | solution.py:213
  5.4 0.0 collective-permute-done.1.in_ref
  5.4 0.1 collective-permute-start.2
  5.5 0.8 %collective-permute-done.refs_1_ = f32[64,256]{1,0:T(8,128)S(1)} collective-permute-done((f32[64,256]{1,0:T(8,128)S(1)}, f32[64,256]{1,0:T(8,128)S(1)}, u32[]{:S(2)}, u32[]{:S(2)}) %collective-permute-start) | collective-permute-done | bytes 65568 | tf_op jit(solution)/shard_map/ppermute | solution.py:213
  6.3 0.5 %grads.1 = bf16[16,512]{1,0:T(8,128)(2,1)S(1)} custom-call(f32[64,256]{1,0:T(8,128)S(1)} %pad_maximum_fusion.refs_0_, f32[64,256]{1,0:T(8,128)S(1)} %collective-permute-done.refs_1_, bf16[256,128]{1,0:T(8,128)(2,1)S(1)} %get-tuple-element.10.refs_2_, bf16[256,1024]{1,0:T(8,128)(2,1)S(1)} %get-tuple-element.11.refs_3_), custom_call_target="tpu_custom_call" | custom-call | tf_op jit(solution)/shard_map/grads/pallas_call | solution.py:250
  6.9 0.0 collective-permute-done.2
  6.9 2.3 %collective-permute-start.3 = (bf16[3,16,512]{2,1,0:T(8,128)(2,1)S(1)}, bf16[3,16,512]{2,1,0:T(8,128)(2,1)S(1)}, u32[]{:S(2)}, u32[]{:S(2)}) collective-permute-start(bf16[3,16,512]{2,1,0:T(8,128)(2,1)S(1)} %pad_maximum_fusion.1.refs_0_), channel_id=1, source_target_pairs={{8,0},{13,1},{0,2},{15,3},{12,4},{1,5},{4,6},{3,7},{10,8},{5,9},{2... | collective-permute-start | bytes 147464 | tf_op jit(solution)/shard_map/ppermute | solution.py:263
  9.2 2.1 %collective-permute-start.4 = (bf16[3,16,512]{2,1,0:T(8,128)(2,1)S(1)}, bf16[3,16,512]{2,1,0:T(8,128)(2,1)S(1)}, u32[]{:S(2)}, u32[]{:S(2)}) collective-permute-start(bf16[3,16,512]{2,1,0:T(8,128)(2,1)S(1)} %pad_maximum_fusion.1.refs_0_), channel_id=1, source_target_pairs={{3,0},{4,1},{11,2},{6,3},{7,4},{8,5},{15,6},{10,7},{1,8},{12,9},{9... | collective-permute-start | bytes 147464 | tf_op jit(solution)/shard_map/ppermute | solution.py:263
  11.3 1.2 %collective-permute-done.3.first_ref.refs_1_ = bf16[3,16,512]{2,1,0:T(8,128)(2,1)S(1)} collective-permute-done((bf16[3,16,512]{2,1,0:T(8,128)(2,1)S(1)}, bf16[3,16,512]{2,1,0:T(8,128)(2,1)S(1)}, u32[]{:S(2)}, u32[]{:S(2)}) %collective-permute-start.3) | collective-permute-done | bytes 49184 | tf_op jit(solution)/shard_map/ppermute | solution.py:263
  12.5 0.5 %collective-permute-done.4.second_ref.refs_2_ = bf16[3,16,512]{2,1,0:T(8,128)(2,1)S(1)} collective-permute-done((bf16[3,16,512]{2,1,0:T(8,128)(2,1)S(1)}, bf16[3,16,512]{2,1,0:T(8,128)(2,1)S(1)}, u32[]{:S(2)}, u32[]{:S(2)}) %collective-permute-start.4) | collective-permute-done | bytes 49184 | tf_op jit(solution)/shard_map/ppermute | solution.py:263
  13.0 0.3 %collective-permute-start.5 = (bf16[4,16,512]{2,1,0:T(8,128)(2,1)S(1)}, bf16[4,16,512]{2,1,0:T(8,128)(2,1)S(1)}, u32[]{:S(2)}, u32[]{:S(2)}) collective-permute-start(bf16[4,16,512]{2,1,0:T(8,128)(2,1)S(1)} %swap.1), channel_id=1, source_target_pairs={{1,0},{0,1},{3,2},{2,3},{5,4},{4,5},{7,6},{6,7},{9,8},{8,9},{11,10... | collective-permute-start | bytes 196616 | tf_op jit(solution)/shard_map/ppermute | solution.py:213
  13.4 0.9 %collective-permute-done.5.refs_3_ = bf16[4,16,512]{2,1,0:T(8,128)(2,1)S(1)} collective-permute-done((bf16[4,16,512]{2,1,0:T(8,128)(2,1)S(1)}, bf16[4,16,512]{2,1,0:T(8,128)(2,1)S(1)}, u32[]{:S(2)}, u32[]{:S(2)}) %collective-permute-start.5) | collective-permute-done | bytes 65568 | tf_op jit(solution)/shard_map/ppermute | solution.py:213
  14.3 1.1 %gram_and_scores.1 = (f32[1,256,512]{2,1,0:T(8,128)}, f32[4,16]{1,0:T(4,128)}) custom-call(bf16[3,16,512]{2,1,0:T(8,128)(2,1)S(1)} %pad_maximum_fusion.1.refs_0_, bf16[3,16,512]{2,1,0:T(8,128)(2,1)S(1)} %collective-permute-done.3.first_ref.refs_1_, bf16[3,16,512]{2,1,0:T(8,128)(2,1)S(1)} %collective-permute-done.4.second_ref.refs_2_, ...), custom_call_target="tpu_custom_call" | custom-call | tf_op jit(solution)/shard_map/gram_and_scores/pallas_call | solution.py:279
  (4 shorter events, 0.0 us)
Async XLA Ops:
  0.6 2.7 %copy-start = (bf16[1,256,2048]{2,1,0:T(8,128)(2,1)S(1)}, bf16[1,256,2048]{2,1,0:T(8,128)(2,1)}, u32[]{:S(2)}) copy-start(bf16[1,256,2048]{2,1,0:T(8,128)(2,1)} %param.6) | copy-start | bytes 3145732
  0.6 2.7 %copy-start.2 = (bf16[1,32,2048]{2,1,0:T(8,128)(2,1)S(1)}, bf16[1,32,2048]{2,1,0:T(8,128)(2,1)}, u32[]{:S(2)}) copy-start(bf16[1,32,2048]{2,1,0:T(8,128)(2,1)} %param.8) | copy-start | bytes 393220
  0.7 3.1 %copy-start.1 = (bf16[1,256,2048]{2,1,0:T(8,128)(2,1)S(1)}, bf16[1,256,2048]{2,1,0:T(8,128)(2,1)}, u32[]{:S(2)}) copy-start(bf16[1,256,2048]{2,1,0:T(8,128)(2,1)} %param.5) | copy-start | bytes 3145732
  0.7 4.8 %collective-permute-start.1 = (bf16[16,512]{1,0:T(8,128)(2,1)}, bf16[16,512]{1,0:T(8,128)(2,1)S(1)}, u32[]{:S(2)}, u32[]{:S(2)}) collective-permute-start(bf16[16,512]{1,0:T(8,128)(2,1)} %bitcast.19), channel_id=1, source_target_pairs={{0,5},{1,4},{2,1},{3,0},{4,13},{5,12},{6,9},{7,8},{8,7},{9,6},{10,... | collective-permute-start | bytes 49160 | tf_op jit(solution)/shard_map/ppermute | solution.py:222
  3.4 0.9 %copy-start.3 = (bf16[1,32,2048]{2,1,0:T(8,128)(2,1)S(1)}, bf16[1,32,2048]{2,1,0:T(8,128)(2,1)}, u32[]{:S(2)}) copy-start(bf16[1,32,2048]{2,1,0:T(8,128)(2,1)} %param.7) | copy-start | bytes 393220
  4.7 1.6 %collective-permute-start = (f32[64,256]{1,0:T(8,128)S(1)}, f32[64,256]{1,0:T(8,128)S(1)}, u32[]{:S(2)}, u32[]{:S(2)}) collective-permute-start(f32[64,256]{1,0:T(8,128)S(1)} %pad_maximum_fusion.refs_0_), channel_id=1, source_target_pairs={{1,0},{0,1},{3,2},{2,3},{5,4},{4,5},{7,6},{6,7},{9,8},{8,9},{11,10... | collective-permute-start | bytes 196616 | tf_op jit(solution)/shard_map/ppermute | solution.py:213
  5.4 1.4 %collective-permute-start.2 = (bf16[16,512]{1,0:T(8,128)(2,1)S(1)}, bf16[16,512]{1,0:T(8,128)(2,1)S(1)}, u32[]{:S(2)}, u32[]{:S(2)}) collective-permute-start(bf16[16,512]{1,0:T(8,128)(2,1)S(1)} %chunk.1), channel_id=1, source_target_pairs={{1,0},{0,1},{3,2},{2,3},{5,4},{4,5},{7,6},{6,7},{9,8},{8,9},{11,10... | collective-permute-start | bytes 49160 | tf_op jit(solution)/shard_map/ppermute | solution.py:213
  6.9 5.6 %collective-permute-start.3 = (bf16[3,16,512]{2,1,0:T(8,128)(2,1)S(1)}, bf16[3,16,512]{2,1,0:T(8,128)(2,1)S(1)}, u32[]{:S(2)}, u32[]{:S(2)}) collective-permute-start(bf16[3,16,512]{2,1,0:T(8,128)(2,1)S(1)} %pad_maximum_fusion.1.refs_0_), channel_id=1, source_target_pairs={{8,0},{13,1},{0,2},{15,3},{12,4},{1,5},{4,6},{3,7},{10,8},{5,9},{2... | collective-permute-start | bytes 147464 | tf_op jit(solution)/shard_map/ppermute | solution.py:263
  9.2 3.8 %collective-permute-start.4 = (bf16[3,16,512]{2,1,0:T(8,128)(2,1)S(1)}, bf16[3,16,512]{2,1,0:T(8,128)(2,1)S(1)}, u32[]{:S(2)}, u32[]{:S(2)}) collective-permute-start(bf16[3,16,512]{2,1,0:T(8,128)(2,1)S(1)} %pad_maximum_fusion.1.refs_0_), channel_id=1, source_target_pairs={{3,0},{4,1},{11,2},{6,3},{7,4},{8,5},{15,6},{10,7},{1,8},{12,9},{9... | collective-permute-start | bytes 147464 | tf_op jit(solution)/shard_map/ppermute | solution.py:263
  13.0 1.3 %collective-permute-start.5 = (bf16[4,16,512]{2,1,0:T(8,128)(2,1)S(1)}, bf16[4,16,512]{2,1,0:T(8,128)(2,1)S(1)}, u32[]{:S(2)}, u32[]{:S(2)}) collective-permute-start(bf16[4,16,512]{2,1,0:T(8,128)(2,1)S(1)} %swap.1), channel_id=1, source_target_pairs={{1,0},{0,1},{3,2},{2,3},{5,4},{4,5},{7,6},{6,7},{9,8},{8,9},{11,10... | collective-permute-start | bytes 196616 | tf_op jit(solution)/shard_map/ppermute | solution.py:213

commit v16 on v15

--- a/solution.py
+++ b/solution.py
@@ -14,6 +14,16 @@
 ANY = pl.BlockSpec(memory_space=pl.ANY)
 LAST = (((1,), (1,)), ((), ()))
 FIRST = (((0,), (0,)), ((), ()))
+DEAL = (
+    (5, 7, 1, 3),
+    (2, 5, 7, 1),
+    (0, 5, 7, 3),
+    (3, 6, 5, 0),
+    (2, 4, 6, 0),
+    (4, 6, 3, 1),
+    (0, 7, 4, 2),
+    (2, 6, 4, 1),
+)
 PARAMS = pltpu.CompilerParams(vmem_limit_bytes=16 * 1024 * 1024)
 
 
@@ -151,42 +161,57 @@
         for ex, lay, sub in devices
     ]
 
-    moves = [("lay", 1), ("ex", n_ex - 1), ("ex", n_ex // 2), ("ex", 1)]
-    moves += [("ex", k) for k in range(2, n_ex - 1) if k != n_ex // 2] + [("lay", k) for k in range(2, n_lay)]
+    compact = (n_ex, n_lay, n_sub) == (4, 2, 2)
+    moves = [("ex", k) for k in range(1, n_ex)] + [("lay", k) for k in range(1, n_lay)]
     rounds = -(-len(moves) // n_sub)
 
-    def sender_of(at, sub):
-        return (sub + (at == 1)) % n_sub
-
-    def turned(ex, lay):
-        return (ex // (n_ex // 2) + lay) % 2 == 0
-
     def source_of(at, ex, lay, sub):
-        sender = sender_of(at, sub)
-        if sub == 0 and at < 2 and turned(ex, lay):
-            at = 1 - at
-        axis, k = moves[min(at * n_sub + sub, len(moves) - 1)]
+        if compact:
+            row = DEAL[ex * n_lay + lay]
+            kind = [value // 2 for value in row].index(2 * at + sub)
+            sender = row[kind] % 2
+            (axis, k) = ("ex", kind) if kind else ("lay", 1)
+        else:
+            sender = sub
+            axis, k = moves[min(at * n_sub + sub, len(moves) - 1)]
         return flat((ex + k) % n_ex, lay, sender) if axis == "ex" else flat(ex, (lay + k) % n_lay, sender)
 
-    compact = (n_ex, n_lay, n_sub) == (4, 2, 2)
+    def dealt(kind, ex, lay):
+        values = [row[kind] for row in DEAL]
+        result = values[0]
+        for chip in range(1, len(values)):
+            result = jnp.where(ex * n_lay + lay == chip, values[chip], result)
+        return result // 4, result // 2 % 2, result % 2
+
+    def unit_kinds(ex, lay):
+        up, down = dealt(1, ex, lay), dealt(3, ex, lay)
+        odd = ex % 2 == 1
+        beside = [jnp.where(odd, b, a) for a, b in zip(up, down)]
+        beyond = [jnp.where(odd, a, b) for a, b in zip(up, down)]
+        return beside, dealt(2, ex, lay), beyond
 
     def lacked(ex, lay, sub):
-        return jnp.where(sub == 0, jnp.where(turned(ex, lay), 0, 1), 1 - (ex + ex // 2) % 2)
+        beside, across, beyond = unit_kinds(ex, lay)
+        later = jnp.where(across[1] == sub, across[0], beyond[0])
+        return jnp.where(ex // 2 == sub, later, beside[0])
 
     def compact_plan(ex, lay, sub):
-        across = lacked(ex, lay, 0)
-        beside = lacked(ex, lay, 1)
-
-        def grads_at(core, turn):
+        def grads_at(kind):
+            turn, core, _ = dealt(kind, ex, lay)
             return jnp.where(sub == core, 3 + 3 * turn, 9 + turn)
 
-        slots = [0, grads_at(0, across), grads_at(1, 0), grads_at(1, 1)]
-        layers = [0, grads_at(0, 1 - across)]
-        same = jnp.where(ex // 2 == sub, 1, jnp.where(sub == 0, 4 + 3 * across, 11))
-        other = jnp.where(sub == 0, 11, 4 + 3 * (1 - beside))
-        near = jnp.where(ex // 2 == sub, sub, across)
-        far = jnp.where(sub == 0, 1 - beside, beside)
-        units = [(same, (ex + 1 + lay) % 2, near, 0, None), (other, (ex + lay) % 2, far, 0, None)]
+        def unit_at(kind):
+            turn, core, _ = kind
+            return jnp.where(sub == core, 4 + 3 * turn, 11)
+
+        slots = [0, grads_at(1), grads_at(2), grads_at(3)]
+        layers = [0, grads_at(0)]
+        beside, across, beyond = unit_kinds(ex, lay)
+        mine = ex // 2 == sub
+        first, first_core = jnp.where(mine, 1, unit_at(across)), jnp.where(mine, sub, across[2])
+        second = jnp.where(mine, unit_at(beside), unit_at(beyond))
+        second_core = jnp.where(mine, beside[2], beyond[2])
+        units = [(first, (ex + 1 + lay) % 2, first_core, 0, None), (second, (ex + lay) % 2, second_core, 0, None)]
         return slots, layers, units
 
     def general_plan(ex, lay, sub):
@@ -194,12 +219,10 @@
         slots, layers, sources = [0], [0], [(ex, sub)]
         for at, (axis, k) in enumerate(moves):
             core, turn = at % n_sub, at // n_sub
-            if core == 0 and turn < 2:
-                turn = jnp.where(turned(ex, lay), 1 - turn, turn)
             block = (1 + (core - sub + n_sub) % n_sub * rounds + turn) * size
             if axis == "ex":
                 slots.append(block)
-                sources.append(((ex + k) % n_ex, sender_of(turn, core)))
+                sources.append(((ex + k) % n_ex, core))
             else:
                 layers.append(block)
         units = []

time: 15.5 us -> 15.6 us (level)
  the two profiles are of different devices: /device:TPU:0 before, /device:TPU:3 now
where the time goes in v16:
time: 15.6 us; the launch traced here: 15.5 us
  waiting for transfers between devices  7.6 us (49%)
  starting transfers between devices  2.99 us (19%)
  Pallas kernels  1.77 us (11%)
  local copies, waits for them, and re-layouts  1.55 us (10%)
  matrix products  0.82 us (5%)
  between operations  0.7 us (4%)
    ppermute x2, waiting for transfers between devices, body(): received.append(lax.ppermute(mine, AXES, pairs))  4.81 us
    ppermute x2, starting transfers between devices, body(): received.append(lax.ppermute(mine, AXES, pairs))  1.8 us
    unnamed x8, local copies, waits for them, and re-layouts  1.55 us
    ppermute x3, waiting for transfers between devices, rotate(): lax.ppermute(value, 'sub', [((i + k) % n_sub, i) for i in range(n_sub)])  1.55 us
    ppermute x1, waiting for transfers between devices, body(): chunk = lax.ppermute(queries[0], AXES, query_pairs)  1.25 us
    ppermute x3, starting transfers between devices, rotate(): lax.ppermute(value, 'sub', [((i + k) % n_sub, i) for i in range(n_sub)])  1.14 us
    pallas_call x1, Pallas kernels, body(): pl.pallas_call(functools.partial(final_kernel, compact_plan if compact el...  1.08 us
    pallas_call x1, Pallas kernels, body(): pl.pallas_call(functools.partial(grads_kernel, n_sub), out_shape=jax.Shap...  0.53 us
  transfers between devices with their start and end apart: 6, of which 5 were waited for; matrix products, arithmetic and copies ran while one was open for 5% of the time, Pallas kernels for 4%

profile of v16, /device:TPU:3, one launch (start us, length us, event | category | flops | bytes accessed | tf_op | source)
XLA Modules:
  0.0 15.5 jit_solution(17618439836269201344)
XLA Ops:
  0.6 0.0 copy-start
  0.6 0.0 copy-start.2
  0.7 0.0 copy-start.1
  0.7 0.1 collective-permute-start.1
  0.7 0.2 picks.1
  0.9 1.0 %copy-done = bf16[1,256,2048]{2,1,0:T(8,128)(2,1)S(1)} copy-done((bf16[1,256,2048]{2,1,0:T(8,128)(2,1)S(1)}, bf16[1,256,2048]{2,1,0:T(8,128)(2,1)}, u32[]{:S(2)}) %copy-start) | copy-done | bytes 1048600
  1.9 0.0 copy-done.2
  1.9 0.0 copy-start.3
  1.9 0.4 %fusion = f32[32,256]{1,0:T(8,128)S(1)} fusion(bf16[1,256,2048]{2,1,0:T(8,128)(2,1)S(1)} %copy-done, bf16[1,32,2048]{2,1,0:T(8,128)(2,1)S(1)} %copy-done.2), kind=kOutput, calls=%fused_computation | convolution fusion | flops 33554432 | bytes 1212416 | tf_op jit(solution)/shard_map/dot_general | solution.py:259
  2.3 0.0 copy-done.1
  2.3 0.5 %copy-done.3 = bf16[1,32,2048]{2,1,0:T(8,128)(2,1)S(1)} copy-done((bf16[1,32,2048]{2,1,0:T(8,128)(2,1)S(1)}, bf16[1,32,2048]{2,1,0:T(8,128)(2,1)}, u32[]{:S(2)}) %copy-start.3) | copy-done | bytes 131096
  2.8 0.4 %fusion.2 = f32[32,256]{1,0:T(8,128)S(1)} fusion(bf16[1,256,2048]{2,1,0:T(8,128)(2,1)S(1)} %copy-done.1, bf16[1,32,2048]{2,1,0:T(8,128)(2,1)S(1)} %copy-done.3), kind=kOutput, calls=%fused_computation.2 | convolution fusion | flops 33554432 | bytes 1212416 | tf_op jit(solution)/shard_map/dot_general | solution.py:258
  3.3 0.7 %collective-permute-start = (f32[64,256]{1,0:T(8,128)S(1)}, f32[64,256]{1,0:T(8,128)S(1)}, u32[]{:S(2)}, u32[]{:S(2)}) collective-permute-start(f32[64,256]{1,0:T(8,128)S(1)} %pad_maximum_fusion.refs_0_), channel_id=1, source_target_pairs={{1,0},{0,1},{3,2},{2,3},{5,4},{4,5},{7,6},{6,7},{9,8},{8,9},{11,10... | collective-permute-start | bytes 196616 | tf_op jit(solution)/shard_map/ppermute | solution.py:236
  4.0 1.2 %collective-permute-done.1.in_ref = bf16[16,512]{1,0:T(8,128)(2,1)S(1)} collective-permute-done((bf16[16,512]{1,0:T(8,128)(2,1)}, bf16[16,512]{1,0:T(8,128)(2,1)S(1)}, u32[]{:S(2)}, u32[]{:S(2)}) %collective-permute-start.1) | collective-permute-done | bytes 16416 | tf_op jit(solution)/shard_map/ppermute | solution.py:245
  5.3 0.4 %collective-permute-start.2 = (bf16[16,512]{1,0:T(8,128)(2,1)S(1)}, bf16[16,512]{1,0:T(8,128)(2,1)S(1)}, u32[]{:S(2)}, u32[]{:S(2)}) collective-permute-start(bf16[16,512]{1,0:T(8,128)(2,1)S(1)} %chunk.1), channel_id=1, source_target_pairs={{1,0},{0,1},{3,2},{2,3},{5,4},{4,5},{7,6},{6,7},{9,8},{8,9},{11,10... | collective-permute-start | bytes 49160 | tf_op jit(solution)/shard_map/ppermute | solution.py:236
  5.7 0.0 collective-permute-done.refs_1_
  5.7 0.5 %grads.1 = bf16[16,512]{1,0:T(8,128)(2,1)S(1)} custom-call(f32[64,256]{1,0:T(8,128)S(1)} %pad_maximum_fusion.refs_0_, f32[64,256]{1,0:T(8,128)S(1)} %collective-permute-done.refs_1_, bf16[256,128]{1,0:T(8,128)(2,1)S(1)} %get-tuple-element.10.refs_2_, bf16[256,1024]{1,0:T(8,128)(2,1)S(1)} %get-tuple-element.11.refs_3_), custom_call_target="tpu_custom_call" | custom-call | tf_op jit(solution)/shard_map/grads/pallas_call | solution.py:273
  6.2 0.3 %collective-permute-done.2 = bf16[16,512]{1,0:T(8,128)(2,1)S(1)} collective-permute-done((bf16[16,512]{1,0:T(8,128)(2,1)S(1)}, bf16[16,512]{1,0:T(8,128)(2,1)S(1)}, u32[]{:S(2)}, u32[]{:S(2)}) %collective-permute-start.2) | collective-permute-done | bytes 16416 | tf_op jit(solution)/shard_map/ppermute | solution.py:236
  6.5 1.5 %collective-permute-start.3 = (bf16[3,16,512]{2,1,0:T(8,128)(2,1)S(1)}, bf16[3,16,512]{2,1,0:T(8,128)(2,1)S(1)}, u32[]{:S(2)}, u32[]{:S(2)}) collective-permute-start(bf16[3,16,512]{2,1,0:T(8,128)(2,1)S(1)} %pad_maximum_fusion.1.refs_0_), channel_id=1, source_target_pairs={{9,0},{13,1},{15,2},{0,3},{6,4},{1,5},{2,6},{5,7},{4,8},{10,9},{7,... | collective-permute-start | bytes 147464 | tf_op jit(solution)/shard_map/ppermute | solution.py:286
  8.0 0.3 %collective-permute-start.4 = (bf16[3,16,512]{2,1,0:T(8,128)(2,1)S(1)}, bf16[3,16,512]{2,1,0:T(8,128)(2,1)S(1)}, u32[]{:S(2)}, u32[]{:S(2)}) collective-permute-start(bf16[3,16,512]{2,1,0:T(8,128)(2,1)S(1)} %pad_maximum_fusion.1.refs_0_), channel_id=1, source_target_pairs={{3,0},{5,1},{7,2},{11,3},{9,4},{13,5},{15,6},{10,7},{12,8},{0,9},{... | collective-permute-start | bytes 147464 | tf_op jit(solution)/shard_map/ppermute | solution.py:286
  8.3 1.8 %collective-permute-done.3.first_ref.refs_1_ = bf16[3,16,512]{2,1,0:T(8,128)(2,1)S(1)} collective-permute-done((bf16[3,16,512]{2,1,0:T(8,128)(2,1)S(1)}, bf16[3,16,512]{2,1,0:T(8,128)(2,1)S(1)}, u32[]{:S(2)}, u32[]{:S(2)}) %collective-permute-start.3) | collective-permute-done | bytes 49184 | tf_op jit(solution)/shard_map/ppermute | solution.py:286
  10.1 3.0 %collective-permute-done.4.second_ref.refs_2_ = bf16[3,16,512]{2,1,0:T(8,128)(2,1)S(1)} collective-permute-done((bf16[3,16,512]{2,1,0:T(8,128)(2,1)S(1)}, bf16[3,16,512]{2,1,0:T(8,128)(2,1)S(1)}, u32[]{:S(2)}, u32[]{:S(2)}) %collective-permute-start.4) | collective-permute-done | bytes 49184 | tf_op jit(solution)/shard_map/ppermute | solution.py:286
  13.1 0.0 collective-permute-start.5
  13.1 1.2 %collective-permute-done.5.refs_3_ = bf16[4,16,512]{2,1,0:T(8,128)(2,1)S(1)} collective-permute-done((bf16[4,16,512]{2,1,0:T(8,128)(2,1)S(1)}, bf16[4,16,512]{2,1,0:T(8,128)(2,1)S(1)}, u32[]{:S(2)}, u32[]{:S(2)}) %collective-permute-start.5) | collective-permute-done | bytes 65568 | tf_op jit(solution)/shard_map/ppermute | solution.py:236
  14.4 1.1 %gram_and_scores.1 = (f32[1,256,512]{2,1,0:T(8,128)}, f32[4,16]{1,0:T(4,128)}) custom-call(bf16[3,16,512]{2,1,0:T(8,128)(2,1)S(1)} %pad_maximum_fusion.1.refs_0_, bf16[3,16,512]{2,1,0:T(8,128)(2,1)S(1)} %collective-permute-done.3.first_ref.refs_1_, bf16[3,16,512]{2,1,0:T(8,128)(2,1)S(1)} %collective-permute-done.4.second_ref.refs_2_, ...), custom_call_target="tpu_custom_call" | custom-call | tf_op jit(solution)/shard_map/gram_and_scores/pallas_call | solution.py:302
  (4 shorter events, 0.0 us)
Async XLA Ops:
  0.6 1.2 %copy-start = (bf16[1,256,2048]{2,1,0:T(8,128)(2,1)S(1)}, bf16[1,256,2048]{2,1,0:T(8,128)(2,1)}, u32[]{:S(2)}) copy-start(bf16[1,256,2048]{2,1,0:T(8,128)(2,1)} %param.6) | copy-start | bytes 3145732
  0.6 1.2 %copy-start.2 = (bf16[1,32,2048]{2,1,0:T(8,128)(2,1)S(1)}, bf16[1,32,2048]{2,1,0:T(8,128)(2,1)}, u32[]{:S(2)}) copy-start(bf16[1,32,2048]{2,1,0:T(8,128)(2,1)} %param.8) | copy-start | bytes 393220
  0.7 1.6 %copy-start.1 = (bf16[1,256,2048]{2,1,0:T(8,128)(2,1)S(1)}, bf16[1,256,2048]{2,1,0:T(8,128)(2,1)}, u32[]{:S(2)}) copy-start(bf16[1,256,2048]{2,1,0:T(8,128)(2,1)} %param.5) | copy-start | bytes 3145732
  0.7 4.6 %collective-permute-start.1 = (bf16[16,512]{1,0:T(8,128)(2,1)}, bf16[16,512]{1,0:T(8,128)(2,1)S(1)}, u32[]{:S(2)}, u32[]{:S(2)}) collective-permute-start(bf16[16,512]{1,0:T(8,128)(2,1)} %bitcast.19), channel_id=1, source_target_pairs={{0,5},{1,4},{2,1},{3,0},{4,13},{5,12},{6,9},{7,8},{8,7},{9,6},{10,... | collective-permute-start | bytes 49160 | tf_op jit(solution)/shard_map/ppermute | solution.py:245
  1.9 1.0 %copy-start.3 = (bf16[1,32,2048]{2,1,0:T(8,128)(2,1)S(1)}, bf16[1,32,2048]{2,1,0:T(8,128)(2,1)}, u32[]{:S(2)}) copy-start(bf16[1,32,2048]{2,1,0:T(8,128)(2,1)} %param.7) | copy-start | bytes 393220
  3.3 2.4 %collective-permute-start = (f32[64,256]{1,0:T(8,128)S(1)}, f32[64,256]{1,0:T(8,128)S(1)}, u32[]{:S(2)}, u32[]{:S(2)}) collective-permute-start(f32[64,256]{1,0:T(8,128)S(1)} %pad_maximum_fusion.refs_0_), channel_id=1, source_target_pairs={{1,0},{0,1},{3,2},{2,3},{5,4},{4,5},{7,6},{6,7},{9,8},{8,9},{11,10... | collective-permute-start | bytes 196616 | tf_op jit(solution)/shard_map/ppermute | solution.py:236
  5.3 1.2 %collective-permute-start.2 = (bf16[16,512]{1,0:T(8,128)(2,1)S(1)}, bf16[16,512]{1,0:T(8,128)(2,1)S(1)}, u32[]{:S(2)}, u32[]{:S(2)}) collective-permute-start(bf16[16,512]{1,0:T(8,128)(2,1)S(1)} %chunk.1), channel_id=1, source_target_pairs={{1,0},{0,1},{3,2},{2,3},{5,4},{4,5},{7,6},{6,7},{9,8},{8,9},{11,10... | collective-permute-start | bytes 49160 | tf_op jit(solution)/shard_map/ppermute | solution.py:236
  6.5 3.6 %collective-permute-start.3 = (bf16[3,16,512]{2,1,0:T(8,128)(2,1)S(1)}, bf16[3,16,512]{2,1,0:T(8,128)(2,1)S(1)}, u32[]{:S(2)}, u32[]{:S(2)}) collective-permute-start(bf16[3,16,512]{2,1,0:T(8,128)(2,1)S(1)} %pad_maximum_fusion.1.refs_0_), channel_id=1, source_target_pairs={{9,0},{13,1},{15,2},{0,3},{6,4},{1,5},{2,6},{5,7},{4,8},{10,9},{7,... | collective-permute-start | bytes 147464 | tf_op jit(solution)/shard_map/ppermute | solution.py:286
  8.0 5.1 %collective-permute-start.4 = (bf16[3,16,512]{2,1,0:T(8,128)(2,1)S(1)}, bf16[3,16,512]{2,1,0:T(8,128)(2,1)S(1)}, u32[]{:S(2)}, u32[]{:S(2)}) collective-permute-start(bf16[3,16,512]{2,1,0:T(8,128)(2,1)S(1)} %pad_maximum_fusion.1.refs_0_), channel_id=1, source_target_pairs={{3,0},{5,1},{7,2},{11,3},{9,4},{13,5},{15,6},{10,7},{12,8},{0,9},{... | collective-permute-start | bytes 147464 | tf_op jit(solution)/shard_map/ppermute | solution.py:286
  13.1 1.3 %collective-permute-start.5 = (bf16[4,16,512]{2,1,0:T(8,128)(2,1)S(1)}, bf16[4,16,512]{2,1,0:T(8,128)(2,1)S(1)}, u32[]{:S(2)}, u32[]{:S(2)}) collective-permute-start(bf16[4,16,512]{2,1,0:T(8,128)(2,1)S(1)} %swap.1), channel_id=1, source_target_pairs={{1,0},{0,1},{3,2},{2,3},{5,4},{4,5},{7,6},{6,7},{9,8},{8,9},{11,10... | collective-permute-start | bytes 196616 | tf_op jit(solution)/shard_map/ppermute | solution.py:236

commit v17 on v16

--- a/solution.py
+++ b/solution.py
@@ -15,14 +15,14 @@
 LAST = (((1,), (1,)), ((), ()))
 FIRST = (((0,), (0,)), ((), ()))
 DEAL = (
-    (5, 7, 1, 3),
+    (5, 7, 0, 3),
     (2, 5, 7, 1),
-    (0, 5, 7, 3),
-    (3, 6, 5, 0),
-    (2, 4, 6, 0),
-    (4, 6, 3, 1),
+    (4, 6, 0, 3),
+    (1, 4, 7, 2),
     (0, 7, 4, 2),
-    (2, 6, 4, 1),
+    (5, 6, 3, 0),
+    (2, 5, 6, 1),
+    (4, 6, 1, 3),
 )
 PARAMS = pltpu.CompilerParams(vmem_limit_bytes=16 * 1024 * 1024)
 

time: 15.6 us -> 15.5 us (level)
  the two profiles are of different devices: /device:TPU:3 before, /device:TPU:0 now
where the time goes in v17:
time: 15.5 us; the launch traced here: 15.4 us
  starting transfers between devices  7.79 us (50%)
  waiting for transfers between devices  3.74 us (24%)
  Pallas kernels  1.77 us (11%)
  matrix products  0.82 us (5%)
  between operations  0.73 us (5%)
  local copies, waits for them, and re-layouts  0.5 us (3%)
    ppermute x2, starting transfers between devices, body(): received.append(lax.ppermute(mine, AXES, pairs))  3.61 us
    ppermute x1, starting transfers between devices, body(): chunk = lax.ppermute(queries[0], AXES, query_pairs)  2.52 us
    ppermute x2, waiting for transfers between devices, body(): received.append(lax.ppermute(mine, AXES, pairs))  2.03 us
    ppermute x3, waiting for transfers between devices, rotate(): lax.ppermute(value, 'sub', [((i + k) % n_sub, i) for i in range(n_sub)])  1.71 us
    ppermute x3, starting transfers between devices, rotate(): lax.ppermute(value, 'sub', [((i + k) % n_sub, i) for i in range(n_sub)])  1.66 us
    pallas_call x1, Pallas kernels, body(): pl.pallas_call(functools.partial(final_kernel, compact_plan if compact el...  1.08 us
    pallas_call x1, Pallas kernels, body(): pl.pallas_call(functools.partial(grads_kernel, n_sub), out_shape=jax.Shap...  0.53 us
    unnamed x8, local copies, waits for them, and re-layouts  0.5 us
  transfers between devices with their start and end apart: 6, of which 3 were waited for; matrix products, arithmetic and copies ran while one was open for 5% of the time, Pallas kernels for 4%

profile of v17, /device:TPU:0, one launch (start us, length us, event | category | flops | bytes accessed | tf_op | source)
XLA Modules:
  0.0 15.4 jit_solution(12920725264638170231)
XLA Ops:
  0.6 0.0 copy-start
  0.6 0.0 copy-start.2
  0.7 0.0 copy-start.1
  0.7 2.5 %collective-permute-start.1 = (bf16[16,512]{1,0:T(8,128)(2,1)}, bf16[16,512]{1,0:T(8,128)(2,1)S(1)}, u32[]{:S(2)}, u32[]{:S(2)}) collective-permute-start(bf16[16,512]{1,0:T(8,128)(2,1)} %bitcast.19), channel_id=1, source_target_pairs={{0,5},{1,4},{2,1},{3,0},{4,13},{5,12},{6,9},{7,8},{8,7},{9,6},{10,... | collective-permute-start | bytes 49160 | tf_op jit(solution)/shard_map/ppermute | solution.py:245
  3.2 0.1 picks.1
  3.3 0.0 copy-done
  3.3 0.0 copy-done.2
  3.4 0.0 copy-start.3
  3.4 0.4 %fusion = f32[32,256]{1,0:T(8,128)S(1)} fusion(bf16[1,256,2048]{2,1,0:T(8,128)(2,1)S(1)} %copy-done, bf16[1,32,2048]{2,1,0:T(8,128)(2,1)S(1)} %copy-done.2), kind=kOutput, calls=%fused_computation | convolution fusion | flops 33554432 | bytes 1212416 | tf_op jit(solution)/shard_map/dot_general | solution.py:259
  3.8 0.0 copy-done.1
  3.8 0.5 %copy-done.3 = bf16[1,32,2048]{2,1,0:T(8,128)(2,1)S(1)} copy-done((bf16[1,32,2048]{2,1,0:T(8,128)(2,1)S(1)}, bf16[1,32,2048]{2,1,0:T(8,128)(2,1)}, u32[]{:S(2)}) %copy-start.3) | copy-done | bytes 131096
  4.3 0.4 %fusion.2 = f32[32,256]{1,0:T(8,128)S(1)} fusion(bf16[1,256,2048]{2,1,0:T(8,128)(2,1)S(1)} %copy-done.1, bf16[1,32,2048]{2,1,0:T(8,128)(2,1)S(1)} %copy-done.3), kind=kOutput, calls=%fused_computation.2 | convolution fusion | flops 33554432 | bytes 1212416 | tf_op jit(solution)/shard_map/dot_general | solution.py:258
  4.7 0.7 %collective-permute-start = (f32[64,256]{1,0:T(8,128)S(1)}, f32[64,256]{1,0:T(8,128)S(1)}, u32[]{:S(2)}, u32[]{:S(2)}) collective-permute-start(f32[64,256]{1,0:T(8,128)S(1)} %pad_maximum_fusion.refs_0_), channel_id=1, source_target_pairs={{1,0},{0,1},{3,2},{2,3},{5,4},{4,5},{7,6},{6,7},{9,8},{8,9},{11,10... | collective-permute-start | bytes 196616 | tf_op jit(solution)/shard_map/ppermute | solution.py:236
  5.4 0.0 collective-permute-done.1.in_ref
  5.4 0.1 collective-permute-start.2
  5.5 0.8 %collective-permute-done.refs_1_ = f32[64,256]{1,0:T(8,128)S(1)} collective-permute-done((f32[64,256]{1,0:T(8,128)S(1)}, f32[64,256]{1,0:T(8,128)S(1)}, u32[]{:S(2)}, u32[]{:S(2)}) %collective-permute-start) | collective-permute-done | bytes 65568 | tf_op jit(solution)/shard_map/ppermute | solution.py:236
  6.3 0.5 %grads.1 = bf16[16,512]{1,0:T(8,128)(2,1)S(1)} custom-call(f32[64,256]{1,0:T(8,128)S(1)} %pad_maximum_fusion.refs_0_, f32[64,256]{1,0:T(8,128)S(1)} %collective-permute-done.refs_1_, bf16[256,128]{1,0:T(8,128)(2,1)S(1)} %get-tuple-element.10.refs_2_, bf16[256,1024]{1,0:T(8,128)(2,1)S(1)} %get-tuple-element.11.refs_3_), custom_call_target="tpu_custom_call" | custom-call | tf_op jit(solution)/shard_map/grads/pallas_call | solution.py:273
  6.9 0.0 collective-permute-done.2
  6.9 2.0 %collective-permute-start.3 = (bf16[3,16,512]{2,1,0:T(8,128)(2,1)S(1)}, bf16[3,16,512]{2,1,0:T(8,128)(2,1)S(1)}, u32[]{:S(2)}, u32[]{:S(2)}) collective-permute-start(bf16[3,16,512]{2,1,0:T(8,128)(2,1)S(1)} %pad_maximum_fusion.1.refs_0_), channel_id=1, source_target_pairs={{8,0},{13,1},{15,2},{0,3},{12,4},{1,5},{5,6},{2,7},{10,8},{4,9},{6... | collective-permute-start | bytes 147464 | tf_op jit(solution)/shard_map/ppermute | solution.py:286
  9.0 1.6 %collective-permute-start.4 = (bf16[3,16,512]{2,1,0:T(8,128)(2,1)S(1)}, bf16[3,16,512]{2,1,0:T(8,128)(2,1)S(1)}, u32[]{:S(2)}, u32[]{:S(2)}) collective-permute-start(bf16[3,16,512]{2,1,0:T(8,128)(2,1)S(1)} %pad_maximum_fusion.1.refs_0_), channel_id=1, source_target_pairs={{3,0},{5,1},{7,2},{11,3},{6,4},{8,5},{10,6},{15,7},{0,8},{13,9},{9... | collective-permute-start | bytes 147464 | tf_op jit(solution)/shard_map/ppermute | solution.py:286
  10.5 2.0 %collective-permute-done.3.first_ref.refs_1_ = bf16[3,16,512]{2,1,0:T(8,128)(2,1)S(1)} collective-permute-done((bf16[3,16,512]{2,1,0:T(8,128)(2,1)S(1)}, bf16[3,16,512]{2,1,0:T(8,128)(2,1)S(1)}, u32[]{:S(2)}, u32[]{:S(2)}) %collective-permute-start.3) | collective-permute-done | bytes 49184 | tf_op jit(solution)/shard_map/ppermute | solution.py:286
  12.6 0.0 collective-permute-done.4.second_ref.refs_2_
  12.6 0.8 %collective-permute-start.5 = (bf16[4,16,512]{2,1,0:T(8,128)(2,1)S(1)}, bf16[4,16,512]{2,1,0:T(8,128)(2,1)S(1)}, u32[]{:S(2)}, u32[]{:S(2)}) collective-permute-start(bf16[4,16,512]{2,1,0:T(8,128)(2,1)S(1)} %swap.1), channel_id=1, source_target_pairs={{1,0},{0,1},{3,2},{2,3},{5,4},{4,5},{7,6},{6,7},{9,8},{8,9},{11,10... | collective-permute-start | bytes 196616 | tf_op jit(solution)/shard_map/ppermute | solution.py:236
  13.4 0.9 %collective-permute-done.5.refs_3_ = bf16[4,16,512]{2,1,0:T(8,128)(2,1)S(1)} collective-permute-done((bf16[4,16,512]{2,1,0:T(8,128)(2,1)S(1)}, bf16[4,16,512]{2,1,0:T(8,128)(2,1)S(1)}, u32[]{:S(2)}, u32[]{:S(2)}) %collective-permute-start.5) | collective-permute-done | bytes 65568 | tf_op jit(solution)/shard_map/ppermute | solution.py:236
  14.3 1.1 %gram_and_scores.1 = (f32[1,256,512]{2,1,0:T(8,128)}, f32[4,16]{1,0:T(4,128)}) custom-call(bf16[3,16,512]{2,1,0:T(8,128)(2,1)S(1)} %pad_maximum_fusion.1.refs_0_, bf16[3,16,512]{2,1,0:T(8,128)(2,1)S(1)} %collective-permute-done.3.first_ref.refs_1_, bf16[3,16,512]{2,1,0:T(8,128)(2,1)S(1)} %collective-permute-done.4.second_ref.refs_2_, ...), custom_call_target="tpu_custom_call" | custom-call | tf_op jit(solution)/shard_map/gram_and_scores/pallas_call | solution.py:302
  (4 shorter events, 0.0 us)
Async XLA Ops:
  0.6 2.7 %copy-start = (bf16[1,256,2048]{2,1,0:T(8,128)(2,1)S(1)}, bf16[1,256,2048]{2,1,0:T(8,128)(2,1)}, u32[]{:S(2)}) copy-start(bf16[1,256,2048]{2,1,0:T(8,128)(2,1)} %param.6) | copy-start | bytes 3145732
  0.6 2.7 %copy-start.2 = (bf16[1,32,2048]{2,1,0:T(8,128)(2,1)S(1)}, bf16[1,32,2048]{2,1,0:T(8,128)(2,1)}, u32[]{:S(2)}) copy-start(bf16[1,32,2048]{2,1,0:T(8,128)(2,1)} %param.8) | copy-start | bytes 393220
  0.7 3.1 %copy-start.1 = (bf16[1,256,2048]{2,1,0:T(8,128)(2,1)S(1)}, bf16[1,256,2048]{2,1,0:T(8,128)(2,1)}, u32[]{:S(2)}) copy-start(bf16[1,256,2048]{2,1,0:T(8,128)(2,1)} %param.5) | copy-start | bytes 3145732
  0.7 4.8 %collective-permute-start.1 = (bf16[16,512]{1,0:T(8,128)(2,1)}, bf16[16,512]{1,0:T(8,128)(2,1)S(1)}, u32[]{:S(2)}, u32[]{:S(2)}) collective-permute-start(bf16[16,512]{1,0:T(8,128)(2,1)} %bitcast.19), channel_id=1, source_target_pairs={{0,5},{1,4},{2,1},{3,0},{4,13},{5,12},{6,9},{7,8},{8,7},{9,6},{10,... | collective-permute-start | bytes 49160 | tf_op jit(solution)/shard_map/ppermute | solution.py:245
  3.4 0.9 %copy-start.3 = (bf16[1,32,2048]{2,1,0:T(8,128)(2,1)S(1)}, bf16[1,32,2048]{2,1,0:T(8,128)(2,1)}, u32[]{:S(2)}) copy-start(bf16[1,32,2048]{2,1,0:T(8,128)(2,1)} %param.7) | copy-start | bytes 393220
  4.7 1.6 %collective-permute-start = (f32[64,256]{1,0:T(8,128)S(1)}, f32[64,256]{1,0:T(8,128)S(1)}, u32[]{:S(2)}, u32[]{:S(2)}) collective-permute-start(f32[64,256]{1,0:T(8,128)S(1)} %pad_maximum_fusion.refs_0_), channel_id=1, source_target_pairs={{1,0},{0,1},{3,2},{2,3},{5,4},{4,5},{7,6},{6,7},{9,8},{8,9},{11,10... | collective-permute-start | bytes 196616 | tf_op jit(solution)/shard_map/ppermute | solution.py:236
  5.4 1.4 %collective-permute-start.2 = (bf16[16,512]{1,0:T(8,128)(2,1)S(1)}, bf16[16,512]{1,0:T(8,128)(2,1)S(1)}, u32[]{:S(2)}, u32[]{:S(2)}) collective-permute-start(bf16[16,512]{1,0:T(8,128)(2,1)S(1)} %chunk.1), channel_id=1, source_target_pairs={{1,0},{0,1},{3,2},{2,3},{5,4},{4,5},{7,6},{6,7},{9,8},{8,9},{11,10... | collective-permute-start | bytes 49160 | tf_op jit(solution)/shard_map/ppermute | solution.py:236
  6.9 5.6 %collective-permute-start.3 = (bf16[3,16,512]{2,1,0:T(8,128)(2,1)S(1)}, bf16[3,16,512]{2,1,0:T(8,128)(2,1)S(1)}, u32[]{:S(2)}, u32[]{:S(2)}) collective-permute-start(bf16[3,16,512]{2,1,0:T(8,128)(2,1)S(1)} %pad_maximum_fusion.1.refs_0_), channel_id=1, source_target_pairs={{8,0},{13,1},{15,2},{0,3},{12,4},{1,5},{5,6},{2,7},{10,8},{4,9},{6... | collective-permute-start | bytes 147464 | tf_op jit(solution)/shard_map/ppermute | solution.py:286
  9.0 3.6 %collective-permute-start.4 = (bf16[3,16,512]{2,1,0:T(8,128)(2,1)S(1)}, bf16[3,16,512]{2,1,0:T(8,128)(2,1)S(1)}, u32[]{:S(2)}, u32[]{:S(2)}) collective-permute-start(bf16[3,16,512]{2,1,0:T(8,128)(2,1)S(1)} %pad_maximum_fusion.1.refs_0_), channel_id=1, source_target_pairs={{3,0},{5,1},{7,2},{11,3},{6,4},{8,5},{10,6},{15,7},{0,8},{13,9},{9... | collective-permute-start | bytes 147464 | tf_op jit(solution)/shard_map/ppermute | solution.py:286
  12.6 1.7 %collective-permute-start.5 = (bf16[4,16,512]{2,1,0:T(8,128)(2,1)S(1)}, bf16[4,16,512]{2,1,0:T(8,128)(2,1)S(1)}, u32[]{:S(2)}, u32[]{:S(2)}) collective-permute-start(bf16[4,16,512]{2,1,0:T(8,128)(2,1)S(1)} %swap.1), channel_id=1, source_target_pairs={{1,0},{0,1},{3,2},{2,3},{5,4},{4,5},{7,6},{6,7},{9,8},{8,9},{11,10... | collective-permute-start | bytes 196616 | tf_op jit(solution)/shard_map/ppermute | solution.py:236

commit v18 on v15

--- a/solution.py
+++ b/solution.py
@@ -47,10 +47,12 @@
     lanes, width = pick_x_ref.shape[1], pick_g_ref.shape[1]
     tiled_x = jnp.dot(pieces, pick_x_ref[...], preferred_element_type=F32)
     tiles = []
-    for j in range(width // lanes):
-        pick_g = pick_g_ref[:, j * lanes : (j + 1) * lanes]
+    wide = 2 * lanes if width % (2 * lanes) == 0 else lanes
+    tiled_x = jnp.concatenate([tiled_x] * (wide // lanes), axis=1)
+    for j in range(width // wide):
+        pick_g = pick_g_ref[:, j * wide : (j + 1) * wide]
         product = jnp.dot(pieces, pick_g, preferred_element_type=F32) * tiled_x
-        tiles.append(product.reshape(own, LEN, lanes).sum(axis=1))
+        tiles.append(product.reshape(own, LEN, wide).sum(axis=1))
     grads = jnp.concatenate(tiles, axis=1)
     high = grads.astype(BF16).astype(F32)
     low = grads - high

time: 15.5 us -> 15.5 us (level)
  no operation moved by 1% of the time
where the time goes in v18:
time: 15.5 us; the launch traced here: 15.3 us
  starting transfers between devices  8.19 us (53%)
  waiting for transfers between devices  3.46 us (22%)
  Pallas kernels  1.61 us (10%)
  matrix products  0.82 us (5%)
  between operations  0.73 us (5%)
  local copies, waits for them, and re-layouts  0.5 us (3%)
    ppermute x2, starting transfers between devices, body(): received.append(lax.ppermute(mine, AXES, pairs))  4.49 us
    ppermute x1, starting transfers between devices, body(): chunk = lax.ppermute(queries[0], AXES, query_pairs)  2.52 us
    ppermute x2, waiting for transfers between devices, body(): received.append(lax.ppermute(mine, AXES, pairs))  1.75 us
    ppermute x3, waiting for transfers between devices, rotate(): lax.ppermute(value, 'sub', [((i + k) % n_sub, i) for i in range(n_sub)])  1.71 us
    ppermute x3, starting transfers between devices, rotate(): lax.ppermute(value, 'sub', [((i + k) % n_sub, i) for i in range(n_sub)])  1.18 us
    pallas_call x1, Pallas kernels, body(): pl.pallas_call(functools.partial(final_kernel, compact_plan if compact el...  1.05 us
    unnamed x8, local copies, waits for them, and re-layouts  0.5 us
    dot_general x1, matrix products, body(): lax.dot_general(basis_out[0], output_grads[0], LAST, preferred_element_ty...  0.41 us
  transfers between devices with their start and end apart: 6, of which 4 were waited for; matrix products, arithmetic and copies ran while one was open for 5% of the time, Pallas kernels for 4%

profile of v18, /device:TPU:0, one launch (start us, length us, event | category | flops | bytes accessed | tf_op | source)
XLA Modules:
  0.0 15.3 jit_solution(13920277541339939696)
XLA Ops:
  0.6 0.0 copy-start
  0.6 0.0 copy-start.2
  0.7 0.0 copy-start.1
  0.7 2.5 %collective-permute-start.1 = (bf16[16,512]{1,0:T(8,128)(2,1)}, bf16[16,512]{1,0:T(8,128)(2,1)S(1)}, u32[]{:S(2)}, u32[]{:S(2)}) collective-permute-start(bf16[16,512]{1,0:T(8,128)(2,1)} %bitcast.19), channel_id=1, source_target_pairs={{0,5},{1,4},{2,1},{3,0},{4,13},{5,12},{6,9},{7,8},{8,7},{9,6},{10,... | collective-permute-start | bytes 49160 | tf_op jit(solution)/shard_map/ppermute | solution.py:224
  3.2 0.1 picks.1
  3.3 0.0 copy-done
  3.3 0.0 copy-done.2
  3.4 0.0 copy-start.3
  3.4 0.4 %fusion = f32[32,256]{1,0:T(8,128)S(1)} fusion(bf16[1,256,2048]{2,1,0:T(8,128)(2,1)S(1)} %copy-done, bf16[1,32,2048]{2,1,0:T(8,128)(2,1)S(1)} %copy-done.2), kind=kOutput, calls=%fused_computation | convolution fusion | flops 33554432 | bytes 1212416 | tf_op jit(solution)/shard_map/dot_general | solution.py:238
  3.8 0.0 copy-done.1
  3.8 0.5 %copy-done.3 = bf16[1,32,2048]{2,1,0:T(8,128)(2,1)S(1)} copy-done((bf16[1,32,2048]{2,1,0:T(8,128)(2,1)S(1)}, bf16[1,32,2048]{2,1,0:T(8,128)(2,1)}, u32[]{:S(2)}) %copy-start.3) | copy-done | bytes 131096
  4.3 0.4 %fusion.2 = f32[32,256]{1,0:T(8,128)S(1)} fusion(bf16[1,256,2048]{2,1,0:T(8,128)(2,1)S(1)} %copy-done.1, bf16[1,32,2048]{2,1,0:T(8,128)(2,1)S(1)} %copy-done.3), kind=kOutput, calls=%fused_computation.2 | convolution fusion | flops 33554432 | bytes 1212416 | tf_op jit(solution)/shard_map/dot_general | solution.py:237
  4.7 0.7 %collective-permute-start = (f32[64,256]{1,0:T(8,128)S(1)}, f32[64,256]{1,0:T(8,128)S(1)}, u32[]{:S(2)}, u32[]{:S(2)}) collective-permute-start(f32[64,256]{1,0:T(8,128)S(1)} %pad_maximum_fusion.refs_0_), channel_id=1, source_target_pairs={{1,0},{0,1},{3,2},{2,3},{5,4},{4,5},{7,6},{6,7},{9,8},{8,9},{11,10... | collective-permute-start | bytes 196616 | tf_op jit(solution)/shard_map/ppermute | solution.py:215
  5.4 0.0 collective-permute-done.1.in_ref
  5.4 0.1 collective-permute-start.2
  5.5 0.8 %collective-permute-done.refs_1_ = f32[64,256]{1,0:T(8,128)S(1)} collective-permute-done((f32[64,256]{1,0:T(8,128)S(1)}, f32[64,256]{1,0:T(8,128)S(1)}, u32[]{:S(2)}, u32[]{:S(2)}) %collective-permute-start) | collective-permute-done | bytes 65568 | tf_op jit(solution)/shard_map/ppermute | solution.py:215
  6.3 0.4 %grads.1 = bf16[16,512]{1,0:T(8,128)(2,1)S(1)} custom-call(f32[64,256]{1,0:T(8,128)S(1)} %pad_maximum_fusion.refs_0_, f32[64,256]{1,0:T(8,128)S(1)} %collective-permute-done.refs_1_, bf16[256,128]{1,0:T(8,128)(2,1)S(1)} %get-tuple-element.10.refs_2_, bf16[256,1024]{1,0:T(8,128)(2,1)S(1)} %get-tuple-element.11.refs_3_), custom_call_target="tpu_custom_call" | custom-call | tf_op jit(solution)/shard_map/grads/pallas_call | solution.py:252
  6.8 0.0 collective-permute-done.2
  6.8 2.4 %collective-permute-start.3 = (bf16[3,16,512]{2,1,0:T(8,128)(2,1)S(1)}, bf16[3,16,512]{2,1,0:T(8,128)(2,1)S(1)}, u32[]{:S(2)}, u32[]{:S(2)}) collective-permute-start(bf16[3,16,512]{2,1,0:T(8,128)(2,1)S(1)} %pad_maximum_fusion.1.refs_0_), channel_id=1, source_target_pairs={{8,0},{13,1},{0,2},{15,3},{12,4},{1,5},{4,6},{3,7},{10,8},{5,9},{2... | collective-permute-start | bytes 147464 | tf_op jit(solution)/shard_map/ppermute | solution.py:265
  9.2 2.1 %collective-permute-start.4 = (bf16[3,16,512]{2,1,0:T(8,128)(2,1)S(1)}, bf16[3,16,512]{2,1,0:T(8,128)(2,1)S(1)}, u32[]{:S(2)}, u32[]{:S(2)}) collective-permute-start(bf16[3,16,512]{2,1,0:T(8,128)(2,1)S(1)} %pad_maximum_fusion.1.refs_0_), channel_id=1, source_target_pairs={{3,0},{4,1},{11,2},{6,3},{7,4},{8,5},{15,6},{10,7},{1,8},{12,9},{9... | collective-permute-start | bytes 147464 | tf_op jit(solution)/shard_map/ppermute | solution.py:265
  11.3 1.2 %collective-permute-done.3.first_ref.refs_1_ = bf16[3,16,512]{2,1,0:T(8,128)(2,1)S(1)} collective-permute-done((bf16[3,16,512]{2,1,0:T(8,128)(2,1)S(1)}, bf16[3,16,512]{2,1,0:T(8,128)(2,1)S(1)}, u32[]{:S(2)}, u32[]{:S(2)}) %collective-permute-start.3) | collective-permute-done | bytes 49184 | tf_op jit(solution)/shard_map/ppermute | solution.py:265
  12.5 0.5 %collective-permute-done.4.second_ref.refs_2_ = bf16[3,16,512]{2,1,0:T(8,128)(2,1)S(1)} collective-permute-done((bf16[3,16,512]{2,1,0:T(8,128)(2,1)S(1)}, bf16[3,16,512]{2,1,0:T(8,128)(2,1)S(1)}, u32[]{:S(2)}, u32[]{:S(2)}) %collective-permute-start.4) | collective-permute-done | bytes 49184 | tf_op jit(solution)/shard_map/ppermute | solution.py:265
  13.0 0.3 %collective-permute-start.5 = (bf16[4,16,512]{2,1,0:T(8,128)(2,1)S(1)}, bf16[4,16,512]{2,1,0:T(8,128)(2,1)S(1)}, u32[]{:S(2)}, u32[]{:S(2)}) collective-permute-start(bf16[4,16,512]{2,1,0:T(8,128)(2,1)S(1)} %swap.1), channel_id=1, source_target_pairs={{1,0},{0,1},{3,2},{2,3},{5,4},{4,5},{7,6},{6,7},{9,8},{8,9},{11,10... | collective-permute-start | bytes 196616 | tf_op jit(solution)/shard_map/ppermute | solution.py:215
  13.4 0.9 %collective-permute-done.5.refs_3_ = bf16[4,16,512]{2,1,0:T(8,128)(2,1)S(1)} collective-permute-done((bf16[4,16,512]{2,1,0:T(8,128)(2,1)S(1)}, bf16[4,16,512]{2,1,0:T(8,128)(2,1)S(1)}, u32[]{:S(2)}, u32[]{:S(2)}) %collective-permute-start.5) | collective-permute-done | bytes 65568 | tf_op jit(solution)/shard_map/ppermute | solution.py:215
  14.3 1.1 %gram_and_scores.1 = (f32[1,256,512]{2,1,0:T(8,128)}, f32[4,16]{1,0:T(4,128)}) custom-call(bf16[3,16,512]{2,1,0:T(8,128)(2,1)S(1)} %pad_maximum_fusion.1.refs_0_, bf16[3,16,512]{2,1,0:T(8,128)(2,1)S(1)} %collective-permute-done.3.first_ref.refs_1_, bf16[3,16,512]{2,1,0:T(8,128)(2,1)S(1)} %collective-permute-done.4.second_ref.refs_2_, ...), custom_call_target="tpu_custom_call" | custom-call | tf_op jit(solution)/shard_map/gram_and_scores/pallas_call | solution.py:281
  (4 shorter events, 0.0 us)
Async XLA Ops:
  0.6 2.7 %copy-start = (bf16[1,256,2048]{2,1,0:T(8,128)(2,1)S(1)}, bf16[1,256,2048]{2,1,0:T(8,128)(2,1)}, u32[]{:S(2)}) copy-start(bf16[1,256,2048]{2,1,0:T(8,128)(2,1)} %param.6) | copy-start | bytes 3145732
  0.6 2.7 %copy-start.2 = (bf16[1,32,2048]{2,1,0:T(8,128)(2,1)S(1)}, bf16[1,32,2048]{2,1,0:T(8,128)(2,1)}, u32[]{:S(2)}) copy-start(bf16[1,32,2048]{2,1,0:T(8,128)(2,1)} %param.8) | copy-start | bytes 393220
  0.7 3.1 %copy-start.1 = (bf16[1,256,2048]{2,1,0:T(8,128)(2,1)S(1)}, bf16[1,256,2048]{2,1,0:T(8,128)(2,1)}, u32[]{:S(2)}) copy-start(bf16[1,256,2048]{2,1,0:T(8,128)(2,1)} %param.5) | copy-start | bytes 3145732
  0.7 4.8 %collective-permute-start.1 = (bf16[16,512]{1,0:T(8,128)(2,1)}, bf16[16,512]{1,0:T(8,128)(2,1)S(1)}, u32[]{:S(2)}, u32[]{:S(2)}) collective-permute-start(bf16[16,512]{1,0:T(8,128)(2,1)} %bitcast.19), channel_id=1, source_target_pairs={{0,5},{1,4},{2,1},{3,0},{4,13},{5,12},{6,9},{7,8},{8,7},{9,6},{10,... | collective-permute-start | bytes 49160 | tf_op jit(solution)/shard_map/ppermute | solution.py:224
  3.4 0.9 %copy-start.3 = (bf16[1,32,2048]{2,1,0:T(8,128)(2,1)S(1)}, bf16[1,32,2048]{2,1,0:T(8,128)(2,1)}, u32[]{:S(2)}) copy-start(bf16[1,32,2048]{2,1,0:T(8,128)(2,1)} %param.7) | copy-start | bytes 393220
  4.7 1.6 %collective-permute-start = (f32[64,256]{1,0:T(8,128)S(1)}, f32[64,256]{1,0:T(8,128)S(1)}, u32[]{:S(2)}, u32[]{:S(2)}) collective-permute-start(f32[64,256]{1,0:T(8,128)S(1)} %pad_maximum_fusion.refs_0_), channel_id=1, source_target_pairs={{1,0},{0,1},{3,2},{2,3},{5,4},{4,5},{7,6},{6,7},{9,8},{8,9},{11,10... | collective-permute-start | bytes 196616 | tf_op jit(solution)/shard_map/ppermute | solution.py:215
  5.4 1.3 %collective-permute-start.2 = (bf16[16,512]{1,0:T(8,128)(2,1)S(1)}, bf16[16,512]{1,0:T(8,128)(2,1)S(1)}, u32[]{:S(2)}, u32[]{:S(2)}) collective-permute-start(bf16[16,512]{1,0:T(8,128)(2,1)S(1)} %chunk.1), channel_id=1, source_target_pairs={{1,0},{0,1},{3,2},{2,3},{5,4},{4,5},{7,6},{6,7},{9,8},{8,9},{11,10... | collective-permute-start | bytes 49160 | tf_op jit(solution)/shard_map/ppermute | solution.py:215
  6.8 5.7 %collective-permute-start.3 = (bf16[3,16,512]{2,1,0:T(8,128)(2,1)S(1)}, bf16[3,16,512]{2,1,0:T(8,128)(2,1)S(1)}, u32[]{:S(2)}, u32[]{:S(2)}) collective-permute-start(bf16[3,16,512]{2,1,0:T(8,128)(2,1)S(1)} %pad_maximum_fusion.1.refs_0_), channel_id=1, source_target_pairs={{8,0},{13,1},{0,2},{15,3},{12,4},{1,5},{4,6},{3,7},{10,8},{5,9},{2... | collective-permute-start | bytes 147464 | tf_op jit(solution)/shard_map/ppermute | solution.py:265
  9.2 3.8 %collective-permute-start.4 = (bf16[3,16,512]{2,1,0:T(8,128)(2,1)S(1)}, bf16[3,16,512]{2,1,0:T(8,128)(2,1)S(1)}, u32[]{:S(2)}, u32[]{:S(2)}) collective-permute-start(bf16[3,16,512]{2,1,0:T(8,128)(2,1)S(1)} %pad_maximum_fusion.1.refs_0_), channel_id=1, source_target_pairs={{3,0},{4,1},{11,2},{6,3},{7,4},{8,5},{15,6},{10,7},{1,8},{12,9},{9... | collective-permute-start | bytes 147464 | tf_op jit(solution)/shard_map/ppermute | solution.py:265
  13.0 1.3 %collective-permute-start.5 = (bf16[4,16,512]{2,1,0:T(8,128)(2,1)S(1)}, bf16[4,16,512]{2,1,0:T(8,128)(2,1)S(1)}, u32[]{:S(2)}, u32[]{:S(2)}) collective-permute-start(bf16[4,16,512]{2,1,0:T(8,128)(2,1)S(1)} %swap.1), channel_id=1, source_target_pairs={{1,0},{0,1},{3,2},{2,3},{5,4},{4,5},{7,6},{6,7},{9,8},{8,9},{11,10... | collective-permute-start | bytes 196616 | tf_op jit(solution)/shard_map/ppermute | solution.py:215

commit v19 on v17

--- a/solution.py
+++ b/solution.py
@@ -15,13 +15,13 @@
 LAST = (((1,), (1,)), ((), ()))
 FIRST = (((0,), (0,)), ((), ()))
 DEAL = (
-    (5, 7, 0, 3),
-    (2, 5, 7, 1),
+    (5, 7, 1, 3),
+    (0, 5, 7, 3),
     (4, 6, 0, 3),
-    (1, 4, 7, 2),
-    (0, 7, 4, 2),
+    (2, 4, 7, 0),
+    (2, 5, 6, 1),
     (5, 6, 3, 0),
-    (2, 5, 6, 1),
+    (0, 5, 6, 2),
     (4, 6, 1, 3),
 )
 PARAMS = pltpu.CompilerParams(vmem_limit_bytes=16 * 1024 * 1024)
@@ -57,10 +57,12 @@
     lanes, width = pick_x_ref.shape[1], pick_g_ref.shape[1]
     tiled_x = jnp.dot(pieces, pick_x_ref[...], preferred_element_type=F32)
     tiles = []
-    for j in range(width // lanes):
-        pick_g = pick_g_ref[:, j * lanes : (j + 1) * lanes]
+    wide = 2 * lanes if width % (2 * lanes) == 0 else lanes
+    tiled_x = jnp.concatenate([tiled_x] * (wide // lanes), axis=1)
+    for j in range(width // wide):
+        pick_g = pick_g_ref[:, j * wide : (j + 1) * wide]
         product = jnp.dot(pieces, pick_g, preferred_element_type=F32) * tiled_x
-        tiles.append(product.reshape(own, LEN, lanes).sum(axis=1))
+        tiles.append(product.reshape(own, LEN, wide).sum(axis=1))
     grads = jnp.concatenate(tiles, axis=1)
     high = grads.astype(BF16).astype(F32)
     low = grads - high

time: 15.5 us -> 15.2 us (0.981)
  starting transfers between devices: 7.79 us -> 7.23 us
  waiting for transfers between devices: 3.74 us -> 4.13 us
    ppermute x3, starting transfers between devices: 1.66 us -> 1.22 us  [rotate(): lax.ppermute(value, 'sub', [((i + k) % n_sub, i) for i in range(n_sub)])]
    ppermute x2, waiting for transfers between devices: 2.03 us -> 2.42 us  [body(): received.append(lax.ppermute(mine, AXES, pairs))]
  transfers between devices with their start and end apart: 6 -> 6, of which waited for: 3 -> 4; matrix products, arithmetic and copies ran while one was open for 5% -> 6% of each run, Pallas kernels for 4% -> 4%
where the time goes in v19:
time: 15.2 us; the launch traced here: 15.1 us
  starting transfers between devices  7.23 us (48%)
  waiting for transfers between devices  4.13 us (27%)
  Pallas kernels  1.64 us (11%)
  matrix products  0.82 us (5%)
  between operations  0.73 us (5%)
  local copies, waits for them, and re-layouts  0.5 us (3%)
    ppermute x2, starting transfers between devices, body(): received.append(lax.ppermute(mine, AXES, pairs))  3.5 us
    ppermute x1, starting transfers between devices, body(): chunk = lax.ppermute(queries[0], AXES, query_pairs)  2.52 us
    ppermute x2, waiting for transfers between devices, body(): received.append(lax.ppermute(mine, AXES, pairs))  2.42 us
    ppermute x3, waiting for transfers between devices, rotate(): lax.ppermute(value, 'sub', [((i + k) % n_sub, i) for i in range(n_sub)])  1.71 us
    ppermute x3, starting transfers between devices, rotate(): lax.ppermute(value, 'sub', [((i + k) % n_sub, i) for i in range(n_sub)])  1.22 us
    pallas_call x1, Pallas kernels, body(): pl.pallas_call(functools.partial(final_kernel, compact_plan if compact el...  1.08 us
    unnamed x8, local copies, waits for them, and re-layouts  0.5 us
    dot_general x1, matrix products, body(): lax.dot_general(basis_out[0], output_grads[0], LAST, preferred_element_ty...  0.41 us
  transfers between devices with their start and end apart: 6, of which 4 were waited for; matrix products, arithmetic and copies ran while one was open for 6% of the time, Pallas kernels for 4%

profile of v19, /device:TPU:0, one launch (start us, length us, event | category | flops | bytes accessed | tf_op | source)
XLA Modules:
  0.0 15.1 jit_solution(12191429266369856844)
XLA Ops:
  0.6 0.0 copy-start
  0.6 0.0 copy-start.2
  0.7 0.0 copy-start.1
  0.7 2.5 %collective-permute-start.1 = (bf16[16,512]{1,0:T(8,128)(2,1)}, bf16[16,512]{1,0:T(8,128)(2,1)S(1)}, u32[]{:S(2)}, u32[]{:S(2)}) collective-permute-start(bf16[16,512]{1,0:T(8,128)(2,1)} %bitcast.19), channel_id=1, source_target_pairs={{0,5},{1,4},{2,1},{3,0},{4,13},{5,12},{6,9},{7,8},{8,7},{9,6},{10,... | collective-permute-start | bytes 49160 | tf_op jit(solution)/shard_map/ppermute | solution.py:247
  3.2 0.1 picks.1
  3.3 0.0 copy-done
  3.3 0.0 copy-done.2
  3.4 0.0 copy-start.3
  3.4 0.4 %fusion = f32[32,256]{1,0:T(8,128)S(1)} fusion(bf16[1,256,2048]{2,1,0:T(8,128)(2,1)S(1)} %copy-done, bf16[1,32,2048]{2,1,0:T(8,128)(2,1)S(1)} %copy-done.2), kind=kOutput, calls=%fused_computation | convolution fusion | flops 33554432 | bytes 1212416 | tf_op jit(solution)/shard_map/dot_general | solution.py:261
  3.8 0.0 copy-done.1
  3.8 0.5 %copy-done.3 = bf16[1,32,2048]{2,1,0:T(8,128)(2,1)S(1)} copy-done((bf16[1,32,2048]{2,1,0:T(8,128)(2,1)S(1)}, bf16[1,32,2048]{2,1,0:T(8,128)(2,1)}, u32[]{:S(2)}) %copy-start.3) | copy-done | bytes 131096
  4.3 0.4 %fusion.2 = f32[32,256]{1,0:T(8,128)S(1)} fusion(bf16[1,256,2048]{2,1,0:T(8,128)(2,1)S(1)} %copy-done.1, bf16[1,32,2048]{2,1,0:T(8,128)(2,1)S(1)} %copy-done.3), kind=kOutput, calls=%fused_computation.2 | convolution fusion | flops 33554432 | bytes 1212416 | tf_op jit(solution)/shard_map/dot_general | solution.py:260
  4.7 0.7 %collective-permute-start = (f32[64,256]{1,0:T(8,128)S(1)}, f32[64,256]{1,0:T(8,128)S(1)}, u32[]{:S(2)}, u32[]{:S(2)}) collective-permute-start(f32[64,256]{1,0:T(8,128)S(1)} %pad_maximum_fusion.refs_0_), channel_id=1, source_target_pairs={{1,0},{0,1},{3,2},{2,3},{5,4},{4,5},{7,6},{6,7},{9,8},{8,9},{11,10... | collective-permute-start | bytes 196616 | tf_op jit(solution)/shard_map/ppermute | solution.py:238
  5.4 0.0 collective-permute-done.1.in_ref
  5.4 0.1 collective-permute-start.2
  5.5 0.8 %collective-permute-done.refs_1_ = f32[64,256]{1,0:T(8,128)S(1)} collective-permute-done((f32[64,256]{1,0:T(8,128)S(1)}, f32[64,256]{1,0:T(8,128)S(1)}, u32[]{:S(2)}, u32[]{:S(2)}) %collective-permute-start) | collective-permute-done | bytes 65568 | tf_op jit(solution)/shard_map/ppermute | solution.py:238
  6.3 0.4 %grads.1 = bf16[16,512]{1,0:T(8,128)(2,1)S(1)} custom-call(f32[64,256]{1,0:T(8,128)S(1)} %pad_maximum_fusion.refs_0_, f32[64,256]{1,0:T(8,128)S(1)} %collective-permute-done.refs_1_, bf16[256,128]{1,0:T(8,128)(2,1)S(1)} %get-tuple-element.10.refs_2_, bf16[256,1024]{1,0:T(8,128)(2,1)S(1)} %get-tuple-element.11.refs_3_), custom_call_target="tpu_custom_call" | custom-call | tf_op jit(solution)/shard_map/grads/pallas_call | solution.py:275
  6.8 0.0 collective-permute-done.2
  6.8 2.4 %collective-permute-start.3 = (bf16[3,16,512]{2,1,0:T(8,128)(2,1)S(1)}, bf16[3,16,512]{2,1,0:T(8,128)(2,1)S(1)}, u32[]{:S(2)}, u32[]{:S(2)}) collective-permute-start(bf16[3,16,512]{2,1,0:T(8,128)(2,1)S(1)} %pad_maximum_fusion.1.refs_0_), channel_id=1, source_target_pairs={{9,0},{13,1},{0,2},{15,3},{12,4},{1,5},{2,6},{4,7},{5,8},{10,9},{6... | collective-permute-start | bytes 147464 | tf_op jit(solution)/shard_map/ppermute | solution.py:288
  9.2 1.1 %collective-permute-start.4 = (bf16[3,16,512]{2,1,0:T(8,128)(2,1)S(1)}, bf16[3,16,512]{2,1,0:T(8,128)(2,1)S(1)}, u32[]{:S(2)}, u32[]{:S(2)}) collective-permute-start(bf16[3,16,512]{2,1,0:T(8,128)(2,1)S(1)} %pad_maximum_fusion.1.refs_0_), channel_id=1, source_target_pairs={{3,0},{5,1},{7,2},{11,3},{6,4},{8,5},{10,6},{15,7},{13,8},{0,9},{9... | collective-permute-start | bytes 147464 | tf_op jit(solution)/shard_map/ppermute | solution.py:288
  10.3 1.7 %collective-permute-done.3.first_ref.refs_1_ = bf16[3,16,512]{2,1,0:T(8,128)(2,1)S(1)} collective-permute-done((bf16[3,16,512]{2,1,0:T(8,128)(2,1)S(1)}, bf16[3,16,512]{2,1,0:T(8,128)(2,1)S(1)}, u32[]{:S(2)}, u32[]{:S(2)}) %collective-permute-start.3) | collective-permute-done | bytes 49184 | tf_op jit(solution)/shard_map/ppermute | solution.py:288
  12.0 0.7 %collective-permute-done.4.second_ref.refs_2_ = bf16[3,16,512]{2,1,0:T(8,128)(2,1)S(1)} collective-permute-done((bf16[3,16,512]{2,1,0:T(8,128)(2,1)S(1)}, bf16[3,16,512]{2,1,0:T(8,128)(2,1)S(1)}, u32[]{:S(2)}, u32[]{:S(2)}) %collective-permute-start.4) | collective-permute-done | bytes 49184 | tf_op jit(solution)/shard_map/ppermute | solution.py:288
  12.7 0.4 %collective-permute-start.5 = (bf16[4,16,512]{2,1,0:T(8,128)(2,1)S(1)}, bf16[4,16,512]{2,1,0:T(8,128)(2,1)S(1)}, u32[]{:S(2)}, u32[]{:S(2)}) collective-permute-start(bf16[4,16,512]{2,1,0:T(8,128)(2,1)S(1)} %swap.1), channel_id=1, source_target_pairs={{1,0},{0,1},{3,2},{2,3},{5,4},{4,5},{7,6},{6,7},{9,8},{8,9},{11,10... | collective-permute-start | bytes 196616 | tf_op jit(solution)/shard_map/ppermute | solution.py:238
  13.1 0.9 %collective-permute-done.5.refs_3_ = bf16[4,16,512]{2,1,0:T(8,128)(2,1)S(1)} collective-permute-done((bf16[4,16,512]{2,1,0:T(8,128)(2,1)S(1)}, bf16[4,16,512]{2,1,0:T(8,128)(2,1)S(1)}, u32[]{:S(2)}, u32[]{:S(2)}) %collective-permute-start.5) | collective-permute-done | bytes 65568 | tf_op jit(solution)/shard_map/ppermute | solution.py:238
  14.0 1.1 %gram_and_scores.1 = (f32[1,256,512]{2,1,0:T(8,128)}, f32[4,16]{1,0:T(4,128)}) custom-call(bf16[3,16,512]{2,1,0:T(8,128)(2,1)S(1)} %pad_maximum_fusion.1.refs_0_, bf16[3,16,512]{2,1,0:T(8,128)(2,1)S(1)} %collective-permute-done.3.first_ref.refs_1_, bf16[3,16,512]{2,1,0:T(8,128)(2,1)S(1)} %collective-permute-done.4.second_ref.refs_2_, ...), custom_call_target="tpu_custom_call" | custom-call | tf_op jit(solution)/shard_map/gram_and_scores/pallas_call | solution.py:304
  (4 shorter events, 0.0 us)
Async XLA Ops:
  0.6 2.7 %copy-start = (bf16[1,256,2048]{2,1,0:T(8,128)(2,1)S(1)}, bf16[1,256,2048]{2,1,0:T(8,128)(2,1)}, u32[]{:S(2)}) copy-start(bf16[1,256,2048]{2,1,0:T(8,128)(2,1)} %param.6) | copy-start | bytes 3145732
  0.6 2.7 %copy-start.2 = (bf16[1,32,2048]{2,1,0:T(8,128)(2,1)S(1)}, bf16[1,32,2048]{2,1,0:T(8,128)(2,1)}, u32[]{:S(2)}) copy-start(bf16[1,32,2048]{2,1,0:T(8,128)(2,1)} %param.8) | copy-start | bytes 393220
  0.7 3.1 %copy-start.1 = (bf16[1,256,2048]{2,1,0:T(8,128)(2,1)S(1)}, bf16[1,256,2048]{2,1,0:T(8,128)(2,1)}, u32[]{:S(2)}) copy-start(bf16[1,256,2048]{2,1,0:T(8,128)(2,1)} %param.5) | copy-start | bytes 3145732
  0.7 4.8 %collective-permute-start.1 = (bf16[16,512]{1,0:T(8,128)(2,1)}, bf16[16,512]{1,0:T(8,128)(2,1)S(1)}, u32[]{:S(2)}, u32[]{:S(2)}) collective-permute-start(bf16[16,512]{1,0:T(8,128)(2,1)} %bitcast.19), channel_id=1, source_target_pairs={{0,5},{1,4},{2,1},{3,0},{4,13},{5,12},{6,9},{7,8},{8,7},{9,6},{10,... | collective-permute-start | bytes 49160 | tf_op jit(solution)/shard_map/ppermute | solution.py:247
  3.4 0.9 %copy-start.3 = (bf16[1,32,2048]{2,1,0:T(8,128)(2,1)S(1)}, bf16[1,32,2048]{2,1,0:T(8,128)(2,1)}, u32[]{:S(2)}) copy-start(bf16[1,32,2048]{2,1,0:T(8,128)(2,1)} %param.7) | copy-start | bytes 393220
  4.7 1.6 %collective-permute-start = (f32[64,256]{1,0:T(8,128)S(1)}, f32[64,256]{1,0:T(8,128)S(1)}, u32[]{:S(2)}, u32[]{:S(2)}) collective-permute-start(f32[64,256]{1,0:T(8,128)S(1)} %pad_maximum_fusion.refs_0_), channel_id=1, source_target_pairs={{1,0},{0,1},{3,2},{2,3},{5,4},{4,5},{7,6},{6,7},{9,8},{8,9},{11,10... | collective-permute-start | bytes 196616 | tf_op jit(solution)/shard_map/ppermute | solution.py:238
  5.4 1.3 %collective-permute-start.2 = (bf16[16,512]{1,0:T(8,128)(2,1)S(1)}, bf16[16,512]{1,0:T(8,128)(2,1)S(1)}, u32[]{:S(2)}, u32[]{:S(2)}) collective-permute-start(bf16[16,512]{1,0:T(8,128)(2,1)S(1)} %chunk.1), channel_id=1, source_target_pairs={{1,0},{0,1},{3,2},{2,3},{5,4},{4,5},{7,6},{6,7},{9,8},{8,9},{11,10... | collective-permute-start | bytes 49160 | tf_op jit(solution)/shard_map/ppermute | solution.py:238
  6.8 5.2 %collective-permute-start.3 = (bf16[3,16,512]{2,1,0:T(8,128)(2,1)S(1)}, bf16[3,16,512]{2,1,0:T(8,128)(2,1)S(1)}, u32[]{:S(2)}, u32[]{:S(2)}) collective-permute-start(bf16[3,16,512]{2,1,0:T(8,128)(2,1)S(1)} %pad_maximum_fusion.1.refs_0_), channel_id=1, source_target_pairs={{9,0},{13,1},{0,2},{15,3},{12,4},{1,5},{2,6},{4,7},{5,8},{10,9},{6... | collective-permute-start | bytes 147464 | tf_op jit(solution)/shard_map/ppermute | solution.py:288
  9.2 3.5 %collective-permute-start.4 = (bf16[3,16,512]{2,1,0:T(8,128)(2,1)S(1)}, bf16[3,16,512]{2,1,0:T(8,128)(2,1)S(1)}, u32[]{:S(2)}, u32[]{:S(2)}) collective-permute-start(bf16[3,16,512]{2,1,0:T(8,128)(2,1)S(1)} %pad_maximum_fusion.1.refs_0_), channel_id=1, source_target_pairs={{3,0},{5,1},{7,2},{11,3},{6,4},{8,5},{10,6},{15,7},{13,8},{0,9},{9... | collective-permute-start | bytes 147464 | tf_op jit(solution)/shard_map/ppermute | solution.py:288
  12.7 1.3 %collective-permute-start.5 = (bf16[4,16,512]{2,1,0:T(8,128)(2,1)S(1)}, bf16[4,16,512]{2,1,0:T(8,128)(2,1)S(1)}, u32[]{:S(2)}, u32[]{:S(2)}) collective-permute-start(bf16[4,16,512]{2,1,0:T(8,128)(2,1)S(1)} %swap.1), channel_id=1, source_target_pairs={{1,0},{0,1},{3,2},{2,3},{5,4},{4,5},{7,6},{6,7},{9,8},{8,9},{11,10... | collective-permute-start | bytes 196616 | tf_op jit(solution)/shard_map/ppermute | solution.py:238

commit v20 on v19

--- a/solution.py
+++ b/solution.py
@@ -119,12 +119,13 @@
     left = jnp.concatenate(lefts, axis=0).astype(BF16)
     right = jnp.concatenate(rights, axis=0).astype(BF16)
     copies = []
-    step = n_rows // gram_buf.shape[0]
+    _, tall, wide = gram_buf.shape
     for at in range(gram_buf.shape[0]):
-        rows = slice(at * step, (at + 1) * step)
-        gram = lax.dot_general(left[:, rows], right, FIRST, preferred_element_type=F32)
+        row, col = at // (half // wide) * tall, at % (half // wide) * wide
+        gram = lax.dot_general(left[:, row : row + tall], right[:, col : col + wide], FIRST, preferred_element_type=F32)
         gram_buf[at] = gram * (1.0 / (own * n_ex))
-        copies.append(pltpu.make_async_copy(gram_buf.at[at], gram_ref.at[0, rows, :], sems.at[at]))
+        target = gram_ref.at[0, pl.ds(row, tall), pl.ds(col, wide)]
+        copies.append(pltpu.make_async_copy(gram_buf.at[at], target, sems.at[at]))
         copies[-1].start()
 
     layers = [halves_of(block) for block in layers]
@@ -300,7 +301,9 @@
             both = jnp.concatenate(received)
             blocks = [mine, both] + [rotate(both, k) for k in range(1, n_sub)]
 
-        pieces = 2 if width // n_ex % 256 == 0 else 1
+        tall = 128 if width // n_ex % 128 == 0 else width // n_ex
+        wide = 256 if half % 256 == 0 else half
+        pieces = width // n_ex // tall * (half // wide)
         return pl.pallas_call(
             functools.partial(final_kernel, compact_plan if compact else general_plan, n_ex, n_sub, own),
             out_shape=(
@@ -311,7 +314,7 @@
             out_specs=(ANY, ANY),
             scratch_shapes=[
                 pltpu.VMEM((sum(block.shape[0] for block in blocks), rows, half), BF16),
-                pltpu.VMEM((pieces, width // n_ex // pieces, half), F32),
+                pltpu.VMEM((pieces, tall, wide), F32),
                 pltpu.VMEM((own, rows * per_blk), F32),
                 pltpu.SemaphoreType.DMA((pieces + 1,)),
             ],

time: 15.2 us -> 15.2 us (level)
  no operation moved by 1% of the time
where the time goes in v20:
time: 15.2 us; the launch traced here: 15.1 us
  starting transfers between devices  7.23 us (48%)
  waiting for transfers between devices  4.13 us (27%)
  Pallas kernels  1.65 us (11%)
  matrix products  0.82 us (5%)
  between operations  0.73 us (5%)
  local copies, waits for them, and re-layouts  0.5 us (3%)
    ppermute x2, starting transfers between devices, body(): received.append(lax.ppermute(mine, AXES, pairs))  3.5 us
    ppermute x1, starting transfers between devices, body(): chunk = lax.ppermute(queries[0], AXES, query_pairs)  2.52 us
    ppermute x2, waiting for transfers between devices, body(): received.append(lax.ppermute(mine, AXES, pairs))  2.42 us
    ppermute x3, waiting for transfers between devices, rotate(): lax.ppermute(value, 'sub', [((i + k) % n_sub, i) for i in range(n_sub)])  1.71 us
    ppermute x3, starting transfers between devices, rotate(): lax.ppermute(value, 'sub', [((i + k) % n_sub, i) for i in range(n_sub)])  1.22 us
    pallas_call x1, Pallas kernels, body(): pl.pallas_call(functools.partial(final_kernel, compact_plan if compact el...  1.09 us
    unnamed x8, local copies, waits for them, and re-layouts  0.5 us
    dot_general x1, matrix products, body(): lax.dot_general(basis_out[0], output_grads[0], LAST, preferred_element_ty...  0.41 us
  transfers between devices with their start and end apart: 6, of which 4 were waited for; matrix products, arithmetic and copies ran while one was open for 6% of the time, Pallas kernels for 4%

profile of v20, /device:TPU:0, one launch (start us, length us, event | category | flops | bytes accessed | tf_op | source)
XLA Modules:
  0.0 15.1 jit_solution(16008063994016595879)
XLA Ops:
  0.6 0.0 copy-start
  0.6 0.0 copy-start.2
  0.7 0.0 copy-start.1
  0.7 2.5 %collective-permute-start.1 = (bf16[16,512]{1,0:T(8,128)(2,1)}, bf16[16,512]{1,0:T(8,128)(2,1)S(1)}, u32[]{:S(2)}, u32[]{:S(2)}) collective-permute-start(bf16[16,512]{1,0:T(8,128)(2,1)} %bitcast.19), channel_id=1, source_target_pairs={{0,5},{1,4},{2,1},{3,0},{4,13},{5,12},{6,9},{7,8},{8,7},{9,6},{10,... | collective-permute-start | bytes 49160 | tf_op jit(solution)/shard_map/ppermute | solution.py:248
  3.2 0.1 picks.1
  3.3 0.0 copy-done
  3.3 0.0 copy-done.2
  3.4 0.0 copy-start.3
  3.4 0.4 %fusion = f32[32,256]{1,0:T(8,128)S(1)} fusion(bf16[1,256,2048]{2,1,0:T(8,128)(2,1)S(1)} %copy-done, bf16[1,32,2048]{2,1,0:T(8,128)(2,1)S(1)} %copy-done.2), kind=kOutput, calls=%fused_computation | convolution fusion | flops 33554432 | bytes 1212416 | tf_op jit(solution)/shard_map/dot_general | solution.py:262
  3.8 0.0 copy-done.1
  3.8 0.5 %copy-done.3 = bf16[1,32,2048]{2,1,0:T(8,128)(2,1)S(1)} copy-done((bf16[1,32,2048]{2,1,0:T(8,128)(2,1)S(1)}, bf16[1,32,2048]{2,1,0:T(8,128)(2,1)}, u32[]{:S(2)}) %copy-start.3) | copy-done | bytes 131096
  4.3 0.4 %fusion.2 = f32[32,256]{1,0:T(8,128)S(1)} fusion(bf16[1,256,2048]{2,1,0:T(8,128)(2,1)S(1)} %copy-done.1, bf16[1,32,2048]{2,1,0:T(8,128)(2,1)S(1)} %copy-done.3), kind=kOutput, calls=%fused_computation.2 | convolution fusion | flops 33554432 | bytes 1212416 | tf_op jit(solution)/shard_map/dot_general | solution.py:261
  4.7 0.7 %collective-permute-start = (f32[64,256]{1,0:T(8,128)S(1)}, f32[64,256]{1,0:T(8,128)S(1)}, u32[]{:S(2)}, u32[]{:S(2)}) collective-permute-start(f32[64,256]{1,0:T(8,128)S(1)} %pad_maximum_fusion.refs_0_), channel_id=1, source_target_pairs={{1,0},{0,1},{3,2},{2,3},{5,4},{4,5},{7,6},{6,7},{9,8},{8,9},{11,10... | collective-permute-start | bytes 196616 | tf_op jit(solution)/shard_map/ppermute | solution.py:239
  5.4 0.0 collective-permute-done.1.in_ref
  5.4 0.1 collective-permute-start.2
  5.5 0.8 %collective-permute-done.refs_1_ = f32[64,256]{1,0:T(8,128)S(1)} collective-permute-done((f32[64,256]{1,0:T(8,128)S(1)}, f32[64,256]{1,0:T(8,128)S(1)}, u32[]{:S(2)}, u32[]{:S(2)}) %collective-permute-start) | collective-permute-done | bytes 65568 | tf_op jit(solution)/shard_map/ppermute | solution.py:239
  6.3 0.4 %grads.1 = bf16[16,512]{1,0:T(8,128)(2,1)S(1)} custom-call(f32[64,256]{1,0:T(8,128)S(1)} %pad_maximum_fusion.refs_0_, f32[64,256]{1,0:T(8,128)S(1)} %collective-permute-done.refs_1_, bf16[256,128]{1,0:T(8,128)(2,1)S(1)} %get-tuple-element.10.refs_2_, bf16[256,1024]{1,0:T(8,128)(2,1)S(1)} %get-tuple-element.11.refs_3_), custom_call_target="tpu_custom_call" | custom-call | tf_op jit(solution)/shard_map/grads/pallas_call | solution.py:276
  6.8 0.0 collective-permute-done.2
  6.8 2.4 %collective-permute-start.3 = (bf16[3,16,512]{2,1,0:T(8,128)(2,1)S(1)}, bf16[3,16,512]{2,1,0:T(8,128)(2,1)S(1)}, u32[]{:S(2)}, u32[]{:S(2)}) collective-permute-start(bf16[3,16,512]{2,1,0:T(8,128)(2,1)S(1)} %pad_maximum_fusion.1.refs_0_), channel_id=1, source_target_pairs={{9,0},{13,1},{0,2},{15,3},{12,4},{1,5},{2,6},{4,7},{5,8},{10,9},{6... | collective-permute-start | bytes 147464 | tf_op jit(solution)/shard_map/ppermute | solution.py:289
  9.2 1.1 %collective-permute-start.4 = (bf16[3,16,512]{2,1,0:T(8,128)(2,1)S(1)}, bf16[3,16,512]{2,1,0:T(8,128)(2,1)S(1)}, u32[]{:S(2)}, u32[]{:S(2)}) collective-permute-start(bf16[3,16,512]{2,1,0:T(8,128)(2,1)S(1)} %pad_maximum_fusion.1.refs_0_), channel_id=1, source_target_pairs={{3,0},{5,1},{7,2},{11,3},{6,4},{8,5},{10,6},{15,7},{13,8},{0,9},{9... | collective-permute-start | bytes 147464 | tf_op jit(solution)/shard_map/ppermute | solution.py:289
  10.3 1.7 %collective-permute-done.3.first_ref.refs_1_ = bf16[3,16,512]{2,1,0:T(8,128)(2,1)S(1)} collective-permute-done((bf16[3,16,512]{2,1,0:T(8,128)(2,1)S(1)}, bf16[3,16,512]{2,1,0:T(8,128)(2,1)S(1)}, u32[]{:S(2)}, u32[]{:S(2)}) %collective-permute-start.3) | collective-permute-done | bytes 49184 | tf_op jit(solution)/shard_map/ppermute | solution.py:289
  12.0 0.7 %collective-permute-done.4.second_ref.refs_2_ = bf16[3,16,512]{2,1,0:T(8,128)(2,1)S(1)} collective-permute-done((bf16[3,16,512]{2,1,0:T(8,128)(2,1)S(1)}, bf16[3,16,512]{2,1,0:T(8,128)(2,1)S(1)}, u32[]{:S(2)}, u32[]{:S(2)}) %collective-permute-start.4) | collective-permute-done | bytes 49184 | tf_op jit(solution)/shard_map/ppermute | solution.py:289
  12.7 0.4 %collective-permute-start.5 = (bf16[4,16,512]{2,1,0:T(8,128)(2,1)S(1)}, bf16[4,16,512]{2,1,0:T(8,128)(2,1)S(1)}, u32[]{:S(2)}, u32[]{:S(2)}) collective-permute-start(bf16[4,16,512]{2,1,0:T(8,128)(2,1)S(1)} %swap.1), channel_id=1, source_target_pairs={{1,0},{0,1},{3,2},{2,3},{5,4},{4,5},{7,6},{6,7},{9,8},{8,9},{11,10... | collective-permute-start | bytes 196616 | tf_op jit(solution)/shard_map/ppermute | solution.py:239
  13.1 0.9 %collective-permute-done.5.refs_3_ = bf16[4,16,512]{2,1,0:T(8,128)(2,1)S(1)} collective-permute-done((bf16[4,16,512]{2,1,0:T(8,128)(2,1)S(1)}, bf16[4,16,512]{2,1,0:T(8,128)(2,1)S(1)}, u32[]{:S(2)}, u32[]{:S(2)}) %collective-permute-start.5) | collective-permute-done | bytes 65568 | tf_op jit(solution)/shard_map/ppermute | solution.py:239
  14.0 1.1 %gram_and_scores.1 = (f32[1,256,512]{2,1,0:T(8,128)}, f32[4,16]{1,0:T(4,128)}) custom-call(bf16[3,16,512]{2,1,0:T(8,128)(2,1)S(1)} %pad_maximum_fusion.1.refs_0_, bf16[3,16,512]{2,1,0:T(8,128)(2,1)S(1)} %collective-permute-done.3.first_ref.refs_1_, bf16[3,16,512]{2,1,0:T(8,128)(2,1)S(1)} %collective-permute-done.4.second_ref.refs_2_, ...), custom_call_target="tpu_custom_call" | custom-call | tf_op jit(solution)/shard_map/gram_and_scores/pallas_call | solution.py:307
  (4 shorter events, 0.0 us)
Async XLA Ops:
  0.6 2.7 %copy-start = (bf16[1,256,2048]{2,1,0:T(8,128)(2,1)S(1)}, bf16[1,256,2048]{2,1,0:T(8,128)(2,1)}, u32[]{:S(2)}) copy-start(bf16[1,256,2048]{2,1,0:T(8,128)(2,1)} %param.6) | copy-start | bytes 3145732
  0.6 2.7 %copy-start.2 = (bf16[1,32,2048]{2,1,0:T(8,128)(2,1)S(1)}, bf16[1,32,2048]{2,1,0:T(8,128)(2,1)}, u32[]{:S(2)}) copy-start(bf16[1,32,2048]{2,1,0:T(8,128)(2,1)} %param.8) | copy-start | bytes 393220
  0.7 3.1 %copy-start.1 = (bf16[1,256,2048]{2,1,0:T(8,128)(2,1)S(1)}, bf16[1,256,2048]{2,1,0:T(8,128)(2,1)}, u32[]{:S(2)}) copy-start(bf16[1,256,2048]{2,1,0:T(8,128)(2,1)} %param.5) | copy-start | bytes 3145732
  0.7 4.8 %collective-permute-start.1 = (bf16[16,512]{1,0:T(8,128)(2,1)}, bf16[16,512]{1,0:T(8,128)(2,1)S(1)}, u32[]{:S(2)}, u32[]{:S(2)}) collective-permute-start(bf16[16,512]{1,0:T(8,128)(2,1)} %bitcast.19), channel_id=1, source_target_pairs={{0,5},{1,4},{2,1},{3,0},{4,13},{5,12},{6,9},{7,8},{8,7},{9,6},{10,... | collective-permute-start | bytes 49160 | tf_op jit(solution)/shard_map/ppermute | solution.py:248
  3.4 0.9 %copy-start.3 = (bf16[1,32,2048]{2,1,0:T(8,128)(2,1)S(1)}, bf16[1,32,2048]{2,1,0:T(8,128)(2,1)}, u32[]{:S(2)}) copy-start(bf16[1,32,2048]{2,1,0:T(8,128)(2,1)} %param.7) | copy-start | bytes 393220
  4.7 1.6 %collective-permute-start = (f32[64,256]{1,0:T(8,128)S(1)}, f32[64,256]{1,0:T(8,128)S(1)}, u32[]{:S(2)}, u32[]{:S(2)}) collective-permute-start(f32[64,256]{1,0:T(8,128)S(1)} %pad_maximum_fusion.refs_0_), channel_id=1, source_target_pairs={{1,0},{0,1},{3,2},{2,3},{5,4},{4,5},{7,6},{6,7},{9,8},{8,9},{11,10... | collective-permute-start | bytes 196616 | tf_op jit(solution)/shard_map/ppermute | solution.py:239
  5.4 1.3 %collective-permute-start.2 = (bf16[16,512]{1,0:T(8,128)(2,1)S(1)}, bf16[16,512]{1,0:T(8,128)(2,1)S(1)}, u32[]{:S(2)}, u32[]{:S(2)}) collective-permute-start(bf16[16,512]{1,0:T(8,128)(2,1)S(1)} %chunk.1), channel_id=1, source_target_pairs={{1,0},{0,1},{3,2},{2,3},{5,4},{4,5},{7,6},{6,7},{9,8},{8,9},{11,10... | collective-permute-start | bytes 49160 | tf_op jit(solution)/shard_map/ppermute | solution.py:239
  6.8 5.2 %collective-permute-start.3 = (bf16[3,16,512]{2,1,0:T(8,128)(2,1)S(1)}, bf16[3,16,512]{2,1,0:T(8,128)(2,1)S(1)}, u32[]{:S(2)}, u32[]{:S(2)}) collective-permute-start(bf16[3,16,512]{2,1,0:T(8,128)(2,1)S(1)} %pad_maximum_fusion.1.refs_0_), channel_id=1, source_target_pairs={{9,0},{13,1},{0,2},{15,3},{12,4},{1,5},{2,6},{4,7},{5,8},{10,9},{6... | collective-permute-start | bytes 147464 | tf_op jit(solution)/shard_map/ppermute | solution.py:289
  9.2 3.5 %collective-permute-start.4 = (bf16[3,16,512]{2,1,0:T(8,128)(2,1)S(1)}, bf16[3,16,512]{2,1,0:T(8,128)(2,1)S(1)}, u32[]{:S(2)}, u32[]{:S(2)}) collective-permute-start(bf16[3,16,512]{2,1,0:T(8,128)(2,1)S(1)} %pad_maximum_fusion.1.refs_0_), channel_id=1, source_target_pairs={{3,0},{5,1},{7,2},{11,3},{6,4},{8,5},{10,6},{15,7},{13,8},{0,9},{9... | collective-permute-start | bytes 147464 | tf_op jit(solution)/shard_map/ppermute | solution.py:289
  12.7 1.3 %collective-permute-start.5 = (bf16[4,16,512]{2,1,0:T(8,128)(2,1)S(1)}, bf16[4,16,512]{2,1,0:T(8,128)(2,1)S(1)}, u32[]{:S(2)}, u32[]{:S(2)}) collective-permute-start(bf16[4,16,512]{2,1,0:T(8,128)(2,1)S(1)} %swap.1), channel_id=1, source_target_pairs={{1,0},{0,1},{3,2},{2,3},{5,4},{4,5},{7,6},{6,7},{9,8},{8,9},{11,10... | collective-permute-start | bytes 196616 | tf_op jit(solution)/shard_map/ppermute | solution.py:239

commit v21 on v19

--- a/solution.py
+++ b/solution.py
@@ -17,12 +17,12 @@
 DEAL = (
     (5, 7, 1, 3),
     (0, 5, 7, 3),
-    (4, 6, 0, 3),
-    (2, 4, 7, 0),
-    (2, 5, 6, 1),
-    (5, 6, 3, 0),
-    (0, 5, 6, 2),
-    (4, 6, 1, 3),
+    (3, 5, 7, 1),
+    (1, 6, 4, 2),
+    (2, 4, 6, 0),
+    (4, 7, 3, 0),
+    (2, 7, 4, 0),
+    (2, 6, 4, 1),
 )
 PARAMS = pltpu.CompilerParams(vmem_limit_bytes=16 * 1024 * 1024)
 

time: 15.2 us -> 15.2 us (level)
  no operation moved by 1% of the time
where the time goes in v21:
time: 15.2 us; the launch traced here: 15 us
  starting transfers between devices  7.18 us (47%)
  waiting for transfers between devices  4.16 us (27%)
  Pallas kernels  1.64 us (11%)
  matrix products  0.82 us (5%)
  between operations  0.73 us (5%)
  local copies, waits for them, and re-layouts  0.5 us (3%)
    ppermute x2, starting transfers between devices, body(): received.append(lax.ppermute(mine, AXES, pairs))  3.5 us
    ppermute x1, starting transfers between devices, body(): chunk = lax.ppermute(queries[0], AXES, query_pairs)  2.52 us
    ppermute x2, waiting for transfers between devices, body(): received.append(lax.ppermute(mine, AXES, pairs))  2.43 us
    ppermute x3, waiting for transfers between devices, rotate(): lax.ppermute(value, 'sub', [((i + k) % n_sub, i) for i in range(n_sub)])  1.73 us
    ppermute x3, starting transfers between devices, rotate(): lax.ppermute(value, 'sub', [((i + k) % n_sub, i) for i in range(n_sub)])  1.16 us
    pallas_call x1, Pallas kernels, body(): pl.pallas_call(functools.partial(final_kernel, compact_plan if compact el...  1.08 us
    unnamed x8, local copies, waits for them, and re-layouts  0.5 us
    dot_general x1, matrix products, body(): lax.dot_general(basis_out[0], output_grads[0], LAST, preferred_element_ty...  0.41 us
  transfers between devices with their start and end apart: 6, of which 4 were waited for; matrix products, arithmetic and copies ran while one was open for 6% of the time, Pallas kernels for 4%

profile of v21, /device:TPU:0, one launch (start us, length us, event | category | flops | bytes accessed | tf_op | source)
XLA Modules:
  0.0 15.0 jit_solution(17818717940189878371)
XLA Ops:
  0.6 0.0 copy-start
  0.6 0.0 copy-start.2
  0.7 0.0 copy-start.1
  0.7 2.5 %collective-permute-start.1 = (bf16[16,512]{1,0:T(8,128)(2,1)}, bf16[16,512]{1,0:T(8,128)(2,1)S(1)}, u32[]{:S(2)}, u32[]{:S(2)}) collective-permute-start(bf16[16,512]{1,0:T(8,128)(2,1)} %bitcast.19), channel_id=1, source_target_pairs={{0,5},{1,4},{2,1},{3,0},{4,13},{5,12},{6,9},{7,8},{8,7},{9,6},{10,... | collective-permute-start | bytes 49160 | tf_op jit(solution)/shard_map/ppermute | solution.py:247
  3.2 0.1 picks.1
  3.3 0.0 copy-done
  3.3 0.0 copy-done.2
  3.4 0.0 copy-start.3
  3.4 0.4 %fusion = f32[32,256]{1,0:T(8,128)S(1)} fusion(bf16[1,256,2048]{2,1,0:T(8,128)(2,1)S(1)} %copy-done, bf16[1,32,2048]{2,1,0:T(8,128)(2,1)S(1)} %copy-done.2), kind=kOutput, calls=%fused_computation | convolution fusion | flops 33554432 | bytes 1212416 | tf_op jit(solution)/shard_map/dot_general | solution.py:261
  3.8 0.0 copy-done.1
  3.8 0.5 %copy-done.3 = bf16[1,32,2048]{2,1,0:T(8,128)(2,1)S(1)} copy-done((bf16[1,32,2048]{2,1,0:T(8,128)(2,1)S(1)}, bf16[1,32,2048]{2,1,0:T(8,128)(2,1)}, u32[]{:S(2)}) %copy-start.3) | copy-done | bytes 131096
  4.3 0.4 %fusion.2 = f32[32,256]{1,0:T(8,128)S(1)} fusion(bf16[1,256,2048]{2,1,0:T(8,128)(2,1)S(1)} %copy-done.1, bf16[1,32,2048]{2,1,0:T(8,128)(2,1)S(1)} %copy-done.3), kind=kOutput, calls=%fused_computation.2 | convolution fusion | flops 33554432 | bytes 1212416 | tf_op jit(solution)/shard_map/dot_general | solution.py:260
  4.7 0.7 %collective-permute-start = (f32[64,256]{1,0:T(8,128)S(1)}, f32[64,256]{1,0:T(8,128)S(1)}, u32[]{:S(2)}, u32[]{:S(2)}) collective-permute-start(f32[64,256]{1,0:T(8,128)S(1)} %pad_maximum_fusion.refs_0_), channel_id=1, source_target_pairs={{1,0},{0,1},{3,2},{2,3},{5,4},{4,5},{7,6},{6,7},{9,8},{8,9},{11,10... | collective-permute-start | bytes 196616 | tf_op jit(solution)/shard_map/ppermute | solution.py:238
  5.4 0.0 collective-permute-done.1.in_ref
  5.4 0.1 collective-permute-start.2
  5.5 0.8 %collective-permute-done.refs_1_ = f32[64,256]{1,0:T(8,128)S(1)} collective-permute-done((f32[64,256]{1,0:T(8,128)S(1)}, f32[64,256]{1,0:T(8,128)S(1)}, u32[]{:S(2)}, u32[]{:S(2)}) %collective-permute-start) | collective-permute-done | bytes 65568 | tf_op jit(solution)/shard_map/ppermute | solution.py:238
  6.3 0.4 %grads.1 = bf16[16,512]{1,0:T(8,128)(2,1)S(1)} custom-call(f32[64,256]{1,0:T(8,128)S(1)} %pad_maximum_fusion.refs_0_, f32[64,256]{1,0:T(8,128)S(1)} %collective-permute-done.refs_1_, bf16[256,128]{1,0:T(8,128)(2,1)S(1)} %get-tuple-element.10.refs_2_, bf16[256,1024]{1,0:T(8,128)(2,1)S(1)} %get-tuple-element.11.refs_3_), custom_call_target="tpu_custom_call" | custom-call | tf_op jit(solution)/shard_map/grads/pallas_call | solution.py:275
  6.8 0.0 collective-permute-done.2
  6.8 2.4 %collective-permute-start.3 = (bf16[3,16,512]{2,1,0:T(8,128)(2,1)S(1)}, bf16[3,16,512]{2,1,0:T(8,128)(2,1)S(1)}, u32[]{:S(2)}, u32[]{:S(2)}) collective-permute-start(bf16[3,16,512]{2,1,0:T(8,128)(2,1)S(1)} %pad_maximum_fusion.1.refs_0_), channel_id=1, source_target_pairs={{9,0},{13,1},{0,2},{15,3},{1,4},{7,5},{5,6},{2,7},{4,8},{10,9},{6,... | collective-permute-start | bytes 147464 | tf_op jit(solution)/shard_map/ppermute | solution.py:288
  9.2 1.1 %collective-permute-start.4 = (bf16[3,16,512]{2,1,0:T(8,128)(2,1)S(1)}, bf16[3,16,512]{2,1,0:T(8,128)(2,1)S(1)}, u32[]{:S(2)}, u32[]{:S(2)}) collective-permute-start(bf16[3,16,512]{2,1,0:T(8,128)(2,1)S(1)} %pad_maximum_fusion.1.refs_0_), channel_id=1, source_target_pairs={{3,0},{5,1},{7,2},{11,3},{9,4},{13,5},{14,6},{10,7},{12,8},{0,9},{... | collective-permute-start | bytes 147464 | tf_op jit(solution)/shard_map/ppermute | solution.py:288
  10.3 1.7 %collective-permute-done.3.first_ref.refs_1_ = bf16[3,16,512]{2,1,0:T(8,128)(2,1)S(1)} collective-permute-done((bf16[3,16,512]{2,1,0:T(8,128)(2,1)S(1)}, bf16[3,16,512]{2,1,0:T(8,128)(2,1)S(1)}, u32[]{:S(2)}, u32[]{:S(2)}) %collective-permute-start.3) | collective-permute-done | bytes 49184 | tf_op jit(solution)/shard_map/ppermute | solution.py:288
  12.0 0.7 %collective-permute-done.4.second_ref.refs_2_ = bf16[3,16,512]{2,1,0:T(8,128)(2,1)S(1)} collective-permute-done((bf16[3,16,512]{2,1,0:T(8,128)(2,1)S(1)}, bf16[3,16,512]{2,1,0:T(8,128)(2,1)S(1)}, u32[]{:S(2)}, u32[]{:S(2)}) %collective-permute-start.4) | collective-permute-done | bytes 49184 | tf_op jit(solution)/shard_map/ppermute | solution.py:288
  12.7 0.3 %collective-permute-start.5 = (bf16[4,16,512]{2,1,0:T(8,128)(2,1)S(1)}, bf16[4,16,512]{2,1,0:T(8,128)(2,1)S(1)}, u32[]{:S(2)}, u32[]{:S(2)}) collective-permute-start(bf16[4,16,512]{2,1,0:T(8,128)(2,1)S(1)} %swap.1), channel_id=1, source_target_pairs={{1,0},{0,1},{3,2},{2,3},{5,4},{4,5},{7,6},{6,7},{9,8},{8,9},{11,10... | collective-permute-start | bytes 196616 | tf_op jit(solution)/shard_map/ppermute | solution.py:238
  13.0 0.9 %collective-permute-done.5.refs_3_ = bf16[4,16,512]{2,1,0:T(8,128)(2,1)S(1)} collective-permute-done((bf16[4,16,512]{2,1,0:T(8,128)(2,1)S(1)}, bf16[4,16,512]{2,1,0:T(8,128)(2,1)S(1)}, u32[]{:S(2)}, u32[]{:S(2)}) %collective-permute-start.5) | collective-permute-done | bytes 65568 | tf_op jit(solution)/shard_map/ppermute | solution.py:238
  14.0 1.1 %gram_and_scores.1 = (f32[1,256,512]{2,1,0:T(8,128)}, f32[4,16]{1,0:T(4,128)}) custom-call(bf16[3,16,512]{2,1,0:T(8,128)(2,1)S(1)} %pad_maximum_fusion.1.refs_0_, bf16[3,16,512]{2,1,0:T(8,128)(2,1)S(1)} %collective-permute-done.3.first_ref.refs_1_, bf16[3,16,512]{2,1,0:T(8,128)(2,1)S(1)} %collective-permute-done.4.second_ref.refs_2_, ...), custom_call_target="tpu_custom_call" | custom-call | tf_op jit(solution)/shard_map/gram_and_scores/pallas_call | solution.py:304
  (4 shorter events, 0.0 us)
Async XLA Ops:
  0.6 2.7 %copy-start = (bf16[1,256,2048]{2,1,0:T(8,128)(2,1)S(1)}, bf16[1,256,2048]{2,1,0:T(8,128)(2,1)}, u32[]{:S(2)}) copy-start(bf16[1,256,2048]{2,1,0:T(8,128)(2,1)} %param.6) | copy-start | bytes 3145732
  0.6 2.7 %copy-start.2 = (bf16[1,32,2048]{2,1,0:T(8,128)(2,1)S(1)}, bf16[1,32,2048]{2,1,0:T(8,128)(2,1)}, u32[]{:S(2)}) copy-start(bf16[1,32,2048]{2,1,0:T(8,128)(2,1)} %param.8) | copy-start | bytes 393220
  0.7 3.1 %copy-start.1 = (bf16[1,256,2048]{2,1,0:T(8,128)(2,1)S(1)}, bf16[1,256,2048]{2,1,0:T(8,128)(2,1)}, u32[]{:S(2)}) copy-start(bf16[1,256,2048]{2,1,0:T(8,128)(2,1)} %param.5) | copy-start | bytes 3145732
  0.7 4.8 %collective-permute-start.1 = (bf16[16,512]{1,0:T(8,128)(2,1)}, bf16[16,512]{1,0:T(8,128)(2,1)S(1)}, u32[]{:S(2)}, u32[]{:S(2)}) collective-permute-start(bf16[16,512]{1,0:T(8,128)(2,1)} %bitcast.19), channel_id=1, source_target_pairs={{0,5},{1,4},{2,1},{3,0},{4,13},{5,12},{6,9},{7,8},{8,7},{9,6},{10,... | collective-permute-start | bytes 49160 | tf_op jit(solution)/shard_map/ppermute | solution.py:247
  3.4 0.9 %copy-start.3 = (bf16[1,32,2048]{2,1,0:T(8,128)(2,1)S(1)}, bf16[1,32,2048]{2,1,0:T(8,128)(2,1)}, u32[]{:S(2)}) copy-start(bf16[1,32,2048]{2,1,0:T(8,128)(2,1)} %param.7) | copy-start | bytes 393220
  4.7 1.6 %collective-permute-start = (f32[64,256]{1,0:T(8,128)S(1)}, f32[64,256]{1,0:T(8,128)S(1)}, u32[]{:S(2)}, u32[]{:S(2)}) collective-permute-start(f32[64,256]{1,0:T(8,128)S(1)} %pad_maximum_fusion.refs_0_), channel_id=1, source_target_pairs={{1,0},{0,1},{3,2},{2,3},{5,4},{4,5},{7,6},{6,7},{9,8},{8,9},{11,10... | collective-permute-start | bytes 196616 | tf_op jit(solution)/shard_map/ppermute | solution.py:238
  5.4 1.3 %collective-permute-start.2 = (bf16[16,512]{1,0:T(8,128)(2,1)S(1)}, bf16[16,512]{1,0:T(8,128)(2,1)S(1)}, u32[]{:S(2)}, u32[]{:S(2)}) collective-permute-start(bf16[16,512]{1,0:T(8,128)(2,1)S(1)} %chunk.1), channel_id=1, source_target_pairs={{1,0},{0,1},{3,2},{2,3},{5,4},{4,5},{7,6},{6,7},{9,8},{8,9},{11,10... | collective-permute-start | bytes 49160 | tf_op jit(solution)/shard_map/ppermute | solution.py:238
  6.8 5.2 %collective-permute-start.3 = (bf16[3,16,512]{2,1,0:T(8,128)(2,1)S(1)}, bf16[3,16,512]{2,1,0:T(8,128)(2,1)S(1)}, u32[]{:S(2)}, u32[]{:S(2)}) collective-permute-start(bf16[3,16,512]{2,1,0:T(8,128)(2,1)S(1)} %pad_maximum_fusion.1.refs_0_), channel_id=1, source_target_pairs={{9,0},{13,1},{0,2},{15,3},{1,4},{7,5},{5,6},{2,7},{4,8},{10,9},{6,... | collective-permute-start | bytes 147464 | tf_op jit(solution)/shard_map/ppermute | solution.py:288
  9.2 3.5 %collective-permute-start.4 = (bf16[3,16,512]{2,1,0:T(8,128)(2,1)S(1)}, bf16[3,16,512]{2,1,0:T(8,128)(2,1)S(1)}, u32[]{:S(2)}, u32[]{:S(2)}) collective-permute-start(bf16[3,16,512]{2,1,0:T(8,128)(2,1)S(1)} %pad_maximum_fusion.1.refs_0_), channel_id=1, source_target_pairs={{3,0},{5,1},{7,2},{11,3},{9,4},{13,5},{14,6},{10,7},{12,8},{0,9},{... | collective-permute-start | bytes 147464 | tf_op jit(solution)/shard_map/ppermute | solution.py:288
  12.7 1.3 %collective-permute-start.5 = (bf16[4,16,512]{2,1,0:T(8,128)(2,1)S(1)}, bf16[4,16,512]{2,1,0:T(8,128)(2,1)S(1)}, u32[]{:S(2)}, u32[]{:S(2)}) collective-permute-start(bf16[4,16,512]{2,1,0:T(8,128)(2,1)S(1)} %swap.1), channel_id=1, source_target_pairs={{1,0},{0,1},{3,2},{2,3},{5,4},{4,5},{7,6},{6,7},{9,8},{8,9},{11,10... | collective-permute-start | bytes 196616 | tf_op jit(solution)/shard_map/ppermute | solution.py:238

commit v22 on v21

--- a/solution.py
+++ b/solution.py
@@ -17,12 +17,12 @@
 DEAL = (
     (5, 7, 1, 3),
     (0, 5, 7, 3),
-    (3, 5, 7, 1),
-    (1, 6, 4, 2),
-    (2, 4, 6, 0),
-    (4, 7, 3, 0),
+    (1, 5, 7, 3),
+    (1, 6, 4, 3),
+    (3, 4, 6, 0),
+    (4, 7, 2, 0),
     (2, 7, 4, 0),
-    (2, 6, 4, 1),
+    (2, 6, 4, 0),
 )
 PARAMS = pltpu.CompilerParams(vmem_limit_bytes=16 * 1024 * 1024)
 

time: 15.2 us -> 15.2 us (level)
  no operation moved by 1% of the time
where the time goes in v22:
time: 15.2 us; the launch traced here: 15 us
  starting transfers between devices  7.16 us (47%)
  waiting for transfers between devices  4.18 us (28%)
  Pallas kernels  1.64 us (11%)
  matrix products  0.82 us (5%)
  between operations  0.73 us (5%)
  local copies, waits for them, and re-layouts  0.5 us (3%)
    ppermute x2, starting transfers between devices, body(): received.append(lax.ppermute(mine, AXES, pairs))  3.5 us
    ppermute x1, starting transfers between devices, body(): chunk = lax.ppermute(queries[0], AXES, query_pairs)  2.52 us
    ppermute x2, waiting for transfers between devices, body(): received.append(lax.ppermute(mine, AXES, pairs))  2.43 us
    ppermute x3, waiting for transfers between devices, rotate(): lax.ppermute(value, 'sub', [((i + k) % n_sub, i) for i in range(n_sub)])  1.75 us
    ppermute x3, starting transfers between devices, rotate(): lax.ppermute(value, 'sub', [((i + k) % n_sub, i) for i in range(n_sub)])  1.14 us
    pallas_call x1, Pallas kernels, body(): pl.pallas_call(functools.partial(final_kernel, compact_plan if compact el...  1.08 us
    unnamed x8, local copies, waits for them, and re-layouts  0.5 us
    dot_general x1, matrix products, body(): lax.dot_general(basis_out[0], output_grads[0], LAST, preferred_element_ty...  0.41 us
  transfers between devices with their start and end apart: 6, of which 4 were waited for; matrix products, arithmetic and copies ran while one was open for 6% of the time, Pallas kernels for 4%

profile of v22, /device:TPU:0, one launch (start us, length us, event | category | flops | bytes accessed | tf_op | source)
XLA Modules:
  0.0 15.0 jit_solution(15062737187005273570)
XLA Ops:
  0.6 0.0 copy-start
  0.6 0.0 copy-start.2
  0.7 0.0 copy-start.1
  0.7 2.5 %collective-permute-start.1 = (bf16[16,512]{1,0:T(8,128)(2,1)}, bf16[16,512]{1,0:T(8,128)(2,1)S(1)}, u32[]{:S(2)}, u32[]{:S(2)}) collective-permute-start(bf16[16,512]{1,0:T(8,128)(2,1)} %bitcast.19), channel_id=1, source_target_pairs={{0,5},{1,4},{2,1},{3,0},{4,13},{5,12},{6,9},{7,8},{8,7},{9,6},{10,... | collective-permute-start | bytes 49160 | tf_op jit(solution)/shard_map/ppermute | solution.py:247
  3.2 0.1 picks.1
  3.3 0.0 copy-done
  3.3 0.0 copy-done.2
  3.4 0.0 copy-start.3
  3.4 0.4 %fusion = f32[32,256]{1,0:T(8,128)S(1)} fusion(bf16[1,256,2048]{2,1,0:T(8,128)(2,1)S(1)} %copy-done, bf16[1,32,2048]{2,1,0:T(8,128)(2,1)S(1)} %copy-done.2), kind=kOutput, calls=%fused_computation | convolution fusion | flops 33554432 | bytes 1212416 | tf_op jit(solution)/shard_map/dot_general | solution.py:261
  3.8 0.0 copy-done.1
  3.8 0.5 %copy-done.3 = bf16[1,32,2048]{2,1,0:T(8,128)(2,1)S(1)} copy-done((bf16[1,32,2048]{2,1,0:T(8,128)(2,1)S(1)}, bf16[1,32,2048]{2,1,0:T(8,128)(2,1)}, u32[]{:S(2)}) %copy-start.3) | copy-done | bytes 131096
  4.3 0.4 %fusion.2 = f32[32,256]{1,0:T(8,128)S(1)} fusion(bf16[1,256,2048]{2,1,0:T(8,128)(2,1)S(1)} %copy-done.1, bf16[1,32,2048]{2,1,0:T(8,128)(2,1)S(1)} %copy-done.3), kind=kOutput, calls=%fused_computation.2 | convolution fusion | flops 33554432 | bytes 1212416 | tf_op jit(solution)/shard_map/dot_general | solution.py:260
  4.7 0.7 %collective-permute-start = (f32[64,256]{1,0:T(8,128)S(1)}, f32[64,256]{1,0:T(8,128)S(1)}, u32[]{:S(2)}, u32[]{:S(2)}) collective-permute-start(f32[64,256]{1,0:T(8,128)S(1)} %pad_maximum_fusion.refs_0_), channel_id=1, source_target_pairs={{1,0},{0,1},{3,2},{2,3},{5,4},{4,5},{7,6},{6,7},{9,8},{8,9},{11,10... | collective-permute-start | bytes 196616 | tf_op jit(solution)/shard_map/ppermute | solution.py:238
  5.4 0.0 collective-permute-done.1.in_ref
  5.4 0.1 collective-permute-start.2
  5.5 0.8 %collective-permute-done.refs_1_ = f32[64,256]{1,0:T(8,128)S(1)} collective-permute-done((f32[64,256]{1,0:T(8,128)S(1)}, f32[64,256]{1,0:T(8,128)S(1)}, u32[]{:S(2)}, u32[]{:S(2)}) %collective-permute-start) | collective-permute-done | bytes 65568 | tf_op jit(solution)/shard_map/ppermute | solution.py:238
  6.3 0.4 %grads.1 = bf16[16,512]{1,0:T(8,128)(2,1)S(1)} custom-call(f32[64,256]{1,0:T(8,128)S(1)} %pad_maximum_fusion.refs_0_, f32[64,256]{1,0:T(8,128)S(1)} %collective-permute-done.refs_1_, bf16[256,128]{1,0:T(8,128)(2,1)S(1)} %get-tuple-element.10.refs_2_, bf16[256,1024]{1,0:T(8,128)(2,1)S(1)} %get-tuple-element.11.refs_3_), custom_call_target="tpu_custom_call" | custom-call | tf_op jit(solution)/shard_map/grads/pallas_call | solution.py:275
  6.8 0.0 collective-permute-done.2
  6.8 2.4 %collective-permute-start.3 = (bf16[3,16,512]{2,1,0:T(8,128)(2,1)S(1)}, bf16[3,16,512]{2,1,0:T(8,128)(2,1)S(1)}, u32[]{:S(2)}, u32[]{:S(2)}) collective-permute-start(bf16[3,16,512]{2,1,0:T(8,128)(2,1)S(1)} %pad_maximum_fusion.1.refs_0_), channel_id=1, source_target_pairs={{9,0},{13,1},{0,2},{15,3},{7,4},{1,5},{5,6},{3,7},{4,8},{11,9},{6,... | collective-permute-start | bytes 147464 | tf_op jit(solution)/shard_map/ppermute | solution.py:288
  9.2 1.1 %collective-permute-start.4 = (bf16[3,16,512]{2,1,0:T(8,128)(2,1)S(1)}, bf16[3,16,512]{2,1,0:T(8,128)(2,1)S(1)}, u32[]{:S(2)}, u32[]{:S(2)}) collective-permute-start(bf16[3,16,512]{2,1,0:T(8,128)(2,1)S(1)} %pad_maximum_fusion.1.refs_0_), channel_id=1, source_target_pairs={{3,0},{5,1},{7,2},{11,3},{9,4},{13,5},{14,6},{10,7},{12,8},{0,9},{... | collective-permute-start | bytes 147464 | tf_op jit(solution)/shard_map/ppermute | solution.py:288
  10.3 1.7 %collective-permute-done.3.first_ref.refs_1_ = bf16[3,16,512]{2,1,0:T(8,128)(2,1)S(1)} collective-permute-done((bf16[3,16,512]{2,1,0:T(8,128)(2,1)S(1)}, bf16[3,16,512]{2,1,0:T(8,128)(2,1)S(1)}, u32[]{:S(2)}, u32[]{:S(2)}) %collective-permute-start.3) | collective-permute-done | bytes 49184 | tf_op jit(solution)/shard_map/ppermute | solution.py:288
  12.0 0.7 %collective-permute-done.4.second_ref.refs_2_ = bf16[3,16,512]{2,1,0:T(8,128)(2,1)S(1)} collective-permute-done((bf16[3,16,512]{2,1,0:T(8,128)(2,1)S(1)}, bf16[3,16,512]{2,1,0:T(8,128)(2,1)S(1)}, u32[]{:S(2)}, u32[]{:S(2)}) %collective-permute-start.4) | collective-permute-done | bytes 49184 | tf_op jit(solution)/shard_map/ppermute | solution.py:288
  12.7 0.3 %collective-permute-start.5 = (bf16[4,16,512]{2,1,0:T(8,128)(2,1)S(1)}, bf16[4,16,512]{2,1,0:T(8,128)(2,1)S(1)}, u32[]{:S(2)}, u32[]{:S(2)}) collective-permute-start(bf16[4,16,512]{2,1,0:T(8,128)(2,1)S(1)} %swap.1), channel_id=1, source_target_pairs={{1,0},{0,1},{3,2},{2,3},{5,4},{4,5},{7,6},{6,7},{9,8},{8,9},{11,10... | collective-permute-start | bytes 196616 | tf_op jit(solution)/shard_map/ppermute | solution.py:238
  13.0 0.9 %collective-permute-done.5.refs_3_ = bf16[4,16,512]{2,1,0:T(8,128)(2,1)S(1)} collective-permute-done((bf16[4,16,512]{2,1,0:T(8,128)(2,1)S(1)}, bf16[4,16,512]{2,1,0:T(8,128)(2,1)S(1)}, u32[]{:S(2)}, u32[]{:S(2)}) %collective-permute-start.5) | collective-permute-done | bytes 65568 | tf_op jit(solution)/shard_map/ppermute | solution.py:238
  14.0 1.1 %gram_and_scores.1 = (f32[1,256,512]{2,1,0:T(8,128)}, f32[4,16]{1,0:T(4,128)}) custom-call(bf16[3,16,512]{2,1,0:T(8,128)(2,1)S(1)} %pad_maximum_fusion.1.refs_0_, bf16[3,16,512]{2,1,0:T(8,128)(2,1)S(1)} %collective-permute-done.3.first_ref.refs_1_, bf16[3,16,512]{2,1,0:T(8,128)(2,1)S(1)} %collective-permute-done.4.second_ref.refs_2_, ...), custom_call_target="tpu_custom_call" | custom-call | tf_op jit(solution)/shard_map/gram_and_scores/pallas_call | solution.py:304
  (4 shorter events, 0.0 us)
Async XLA Ops:
  0.6 2.7 %copy-start = (bf16[1,256,2048]{2,1,0:T(8,128)(2,1)S(1)}, bf16[1,256,2048]{2,1,0:T(8,128)(2,1)}, u32[]{:S(2)}) copy-start(bf16[1,256,2048]{2,1,0:T(8,128)(2,1)} %param.6) | copy-start | bytes 3145732
  0.6 2.7 %copy-start.2 = (bf16[1,32,2048]{2,1,0:T(8,128)(2,1)S(1)}, bf16[1,32,2048]{2,1,0:T(8,128)(2,1)}, u32[]{:S(2)}) copy-start(bf16[1,32,2048]{2,1,0:T(8,128)(2,1)} %param.8) | copy-start | bytes 393220
  0.7 3.1 %copy-start.1 = (bf16[1,256,2048]{2,1,0:T(8,128)(2,1)S(1)}, bf16[1,256,2048]{2,1,0:T(8,128)(2,1)}, u32[]{:S(2)}) copy-start(bf16[1,256,2048]{2,1,0:T(8,128)(2,1)} %param.5) | copy-start | bytes 3145732
  0.7 4.8 %collective-permute-start.1 = (bf16[16,512]{1,0:T(8,128)(2,1)}, bf16[16,512]{1,0:T(8,128)(2,1)S(1)}, u32[]{:S(2)}, u32[]{:S(2)}) collective-permute-start(bf16[16,512]{1,0:T(8,128)(2,1)} %bitcast.19), channel_id=1, source_target_pairs={{0,5},{1,4},{2,1},{3,0},{4,13},{5,12},{6,9},{7,8},{8,7},{9,6},{10,... | collective-permute-start | bytes 49160 | tf_op jit(solution)/shard_map/ppermute | solution.py:247
  3.4 0.9 %copy-start.3 = (bf16[1,32,2048]{2,1,0:T(8,128)(2,1)S(1)}, bf16[1,32,2048]{2,1,0:T(8,128)(2,1)}, u32[]{:S(2)}) copy-start(bf16[1,32,2048]{2,1,0:T(8,128)(2,1)} %param.7) | copy-start | bytes 393220
  4.7 1.6 %collective-permute-start = (f32[64,256]{1,0:T(8,128)S(1)}, f32[64,256]{1,0:T(8,128)S(1)}, u32[]{:S(2)}, u32[]{:S(2)}) collective-permute-start(f32[64,256]{1,0:T(8,128)S(1)} %pad_maximum_fusion.refs_0_), channel_id=1, source_target_pairs={{1,0},{0,1},{3,2},{2,3},{5,4},{4,5},{7,6},{6,7},{9,8},{8,9},{11,10... | collective-permute-start | bytes 196616 | tf_op jit(solution)/shard_map/ppermute | solution.py:238
  5.4 1.3 %collective-permute-start.2 = (bf16[16,512]{1,0:T(8,128)(2,1)S(1)}, bf16[16,512]{1,0:T(8,128)(2,1)S(1)}, u32[]{:S(2)}, u32[]{:S(2)}) collective-permute-start(bf16[16,512]{1,0:T(8,128)(2,1)S(1)} %chunk.1), channel_id=1, source_target_pairs={{1,0},{0,1},{3,2},{2,3},{5,4},{4,5},{7,6},{6,7},{9,8},{8,9},{11,10... | collective-permute-start | bytes 49160 | tf_op jit(solution)/shard_map/ppermute | solution.py:238
  6.8 5.2 %collective-permute-start.3 = (bf16[3,16,512]{2,1,0:T(8,128)(2,1)S(1)}, bf16[3,16,512]{2,1,0:T(8,128)(2,1)S(1)}, u32[]{:S(2)}, u32[]{:S(2)}) collective-permute-start(bf16[3,16,512]{2,1,0:T(8,128)(2,1)S(1)} %pad_maximum_fusion.1.refs_0_), channel_id=1, source_target_pairs={{9,0},{13,1},{0,2},{15,3},{7,4},{1,5},{5,6},{3,7},{4,8},{11,9},{6,... | collective-permute-start | bytes 147464 | tf_op jit(solution)/shard_map/ppermute | solution.py:288
  9.2 3.5 %collective-permute-start.4 = (bf16[3,16,512]{2,1,0:T(8,128)(2,1)S(1)}, bf16[3,16,512]{2,1,0:T(8,128)(2,1)S(1)}, u32[]{:S(2)}, u32[]{:S(2)}) collective-permute-start(bf16[3,16,512]{2,1,0:T(8,128)(2,1)S(1)} %pad_maximum_fusion.1.refs_0_), channel_id=1, source_target_pairs={{3,0},{5,1},{7,2},{11,3},{9,4},{13,5},{14,6},{10,7},{12,8},{0,9},{... | collective-permute-start | bytes 147464 | tf_op jit(solution)/shard_map/ppermute | solution.py:288
  12.7 1.3 %collective-permute-start.5 = (bf16[4,16,512]{2,1,0:T(8,128)(2,1)S(1)}, bf16[4,16,512]{2,1,0:T(8,128)(2,1)S(1)}, u32[]{:S(2)}, u32[]{:S(2)}) collective-permute-start(bf16[4,16,512]{2,1,0:T(8,128)(2,1)S(1)} %swap.1), channel_id=1, source_target_pairs={{1,0},{0,1},{3,2},{2,3},{5,4},{4,5},{7,6},{6,7},{9,8},{8,9},{11,10... | collective-permute-start | bytes 196616 | tf_op jit(solution)/shard_map/ppermute | solution.py:238
